TPU v7x, 32 devices: a whole 2x2x4 slice. The times are simulated.
32 devices in a mesh: ctx: 8 (over z, core), fsdp: 4 (over y, x).
Axes of the slice: x: 2, y: 2, z: 4, core: 2. Of those that a mesh axis runs over, the one named last changes fastest.
Arguments:
- layer_input: bfloat16 [4, 1024, 2304], P('fsdp', 'ctx'), may hold values from -6 to 6
- attn_weights: bfloat16 [2304, 6144], P('fsdp'), may hold values from -0.125 to 0.125
- mlp_in_weights: bfloat16 [2304, 18432], P('fsdp'), may hold values from -0.125 to 0.125
- mlp_out_weights: bfloat16 [2304, 9216], P('fsdp'), may hold values from -0.0625 to 0.0625
- norm_gains: bfloat16 [2304, 4], P('fsdp'), may hold values from 0.5 to 1.5
- output_grad: bfloat16 [4, 1024, 2304], P('fsdp', 'ctx'), may hold values from -6 to 6
Outputs:
- layer_output: bfloat16 [4, 1024, 2304], P('fsdp', 'ctx')
- input_grad: float32 [4, 1024, 2304], P('fsdp', 'ctx')
- attn_weights_grad: float32 [2304, 6144], P(('ctx', 'fsdp'))
- mlp_in_grad: float32 [2304, 18432], P(('ctx', 'fsdp'))
- mlp_out_grad: float32 [2304, 9216], P(('ctx', 'fsdp'))
- norm_gains_grad: float32 [2304, 4], P(('ctx', 'fsdp'))
All inputs are finite; a program needn't handle non-finite values.
Results may differ from a plain program's by a relative error of at most 0.02.
Values may be sent and summed in bfloat16 or wider, within the bound.
No kernel may reach another device: no remote copies, remote signals or barrier semaphores. Data moves between devices by JAX's collectives and lax.ppermute only.
A program may use at most 448 MiB of HBM per device.

v0:
```python
import jax
import jax.numpy as jnp
from jax import lax
from jax.sharding import PartitionSpec as P

HEADS = 8
KV_HEADS = 4
HEAD_DIM = 256


EPSILON = 1e-06
SOFT_CAP = 50.0
ROTARY_BASE = 10000.0
MASKED_SCORE = -1e30


def positions_of(rows, half_block, ctx_count):
    owners = rows // (2 * half_block)
    within = rows % (2 * half_block)
    return jnp.where(
        within < half_block,
        owners * half_block + within,
        (2 * ctx_count - 1 - owners) * half_block + within - half_block,
    )


def rotary_tables(places, head_dim):
    half_width = head_dim // 2
    frequency = ROTARY_BASE ** (-jnp.arange(half_width, dtype=jnp.float32) * 2.0 / head_dim)
    angles = places.astype(jnp.float32)[:, None] * frequency[None, :]
    cosine = jnp.concatenate([jnp.cos(angles), jnp.cos(angles)], -1)[:, None, :]
    sine_table = jnp.concatenate([jnp.sin(angles), jnp.sin(angles)], -1)[:, None, :]
    return (cosine, sine_table)


def turned(values):
    half_width = values.shape[-1] // 2
    return jnp.concatenate([-values[..., half_width:], values[..., :half_width]], -1)


def rotate(values, cosine, sine_table):
    return values * cosine + turned(values) * sine_table


def rotate_back(grads, cosine, sine_table):
    return grads * cosine - turned(grads * sine_table)


def inverse_rms(values):
    return lax.rsqrt(jnp.mean(values * values, -1, keepdims=True) + EPSILON)


def norm_backward(values, scale, grad_normed):
    normed = values * scale
    return scale * (grad_normed - normed * jnp.mean(grad_normed * normed, -1, keepdims=True))


def geglu(gate, upper):
    return jax.nn.gelu(gate, approximate=True) * upper


def local(layer_input, attn_weights, mlp_in_weights, mlp_out_weights, norm_gains, output_grad):
    tokens = layer_input.shape[1]
    model_width = layer_input.shape[2]
    half_block = tokens // 2
    ctx_count = lax.axis_size("ctx")
    fsdp_count = lax.axis_size("fsdp")
    head_dim = HEAD_DIM
    head_count = HEADS
    kv_heads = KV_HEADS
    groups = head_count // kv_heads
    query_cols = head_count * head_dim
    key_cols = kv_heads * head_dim
    scaling = head_dim ** (-0.5)
    attn_all, gain_all = (
        lax.all_gather(attn_weights, "fsdp", axis=0, tiled=True),
        lax.all_gather(norm_gains, "fsdp", axis=0, tiled=True),
    )
    gain_f = gain_all.astype(jnp.float32)
    g_pre = gain_f[:, 0]
    g_post = gain_f[:, 1]
    g_mid = gain_f[:, 2]
    g_out = gain_f[:, 3]
    source = layer_input.reshape(tokens, model_width).astype(jnp.float32)
    own_rows = lax.axis_index("ctx") * tokens + jnp.arange(tokens, dtype=jnp.int32)
    own_place = positions_of(own_rows, half_block, ctx_count)
    cosine, sine_table = rotary_tables(own_place, head_dim)
    scale_in = inverse_rms(source)
    normed_in = (source * scale_in * g_pre).astype(jnp.bfloat16)
    projected = jnp.dot(
        normed_in, attn_all[:, : query_cols + 2 * key_cols], preferred_element_type=jnp.float32
    )
    query_raw = projected[:, :query_cols].reshape(tokens, head_count, head_dim)
    key_raw = projected[:, query_cols : query_cols + key_cols].reshape(tokens, kv_heads, head_dim)
    query = (
        rotate(query_raw, cosine, sine_table)
        .astype(jnp.bfloat16)
        .reshape(tokens, kv_heads, groups, head_dim)
    )
    key_own = rotate(key_raw, cosine, sine_table).astype(jnp.bfloat16).reshape(tokens, key_cols)
    value_own = projected[:, query_cols + key_cols :].astype(jnp.bfloat16)
    key_all, value_all = (
        lax.all_gather(key_own, "ctx", axis=0, tiled=True),
        lax.all_gather(value_own, "ctx", axis=0, tiled=True),
    )
    length = key_all.shape[0]
    key_all = key_all.reshape(length, kv_heads, head_dim)
    value_all = value_all.reshape(length, kv_heads, head_dim)
    key_place = positions_of(jnp.arange(length, dtype=jnp.int32), half_block, ctx_count)
    allowed = key_place[None, :] <= own_place[:, None]

    def score_rows(query_rows):
        raw_scores = jnp.einsum(
            "tkgd,lkd->kgtl", query_rows, key_all, preferred_element_type=jnp.float32
        )
        tanh_part = jnp.tanh(raw_scores * scaling / SOFT_CAP)
        capped = jnp.where(allowed, SOFT_CAP * tanh_part, MASKED_SCORE)
        return (tanh_part, capped)

    tanh_part, capped = score_rows(query)
    row_max = jnp.max(capped, -1, keepdims=True)
    weights = jnp.exp(capped - row_max)
    row_total = jnp.sum(weights, -1, keepdims=True)
    log_total = row_max + jnp.log(row_total)
    chances = (weights / row_total).astype(jnp.bfloat16)
    attended = jnp.einsum("kgtl,lkd->tkgd", chances, value_all, preferred_element_type=jnp.float32)
    attended = attended.reshape(tokens, query_cols).astype(jnp.bfloat16)
    out_proj = attn_all[:, query_cols + 2 * key_cols :]
    branch = jnp.einsum("tq,dq->td", attended, out_proj, preferred_element_type=jnp.float32)
    scale_branch = inverse_rms(branch)
    residual = source + branch * scale_branch * g_post
    scale_mid = inverse_rms(residual)
    normed_mid = (residual * scale_mid * g_mid).astype(jnp.bfloat16)
    mlp_in_all, mlp_out_all = (
        lax.all_gather(mlp_in_weights, "fsdp", axis=0, tiled=True),
        lax.all_gather(mlp_out_weights, "fsdp", axis=0, tiled=True),
    )
    hidden_width = mlp_out_all.shape[1]
    gate_up = jnp.dot(normed_mid, mlp_in_all, preferred_element_type=jnp.float32)
    hidden, geglu_back = jax.vjp(geglu, gate_up[:, :hidden_width], gate_up[:, hidden_width:])
    hidden_b = hidden.astype(jnp.bfloat16)
    mixed = jnp.einsum("tf,df->td", hidden_b, mlp_out_all, preferred_element_type=jnp.float32)
    scale_mixed = inverse_rms(mixed)
    block_out = (
        (residual + mixed * scale_mixed * g_out).astype(jnp.bfloat16).reshape(layer_input.shape)
    )
    attn_back = lax.all_gather(attn_weights, "fsdp", axis=0, tiled=True)
    mlp_in_back, mlp_out_back = (
        lax.all_gather(mlp_in_weights, "fsdp", axis=0, tiled=True),
        lax.all_gather(mlp_out_weights, "fsdp", axis=0, tiled=True),
    )
    upstream = output_grad.reshape(tokens, model_width).astype(jnp.float32)
    shard_rows = model_width // lax.axis_size(("ctx", "fsdp"))
    grad_out_gain = jnp.sum(upstream * mixed * scale_mixed, 0)
    d_mixed = norm_backward(mixed, scale_mixed, upstream * g_out).astype(jnp.bfloat16)
    d_hidden = jnp.dot(d_mixed, mlp_out_back, preferred_element_type=jnp.float32)
    d_gate, d_upper = geglu_back(d_hidden)
    d_gate_up = jnp.concatenate([d_gate, d_upper], 1).astype(jnp.bfloat16)
    d_normed_mid = jnp.einsum(
        "tf,df->td", d_gate_up, mlp_in_back, preferred_element_type=jnp.float32
    )
    grad_mid_gain = jnp.sum(d_normed_mid * residual * scale_mid, 0)
    d_residual = upstream + norm_backward(residual, scale_mid, d_normed_mid * g_mid)
    grad_post_gain = jnp.sum(d_residual * branch * scale_branch, 0)
    d_branch = norm_backward(branch, scale_branch, d_residual * g_post).astype(jnp.bfloat16)
    back_proj = attn_back[:, query_cols + 2 * key_cols :]
    d_attended = jnp.dot(d_branch, back_proj, preferred_element_type=jnp.float32)
    d_attended = d_attended.astype(jnp.bfloat16).reshape(tokens, kv_heads, groups, head_dim)
    tanh_again, capped_again = score_rows(query)
    chances_f = jnp.exp(capped_again - log_total)
    chances_b = chances_f.astype(jnp.bfloat16)
    d_values = jnp.einsum(
        "kgtl,tkgd->lkd", chances_b, d_attended, preferred_element_type=jnp.float32
    )
    d_chances = jnp.einsum(
        "tkgd,lkd->kgtl", d_attended, value_all, preferred_element_type=jnp.float32
    )
    row_inner = jnp.sum(chances_f * d_chances, -1, keepdims=True)
    d_raw = (
        chances_f * (d_chances - row_inner) * (1.0 - tanh_again * tanh_again) * scaling
    ).astype(jnp.bfloat16)
    d_query = jnp.einsum("kgtl,lkd->tkgd", d_raw, key_all, preferred_element_type=jnp.float32)
    d_keys = jnp.einsum("kgtl,tkgd->lkd", d_raw, query, preferred_element_type=jnp.float32)
    d_key_own, d_value_own = (
        lax.psum_scatter(
            d_keys.reshape(length, key_cols).astype(jnp.bfloat16),
            "ctx",
            scatter_dimension=0,
            tiled=True,
        ).astype(jnp.float32),
        lax.psum_scatter(
            d_values.reshape(length, key_cols).astype(jnp.bfloat16),
            "ctx",
            scatter_dimension=0,
            tiled=True,
        ).astype(jnp.float32),
    )
    d_query_raw = rotate_back(
        d_query.reshape(tokens, head_count, head_dim), cosine, sine_table
    ).reshape(tokens, query_cols)
    d_key_raw = rotate_back(
        d_key_own.reshape(tokens, kv_heads, head_dim), cosine, sine_table
    ).reshape(tokens, key_cols)
    d_projected = jnp.concatenate([d_query_raw, d_key_raw, d_value_own], 1).astype(jnp.bfloat16)
    d_normed_in = jnp.einsum(
        "tc,dc->td",
        d_projected,
        attn_back[:, : query_cols + 2 * key_cols],
        preferred_element_type=jnp.float32,
    )
    grad_pre_gain = jnp.sum(d_normed_in * source * scale_in, 0)
    d_source = d_residual + norm_backward(source, scale_in, d_normed_in * g_pre)
    grad_gain_local = jnp.stack([grad_pre_gain, grad_post_gain, grad_mid_gain, grad_out_gain], 1)
    mid_rows, dmix_rows, in_rows, dbranch_rows = (
        lax.all_gather(normed_mid, "ctx", axis=0, tiled=True),
        lax.all_gather(d_mixed, "ctx", axis=0, tiled=True),
        lax.all_gather(normed_in, "ctx", axis=0, tiled=True),
        lax.all_gather(d_branch, "ctx", axis=0, tiled=True),
    )
    hidden_cols, dgu_cols, dproj_cols, attended_cols = (
        lax.all_to_all(hidden_b, "ctx", split_axis=1, concat_axis=0, tiled=True),
        lax.all_to_all(d_gate_up, "ctx", split_axis=1, concat_axis=0, tiled=True),
        lax.all_to_all(d_projected, "ctx", split_axis=1, concat_axis=0, tiled=True),
        lax.all_to_all(attended, "ctx", split_axis=1, concat_axis=0, tiled=True),
    )

    def owner_term(left_rows, right_cols):
        grouped = left_rows.reshape(left_rows.shape[0], ctx_count, fsdp_count, shard_rows)
        product = jnp.einsum(
            "tcfr,tn->fcrn", grouped, right_cols, preferred_element_type=jnp.float32
        )
        return product.reshape(model_width, right_cols.shape[1])

    part_down = owner_term(dmix_rows, hidden_cols)
    part_gate_up = owner_term(mid_rows, dgu_cols)
    part_projection = owner_term(in_rows, dproj_cols)
    part_out_proj = owner_term(dbranch_rows, attended_cols)
    part_gains = (
        grad_gain_local.reshape(ctx_count, fsdp_count, shard_rows, 4)
        .transpose(1, 0, 2, 3)
        .reshape(model_width, 4)
    )
    sum_down, sum_gate_up, sum_projection, sum_out_proj, sum_gains = (
        lax.psum_scatter(
            part_down.astype(jnp.bfloat16), "fsdp", scatter_dimension=0, tiled=True
        ).astype(jnp.float32),
        lax.psum_scatter(
            part_gate_up.astype(jnp.bfloat16), "fsdp", scatter_dimension=0, tiled=True
        ).astype(jnp.float32),
        lax.psum_scatter(
            part_projection.astype(jnp.bfloat16), "fsdp", scatter_dimension=0, tiled=True
        ).astype(jnp.float32),
        lax.psum_scatter(
            part_out_proj.astype(jnp.bfloat16), "fsdp", scatter_dimension=0, tiled=True
        ).astype(jnp.float32),
        lax.psum_scatter(
            part_gains.astype(jnp.bfloat16), "fsdp", scatter_dimension=0, tiled=True
        ).astype(jnp.float32),
    )
    grad_mlp_out, grad_mlp_in, owned_projection, owned_out_proj, owned_gains = (
        lax.all_to_all(
            sum_down.astype(jnp.bfloat16), "ctx", split_axis=0, concat_axis=1, tiled=True
        ).astype(sum_down.dtype),
        lax.all_to_all(
            sum_gate_up.astype(jnp.bfloat16), "ctx", split_axis=0, concat_axis=1, tiled=True
        ).astype(sum_gate_up.dtype),
        lax.all_to_all(
            sum_projection.astype(jnp.bfloat16), "ctx", split_axis=0, concat_axis=1, tiled=True
        ).astype(sum_projection.dtype),
        lax.all_to_all(
            sum_out_proj.astype(jnp.bfloat16), "ctx", split_axis=0, concat_axis=1, tiled=True
        ).astype(sum_out_proj.dtype),
        lax.all_to_all(
            sum_gains.astype(jnp.bfloat16), "ctx", split_axis=0, concat_axis=1, tiled=True
        ).astype(sum_gains.dtype),
    )
    grad_attn = jnp.concatenate([owned_projection, owned_out_proj], 1)
    grad_gains = jnp.sum(owned_gains.reshape(shard_rows, ctx_count, 4), 1)
    return (
        block_out,
        d_source.reshape(layer_input.shape),
        grad_attn,
        grad_mlp_in,
        grad_mlp_out,
        grad_gains,
    )


def solution(mesh):
    in_specs = (
        P("fsdp", "ctx", None),
        P("fsdp", None),
        P("fsdp", None),
        P("fsdp", None),
        P("fsdp", None),
        P("fsdp", "ctx", None),
    )
    out_specs = (
        P("fsdp", "ctx", None),
        P("fsdp", "ctx", None),
        P(("ctx", "fsdp"), None),
        P(("ctx", "fsdp"), None),
        P(("ctx", "fsdp"), None),
        P(("ctx", "fsdp"), None),
    )
    return jax.shard_map(local, mesh=mesh, in_specs=in_specs, out_specs=out_specs, check_vma=False)
```

profile of v0, /device:TPU:13, one launch (start us, length us, event | category | flops | bytes accessed | tf_op | source)
XLA Modules:
  0.0 2335.9 jit_solution(6841066908514255005)
XLA Ops:
  8.0 6.1 all-gather
  16.3 248.3 %all-gather.11.cloned.1.call-done = bf16[2304,6144]{1,0:T(8,128)(2,1)} async-done(((bf16[576,6144]{1,0:T(8,128)(2,1)}), bf16[2304,6144]{1,0:T(8,128)(2,1)}) %all-gather.11.cloned.1.call-update) | async-done | bytes 28311568 | tf_op jit(solution)/shard_map/all_gather | solution.py:76
  264.6 7.8 fusion.3
  274.5 1.8 add_convert_fusion.1
  276.4 1.8 slice.131
  283.0 23.0 all-gather.15.cloned.1.call-done
  306.0 4.6 reshape.292
  310.7 4.4 copy.149
  315.1 21.8 all-gather.13.cloned.1.call-done
  336.8 4.5 reshape.290
  341.4 2.9 fusion.39
  345.6 2.1 copy-done.6
  347.7 1.9 fusion.42
  349.7 9.3 multiply_reduce_fusion.6
  361.2 703.0 %all-gather.17.cloned.1.call-done = bf16[2304,18432]{1,0:T(8,128)(2,1)} async-done(((bf16[576,18432]{1,0:T(8,128)(2,1)}), bf16[2304,18432]{1,0:T(8,128)(2,1)}) %all-gather.17.cloned.1.call-update) | async-done | bytes 84934672 | tf_op jit(solution)/shard_map/all_gather | solution.py:135
  1064.2 42.7 %fusion.104 = f32[128,18432]{1,0:T(8,128)} fusion(bf16[128,2304]{1,0:T(8,128)(2,1)S(1)} %multiply_convert_fusion.3, bf16[2304,18432]{1,0:T(8,128)(2,1)} %all-gather.17.cloned.1.call-done), kind=kOutput, calls=%fused_computation.182 | convolution fusion | flops 10871635968 | bytes 94961664 | tf_op jit(solution)/shard_map/dot_general | solution.py:139
  1106.9 4.6 multiply_convert_fusion.1
  1111.5 326.3 %all-gather.19.cloned.1.call-done = bf16[2304,9216]{1,0:T(8,128)(2,1)} async-done(((bf16[576,9216]{1,0:T(8,128)(2,1)}), bf16[2304,9216]{1,0:T(8,128)(2,1)}) %all-gather.19.cloned.1.call-update) | async-done | bytes 42467344 | tf_op jit(solution)/shard_map/all_gather | solution.py:136
  1437.8 21.5 multiply_reduce_fusion.4
  1460.0 2.5 fusion.55
  1462.4 2.8 fusion.47
  1465.3 21.8 fusion.15
  1487.1 37.9 %multiply_reduce_fusion = (bf16[2304]{0:T(1024)(128)(2,1)}, f32[128]{0:T(128)}, f32[128,2304]{1,0:T(8,128)}) fusion(f32[128,2304]{1,0:T(8,128)S(1)} %get-tuple-element.20, f32[128]{0:T(128)} %copy-done.36, f32[2304]{0:T(1024)} %get-tuple-element.15, bf16[2304,18432]{1,0:T(8,128)(2,1)} %all-gather.17.cloned.1.call-done, ...), kind=kOutput, calls=%fused_computation.86 | convolution fusion | flops 10883135488 | bytes 92027392 | tf_op jit(solution)/shard_map/tf,df->td/dot_general | solution.py:159
  1525.7 3.1 multiply_reduce_fusion.1
  1530.1 6.1 fusion.25
  1537.5 4.3 fusion.33
  1541.8 11.3 bitcast_convert_fusion.1
  1553.1 4.0 copy.164
  1557.2 5.2 bitcast_convert_fusion
  1562.4 4.0 copy.165
  1569.3 24.9 %all_to_all.132 = bf16[128,8,256]{0,2,1:T(8,128)(2,1)S(1)} all-to-all(bf16[128,8,256]{0,2,1:T(8,128)(2,1)S(1)} %bitcast.275), channel_id=1, replica_groups=mesh['ctx'=8,'fsdp'=4] {'ctx'}, dimensions={1} | all-to-all | bytes 1048576 | tf_op jit(solution)/shard_map/all_to_all | solution.py:224
  1595.2 10.4 fusion.38
  1611.6 20.3 reduce-scatter.22.cloned.1.call-done
  1634.5 10.4 all-to-all-start
  1644.9 16.1 fusion.58
  1662.2 44.0 %all-gather.23.cloned.1.call-done = bf16[1024,2304]{1,0:T(8,128)(2,1)} async-done(((bf16[128,2304]{1,0:T(8,128)(2,1)}), bf16[1024,2304]{1,0:T(8,128)(2,1)}) %all-gather.23.cloned.1.call-update) | async-done | bytes 4718608 | tf_op jit(solution)/shard_map/all_gather | solution.py:218
  1706.2 3.9 fusion.106
  1710.1 9.2 all-to-all-start.6
  1720.6 81.1 %all-gather.21.cloned.1.call-done = bf16[1024,2304]{1,0:T(8,128)(2,1)} async-done(((bf16[128,2304]{1,0:T(8,128)(2,1)}), bf16[1024,2304]{1,0:T(8,128)(2,1)}) %all-gather.21.cloned.1.call-update) | async-done | bytes 4718608 | tf_op jit(solution)/shard_map/all_gather | solution.py:217
  1801.7 4.8 fusion.105
  1808.5 2.0 copy.195
  1811.0 2.6 pad_maximum_fusion
  1813.6 10.1 all-to-all-start.4
  1823.7 70.4 %all-gather.27.cloned.1.call-done = bf16[1024,2304]{1,0:T(8,128)(2,1)} async-done(((bf16[128,2304]{1,0:T(8,128)(2,1)}), bf16[1024,2304]{1,0:T(8,128)(2,1)}) %all-gather.27.cloned.1.call-update) | async-done | bytes 4718608 | tf_op jit(solution)/shard_map/all_gather | solution.py:216
  1894.1 11.6 fusion.108
  1905.6 5.3 convert_bitcast_fusion.2
  1910.9 2.8 copy.140
  1913.8 68.7 %all-gather.25.cloned.1.call-done = bf16[1024,2304]{1,0:T(8,128)(2,1)} async-done(((bf16[128,2304]{1,0:T(8,128)(2,1)}), bf16[1024,2304]{1,0:T(8,128)(2,1)}) %all-gather.25.cloned.1.call-update) | async-done | bytes 4718608 | tf_op jit(solution)/shard_map/all_gather | solution.py:215
  1982.5 9.7 all-to-all-done.4
  1992.3 14.8 fusion.107
  2008.2 4.7 copy.136
  2013.0 4.0 reduce-scatter.24.cloned.1.call-done
  2018.1 9.1 all_to_all.133
  2027.2 21.7 reduce-scatter.16.cloned.1.call-done
  2048.9 5.4 all-to-all-start.3
  2054.3 35.2 %reduce-scatter.14.cloned.1.call-done = bf16[576,512]{1,0:T(8,128)(2,1)} async-done(((bf16[2304,512]{1,0:T(8,128)(2,1)}), bf16[576,512]{1,0:T(8,128)(2,1)}) %reduce-scatter.14.cloned.1.call-update) | async-done | bytes 589840 | tf_op jit(solution)/shard_map/reduce_scatter | solution.py:250
  2089.5 20.6 all_to_all.134
  2110.0 45.1 %reduce-scatter.20.cloned.1.call-done = bf16[576,1152]{1,0:T(8,128)(2,1)} async-done(((bf16[2304,1152]{1,0:T(8,128)(2,1)}), bf16[576,1152]{1,0:T(8,128)(2,1)}) %reduce-scatter.20.cloned.1.call-update) | async-done | bytes 1327120 | tf_op jit(solution)/shard_map/reduce_scatter | solution.py:244
  2155.1 36.5 %all_to_all.135 = bf16[8,72,1152]{2,1,0:T(8,128)(2,1)} all-to-all(bf16[8,72,1152]{2,1,0:T(8,128)(2,1)} %bitcast.270), channel_id=1, replica_groups=mesh['ctx'=8,'fsdp'=4] {'ctx'}, dimensions={0} | all-to-all | bytes 2654208 | tf_op jit(solution)/shard_map/all_to_all | solution.py:261
  2191.6 71.4 %reduce-scatter.18.cloned.1.call-done = bf16[576,2304]{1,0:T(8,128)(2,1)} async-done(((bf16[2304,2304]{1,0:T(8,128)(2,1)}), bf16[576,2304]{1,0:T(8,128)(2,1)}) %reduce-scatter.18.cloned.1.call-update) | async-done | bytes 2654224 | tf_op jit(solution)/shard_map/reduce_scatter | solution.py:247
  2263.0 5.4 all-to-all-start.5
  2269.2 3.1 fusion.53
  2277.0 48.9 %all-to-all-done.5 = bf16[8,72,2304]{2,1,0:T(8,128)(2,1)S(1)} async-done(((bf16[8,72,2304]{2,1,0:T(8,128)(2,1)}), bf16[8,72,2304]{2,1,0:T(8,128)(2,1)S(1)}, u32[]{:S(2)}, u32[]{:S(2)}) %all-to-all-start.5) | async-done | bytes 2654240 | tf_op jit(solution)/shard_map/all_to_all | solution.py:264
  2326.3 2.8 copy.179
  (193 shorter events, 42.4 us)
Async XLA Ops:
  7.2 0.8 copy-start.35
  7.2 8.7 copy-start.4
  7.2 257.4 %all-gather.11.cloned.1.call-start = ((), (), s32[]{:S(2)}) async-start(), calls=%async_computation.16 | async-start | bytes 35389440 | tf_op jit(solution)/shard_map/all_gather | solution.py:76
  7.9 298.1 %all-gather.15.cloned.1.call-start = ((), (), s32[]{:S(2)}) async-start(), calls=%async_computation.18 | async-start | bytes 2359296 | tf_op jit(solution)/shard_map/all_gather | solution.py:103
  14.6 268.3 %copy-start.16 = (f32[128,256]{0,1:T(8,128)}, f32[128,256]{0,1:T(8,128)S(1)}, u32[]{:S(2)}) copy-start(f32[128,256]{0,1:T(8,128)S(1)} %get-tuple-element.44) | copy-start | bytes 393220
  14.6 268.3 %copy-start.19 = (f32[128,256]{0,1:T(8,128)}, f32[128,256]{0,1:T(8,128)S(1)}, u32[]{:S(2)}) copy-start(f32[128,256]{0,1:T(8,128)S(1)} %get-tuple-element.43) | copy-start | bytes 393220
  14.7 259.5 %copy-start.21 = (f32[128,256]{1,0:T(8,128)}, f32[128,256]{1,0:T(8,128)S(1)}, u32[]{:S(2)}) copy-start(f32[128,256]{1,0:T(8,128)S(1)} %copy.108) | copy-start | bytes 393220
  15.0 259.5 %copy-start.9 = (f32[16,8,4,256]{3,1,2,0:T(8,128)}, f32[16,8,4,256]{3,1,2,0:T(8,128)S(1)}, u32[]{:S(2)}) copy-start(f32[16,8,4,256]{3,1,2,0:T(8,128)S(1)} %copy.181) | copy-start | bytes 1572868
  15.8 256.6 %copy-start.30 = (f32[2304]{0:T(1024)}, f32[2304]{0:T(1024)S(1)}, u32[]{:S(2)}) copy-start(f32[2304]{0:T(1024)S(1)} %get-tuple-element.17) | copy-start | bytes 27652
  16.1 256.4 %copy-start.38 = (f32[128]{0:T(128)}, f32[128]{0:T(128)S(1)}, u32[]{:S(2)}) copy-start(f32[128]{0:T(128)S(1)} %add_rsqrt_fusion.3) | copy-start | bytes 1540
  16.3 256.2 %copy-start.13 = (bf16[128,2304]{1,0:T(8,128)(2,1)}, bf16[128,2304]{1,0:T(8,128)(2,1)S(1)}, u32[]{:S(2)}) copy-start(bf16[128,2304]{1,0:T(8,128)(2,1)S(1)} %fusion.48) | copy-start | bytes 1769476
  272.5 1.3 copy-start.12
  276.4 60.5 %all-gather.13.cloned.1.call-start = ((), (), s32[]{:S(2)}) async-start(), calls=%async_computation.17 | async-start | bytes 2359296 | tf_op jit(solution)/shard_map/all_gather | solution.py:104
  278.2 786.0 %all-gather.17.cloned.1.call-start = ((), (), s32[]{:S(2)}) async-start(), calls=%async_computation.19 | async-start | bytes 106168320 | tf_op jit(solution)/shard_map/all_gather | solution.py:135
  278.8 1159.0 %all-gather.19.cloned.1.call-start = ((), (), s32[]{:S(2)}) async-start(), calls=%async_computation.20 | async-start | bytes 53084160 | tf_op jit(solution)/shard_map/all_gather | solution.py:136
  279.4 1330.1 %reduce-scatter.12.cloned.1.call-start = ((), (), s32[]{:S(2)}) async-start(), calls=%async_computation.21 | async-start | bytes 2359296 | tf_op jit(solution)/shard_map/reduce_scatter | solution.py:185
  283.0 58.3 %copy-start.28 = (bf16[128,4,2,256]{0,3,2,1:T(8,128)(2,1)}, bf16[128,4,2,256]{0,3,2,1:T(8,128)(2,1)S(1)}, u32[]{:S(2)}) copy-start(bf16[128,4,2,256]{0,3,2,1:T(8,128)(2,1)S(1)} %fusion.60) | copy-start | bytes 1572868
  310.7 30.7 %copy-start.24 = (pred[128,1024]{0,1:T(8,128)(4,1)S(1)}, pred[128,1024]{0,1:T(8,128)(4,1)}, u32[]{:S(2)}) copy-start(pred[128,1024]{0,1:T(8,128)(4,1)} %broadcast_compare_fusion) | copy-start | bytes 393220
  344.3 5.3 copy-start.11
  344.3 3.4 copy-start.6
  349.7 9.3 copy-start.26
  349.7 11.3 copy-start.29
  359.0 1.0 copy-start.1
  360.4 703.8 %copy-start.36 = (f32[128]{0:T(128)}, f32[128]{0:T(128)S(1)}, u32[]{:S(2)}) copy-start(f32[128]{0:T(128)S(1)} %add_rsqrt_fusion.1) | copy-start | bytes 1540
  361.2 703.0 %copy-start.7 = (bf16[128,2304]{1,0:T(8,128)(2,1)}, bf16[128,2304]{1,0:T(8,128)(2,1)S(1)}, u32[]{:S(2)}) copy-start(bf16[128,2304]{1,0:T(8,128)(2,1)S(1)} %multiply_convert_fusion.3) | copy-start | bytes 1769476
  1525.0 4.8 copy-start.2
  1528.8 1.0 copy-start
  1530.1 6.1 copy-start.15
  1536.2 5.6 copy-start.37
  1537.5 4.3 copy-start.25
  1557.2 74.8 %reduce-scatter.22.cloned.1.call-start = ((), (), s32[]{:S(2)}) async-start(), calls=%async_computation.30 | async-start | bytes 2359296
  1562.4 6.9 copy-start.27
  1566.4 139.8 %all-gather.23.cloned.1.call-start = ((), (), s32[]{:S(2)}) async-start(), calls=%async_computation.24 | async-start | bytes 5308416 | tf_op jit(solution)/shard_map/all_gather | solution.py:218
  1567.2 234.6 %all-gather.21.cloned.1.call-start = ((), (), s32[]{:S(2)}) async-start(), calls=%async_computation.22 | async-start | bytes 5308416 | tf_op jit(solution)/shard_map/all_gather | solution.py:217
  1567.9 326.1 %all-gather.27.cloned.1.call-start = ((), (), s32[]{:S(2)}) async-start(), calls=%async_computation.28 | async-start | bytes 5308416 | tf_op jit(solution)/shard_map/all_gather | solution.py:216
  1568.5 414.0 %all-gather.25.cloned.1.call-start = ((), (), s32[]{:S(2)}) async-start(), calls=%async_computation.26 | async-start | bytes 5308416 | tf_op jit(solution)/shard_map/all_gather | solution.py:215
  1595.2 10.4 copy-start.17
  1605.6 0.9 copy-start.20
  1606.5 2.7 copy-start.33
  1606.5 2.8 copy-start.32
  1606.5 4.3 copy-start.22
  1607.5 1.9 copy-start.34
  1609.2 2.1 copy-start.10
  1609.2 23.8 %copy-start.18 = (bf16[128,2048]{0,1:T(8,128)(2,1)S(1)}, bf16[128,2048]{0,1:T(8,128)(2,1)}, u32[]{:S(2)}) copy-start(bf16[128,2048]{0,1:T(8,128)(2,1)} %fusion.61) | copy-start | bytes 1572868
  1609.5 1.8 copy-start.23
  1611.3 33.5 %copy-start.5 = (bf16[1,128,2304]{2,1,0:T(8,128)(2,1)S(1)}, bf16[1,128,2304]{2,1,0:T(8,128)(2,1)}, u32[]{:S(2)}) copy-start(bf16[1,128,2304]{2,1,0:T(8,128)(2,1)} %param.6) | copy-start | bytes 1769476
  1611.3 33.5 %copy-start.31 = (f32[2304]{0:T(1024)S(1)}, f32[2304]{0:T(1024)}, u32[]{:S(2)}) copy-start(f32[2304]{0:T(1024)} %copy-done.30) | copy-start | bytes 27652
  1611.3 33.5 %copy-start.39 = (f32[128]{0:T(128)S(1)}, f32[128]{0:T(128)}, u32[]{:S(2)}) copy-start(f32[128]{0:T(128)} %copy-done.38) | copy-start | bytes 1540
  1634.5 75.7 %all-to-all-start = ((bf16[128,8,512]{2,0,1:T(8,128)(2,1)}), bf16[128,8,512]{2,0,1:T(8,128)(2,1)}, u32[]{:S(2)}, u32[]{:S(2)}) async-start(bf16[128,8,512]{2,0,1:T(8,128)(2,1)} %copy.125), calls=%async_computation.1 | async-start | bytes 2097152 | tf_op jit(solution)/shard_map/all_to_all | solution.py:223
  1644.8 372.2 %reduce-scatter.24.cloned.1.call-start = ((), (), s32[]{:S(2)}) async-start(), calls=%async_computation.31 | async-start | bytes 737280
  1710.1 103.4 %all-to-all-start.6 = ((bf16[128,8,1152]{2,0,1:T(8,128)(2,1)}), bf16[128,8,1152]{2,0,1:T(8,128)(2,1)}, u32[]{:S(2)}, u32[]{:S(2)}) async-start(bf16[128,8,1152]{2,0,1:T(8,128)(2,1)} %bitcast.224), calls=%async_computation.10 | async-start | bytes 4718592 | tf_op jit(solution)/shard_map/all_to_all | solution.py:221
  1719.3 329.6 %reduce-scatter.16.cloned.1.call-start = ((), (), s32[]{:S(2)}) async-start(), calls=%async_computation.25 | async-start | bytes 1474560 | tf_op jit(solution)/shard_map/reduce_scatter | solution.py:253
  1720.6 368.9 %reduce-scatter.14.cloned.1.call-start = ((), (), s32[]{:S(2)}) async-start(), calls=%async_computation.23 | async-start | bytes 2949120 | tf_op jit(solution)/shard_map/reduce_scatter | solution.py:250
  1808.5 2.4 copy-start.3
  1813.6 178.7 %all-to-all-start.4 = ((bf16[128,8,2304]{2,0,1:T(8,128)(2,1)}), bf16[128,8,2304]{2,0,1:T(8,128)(2,1)}, u32[]{:S(2)}, u32[]{:S(2)}) async-start(bf16[128,8,2304]{2,0,1:T(8,128)(2,1)} %pad_maximum_fusion), calls=%async_computation.7 | async-start | bytes 9437184 | tf_op jit(solution)/shard_map/all_to_all | solution.py:222
  1823.7 331.4 %reduce-scatter.20.cloned.1.call-start = ((), (), s32[]{:S(2)}) async-start(), calls=%async_computation.29 | async-start | bytes 6635520 | tf_op jit(solution)/shard_map/reduce_scatter | solution.py:244
  1913.8 349.2 %reduce-scatter.18.cloned.1.call-start = ((), (), s32[]{:S(2)}) async-start(), calls=%async_computation.27 | async-start | bytes 13271040 | tf_op jit(solution)/shard_map/reduce_scatter | solution.py:247
  2048.9 40.6 %all-to-all-start.3 = ((bf16[8,72,256]{2,1,0:T(8,128)(2,1)}), bf16[8,72,256]{2,1,0:T(8,128)(2,1)S(1)}, u32[]{:S(2)}, u32[]{:S(2)}) async-start(bf16[8,72,256]{2,1,0:T(8,128)(2,1)} %bitcast.277), calls=%async_computation.6 | async-start | bytes 589824 | tf_op jit(solution)/shard_map/all_to_all | solution.py:270
  2263.0 62.9 %all-to-all-start.5 = ((bf16[8,72,2304]{2,1,0:T(8,128)(2,1)}), bf16[8,72,2304]{2,1,0:T(8,128)(2,1)S(1)}, u32[]{:S(2)}, u32[]{:S(2)}) async-start(bf16[8,72,2304]{2,1,0:T(8,128)(2,1)} %bitcast.252), calls=%async_computation.9 | async-start | bytes 5308416 | tf_op jit(solution)/shard_map/all_to_all | solution.py:264
  2268.5 5.2 copy-start.14
  2269.2 5.9 copy-start.8
Sparse Core Ops, SparseCore 0:
  9.9 254.6 all-gather.10
  276.5 29.5 all-gather.14
  308.2 28.5 all-gather.12
  338.6 725.5 all-gather.16
  1065.9 371.8 all-gather.18
  1557.3 42.7 reduce-scatter.11
  1602.4 29.4 reduce-scatter.21
  1633.6 72.6 all-gather.22
  1707.9 93.8 all-gather.20
  1803.2 90.7 all-gather.26
  1895.7 86.7 all-gather.24
  1985.2 31.7 reduce-scatter.23
  2020.2 28.6 reduce-scatter.15
  2052.1 37.3 reduce-scatter.13
  2093.2 61.8 reduce-scatter.19
  2158.4 104.6 reduce-scatter.17
where the time goes:
time: 2350 us; the launch traced here: 2340 us
  waiting for transfers between devices  1850 us (79%)
  matrix products  234 us (10%)
  blocking collectives  97.3 us (4%)
  local copies, waits for them, and re-layouts  61.6 us (3%)
  starting transfers between devices  41 us (2%)
  other arithmetic  39.4 us (2%)
    all_gather x1, waiting for transfers between devices, local(): lax.all_gather(mlp_in_weights, 'fsdp', axis=0, tiled=True)  703 us
    all_gather x1, waiting for transfers between devices, local(): lax.all_gather(mlp_out_weights, 'fsdp', axis=0, tiled=True)  326 us
    all_gather x1, waiting for transfers between devices, local(): lax.all_gather(attn_weights, 'fsdp', axis=0, tiled=True)  248 us
    all_gather x1, waiting for transfers between devices, local(): lax.all_gather(normed_in, 'ctx', axis=0, tiled=True)  81.1 us
    reduce_scatter x1, waiting for transfers between devices, local(): lax.psum_scatter(part_gate_up.astype(jnp.bfloat16), 'fsdp', scatter_dimen...  71.4 us
    all_gather x1, waiting for transfers between devices, local(): lax.all_gather(d_mixed, 'ctx', axis=0, tiled=True)  70.4 us
    all_gather x1, waiting for transfers between devices, local(): lax.all_gather(normed_mid, 'ctx', axis=0, tiled=True)  68.7 us
    all_to_all x1, waiting for transfers between devices, local(): lax.all_to_all(sum_gate_up.astype(jnp.bfloat16), 'ctx', split_axis=0, con...  48.9 us
  transfers between devices with their start and end apart: 21, of which 17 were waited for; matrix products, arithmetic and copies ran while one was open for 8% of the time, Pallas kernels for 0%

commit v1 on v0

v1 whole, which is shorter than its diff:
```python
import jax
import jax.numpy as jnp
from jax import lax
from jax.sharding import PartitionSpec as P

HEADS = 8
KV_HEADS = 4
HEAD_DIM = 256

EPSILON = 1e-06
SOFT_CAP = 50.0
ROTARY_BASE = 10000.0
MASKED_SCORE = -1e30
STREAMS = 2

F32 = jnp.float32
BF16 = jnp.bfloat16


def positions_of(rows, half_block, ctx_count):
    owners = rows // (2 * half_block)
    within = rows % (2 * half_block)
    return jnp.where(
        within < half_block,
        owners * half_block + within,
        (2 * ctx_count - 1 - owners) * half_block + within - half_block,
    )


def rotary_tables(places, head_dim):
    half_width = head_dim // 2
    frequency = ROTARY_BASE ** (-jnp.arange(half_width, dtype=F32) * 2.0 / head_dim)
    angles = places.astype(F32)[:, None] * frequency[None, :]
    cosine = jnp.concatenate([jnp.cos(angles), jnp.cos(angles)], -1)
    sine_table = jnp.concatenate([jnp.sin(angles), jnp.sin(angles)], -1)
    return (cosine, sine_table)


def turned(values):
    half_width = values.shape[-1] // 2
    return jnp.concatenate([-values[..., half_width:], values[..., :half_width]], -1)


def rotate(values, cosine, sine_table):
    return values * cosine + turned(values) * sine_table


def rotate_back(grads, cosine, sine_table):
    return grads * cosine - turned(grads * sine_table)


def inverse_rms(values):
    return lax.rsqrt(jnp.mean(values * values, -1, keepdims=True) + EPSILON)


def norm_backward(values, scale, grad_normed):
    normed = values * scale
    return scale * (grad_normed - normed * jnp.mean(grad_normed * normed, -1, keepdims=True))


def geglu(gate, upper):
    return jax.nn.gelu(gate, approximate=True) * upper


def dot(a, b):
    return jnp.dot(a, b, preferred_element_type=F32)


def dot_t(a, b):
    return jnp.einsum("tk,dk->td", a, b, preferred_element_type=F32)


def shift(values, step, first, last):
    pairs = [
        (2 * r + core, 2 * (r + step) + core) for r in range(first, last + 1) for core in (0, 1)
    ]
    return lax.ppermute(values, "ctx", pairs)


def from_partner(values, ctx_count):
    return lax.ppermute(values, "ctx", [(i, i ^ 1) for i in range(ctx_count)])


def line_gather(values, rank, ranks):
    ups, downs = [values], [values]
    for k in range(1, ranks):
        ups.append(shift(ups[-1], 1, k - 1, ranks - 2))
        downs.append(shift(downs[-1], -1, 1, ranks - k))
    return [values] + [
        jnp.where(rank + k < ranks, downs[k], ups[ranks - k]) for k in range(1, ranks)
    ]


def line_scatter(parts, ranks):
    up = down = None
    for k in range(ranks - 1, 0, -1):
        up = parts[k] if up is None else parts[k] + up.astype(F32)
        up = shift(up.astype(BF16), 1, 0, ranks - 1 - k)
        down = parts[ranks - k] if down is None else parts[ranks - k] + down.astype(F32)
        down = shift(down.astype(BF16), -1, k, ranks - 1)
    return parts[0] + up.astype(F32) + down.astype(F32)


def local(layer_input, attn_weights, mlp_in_weights, mlp_out_weights, norm_gains, output_grad):
    tokens, width = layer_input.shape[1:]
    half_block = tokens // 2
    ctx_count = lax.axis_size("ctx")
    fsdp_count = lax.axis_size("fsdp")
    ranks = ctx_count // 2
    place = lax.axis_index("ctx")
    rank, core = place // 2, place % 2
    first_core = core == 0
    query_cols, key_cols = HEADS * HEAD_DIM, KV_HEADS * HEAD_DIM
    qkv_cols = query_cols + 2 * key_cols
    heads = HEADS // ranks
    sharing = ranks // KV_HEADS
    hidden_width = mlp_out_weights.shape[1]
    q_own = query_cols // ctx_count
    f_own = hidden_width // ctx_count
    shard_rows = width // (ctx_count * fsdp_count)
    scaling = HEAD_DIM**-0.5

    def partner(values):
        return from_partner(values, ctx_count)

    def columns(array, start, size):
        return lax.dynamic_slice_in_dim(array, start, size, 1)

    def gathered(*pieces):
        piece = pieces[0] if len(pieces) == 1 else jnp.concatenate(pieces, 1)
        return lax.all_gather(piece, "fsdp", axis=0, tiled=True)

    kv_start = query_cols + core * key_cols + rank // sharing * HEAD_DIM
    attn_own = gathered(
        columns(attn_weights, place * q_own, q_own),
        columns(attn_weights, kv_start, HEAD_DIM),
        columns(attn_weights, qkv_cols + place * q_own, q_own),
    )
    in_own = gathered(
        columns(mlp_in_weights, place * f_own, f_own),
        columns(mlp_in_weights, hidden_width + place * f_own, f_own),
    )
    out_own = gathered(columns(mlp_out_weights, place * f_own, f_own))
    gains = lax.all_gather(norm_gains, "fsdp", axis=0, tiled=True).astype(F32)
    g_pre, g_post, g_mid, g_out = [gains[:, i] for i in range(4)]
    attn_other, in_other, out_other = partner(attn_own), partner(in_own), partner(out_own)
    qkv_own, proj_own = attn_own[:, : q_own + HEAD_DIM], attn_own[:, q_own + HEAD_DIM :]
    qkv_other, proj_other = attn_other[:, : q_own + HEAD_DIM], attn_other[:, q_own + HEAD_DIM :]

    own_input = layer_input.reshape(tokens, width)
    source = own_input.astype(F32)
    upstream = output_grad.reshape(tokens, width).astype(F32)
    inputs = jnp.concatenate(line_gather(own_input, rank, ranks), 0).astype(F32)
    scale_in = inverse_rms(inputs)
    plain_in = inputs * scale_in
    normed_in = (plain_in * g_pre).astype(BF16)

    def places_of(which):
        slots = (rank + jnp.arange(ranks, dtype=jnp.int32)) % ranks
        owners = (2 * slots + which)[:, None] * tokens
        rows = owners + jnp.arange(tokens, dtype=jnp.int32)[None, :]
        return positions_of(rows.reshape(-1), half_block, ctx_count)

    own_places, other_places = places_of(core), places_of(1 - core)
    cosine, sine_table = rotary_tables(own_places, HEAD_DIM)
    all_places = jnp.concatenate([own_places, other_places], 0)
    allowed = all_places[None, :] <= own_places[:, None]
    rows = ranks * tokens

    def ordered(mine, theirs):
        return jnp.where(first_core, mine, theirs), jnp.where(first_core, theirs, mine)

    proj_a, proj_b = dot(normed_in, qkv_own), dot(normed_in, qkv_other)
    query_raw = jnp.concatenate(ordered(proj_a[:, :q_own], proj_b[:, :q_own]), 1)
    key_raw, value_raw = ordered(proj_a[:, q_own:], proj_b[:, q_own:])
    query = rotate(
        query_raw.reshape(rows, heads, HEAD_DIM), cosine[:, None], sine_table[:, None]
    ).astype(BF16)
    key_own = rotate(key_raw, cosine, sine_table).astype(BF16)
    value_own = value_raw.astype(BF16)
    key_value = jnp.concatenate([key_own, value_own], 1)
    key_value = jnp.concatenate([key_value, partner(key_value)], 0)
    keys, values = key_value[:, :HEAD_DIM], key_value[:, HEAD_DIM:]

    def score_rows():
        raw_scores = jnp.einsum("tgd,ld->gtl", query, keys, preferred_element_type=F32)
        tanh_part = jnp.tanh(raw_scores * scaling / SOFT_CAP)
        return tanh_part, jnp.where(allowed, SOFT_CAP * tanh_part, MASKED_SCORE)

    tanh_part, capped = score_rows()
    row_max = jnp.max(capped, -1, keepdims=True)
    weights = jnp.exp(capped - row_max)
    row_total = jnp.sum(weights, -1, keepdims=True)
    log_total = row_max + jnp.log(row_total)
    chances = (weights / row_total).astype(BF16)
    attended = jnp.einsum("gtl,ld->tgd", chances, values, preferred_element_type=F32)
    attended = attended.reshape(rows, heads * HEAD_DIM).astype(BF16)
    att_own, att_other = ordered(attended[:, :q_own], attended[:, q_own:])
    branch_parts = (dot_t(att_own, proj_own) + dot_t(att_other, proj_other)).reshape(
        ranks, tokens, width
    )

    span = tokens // STREAMS
    gains_sums = {"out": 0.0, "mid": 0.0, "post": 0.0}
    streams = []
    for s in range(STREAMS):
        cut = slice(s * span, (s + 1) * span)
        st = {"cut": cut}
        branch = line_scatter([branch_parts[k, cut] for k in range(ranks)], ranks)
        scale_branch = inverse_rms(branch)
        residual = source[cut] + branch * scale_branch * g_post
        scale_mid = inverse_rms(residual)
        normed_mid = (residual * scale_mid * g_mid).astype(BF16)
        mids = jnp.concatenate(line_gather(normed_mid, rank, ranks), 0)
        hiddens, backs, mixed = [], [], 0.0
        for w_in, w_out in ((in_own, out_own), (in_other, out_other)):
            gate_up = dot(mids, w_in)
            hidden, back = jax.vjp(geglu, gate_up[:, :f_own], gate_up[:, f_own:])
            hidden = hidden.astype(BF16)
            hiddens.append(hidden)
            backs.append(back)
            mixed = mixed + dot_t(hidden, w_out)
        mixed = mixed.reshape(ranks, span, width)
        mixed = line_scatter([mixed[k] for k in range(ranks)], ranks)
        scale_mixed = inverse_rms(mixed)
        st["out"] = (residual + mixed * scale_mixed * g_out).astype(BF16)
        up = upstream[cut]
        gains_sums["out"] += jnp.sum(up * mixed * scale_mixed, 0)
        d_mixed = norm_backward(mixed, scale_mixed, up * g_out).astype(BF16)
        d_mixeds = jnp.concatenate(line_gather(d_mixed, rank, ranks), 0)
        d_mid, d_gate_ups = 0.0, []
        for w_in, w_out, back in ((in_own, out_own, backs[0]), (in_other, out_other, backs[1])):
            d_gate, d_upper = back(dot(d_mixeds, w_out))
            d_gate_up = jnp.concatenate([d_gate, d_upper], 1).astype(BF16)
            d_gate_ups.append(d_gate_up)
            d_mid = d_mid + dot_t(d_gate_up, w_in)
        d_mid = d_mid.reshape(ranks, span, width)
        d_mid = line_scatter([d_mid[k] for k in range(ranks)], ranks)
        gains_sums["mid"] += jnp.sum(d_mid * residual * scale_mid, 0)
        d_residual = up + norm_backward(residual, scale_mid, d_mid * g_mid)
        gains_sums["post"] += jnp.sum(d_residual * branch * scale_branch, 0)
        d_branch = norm_backward(branch, scale_branch, d_residual * g_post).astype(BF16)
        st["d_residual"] = d_residual
        st["d_branches"] = line_gather(d_branch, rank, ranks)
        st.update(mids=mids, d_mixeds=d_mixeds, hiddens=hiddens, d_gate_ups=d_gate_ups)
        streams.append(st)

    block_out = jnp.concatenate([st["out"] for st in streams], 0).reshape(layer_input.shape)
    d_residual = jnp.concatenate([st["d_residual"] for st in streams], 0)
    d_branches = jnp.concatenate(
        [st["d_branches"][k] for k in range(ranks) for st in streams], 0
    )

    def both_cores(mine, others=None):
        return jnp.concatenate([mine, partner(mine if others is None else others)], 0)

    def weight_grad(left, right):
        grouped = left.reshape(left.shape[0], ctx_count, fsdp_count, shard_rows)
        product = jnp.einsum("tcfr,tn->fcrn", grouped, right, preferred_element_type=F32)
        product = product.reshape(width, right.shape[1]).astype(BF16)
        total = lax.psum_scatter(product, "fsdp", scatter_dimension=0, tiled=True)
        return total.reshape(ranks, 2, shard_rows, right.shape[1])

    def spread(total):
        mine = jnp.where(first_core, total[:, 0], total[:, 1])
        theirs = partner(jnp.where(first_core, total[:, 1], total[:, 0]))
        both = jnp.stack(ordered(mine, theirs), 1)
        got = []
        for k in range(ranks):
            part = lax.dynamic_index_in_dim(both, (rank + k) % ranks, 0, keepdims=False)
            pairs = [(i, (i + 2 * k) % ctx_count) for i in range(ctx_count)]
            got.append(part if k == 0 else lax.ppermute(part, "ctx", pairs))
        return got

    def put(into, piece, start, adds=False):
        piece = piece.astype(F32)
        if adds:
            piece = piece + lax.dynamic_slice_in_dim(into, start, piece.shape[1], 1)
        return lax.dynamic_update_slice_in_dim(into, piece, start, 1)

    mid_rows = both_cores(jnp.concatenate([st["mids"] for st in streams], 0))
    dmix_rows = both_cores(jnp.concatenate([st["d_mixeds"] for st in streams], 0))
    hidden_rows = both_cores(*[jnp.concatenate([st["hiddens"][i] for st in streams], 0) for i in (0, 1)])
    dgu_rows = both_cores(*[jnp.concatenate([st["d_gate_ups"][i] for st in streams], 0) for i in (0, 1)])
    down = spread(weight_grad(dmix_rows, hidden_rows))
    gate_up_terms = spread(weight_grad(mid_rows, dgu_rows))
    grad_mlp_out = jnp.zeros((shard_rows, hidden_width), F32)
    grad_mlp_in = jnp.zeros((shard_rows, 2 * hidden_width), F32)
    for k in range(ranks):
        giver = (rank - k) % ranks
        for which in (0, 1):
            start = (2 * giver + which) * f_own
            grad_mlp_out = put(grad_mlp_out, down[k][which], start)
            grad_mlp_in = put(grad_mlp_in, gate_up_terms[k][which][:, :f_own], start)
            grad_mlp_in = put(grad_mlp_in, gate_up_terms[k][which][:, f_own:], hidden_width + start)

    d_att_own, d_att_other = dot(d_branches, proj_own), dot(d_branches, proj_other)
    d_attended = jnp.concatenate(ordered(d_att_own, d_att_other), 1).astype(BF16)
    d_attended = d_attended.reshape(rows, heads, HEAD_DIM)
    tanh_again, capped_again = score_rows()
    chances_f = jnp.exp(capped_again - log_total)
    d_values = jnp.einsum(
        "gtl,tgd->ld", chances_f.astype(BF16), d_attended, preferred_element_type=F32
    )
    d_chances = jnp.einsum("tgd,ld->gtl", d_attended, values, preferred_element_type=F32)
    row_inner = jnp.sum(chances_f * d_chances, -1, keepdims=True)
    d_raw = (
        chances_f * (d_chances - row_inner) * (1.0 - tanh_again * tanh_again) * scaling
    ).astype(BF16)
    d_query = jnp.einsum("gtl,ld->tgd", d_raw, keys, preferred_element_type=F32)
    d_keys = jnp.einsum("gtl,tgd->ld", d_raw, query, preferred_element_type=F32)
    d_key_value = jnp.concatenate([d_keys, d_values], 1)
    d_key_value = d_key_value[:rows] + partner(d_key_value[rows:].astype(BF16)).astype(F32)
    d_query_raw = rotate_back(d_query, cosine[:, None], sine_table[:, None]).reshape(
        rows, heads * HEAD_DIM
    )
    d_key_raw = rotate_back(d_key_value[:, :HEAD_DIM], cosine, sine_table)
    dq_own, dq_other = ordered(d_query_raw[:, :q_own], d_query_raw[:, q_own:])
    dkv_own, dkv_other = ordered(d_key_raw, d_key_value[:, HEAD_DIM:])
    dproj_own = jnp.concatenate([dq_own, dkv_own], 1).astype(BF16)
    dproj_other = jnp.concatenate([dq_other, dkv_other], 1).astype(BF16)
    d_in = dot_t(dproj_own, qkv_own) + dot_t(dproj_other, qkv_other)
    grad_pre_gain = jnp.sum(d_in * plain_in, 0)
    d_in = d_in.reshape(ranks, tokens, width)
    d_in = line_scatter([d_in[k] for k in range(ranks)], ranks)
    d_source = d_residual + norm_backward(source, scale_in[:tokens], d_in * g_pre)

    in_rows = both_cores(normed_in)
    dbranch_rows = both_cores(d_branches)
    dproj_rows = both_cores(dproj_own, dproj_other)
    att_rows = both_cores(att_own, att_other)
    out_proj = spread(weight_grad(dbranch_rows, att_rows))
    projection = spread(weight_grad(in_rows, dproj_rows))
    grad_attn = jnp.zeros((shard_rows, attn_weights.shape[1]), F32)
    for k in range(ranks):
        giver = (rank - k) % ranks
        for which in (0, 1):
            start = (2 * giver + which) * q_own
            grad_attn = put(grad_attn, out_proj[k][which], qkv_cols + start)
            grad_attn = put(grad_attn, projection[k][which][:, :q_own], start)
            start = query_cols + which * key_cols + giver // sharing * HEAD_DIM
            grad_attn = put(grad_attn, projection[k][which][:, q_own:], start, sharing > 1)

    gain_terms = jnp.stack(
        [grad_pre_gain, gains_sums["post"], gains_sums["mid"], gains_sums["out"]], 1
    )
    grad_gains = lax.psum_scatter(gain_terms, ("ctx", "fsdp"), scatter_dimension=0, tiled=True)
    return (
        block_out,
        d_source.reshape(layer_input.shape),
        grad_attn,
        grad_mlp_in,
        grad_mlp_out,
        grad_gains,
    )


def solution(mesh):
    in_specs = (
        P("fsdp", "ctx", None),
        P("fsdp", None),
        P("fsdp", None),
        P("fsdp", None),
        P("fsdp", None),
        P("fsdp", "ctx", None),
    )
    out_specs = (
        P("fsdp", "ctx", None),
        P("fsdp", "ctx", None),
        P(("ctx", "fsdp"), None),
        P(("ctx", "fsdp"), None),
        P(("ctx", "fsdp"), None),
        P(("ctx", "fsdp"), None),
    )
    return jax.shard_map(local, mesh=mesh, in_specs=in_specs, out_specs=out_specs, check_vma=False)
```

time: 2350 us -> 920 us (0.39)
  waiting for transfers between devices: 1850 us -> 326 us
  starting transfers between devices: 41 us -> 218 us
  matrix products: 234 us -> 161 us
  other arithmetic: 39.4 us -> 88.5 us
  blocking collectives: 97.3 us -> 48.9 us
    all_gather x9 -> x3, waiting for transfers between devices: 1590 us -> 40 us  [gathered(): return lax.all_gather(piece, 'fsdp', axis=0, tiled=True)]
    ppermute x0 -> x113, waiting for transfers between devices: none -> 286 us  [the longest x84 179 us: shift(): return lax.ppermute(values, 'ctx', pairs)]
    ppermute x0 -> x113, starting transfers between devices: none -> 217 us  [the longest x84 177 us: shift(): return lax.ppermute(values, 'ctx', pairs)]
    reduce_scatter x5 -> x4, waiting for transfers between devices: 173 us -> 0.08 us  [weight_grad(): total = lax.psum_scatter(product, 'fsdp', scatter_dimension=0, tiled=True)]
    all_to_all x4 -> x0, blocking collectives: 91.2 us -> none  [the longest x1 36.5 us: local(): lax.all_to_all(sum_down.astype(jnp.bfloat16), 'ctx', split_axis=0, concat...]
    dot_general x14 -> x30, matrix products: 199 us -> 125 us  [the longest x12 48.9 us: dot(): return jnp.dot(a, b, preferred_element_type=F32)]
    all_to_all x5 -> x0, waiting for transfers between devices: 58.7 us -> none  [the longest x1 48.9 us: local(): lax.all_to_all(sum_gate_up.astype(jnp.bfloat16), 'ctx', split_axis=0, con...]
    unnamed x0 -> x1, blocking collectives: none -> 41.9 us
  transfers between devices with their start and end apart: 21 -> 120, of which waited for: 17 -> 58; matrix products, arithmetic and copies ran while one was open for 8% -> 30% of each run, Pallas kernels for 0% -> 0%
where the time goes in v1:
time: 920 us; the launch traced here: 912 us
  waiting for transfers between devices  326 us (35%)
  starting transfers between devices  218 us (24%)
  matrix products  161 us (18%)
  other arithmetic  88.5 us (10%)
  local copies, waits for them, and re-layouts  51.8 us (6%)
  blocking collectives  48.9 us (5%)
  between operations  18.6 us (2%)
    ppermute x84, waiting for transfers between devices, shift(): return lax.ppermute(values, 'ctx', pairs)  179 us
    ppermute x84, starting transfers between devices, shift(): return lax.ppermute(values, 'ctx', pairs)  177 us
    ppermute x12, waiting for transfers between devices, spread(): got.append(part if k == 0 else lax.ppermute(part, 'ctx', pairs))  95.7 us
    dot_general x12, matrix products, dot(): return jnp.dot(a, b, preferred_element_type=F32)  48.9 us
    dot_general x12, matrix products, dot_t(): return jnp.einsum('tk,dk->td', a, b, preferred_element_type=F32)  46.5 us
    unnamed x1, blocking collectives  41.9 us
    all_gather x3, waiting for transfers between devices, gathered(): return lax.all_gather(piece, 'fsdp', axis=0, tiled=True)  40 us
    unnamed x4, matrix products  36 us
  transfers between devices with their start and end apart: 120, of which 58 were waited for; matrix products, arithmetic and copies ran while one was open for 30% of the time, Pallas kernels for 0%

profile of v1, /device:TPU:13, one launch (start us, length us, event | category | flops | bytes accessed | tf_op | source)
XLA Modules:
  0.0 912.2 jit_solution(11990652827607313240)
XLA Ops:
  19.6 6.9 all-gather
  37.0 11.7 %collective-permute-done.4 = bf16[128,2304]{1,0:T(8,128)(2,1)} collective-permute-done((bf16[128,2304]{1,0:T(8,128)(2,1)S(1)}, bf16[128,2304]{1,0:T(8,128)(2,1)}, u32[]{:S(2)}, u32[]{:S(2)}) %collective-permute-start.4) | collective-permute-done | bytes 589856 | tf_op jit(solution)/shard_map/ppermute | solution.py:77
  53.1 5.8 all-gather.5.cloned.1.call-done
  62.3 4.7 fusion.3
  70.3 4.6 fusion.37
  90.4 9.9 %collective-permute-done.8 = bf16[64,2304]{1,0:T(8,128)(2,1)S(1)} collective-permute-done((bf16[64,2304]{1,0:T(8,128)(2,1)S(1)}, bf16[64,2304]{1,0:T(8,128)(2,1)S(1)}, u32[]{:S(2)}, u32[]{:S(2)}) %collective-permute-start.8) | collective-permute-done | bytes 294944 | tf_op jit(solution)/shard_map/ppermute | solution.py:77
  101.7 4.0 collective-permute-start.9
  111.6 3.7 collective-permute-start.10
  118.5 5.5 collective-permute-done.10
  124.1 5.9 collective-permute-done.32
  143.5 4.2 collective-permute-done.30
  152.9 14.6 %all-gather.7.cloned.1.call-done = bf16[2304,2304]{1,0:T(8,128)(2,1)} async-done(((bf16[576,2304]{1,0:T(8,128)(2,1)}), bf16[2304,2304]{1,0:T(8,128)(2,1)}) %all-gather.7.cloned.1.call-update) | async-done | bytes 10616848 | tf_op jit(solution)/shard_map/all_gather | solution.py:131
  173.5 5.2 collective-permute-done.14
  182.3 6.2 collective-permute-done.18
  212.4 19.6 %all-gather.9.cloned.1.call-done = bf16[2304,1152]{1,0:T(8,128)(2,1)} async-done(((bf16[576,1152]{1,0:T(8,128)(2,1)}), bf16[2304,1152]{1,0:T(8,128)(2,1)}) %all-gather.9.cloned.1.call-update) | async-done | bytes 5308432 | tf_op jit(solution)/shard_map/all_gather | solution.py:131
  242.2 6.6 fusion.164
  254.5 4.5 fusion.256
  259.1 6.1 fusion.163
  270.5 6.0 fusion.165
  284.2 5.5 collective-permute-done.22
  291.7 4.3 collective-permute-done.41
  297.5 4.0 collective-permute-start.42
  303.8 4.0 collective-permute-start.24
  312.9 4.7 collective-permute-done.45
  317.8 6.1 collective-permute-done.27
  332.7 3.8 collective-permute-start.46
  339.2 4.1 collective-permute-done.46
  348.4 4.5 collective-permute-done.50
  352.9 3.7 collective-permute-start.51
  364.8 3.7 collective-permute-start.58
  371.7 8.9 fusion.83
  385.7 7.7 convolution_add_fusion.3
  401.0 3.7 collective-permute-start.63
  408.8 3.8 fusion.80
  415.9 6.5 fusion.90
  422.4 6.1 convolution_add_fusion.2
  443.4 4.0 collective-permute-start.54
  461.3 5.8 collective-permute-done.69
  468.5 4.2 collective-permute-start.71
  491.5 9.3 %collective-permute-start.89 = (bf16[512,256]{0,1:T(8,128)(2,1)S(1)}, bf16[512,256]{0,1:T(8,128)(2,1)}, u32[]{:S(2)}, u32[]{:S(2)}) collective-permute-start(bf16[512,256]{0,1:T(8,128)(2,1)S(1)} %copy-done.74), channel_id=1, source_target_pairs={{0,4},{4,0},{8,12},{12,8},{16,20},{20,16},{24,28},{28,24},{1,5},{5... | collective-permute-start | bytes 786440 | tf_op jit(solution)/shard_map/ppermute | solution.py:81
  506.1 8.7 collective-permute-done.78
  515.6 5.5 collective-permute-done.79
  529.3 5.5 collective-permute-done.81
  546.5 10.2 %fusion.49 = f32[1024,256]{0,1:T(8,128)S(1)} fusion(bf16[512,2,256]{0,2,1:T(8,128)(2,1)} %copy-done.96, f32[1024,512,2]{1,0,2:T(8,128)} %fusion.146, f32[1024,512,2]{1,0,2:T(8,128)} %copy-done.19, f32[2,512]{1,0:T(2,128)S(1)} %copy-done.124, pred[512,1024]{0,1:T(8,128)(4,1)S(1)} %copy-done.34), kind=kOutput, calls=%fused_computation.95 | convolution fusion | flops 553650176 | bytes 10489856 | tf_op jit(solution)/shard_map/gtl,tgd->ld/dot_general | solution.py:311
  556.7 4.1 fusion.45
  563.8 9.5 %broadcast_multiply_fusion = (f32[512,2,256]{0,2,1:T(8,128)}, f32[512,2,256]{0,2,1:T(8,128)}) fusion(f32[512,256]{0,1:T(8,128)} %copy-done.35, f32[1024,512,2]{1,0,2:T(8,128)} %fusion.146, f32[1024,512,2]{1,0,2:T(8,128)} %copy-done.19, f32[2,512]{1,0:T(2,128)S(1)} %copy-done.124, pred[512,1024]{0,1:T(8,128)(4,1)S(1)} %copy-done.34, ...), kind=kOutput, calls=%fused_computation.339 | convolution fusion | flops 553912320 | bytes 20979712 | tf_op jit(solution)/shard_map/gtl,ld->tgd/dot_general | solution.py:310
  580.7 4.4 fusion.142
  589.7 4.5 fusion.6
  604.5 11.0 %fusion.25 = f32[1152,2304]{0,1} fusion(bf16[1024,2304]{1,0:T(8,128)(2,1)} %constant_dynamic-update-slice_fusion.30, bf16[512,1152]{1,0:T(8,128)(2,1)} %collective-permute-done.107, bf16[256,1152]{1,0:T(8,128)(2,1)S(1)} %copy-done.93, bf16[256,1152]{1,0:T(8,128)(2,1)S(1)} %copy-done.95), kind=kOutput, calls=%fused_computation.55 | convolution fusion | flops 5442895872 | bytes 17694720
  615.5 4.6 convert_bitcast_fusion.1
  632.1 16.1 %fusion.10 = f32[2304,2304]{0,1} fusion(bf16[1024,2304]{1,0:T(8,128)(2,1)S(1)} %constant_dynamic-update-slice_fusion.13, bf16[512,2304]{1,0:T(8,128)(2,1)S(1)} %collective-permute-done.101, bf16[256,1152]{1,0:T(8,128)(2,1)S(1)} %copy-done.133, bf16[256,1152]{1,0:T(8,128)(2,1)S(1)} %copy-done.131, bf16[256,1152]{1,0:T(8,128)(2,1)S(1)} %copy-done.129, ...), kind=kOutput, calls=%fused_computation.16 | convolution fusion | flops 10895228928 | bytes 30670848
  648.2 8.2 convert_bitcast_fusion
  656.4 4.8 copy.101
  671.5 14.9 %collective-permute-done.83 = bf16[128,2304]{1,0:T(8,128)(2,1)S(1)} collective-permute-done((bf16[128,2304]{1,0:T(8,128)(2,1)S(1)}, bf16[128,2304]{1,0:T(8,128)(2,1)S(1)}, u32[]{:S(2)}, u32[]{:S(2)}) %collective-permute-start.83) | collective-permute-done | bytes 589856 | tf_op jit(solution)/shard_map/ppermute | solution.py:77
  688.5 14.1 %collective-permute-done.84 = bf16[128,2304]{1,0:T(8,128)(2,1)S(1)} collective-permute-done((bf16[128,2304]{1,0:T(8,128)(2,1)S(1)}, bf16[128,2304]{1,0:T(8,128)(2,1)S(1)}, u32[]{:S(2)}, u32[]{:S(2)}) %collective-permute-start.84) | collective-permute-done | bytes 589856 | tf_op jit(solution)/shard_map/ppermute | solution.py:77
  706.1 4.1 collective-permute-start.85
  710.2 8.7 collective-permute-done.87
  726.9 41.9 %all-reduce = f32[2304,4]{0,1:T(4,128)S(1)} all-reduce(f32[2304,4]{0,1:T(4,128)S(1)} %pad_maximum_fusion.26), channel_id=6, replica_groups=mesh['ctx'=8,'fsdp'=4] {'ctx','fsdp'}, use_global_device_ids=true, to_apply=%region_28.29.clone | all-reduce | flops 9216 | bytes 73728
  785.9 10.0 %collective-permute-done.96 = bf16[2,72,512]{2,1,0:T(8,128)(2,1)S(1)} collective-permute-done((bf16[2,72,512]{2,1,0:T(8,128)(2,1)S(1)}, bf16[2,72,512]{2,1,0:T(8,128)(2,1)S(1)}, u32[]{:S(2)}, u32[]{:S(2)}) %collective-permute-start.96) | collective-permute-done | bytes 147488 | tf_op jit(solution)/shard_map/ppermute | solution.py:272
  808.7 6.0 collective-permute-done.110
  814.8 19.3 %collective-permute-done.111 = bf16[2,72,1152]{2,1,0:T(8,128)(2,1)S(1)} collective-permute-done((bf16[2,72,1152]{2,1,0:T(8,128)(2,1)S(1)}, bf16[2,72,1152]{2,1,0:T(8,128)(2,1)S(1)}, u32[]{:S(2)}, u32[]{:S(2)}) %collective-permute-start.111) | collective-permute-done | bytes 331808 | tf_op jit(solution)/shard_map/ppermute | solution.py:272
  846.3 11.0 %collective-permute-done.104 = bf16[2,72,2304]{2,1,0:T(8,128)(2,1)S(1)} collective-permute-done((bf16[2,72,2304]{2,1,0:T(8,128)(2,1)S(1)}, bf16[2,72,2304]{2,1,0:T(8,128)(2,1)S(1)}, u32[]{:S(2)}, u32[]{:S(2)}) %collective-permute-start.104) | collective-permute-done | bytes 663584 | tf_op jit(solution)/shard_map/ppermute | solution.py:272
  857.4 40.6 %collective-permute-done.105 = bf16[2,72,2304]{2,1,0:T(8,128)(2,1)S(1)} collective-permute-done((bf16[2,72,2304]{2,1,0:T(8,128)(2,1)S(1)}, bf16[2,72,2304]{2,1,0:T(8,128)(2,1)S(1)}, u32[]{:S(2)}, u32[]{:S(2)}) %collective-permute-start.105) | collective-permute-done | bytes 663584 | tf_op jit(solution)/shard_map/ppermute | solution.py:272
  898.2 4.1 collective-permute-done.106
  (742 shorter events, 377.8 us)
Async XLA Ops:
  7.2 51.7 %all-gather.5.cloned.1.call-start = ((), (), s32[]{:S(2)}) async-start(), calls=%async_computation.4 | async-start | bytes 4423680 | tf_op jit(solution)/shard_map/all_gather | solution.py:131
  9.5 158.1 %all-gather.7.cloned.1.call-start = ((), (), s32[]{:S(2)}) async-start(), calls=%async_computation.5 | async-start | bytes 13271040 | tf_op jit(solution)/shard_map/all_gather | solution.py:131
  13.2 218.8 %all-gather.9.cloned.1.call-start = ((), (), s32[]{:S(2)}) async-start(), calls=%async_computation.6 | async-start | bytes 6635520 | tf_op jit(solution)/shard_map/all_gather | solution.py:131
  14.2 16.2 %collective-permute-start.1 = (bf16[128,2304]{1,0:T(8,128)(2,1)S(1)}, bf16[128,2304]{1,0:T(8,128)(2,1)S(1)}, u32[]{:S(2)}, u32[]{:S(2)}) collective-permute-start(bf16[128,2304]{1,0:T(8,128)(2,1)S(1)} %bitcast.568), channel_id=1, source_target_pairs={{0,8},{4,12},{8,16},{12,20},{16,24},{20,28},{1,9},{5,13},{9,17},{1... | collective-permute-start | bytes 1769480 | tf_op jit(solution)/shard_map/ppermute | solution.py:77
  17.4 16.2 %collective-permute-start = (bf16[128,2304]{1,0:T(8,128)(2,1)S(1)}, bf16[128,2304]{1,0:T(8,128)(2,1)S(1)}, u32[]{:S(2)}, u32[]{:S(2)}) collective-permute-start(bf16[128,2304]{1,0:T(8,128)(2,1)S(1)} %bitcast.569), channel_id=1, source_target_pairs={{8,0},{12,4},{16,8},{20,12},{24,16},{28,20},{9,1},{13,5},{17,9},{2... | collective-permute-start | bytes 1769480 | tf_op jit(solution)/shard_map/ppermute | solution.py:77
  30.4 21.2 %collective-permute-start.2 = (bf16[128,2304]{1,0:T(8,128)(2,1)S(1)}, bf16[128,2304]{1,0:T(8,128)(2,1)S(1)}, u32[]{:S(2)}, u32[]{:S(2)}) collective-permute-start(bf16[128,2304]{1,0:T(8,128)(2,1)S(1)} %collective-permute-done.1), channel_id=1, source_target_pairs={{8,16},{12,20},{16,24},{20,28},{9,17},{13,21},{17,25},{21,29},{10,... | collective-permute-start | bytes 1769480 | tf_op jit(solution)/shard_map/ppermute | solution.py:77
  33.6 15.1 %collective-permute-start.4 = (bf16[128,2304]{1,0:T(8,128)(2,1)S(1)}, bf16[128,2304]{1,0:T(8,128)(2,1)}, u32[]{:S(2)}, u32[]{:S(2)}) collective-permute-start(bf16[128,2304]{1,0:T(8,128)(2,1)S(1)} %collective-permute-done), channel_id=1, source_target_pairs={{8,0},{12,4},{16,8},{20,12},{9,1},{13,5},{17,9},{21,13},{10,2},{14... | collective-permute-start | bytes 1769480 | tf_op jit(solution)/shard_map/ppermute | solution.py:77
  89.7 17.3 %collective-permute-start.31 = (bf16[64,2304]{1,0:T(8,128)(2,1)S(1)}, bf16[64,2304]{1,0:T(8,128)(2,1)S(1)}, u32[]{:S(2)}, u32[]{:S(2)}) collective-permute-start(bf16[64,2304]{1,0:T(8,128)(2,1)S(1)} %get-tuple-element.93), channel_id=1, source_target_pairs={{24,16},{28,20},{25,17},{29,21},{26,18},{30,22},{27,19},{31,23}} | collective-permute-start | bytes 884744 | tf_op jit(solution)/shard_map/ppermute | solution.py:77
  105.7 12.9 %collective-permute-start.28 = (bf16[64,2304]{1,0:T(8,128)(2,1)S(1)}, bf16[64,2304]{1,0:T(8,128)(2,1)S(1)}, u32[]{:S(2)}, u32[]{:S(2)}) collective-permute-start(bf16[64,2304]{1,0:T(8,128)(2,1)S(1)} %get-tuple-element.95), channel_id=1, source_target_pairs={{0,8},{4,12},{1,9},{5,13},{2,10},{6,14},{3,11},{7,15}} | collective-permute-start | bytes 884744 | tf_op jit(solution)/shard_map/ppermute | solution.py:77
  111.6 12.5 %collective-permute-start.10 = (bf16[64,2304]{1,0:T(8,128)(2,1)S(1)}, bf16[64,2304]{1,0:T(8,128)(2,1)S(1)}, u32[]{:S(2)}, u32[]{:S(2)}) collective-permute-start(bf16[64,2304]{1,0:T(8,128)(2,1)S(1)} %get-tuple-element.87), channel_id=1, source_target_pairs={{0,8},{4,12},{8,16},{12,20},{16,24},{20,28},{1,9},{5,13},{9,17},{1... | collective-permute-start | bytes 884744 | tf_op jit(solution)/shard_map/ppermute | solution.py:77
  117.2 12.7 %collective-permute-start.32 = (bf16[64,2304]{1,0:T(8,128)(2,1)S(1)}, bf16[64,2304]{1,0:T(8,128)(2,1)S(1)}, u32[]{:S(2)}, u32[]{:S(2)}) collective-permute-start(bf16[64,2304]{1,0:T(8,128)(2,1)S(1)} %get-tuple-element.88), channel_id=1, source_target_pairs={{16,8},{20,12},{24,16},{28,20},{17,9},{21,13},{25,17},{29,21},{18,... | collective-permute-start | bytes 884744 | tf_op jit(solution)/shard_map/ppermute | solution.py:77
  135.6 635.7 %reduce-scatter.6.cloned.1.call-start = ((), (), s32[]{:S(2)}) async-start(), calls=%async_computation.7 | async-start | bytes 1474560 | tf_op jit(solution)/shard_map/reduce_scatter | solution.py:261
  150.8 19.6 %collective-permute-start.15 = (bf16[64,2304]{1,0:T(8,128)(2,1)S(1)}, bf16[64,2304]{1,0:T(8,128)(2,1)S(1)}, u32[]{:S(2)}, u32[]{:S(2)}) collective-permute-start(bf16[64,2304]{1,0:T(8,128)(2,1)S(1)} %get-tuple-element.55), channel_id=1, source_target_pairs={{0,8},{4,12},{8,16},{12,20},{16,24},{20,28},{1,9},{5,13},{9,17},{1... | collective-permute-start | bytes 884744 | tf_op jit(solution)/shard_map/ppermute | solution.py:77
  167.5 91.5 %collective-permute-start.20 = (bf16[2304,2304]{1,0:T(8,128)(2,1)}, bf16[2304,2304]{1,0:T(8,128)(2,1)}, u32[]{:S(2)}, u32[]{:S(2)}) collective-permute-start(bf16[2304,2304]{1,0:T(8,128)(2,1)} %all-gather.7.cloned.1.call-done), channel_id=1, source_target_pairs={{0,4},{4,0},{8,12},{12,8},{16,20},{20,16},{24,28},{28,24},{1,5},{5... | collective-permute-start | bytes 31850504 | tf_op jit(solution)/shard_map/ppermute | solution.py:81
  208.0 24.7 %collective-permute-start.38 = (bf16[64,2304]{1,0:T(8,128)(2,1)}, bf16[64,2304]{1,0:T(8,128)(2,1)}, u32[]{:S(2)}, u32[]{:S(2)}) collective-permute-start(bf16[64,2304]{1,0:T(8,128)(2,1)} %collective-permute-done.34), channel_id=1, source_target_pairs={{8,0},{12,4},{16,8},{20,12},{9,1},{13,5},{17,9},{21,13},{10,2},{14... | collective-permute-start | bytes 884744 | tf_op jit(solution)/shard_map/ppermute | solution.py:77
  210.9 23.9 %collective-permute-start.37 = (bf16[64,2304]{1,0:T(8,128)(2,1)}, bf16[64,2304]{1,0:T(8,128)(2,1)}, u32[]{:S(2)}, u32[]{:S(2)}) collective-permute-start(bf16[64,2304]{1,0:T(8,128)(2,1)} %collective-permute-done.36), channel_id=1, source_target_pairs={{16,24},{20,28},{17,25},{21,29},{18,26},{22,30},{19,27},{23,31}} | collective-permute-start | bytes 884744 | tf_op jit(solution)/shard_map/ppermute | solution.py:77
  232.0 34.6 %collective-permute-start.21 = (bf16[2304,1152]{1,0:T(8,128)(2,1)}, bf16[2304,1152]{1,0:T(8,128)(2,1)S(1)}, u32[]{:S(2)}, u32[]{:S(2)}) collective-permute-start(bf16[2304,1152]{1,0:T(8,128)(2,1)} %all-gather.9.cloned.1.call-done), channel_id=1, source_target_pairs={{0,4},{4,0},{8,12},{12,8},{16,20},{20,16},{24,28},{28,24},{1,5},{5... | collective-permute-start | bytes 15925256 | tf_op jit(solution)/shard_map/ppermute | solution.py:81
  268.4 13.9 %collective-permute-start.40 = (bf16[64,2304]{1,0:T(8,128)(2,1)S(1)}, bf16[64,2304]{1,0:T(8,128)(2,1)S(1)}, u32[]{:S(2)}, u32[]{:S(2)}) collective-permute-start(bf16[64,2304]{1,0:T(8,128)(2,1)S(1)} %get-tuple-element.124), channel_id=1, source_target_pairs={{0,8},{4,12},{1,9},{5,13},{2,10},{6,14},{3,11},{7,15}} | collective-permute-start | bytes 884744 | tf_op jit(solution)/shard_map/ppermute | solution.py:77
  269.7 22.1 %collective-permute-start.43 = (bf16[64,2304]{1,0:T(8,128)(2,1)S(1)}, bf16[64,2304]{1,0:T(8,128)(2,1)S(1)}, u32[]{:S(2)}, u32[]{:S(2)}) collective-permute-start(bf16[64,2304]{1,0:T(8,128)(2,1)S(1)} %get-tuple-element.125), channel_id=1, source_target_pairs={{24,16},{28,20},{25,17},{29,21},{26,18},{30,22},{27,19},{31,23}} | collective-permute-start | bytes 884744 | tf_op jit(solution)/shard_map/ppermute | solution.py:77
  281.5 19.9 %collective-permute-start.25 = (bf16[64,2304]{1,0:T(8,128)(2,1)S(1)}, bf16[64,2304]{1,0:T(8,128)(2,1)S(1)}, u32[]{:S(2)}, u32[]{:S(2)}) collective-permute-start(bf16[64,2304]{1,0:T(8,128)(2,1)S(1)} %get-tuple-element.121), channel_id=1, source_target_pairs={{24,16},{28,20},{25,17},{29,21},{26,18},{30,22},{27,19},{31,23}} | collective-permute-start | bytes 884744 | tf_op jit(solution)/shard_map/ppermute | solution.py:77
  282.3 13.8 %collective-permute-start.41 = (bf16[64,2304]{1,0:T(8,128)(2,1)S(1)}, bf16[64,2304]{1,0:T(8,128)(2,1)S(1)}, u32[]{:S(2)}, u32[]{:S(2)}) collective-permute-start(bf16[64,2304]{1,0:T(8,128)(2,1)S(1)} %add_convert_fusion.16), channel_id=1, source_target_pairs={{0,8},{4,12},{8,16},{12,20},{1,9},{5,13},{9,17},{13,21},{2,10},{6,... | collective-permute-start | bytes 884744 | tf_op jit(solution)/shard_map/ppermute | solution.py:77
  289.8 12.6 %collective-permute-start.23 = (bf16[64,2304]{1,0:T(8,128)(2,1)S(1)}, bf16[64,2304]{1,0:T(8,128)(2,1)S(1)}, u32[]{:S(2)}, u32[]{:S(2)}) collective-permute-start(bf16[64,2304]{1,0:T(8,128)(2,1)S(1)} %add_convert_fusion.25), channel_id=1, source_target_pairs={{0,8},{4,12},{8,16},{12,20},{1,9},{5,13},{9,17},{13,21},{2,10},{6,... | collective-permute-start | bytes 884744 | tf_op jit(solution)/shard_map/ppermute | solution.py:77
  297.5 15.4 %collective-permute-start.42 = (bf16[64,2304]{1,0:T(8,128)(2,1)S(1)}, bf16[64,2304]{1,0:T(8,128)(2,1)S(1)}, u32[]{:S(2)}, u32[]{:S(2)}) collective-permute-start(bf16[64,2304]{1,0:T(8,128)(2,1)S(1)} %get-tuple-element.122), channel_id=1, source_target_pairs={{0,8},{4,12},{8,16},{12,20},{16,24},{20,28},{1,9},{5,13},{9,17},{1... | collective-permute-start | bytes 884744 | tf_op jit(solution)/shard_map/ppermute | solution.py:77
  303.8 14.0 %collective-permute-start.24 = (bf16[64,2304]{1,0:T(8,128)(2,1)S(1)}, bf16[64,2304]{1,0:T(8,128)(2,1)S(1)}, u32[]{:S(2)}, u32[]{:S(2)}) collective-permute-start(bf16[64,2304]{1,0:T(8,128)(2,1)S(1)} %get-tuple-element.118), channel_id=1, source_target_pairs={{0,8},{4,12},{8,16},{12,20},{16,24},{20,28},{1,9},{5,13},{9,17},{1... | collective-permute-start | bytes 884744 | tf_op jit(solution)/shard_map/ppermute | solution.py:77
  310.9 12.9 %collective-permute-start.27 = (bf16[64,2304]{1,0:T(8,128)(2,1)S(1)}, bf16[64,2304]{1,0:T(8,128)(2,1)S(1)}, u32[]{:S(2)}, u32[]{:S(2)}) collective-permute-start(bf16[64,2304]{1,0:T(8,128)(2,1)S(1)} %add_convert_fusion.22), channel_id=1, source_target_pairs={{8,0},{12,4},{16,8},{20,12},{24,16},{28,20},{9,1},{13,5},{17,9},{2... | collective-permute-start | bytes 884744 | tf_op jit(solution)/shard_map/ppermute | solution.py:77
  328.8 260.9 %collective-permute-start.93 = (bf16[512,2304]{1,0:T(8,128)(2,1)}, bf16[512,2304]{1,0:T(8,128)(2,1)}, u32[]{:S(2)}, u32[]{:S(2)}) collective-permute-start(bf16[512,2304]{1,0:T(8,128)(2,1)} %fusion.3), channel_id=1, source_target_pairs={{0,4},{4,0},{8,12},{12,8},{16,20},{20,16},{24,28},{28,24},{1,5},{5... | collective-permute-start | bytes 7077896 | tf_op jit(solution)/shard_map/ppermute | solution.py:81
  362.9 20.9 %collective-permute-start.59 = (bf16[64,2304]{1,0:T(8,128)(2,1)S(1)}, bf16[64,2304]{1,0:T(8,128)(2,1)S(1)}, u32[]{:S(2)}, u32[]{:S(2)}) collective-permute-start(bf16[64,2304]{1,0:T(8,128)(2,1)S(1)} %get-tuple-element.31), channel_id=1, source_target_pairs={{0,8},{4,12},{8,16},{12,20},{16,24},{20,28},{1,9},{5,13},{9,17},{1... | collective-permute-start | bytes 884744 | tf_op jit(solution)/shard_map/ppermute | solution.py:77
  364.8 28.6 %collective-permute-start.58 = (bf16[64,2304]{1,0:T(8,128)(2,1)S(1)}, bf16[64,2304]{1,0:T(8,128)(2,1)S(1)}, u32[]{:S(2)}, u32[]{:S(2)}) collective-permute-start(bf16[64,2304]{1,0:T(8,128)(2,1)S(1)} %get-tuple-element.31), channel_id=1, source_target_pairs={{8,0},{12,4},{16,8},{20,12},{24,16},{28,20},{9,1},{13,5},{17,9},{2... | collective-permute-start | bytes 884744 | tf_op jit(solution)/shard_map/ppermute | solution.py:77
  397.0 32.8 %collective-permute-start.52 = (bf16[64,2304]{1,0:T(8,128)(2,1)}, bf16[64,2304]{1,0:T(8,128)(2,1)}, u32[]{:S(2)}, u32[]{:S(2)}) collective-permute-start(bf16[64,2304]{1,0:T(8,128)(2,1)} %get-tuple-element.112), channel_id=1, source_target_pairs={{0,8},{4,12},{1,9},{5,13},{2,10},{6,14},{3,11},{7,15}} | collective-permute-start | bytes 884744 | tf_op jit(solution)/shard_map/ppermute | solution.py:77
  398.3 39.7 %collective-permute-start.55 = (bf16[64,2304]{1,0:T(8,128)(2,1)}, bf16[64,2304]{1,0:T(8,128)(2,1)}, u32[]{:S(2)}, u32[]{:S(2)}) collective-permute-start(bf16[64,2304]{1,0:T(8,128)(2,1)} %get-tuple-element.113), channel_id=1, source_target_pairs={{24,16},{28,20},{25,17},{29,21},{26,18},{30,22},{27,19},{31,23}} | collective-permute-start | bytes 884744 | tf_op jit(solution)/shard_map/ppermute | solution.py:77
  432.8 14.5 %collective-permute-start.67 = (bf16[64,2304]{1,0:T(8,128)(2,1)S(1)}, bf16[64,2304]{1,0:T(8,128)(2,1)S(1)}, u32[]{:S(2)}, u32[]{:S(2)}) collective-permute-start(bf16[64,2304]{1,0:T(8,128)(2,1)S(1)} %get-tuple-element.117), channel_id=1, source_target_pairs={{24,16},{28,20},{25,17},{29,21},{26,18},{30,22},{27,19},{31,23}} | collective-permute-start | bytes 884744 | tf_op jit(solution)/shard_map/ppermute | solution.py:77
  443.4 13.9 %collective-permute-start.54 = (bf16[64,2304]{1,0:T(8,128)(2,1)S(1)}, bf16[64,2304]{1,0:T(8,128)(2,1)S(1)}, u32[]{:S(2)}, u32[]{:S(2)}) collective-permute-start(bf16[64,2304]{1,0:T(8,128)(2,1)S(1)} %get-tuple-element.110), channel_id=1, source_target_pairs={{0,8},{4,12},{8,16},{12,20},{16,24},{20,28},{1,9},{5,13},{9,17},{1... | collective-permute-start | bytes 884744 | tf_op jit(solution)/shard_map/ppermute | solution.py:77
  468.5 12.6 %collective-permute-start.71 = (bf16[64,2304]{1,0:T(8,128)(2,1)S(1)}, bf16[64,2304]{1,0:T(8,128)(2,1)S(1)}, u32[]{:S(2)}, u32[]{:S(2)}) collective-permute-start(bf16[64,2304]{1,0:T(8,128)(2,1)S(1)} %get-tuple-element.59), channel_id=1, source_target_pairs={{0,8},{4,12},{8,16},{12,20},{16,24},{20,28},{1,9},{5,13},{9,17},{1... | collective-permute-start | bytes 884744 | tf_op jit(solution)/shard_map/ppermute | solution.py:77
  472.7 18.8 %collective-permute-start.70 = (bf16[64,2304]{1,0:T(8,128)(2,1)S(1)}, bf16[64,2304]{1,0:T(8,128)(2,1)S(1)}, u32[]{:S(2)}, u32[]{:S(2)}) collective-permute-start(bf16[64,2304]{1,0:T(8,128)(2,1)S(1)} %get-tuple-element.59), channel_id=1, source_target_pairs={{8,0},{12,4},{16,8},{20,12},{24,16},{28,20},{9,1},{13,5},{17,9},{2... | collective-permute-start | bytes 884744 | tf_op jit(solution)/shard_map/ppermute | solution.py:77
  479.2 21.6 %collective-permute-start.74 = (bf16[64,2304]{1,0:T(8,128)(2,1)S(1)}, bf16[64,2304]{1,0:T(8,128)(2,1)S(1)}, u32[]{:S(2)}, u32[]{:S(2)}) collective-permute-start(bf16[64,2304]{1,0:T(8,128)(2,1)S(1)} %get-tuple-element.57), channel_id=1, source_target_pairs={{8,0},{12,4},{16,8},{20,12},{24,16},{28,20},{9,1},{13,5},{17,9},{2... | collective-permute-start | bytes 884744 | tf_op jit(solution)/shard_map/ppermute | solution.py:77
  485.3 17.5 %collective-permute-start.76 = (bf16[64,2304]{1,0:T(8,128)(2,1)S(1)}, bf16[64,2304]{1,0:T(8,128)(2,1)S(1)}, u32[]{:S(2)}, u32[]{:S(2)}) collective-permute-start(bf16[64,2304]{1,0:T(8,128)(2,1)S(1)} %collective-permute-done.75), channel_id=1, source_target_pairs={{8,16},{12,20},{16,24},{20,28},{9,17},{13,21},{17,25},{21,29},{10,... | collective-permute-start | bytes 884744 | tf_op jit(solution)/shard_map/ppermute | solution.py:77
  490.1 14.6 %collective-permute-start.73 = (bf16[64,2304]{1,0:T(8,128)(2,1)S(1)}, bf16[64,2304]{1,0:T(8,128)(2,1)S(1)}, u32[]{:S(2)}, u32[]{:S(2)}) collective-permute-start(bf16[64,2304]{1,0:T(8,128)(2,1)S(1)} %collective-permute-done.72), channel_id=1, source_target_pairs={{16,24},{20,28},{17,25},{21,29},{18,26},{22,30},{19,27},{23,31}} | collective-permute-start | bytes 884744 | tf_op jit(solution)/shard_map/ppermute | solution.py:77
  491.5 89.3 %collective-permute-start.89 = (bf16[512,256]{0,1:T(8,128)(2,1)S(1)}, bf16[512,256]{0,1:T(8,128)(2,1)}, u32[]{:S(2)}, u32[]{:S(2)}) collective-permute-start(bf16[512,256]{0,1:T(8,128)(2,1)S(1)} %copy-done.74), channel_id=1, source_target_pairs={{0,4},{4,0},{8,12},{12,8},{16,20},{20,16},{24,28},{28,24},{1,5},{5... | collective-permute-start | bytes 786440 | tf_op jit(solution)/shard_map/ppermute | solution.py:81
  500.8 14.0 %collective-permute-start.78 = (bf16[64,2304]{1,0:T(8,128)(2,1)S(1)}, bf16[64,2304]{1,0:T(8,128)(2,1)S(1)}, u32[]{:S(2)}, u32[]{:S(2)}) collective-permute-start(bf16[64,2304]{1,0:T(8,128)(2,1)S(1)} %collective-permute-done.70), channel_id=1, source_target_pairs={{8,0},{12,4},{16,8},{20,12},{9,1},{13,5},{17,9},{21,13},{10,2},{14... | collective-permute-start | bytes 884744 | tf_op jit(solution)/shard_map/ppermute | solution.py:77
  502.7 18.4 %collective-permute-start.79 = (bf16[64,2304]{1,0:T(8,128)(2,1)S(1)}, bf16[64,2304]{1,0:T(8,128)(2,1)S(1)}, u32[]{:S(2)}, u32[]{:S(2)}) collective-permute-start(bf16[64,2304]{1,0:T(8,128)(2,1)S(1)} %collective-permute-done.74), channel_id=1, source_target_pairs={{8,0},{12,4},{16,8},{20,12},{9,1},{13,5},{17,9},{21,13},{10,2},{14... | collective-permute-start | bytes 884744 | tf_op jit(solution)/shard_map/ppermute | solution.py:77
  504.7 17.8 %collective-permute-start.77 = (bf16[64,2304]{1,0:T(8,128)(2,1)S(1)}, bf16[64,2304]{1,0:T(8,128)(2,1)S(1)}, u32[]{:S(2)}, u32[]{:S(2)}) collective-permute-start(bf16[64,2304]{1,0:T(8,128)(2,1)S(1)} %collective-permute-done.76), channel_id=1, source_target_pairs={{16,24},{20,28},{17,25},{21,29},{18,26},{22,30},{19,27},{23,31}} | collective-permute-start | bytes 884744 | tf_op jit(solution)/shard_map/ppermute | solution.py:77
  514.8 89.6 %collective-permute-start.107 = (bf16[512,1152]{1,0:T(8,128)(2,1)}, bf16[512,1152]{1,0:T(8,128)(2,1)}, u32[]{:S(2)}, u32[]{:S(2)}) collective-permute-start(bf16[512,1152]{1,0:T(8,128)(2,1)} %pad_maximum_fusion.6), channel_id=1, source_target_pairs={{0,4},{4,0},{8,12},{12,8},{16,20},{20,16},{24,28},{28,24},{1,5},{5... | collective-permute-start | bytes 3538952 | tf_op jit(solution)/shard_map/ppermute | solution.py:81
  535.6 41.9 %collective-permute-start.90 = (bf16[512,2304]{1,0:T(8,128)(2,1)}, bf16[512,2304]{1,0:T(8,128)(2,1)}, u32[]{:S(2)}, u32[]{:S(2)}) collective-permute-start(bf16[512,2304]{1,0:T(8,128)(2,1)} %get-tuple-element.160), channel_id=1, source_target_pairs={{0,4},{4,0},{8,12},{12,8},{16,20},{20,16},{24,28},{28,24},{1,5},{5... | collective-permute-start | bytes 7077896 | tf_op jit(solution)/shard_map/ppermute | solution.py:81
  562.6 13.5 %collective-permute-start.82 = (bf16[512,512]{0,1:T(8,128)(2,1)}, bf16[512,512]{0,1:T(8,128)(2,1)}, u32[]{:S(2)}, u32[]{:S(2)}) collective-permute-start(bf16[512,512]{0,1:T(8,128)(2,1)} %fusion.100), channel_id=1, source_target_pairs={{0,4},{4,0},{8,12},{12,8},{16,20},{20,16},{24,28},{28,24},{1,5},{5... | collective-permute-start | bytes 1572872 | tf_op jit(solution)/shard_map/ppermute | solution.py:81
  586.4 190.7 %reduce-scatter.8.cloned.1.call-start = ((), (), s32[]{:S(2)}) async-start(), calls=%async_computation.8 | async-start | bytes 2949120 | tf_op jit(solution)/shard_map/reduce_scatter | solution.py:261
  589.2 13.7 %collective-permute-start.108 = (bf16[512,2304]{1,0:T(8,128)(2,1)}, bf16[512,2304]{1,0:T(8,128)(2,1)S(1)}, u32[]{:S(2)}, u32[]{:S(2)}) collective-permute-start(bf16[512,2304]{1,0:T(8,128)(2,1)} %get-tuple-element.24), channel_id=1, source_target_pairs={{0,4},{4,0},{8,12},{12,8},{16,20},{20,16},{24,28},{28,24},{1,5},{5... | collective-permute-start | bytes 7077896 | tf_op jit(solution)/shard_map/ppermute | solution.py:81
  596.3 204.7 %reduce-scatter.12.cloned.1.call-start = ((), (), s32[]{:S(2)}) async-start(), calls=%async_computation.10 | async-start | bytes 6635520 | tf_op jit(solution)/shard_map/reduce_scatter | solution.py:261
  623.0 211.9 %reduce-scatter.10.cloned.1.call-start = ((), (), s32[]{:S(2)}) async-start(), calls=%async_computation.9 | async-start | bytes 13271040 | tf_op jit(solution)/shard_map/reduce_scatter | solution.py:261
  669.5 16.9 %collective-permute-start.83 = (bf16[128,2304]{1,0:T(8,128)(2,1)S(1)}, bf16[128,2304]{1,0:T(8,128)(2,1)S(1)}, u32[]{:S(2)}, u32[]{:S(2)}) collective-permute-start(bf16[128,2304]{1,0:T(8,128)(2,1)S(1)} %get-tuple-element.83), channel_id=1, source_target_pairs={{0,8},{4,12},{1,9},{5,13},{2,10},{6,14},{3,11},{7,15}} | collective-permute-start | bytes 1769480 | tf_op jit(solution)/shard_map/ppermute | solution.py:77
  670.8 17.7 %collective-permute-start.86 = (bf16[128,2304]{1,0:T(8,128)(2,1)S(1)}, bf16[128,2304]{1,0:T(8,128)(2,1)S(1)}, u32[]{:S(2)}, u32[]{:S(2)}) collective-permute-start(bf16[128,2304]{1,0:T(8,128)(2,1)S(1)} %get-tuple-element.84), channel_id=1, source_target_pairs={{24,16},{28,20},{25,17},{29,21},{26,18},{30,22},{27,19},{31,23}} | collective-permute-start | bytes 1769480 | tf_op jit(solution)/shard_map/ppermute | solution.py:77
  686.6 16.1 %collective-permute-start.84 = (bf16[128,2304]{1,0:T(8,128)(2,1)S(1)}, bf16[128,2304]{1,0:T(8,128)(2,1)S(1)}, u32[]{:S(2)}, u32[]{:S(2)}) collective-permute-start(bf16[128,2304]{1,0:T(8,128)(2,1)S(1)} %add_convert_fusion.3), channel_id=1, source_target_pairs={{0,8},{4,12},{8,16},{12,20},{1,9},{5,13},{9,17},{13,21},{2,10},{6,... | collective-permute-start | bytes 1769480 | tf_op jit(solution)/shard_map/ppermute | solution.py:77
  703.7 15.3 %collective-permute-start.87 = (bf16[128,2304]{1,0:T(8,128)(2,1)S(1)}, bf16[128,2304]{1,0:T(8,128)(2,1)S(1)}, u32[]{:S(2)}, u32[]{:S(2)}) collective-permute-start(bf16[128,2304]{1,0:T(8,128)(2,1)S(1)} %get-tuple-element.82), channel_id=1, source_target_pairs={{16,8},{20,12},{24,16},{28,20},{17,9},{21,13},{25,17},{29,21},{18,... | collective-permute-start | bytes 1769480 | tf_op jit(solution)/shard_map/ppermute | solution.py:77
  706.1 63.4 %collective-permute-start.85 = (bf16[128,2304]{1,0:T(8,128)(2,1)}, bf16[128,2304]{1,0:T(8,128)(2,1)S(1)}, u32[]{:S(2)}, u32[]{:S(2)}) collective-permute-start(bf16[128,2304]{1,0:T(8,128)(2,1)} %get-tuple-element.81), channel_id=1, source_target_pairs={{0,8},{4,12},{8,16},{12,20},{16,24},{20,28},{1,9},{5,13},{9,17},{1... | collective-permute-start | bytes 1769480 | tf_op jit(solution)/shard_map/ppermute | solution.py:77
  721.2 48.4 %collective-permute-start.88 = (bf16[128,2304]{1,0:T(8,128)(2,1)}, bf16[128,2304]{1,0:T(8,128)(2,1)S(1)}, u32[]{:S(2)}, u32[]{:S(2)}) collective-permute-start(bf16[128,2304]{1,0:T(8,128)(2,1)} %add_convert_fusion), channel_id=1, source_target_pairs={{8,0},{12,4},{16,8},{20,12},{24,16},{28,20},{9,1},{13,5},{17,9},{2... | collective-permute-start | bytes 1769480 | tf_op jit(solution)/shard_map/ppermute | solution.py:77
  779.7 16.3 %collective-permute-start.97 = (bf16[2,72,256]{2,1,0:T(8,128)(2,1)S(1)}, bf16[2,72,256]{2,1,0:T(8,128)(2,1)S(1)}, u32[]{:S(2)}, u32[]{:S(2)}) collective-permute-start(bf16[2,72,256]{2,1,0:T(8,128)(2,1)S(1)} %get-tuple-element.186), channel_id=1, source_target_pairs={{0,16},{4,20},{8,24},{12,28},{16,0},{20,4},{24,8},{28,12},{1,17},{... | collective-permute-start | bytes 221192 | tf_op jit(solution)/shard_map/ppermute | solution.py:272
  781.6 17.7 %collective-permute-start.99 = (bf16[2,72,256]{2,1,0:T(8,128)(2,1)S(1)}, bf16[2,72,256]{2,1,0:T(8,128)(2,1)S(1)}, u32[]{:S(2)}, u32[]{:S(2)}) collective-permute-start(bf16[2,72,256]{2,1,0:T(8,128)(2,1)S(1)} %get-tuple-element.183), channel_id=1, source_target_pairs={{0,24},{4,28},{8,0},{12,4},{16,8},{20,12},{24,16},{28,20},{1,25},{... | collective-permute-start | bytes 221192 | tf_op jit(solution)/shard_map/ppermute | solution.py:272
  782.3 13.6 %collective-permute-start.96 = (bf16[2,72,512]{2,1,0:T(8,128)(2,1)S(1)}, bf16[2,72,512]{2,1,0:T(8,128)(2,1)S(1)}, u32[]{:S(2)}, u32[]{:S(2)}) collective-permute-start(bf16[2,72,512]{2,1,0:T(8,128)(2,1)S(1)} %get-tuple-element.157), channel_id=1, source_target_pairs={{0,8},{4,12},{8,16},{12,20},{16,24},{20,28},{24,0},{28,4},{1,9},{5... | collective-permute-start | bytes 442376 | tf_op jit(solution)/shard_map/ppermute | solution.py:272
  783.5 15.7 %collective-permute-start.98 = (bf16[2,72,512]{2,1,0:T(8,128)(2,1)S(1)}, bf16[2,72,512]{2,1,0:T(8,128)(2,1)S(1)}, u32[]{:S(2)}, u32[]{:S(2)}) collective-permute-start(bf16[2,72,512]{2,1,0:T(8,128)(2,1)S(1)} %get-tuple-element.158), channel_id=1, source_target_pairs={{0,16},{4,20},{8,24},{12,28},{16,0},{20,4},{24,8},{28,12},{1,17},{... | collective-permute-start | bytes 442376 | tf_op jit(solution)/shard_map/ppermute | solution.py:272
  785.8 15.2 %collective-permute-start.100 = (bf16[2,72,512]{2,1,0:T(8,128)(2,1)S(1)}, bf16[2,72,512]{2,1,0:T(8,128)(2,1)S(1)}, u32[]{:S(2)}, u32[]{:S(2)}) collective-permute-start(bf16[2,72,512]{2,1,0:T(8,128)(2,1)S(1)} %get-tuple-element.155), channel_id=1, source_target_pairs={{0,24},{4,28},{8,0},{12,4},{16,8},{20,12},{24,16},{28,20},{1,25},{... | collective-permute-start | bytes 442376 | tf_op jit(solution)/shard_map/ppermute | solution.py:272
  805.6 28.5 %collective-permute-start.111 = (bf16[2,72,1152]{2,1,0:T(8,128)(2,1)S(1)}, bf16[2,72,1152]{2,1,0:T(8,128)(2,1)S(1)}, u32[]{:S(2)}, u32[]{:S(2)}) collective-permute-start(bf16[2,72,1152]{2,1,0:T(8,128)(2,1)S(1)} %get-tuple-element.136), channel_id=1, source_target_pairs={{0,16},{4,20},{8,24},{12,28},{16,0},{20,4},{24,8},{28,12},{1,17},{... | collective-permute-start | bytes 995336 | tf_op jit(solution)/shard_map/ppermute | solution.py:272
  807.0 30.8 %collective-permute-start.112 = (bf16[2,72,1152]{2,1,0:T(8,128)(2,1)S(1)}, bf16[2,72,1152]{2,1,0:T(8,128)(2,1)S(1)}, u32[]{:S(2)}, u32[]{:S(2)}) collective-permute-start(bf16[2,72,1152]{2,1,0:T(8,128)(2,1)S(1)} %get-tuple-element.133), channel_id=1, source_target_pairs={{0,24},{4,28},{8,0},{12,4},{16,8},{20,12},{24,16},{28,20},{1,25},{... | collective-permute-start | bytes 995336 | tf_op jit(solution)/shard_map/ppermute | solution.py:272
  841.1 16.2 %collective-permute-start.104 = (bf16[2,72,2304]{2,1,0:T(8,128)(2,1)S(1)}, bf16[2,72,2304]{2,1,0:T(8,128)(2,1)S(1)}, u32[]{:S(2)}, u32[]{:S(2)}) collective-permute-start(bf16[2,72,2304]{2,1,0:T(8,128)(2,1)S(1)} %get-tuple-element.108), channel_id=1, source_target_pairs={{0,8},{4,12},{8,16},{12,20},{16,24},{20,28},{24,0},{28,4},{1,9},{5... | collective-permute-start | bytes 1990664 | tf_op jit(solution)/shard_map/ppermute | solution.py:272
  841.1 56.9 %collective-permute-start.105 = (bf16[2,72,2304]{2,1,0:T(8,128)(2,1)S(1)}, bf16[2,72,2304]{2,1,0:T(8,128)(2,1)S(1)}, u32[]{:S(2)}, u32[]{:S(2)}) collective-permute-start(bf16[2,72,2304]{2,1,0:T(8,128)(2,1)S(1)} %get-tuple-element.109), channel_id=1, source_target_pairs={{0,16},{4,20},{8,24},{12,28},{16,0},{20,4},{24,8},{28,12},{1,17},{... | collective-permute-start | bytes 1990664 | tf_op jit(solution)/shard_map/ppermute | solution.py:272
  844.3 58.0 %collective-permute-start.106 = (bf16[2,72,2304]{2,1,0:T(8,128)(2,1)S(1)}, bf16[2,72,2304]{2,1,0:T(8,128)(2,1)S(1)}, u32[]{:S(2)}, u32[]{:S(2)}) collective-permute-start(bf16[2,72,2304]{2,1,0:T(8,128)(2,1)S(1)} %get-tuple-element.106), channel_id=1, source_target_pairs={{0,24},{4,28},{8,0},{12,4},{16,8},{20,12},{24,16},{28,20},{1,25},{... | collective-permute-start | bytes 1990664 | tf_op jit(solution)/shard_map/ppermute | solution.py:272
  (199 other events, 1850.5 us)
Sparse Core Ops, SparseCore 0:
  10.4 48.3 all-gather.4
  61.3 106.2 all-gather.6
  170.0 61.9 all-gather.8
  586.5 27.1 reduce-scatter.5
  616.6 37.3 reduce-scatter.7
  657.4 61.9 reduce-scatter.11
  722.5 106.0 reduce-scatter.9

commit v2 on v1

v2 whole, which is shorter than its diff:
```python
import jax
import jax.numpy as jnp
from jax import lax
from jax.experimental import pallas as pl
from jax.experimental.pallas import tpu as pltpu
from jax.sharding import PartitionSpec as P

HEADS = 8
KV_HEADS = 4
HEAD_DIM = 256

EPSILON = 1e-06
SOFT_CAP = 50.0
ROTARY_BASE = 10000.0
MASKED_SCORE = -1e30
STREAMS = 1

F32 = jnp.float32
BF16 = jnp.bfloat16


def positions_of(rows, half_block, ctx_count):
    owners = rows // (2 * half_block)
    within = rows % (2 * half_block)
    return jnp.where(
        within < half_block,
        owners * half_block + within,
        (2 * ctx_count - 1 - owners) * half_block + within - half_block,
    )


def rotary_tables(places, head_dim):
    half_width = head_dim // 2
    frequency = ROTARY_BASE ** (-jnp.arange(half_width, dtype=F32) * 2.0 / head_dim)
    angles = places.astype(F32)[:, None] * frequency[None, :]
    cosine = jnp.concatenate([jnp.cos(angles), jnp.cos(angles)], -1)
    sine_table = jnp.concatenate([jnp.sin(angles), jnp.sin(angles)], -1)
    return (cosine, sine_table)


def turned(values):
    half_width = values.shape[-1] // 2
    return jnp.concatenate([-values[..., half_width:], values[..., :half_width]], -1)


def rotate(values, cosine, sine_table):
    return values * cosine + turned(values) * sine_table


def rotate_back(grads, cosine, sine_table):
    return grads * cosine - turned(grads * sine_table)


def inverse_rms(values):
    return lax.rsqrt(jnp.mean(values * values, -1, keepdims=True) + EPSILON)


def norm_backward(values, scale, grad_normed):
    normed = values * scale
    return scale * (grad_normed - normed * jnp.mean(grad_normed * normed, -1, keepdims=True))


def geglu(gate, upper):
    return jax.nn.gelu(gate, approximate=True) * upper


def dot(a, b):
    return jnp.dot(a, b, preferred_element_type=F32)


def dot_t(a, b):
    return jnp.einsum("tk,dk->td", a, b, preferred_element_type=F32)


def swap(values, axis, distance, count):
    return lax.ppermute(values, axis, [(i, i ^ distance) for i in range(count)])


def line_gather(values, ranks):
    slots = {0: values}
    bit = ranks // 2
    while bit:
        slots.update({k ^ bit: swap(v, "ctx", 2 * bit, 2 * ranks) for k, v in slots.items()})
        bit //= 2
    return [slots[k] for k in range(ranks)]


def line_scatter(parts, ranks, beside=()):
    sums = {k: v.astype(F32) for k, v in enumerate(parts)}
    bit = 1
    while bit < ranks:
        got = {
            k: swap(sums.pop(k).astype(BF16), "ctx", 2 * bit, 2 * ranks)
            for k in sorted(sums, reverse=True)
            if k & bit
        }
        if beside and bit == 1:
            got, beside = together(got, beside)
        for k, v in got.items():
            sums[k ^ bit] = sums[k ^ bit] + v.astype(F32)
        bit *= 2
    return (sums[0], beside) if beside else sums[0]


def square_gather(piece, place, beside):
    rows = piece.shape[0]
    half = rows // 2
    near, far = swap(piece, "fsdp", 1, 4), swap(piece, "fsdp", 2, 4)
    first, then = beside
    near, far, first = together(near, far, first)
    corner_a, corner_b = swap(near[:half], "fsdp", 2, 4), swap(far[half:], "fsdp", 1, 4)
    corner_a, corner_b, second = together(corner_a, corner_b, then(first))
    whole = jnp.zeros((4 * rows, piece.shape[1]), piece.dtype)
    for block, at in (
        (piece, place * rows),
        (near, (place ^ 1) * rows),
        (far, (place ^ 2) * rows),
        (corner_a, (place ^ 3) * rows),
        (corner_b, (place ^ 3) * rows + half),
    ):
        whole = lax.dynamic_update_slice_in_dim(whole, block, at, 0)
    return whole, first, second


def corner_scatter(corner, count):
    half = corner.shape[0] // 2
    corner = corner.astype(BF16)
    return swap(corner[:half], "fsdp", 1, count), swap(corner[half:], "fsdp", 2, count)


def rows_scatter(parts, corners, count):
    half = parts[3].shape[0] // 2
    by_near, by_far = corners[0].astype(F32), corners[1].astype(F32)
    near = jnp.concatenate([parts[1][:half], parts[1][half:] + by_far], 0).astype(BF16)
    far = jnp.concatenate([parts[2][:half] + by_near, parts[2][half:]], 0).astype(BF16)
    near, far = swap(near, "fsdp", 1, count), swap(far, "fsdp", 2, count)
    return parts[0] + near.astype(F32) + far.astype(F32)


def together(*values):
    return lax.optimization_barrier(values)


VMEM_BYTES = 60 * 1024 * 1024


def kernel_call(body, grid, in_specs, out_specs, out_shape, scratch, flops, moved, prefetch=0):
    return pl.pallas_call(
        body,
        grid_spec=pltpu.PrefetchScalarGridSpec(
            num_scalar_prefetch=prefetch,
            grid=grid,
            in_specs=in_specs,
            out_specs=out_specs,
            scratch_shapes=scratch,
        ),
        out_shape=out_shape,
        compiler_params=pltpu.CompilerParams(
            vmem_limit_bytes=VMEM_BYTES, dimension_semantics=("arbitrary",) * len(grid)
        ),
        cost_estimate=pl.CostEstimate(flops=flops, bytes_accessed=moved, transcendentals=0),
    )


def mm(a, b):
    return jnp.dot(a, b, preferred_element_type=F32)


def mm_nt(a, b):
    return lax.dot_general(a, b, (((1,), (1,)), ((), ())), preferred_element_type=F32)


def mm_tn(a, b):
    return lax.dot_general(a, b, (((0,), (0,)), ((), ())), preferred_element_type=F32)


def tile_of(size, most):
    return max(t for t in range(128, most + 1, 128) if size % t == 0)


def gelu_parts(gate):
    rate = 0.7978845608028654
    square = gate * gate
    t = jnp.tanh(rate * gate * (1.0 + 0.044715 * square))
    half = 0.5 * (1.0 + t)
    slope = half + 0.5 * gate * (1.0 - t * t) * rate * (1.0 + 3.0 * 0.044715 * square)
    return gate * half, slope


def core_blocks(shape, steps):
    lead = (0,) * (len(shape) - 1)
    return [
        pl.BlockSpec(shape, lambda h, i, c: (*lead, jnp.where(h == 0, i, steps - 1))),
        pl.BlockSpec(shape, lambda h, i, c: (*lead, jnp.where(h == 0, 0, i))),
    ]


def gate_up_forward(values, w_in, core, most=384):
    rows, width = values.shape
    size = w_in.shape[2] // 2
    tile = tile_of(size, most)
    steps = size // tile

    def body(core_ref, x, g, u, hidden0, hidden1, gate_all, up_all):
        gate, up = mm(x[...], g[0]), mm(x[...], u[0])
        gate_all[0] = gate
        up_all[0] = up
        hidden = (gelu_parts(gate)[0] * up).astype(BF16)

        @pl.when(pl.program_id(0) == 0)
        def _():
            hidden0[0] = hidden

        @pl.when(pl.program_id(0) == 1)
        def _():
            hidden1[0] = hidden

    saved = pl.BlockSpec((1, rows, tile), lambda h, i, c: (h, 0, i))
    return kernel_call(
        body,
        (2, steps),
        [
            pl.BlockSpec((rows, width), lambda h, i, c: (0, 0)),
            pl.BlockSpec((1, width, tile), lambda h, i, c: (c[0] ^ h, 0, i)),
            pl.BlockSpec((1, width, tile), lambda h, i, c: (c[0] ^ h, 0, steps + i)),
        ],
        core_blocks((1, rows, tile), steps) + [saved, saved],
        [jax.ShapeDtypeStruct((1, rows, size), BF16)] * 2
        + [jax.ShapeDtypeStruct((2, rows, size), F32)] * 2,
        [],
        8 * rows * width * size,
        8 * width * size + 20 * rows * size,
        prefetch=1,
    )(core, values, w_in, w_in)


def down_forward(hidden, w_out, core, earlier=(), most=768):
    _, rows, size = hidden[0].shape
    width = w_out.shape[1]
    tile = tile_of(width, most)

    def body(core_ref, h0, h1, o0, o1, *refs):
        out = refs[-1]
        out[...] = (mm_nt(h0[0], o0[0]) + mm_nt(h1[0], o1[0])).astype(BF16)

    whole = pl.BlockSpec((1, rows, size), lambda i, c: (0, 0, 0))
    return kernel_call(
        body,
        (width // tile,),
        [
            whole,
            whole,
            pl.BlockSpec((1, tile, size), lambda i, c: (c[0], i, 0)),
            pl.BlockSpec((1, tile, size), lambda i, c: (1 - c[0], i, 0)),
        ]
        + [pl.BlockSpec(memory_space=pl.ANY)] * len(earlier),
        pl.BlockSpec((rows, tile), lambda i, c: (0, i)),
        jax.ShapeDtypeStruct((rows, width), BF16),
        [],
        4 * rows * width * size,
        4 * width * size + 4 * rows * size,
        prefetch=1,
    )(core, *hidden, w_out, w_out, *earlier)


def down_backward(d_mixed, gate_all, up_all, w_out, core, most=384):
    rows, width = d_mixed.shape
    size = w_out.shape[2]
    tile = tile_of(size, most)
    steps = size // tile

    def body(core_ref, x, gate, up, o, dgu0, dgu1):
        d_hidden = mm(x[...], o[0])
        value, slope = gelu_parts(gate[0])
        d_gate = (d_hidden * up[0] * slope).astype(BF16)
        d_up = (d_hidden * value).astype(BF16)

        @pl.when(pl.program_id(0) == 0)
        def _():
            dgu0[0] = d_gate
            dgu0[1] = d_up

        @pl.when(pl.program_id(0) == 1)
        def _():
            dgu1[0] = d_gate
            dgu1[1] = d_up

    saved = pl.BlockSpec((1, rows, tile), lambda h, i, c: (h, 0, i))
    return kernel_call(
        body,
        (2, steps),
        [
            pl.BlockSpec((rows, width), lambda h, i, c: (0, 0)),
            saved,
            saved,
            pl.BlockSpec((1, width, tile), lambda h, i, c: (c[0] ^ h, 0, i)),
        ],
        core_blocks((2, rows, tile), steps),
        [jax.ShapeDtypeStruct((2, rows, size), BF16)] * 2,
        [],
        4 * rows * width * size,
        4 * width * size + 24 * rows * size,
        prefetch=1,
    )(core, d_mixed, gate_all, up_all, w_out)


def gate_up_backward(dgu, w_in, core, earlier=(), most=768):
    _, rows, size = dgu[0].shape
    width = w_in.shape[1]
    tile = tile_of(width, most)

    def body(core_ref, d0, d1, w0, w1, *refs):
        out = refs[-1]
        total = mm_nt(d0[0], w0[0, :, :size]) + mm_nt(d0[1], w0[0, :, size:])
        total += mm_nt(d1[0], w1[0, :, :size]) + mm_nt(d1[1], w1[0, :, size:])
        out[...] = total.astype(BF16)

    whole = pl.BlockSpec((2, rows, size), lambda i, c: (0, 0, 0))
    return kernel_call(
        body,
        (width // tile,),
        [
            whole,
            whole,
            pl.BlockSpec((1, tile, 2 * size), lambda i, c: (c[0], i, 0)),
            pl.BlockSpec((1, tile, 2 * size), lambda i, c: (1 - c[0], i, 0)),
        ]
        + [pl.BlockSpec(memory_space=pl.ANY)] * len(earlier),
        pl.BlockSpec((rows, tile), lambda i, c: (0, i)),
        jax.ShapeDtypeStruct((rows, width), BF16),
        [],
        8 * rows * width * size,
        8 * width * size + 8 * rows * size,
        prefetch=1,
    )(core, *dgu, w_in, w_in, *earlier)


def weight_grad_kernel(lefts, rights, ctx_count, fsdp_count):
    width = lefts[0].shape[1]
    groups, _, size = rights[0].shape
    counts = [v.shape[0] for v in lefts]
    starts = [sum(counts[:i]) for i in range(len(counts))]
    shard = width // (ctx_count * fsdp_count)
    halves = 2
    part, ctx_part = width // halves, ctx_count // halves
    tile = tile_of(size, 1152)
    steps = size // tile

    def body(*refs):
        left_refs, right_refs = refs[: len(counts)], refs[len(counts) : 2 * len(counts)]
        out, turned_left = refs[2 * len(counts) :]

        @pl.when((pl.program_id(1) == 0) & (pl.program_id(2) == 0))
        def _():
            for ref, start, count in zip(left_refs, starts, counts):
                turned_left[:, start : start + count] = ref[...].T

        product = 0.0
        for ref, start, count in zip(right_refs, starts, counts):
            product = product + mm(turned_left[:, start : start + count], ref[0])
        for f in range(fsdp_count):
            at = [(c * fsdp_count + f) * shard for c in range(ctx_part)]
            out[f] = jnp.concatenate([product[i : i + shard] for i in at], 0).astype(BF16)

    return kernel_call(
        body,
        (halves, groups, steps),
        [pl.BlockSpec((n, part), lambda h, g, t: (0, h)) for n in counts]
        + [pl.BlockSpec((1, n, tile), lambda h, g, t: (g, 0, t)) for n in counts],
        pl.BlockSpec((fsdp_count, ctx_part * shard, tile), lambda h, g, t: (0, h, g * steps + t)),
        jax.ShapeDtypeStruct((fsdp_count, ctx_count * shard, groups * size), BF16),
        [pltpu.VMEM((part, sum(counts)), BF16)],
        2 * sum(counts) * width * groups * size,
        4 * sum(counts) * (width + groups * size) + 2 * width * groups * size,
    )(*lefts, *rights)


def rotated(values, cosine, sine, back=False):
    size = values.shape[1] // 2
    low, high = values[:, :size], values[:, size:]
    if back:
        sine = -sine
    return jnp.concatenate([low * cosine - high * sine, high * cosine + low * sine], 1)


def qkv_kernel(inputs, attn, cosine, sine, core):
    rows, width = inputs.shape
    block = rows // 2
    size = HEAD_DIM

    def body(core_ref, x, gains, w0, w1, cos, sin, normed_out, q0, q1, kv):
        source = x[...].astype(F32)
        gain = gains[...].astype(F32).T[:1]
        normed = (source * inverse_rms(source) * gain).astype(BF16)
        normed_out[...] = normed
        first = core_ref[0] == 0
        own, other = mm(normed, w0[...]), mm(normed, w1[...])
        q0[...] = rotated(own[:, :size], cos[...], sin[...]).astype(BF16)
        q1[...] = rotated(other[:, :size], cos[...], sin[...]).astype(BF16)
        key = jnp.where(first, own[:, size:], other[:, size:])
        kv[:, :size] = rotated(key, cos[...], sin[...]).astype(BF16)
        kv[:, size:] = jnp.where(first, other[:, size:], own[:, size:]).astype(BF16)

    def by_rows(columns):
        return pl.BlockSpec((block, columns), lambda i, c: (i, 0))

    return kernel_call(
        body,
        (2,),
        [
            by_rows(width),
            pl.BlockSpec((width, 128), lambda i, c: (0, 3 * size // 128)),
            pl.BlockSpec((width, 2 * size), lambda i, c: (0, 0)),
            pl.BlockSpec((width, 2 * size), lambda i, c: (0, 0)),
            by_rows(size // 2),
            by_rows(size // 2),
        ],
        [by_rows(width), by_rows(size), by_rows(size), by_rows(2 * size)],
        [
            jax.ShapeDtypeStruct((rows, width), BF16),
            jax.ShapeDtypeStruct((rows, size), BF16),
            jax.ShapeDtypeStruct((rows, size), BF16),
            jax.ShapeDtypeStruct((rows, 2 * size), BF16),
        ],
        [],
        8 * rows * width * size,
        8 * width * size + 4 * rows * width,
        prefetch=1,
    )(core, inputs, attn[0], *attn, cosine, sine)


def scores(query, key, key_place, query_place):
    raw = mm_nt(query, key)
    tanh_part = jnp.tanh(raw * (HEAD_DIM**-0.5 / SOFT_CAP))
    return tanh_part, jnp.where(key_place <= query_place, jnp.exp(SOFT_CAP * tanh_part), 0.0)


def attention_specs(rows, width, block):
    def by_rows(columns):
        return pl.BlockSpec((block, columns), lambda i, c: (i, 0))

    size = HEAD_DIM
    kv = pl.BlockSpec((rows, 2 * size), lambda i, c: (0, 0))
    places = pl.BlockSpec((1, rows), lambda i, c: (0, 0))
    weights = [pl.BlockSpec((width, size), lambda i, c: (0, 2))] * 2
    return by_rows, [by_rows(size), by_rows(size), kv, kv, by_rows(1), places, places] + weights


def attention_forward(core, queries, kvs, row_places, key_places, attn):
    rows, width, size = queries[0].shape[0], attn[0].shape[0], HEAD_DIM
    block = rows // 2

    def body(core_ref, q0, q1, kv0, kv1, place, places0, places1, w0, w1, att0, att1, branch):
        total = 0.0
        for q, att, w in ((q0, att0, w0), (q1, att1, w1)):
            parts = [
                scores(q[...], kv[:, :size], places[...], place[...])[1]
                for kv, places in ((kv0, places0), (kv1, places1))
            ]
            scale = 1.0 / (
                jnp.sum(parts[0], -1, keepdims=True) + jnp.sum(parts[1], -1, keepdims=True)
            )
            attended = mm((parts[0] * scale).astype(BF16), kv0[:, size:])
            attended += mm((parts[1] * scale).astype(BF16), kv1[:, size:])
            attended = attended.astype(BF16)
            att[...] = attended
            total = total + mm_nt(attended, w[...])
        branch[...] = total.astype(BF16)

    by_rows, specs = attention_specs(rows, width, block)
    return kernel_call(
        body,
        (2,),
        specs,
        [by_rows(size), by_rows(size), by_rows(width)],
        [
            jax.ShapeDtypeStruct((rows, size), BF16),
            jax.ShapeDtypeStruct((rows, size), BF16),
            jax.ShapeDtypeStruct((rows, width), BF16),
        ],
        [],
        16 * rows * rows * size + 4 * rows * width * size,
        4 * width * size + 2 * rows * width,
        prefetch=1,
    )(core, *queries, *kvs, row_places, *key_places, *attn)


def attention_backward(
    d_branch, core, queries, kvs, row_places, key_places, attn, cosine, sine
):
    rows, width, size = queries[0].shape[0], attn[0].shape[0], HEAD_DIM
    block = rows // 2
    scaling = size**-0.5

    def body(
        core_ref, q0, q1, kv0, kv1, place, places0, places1, w0, w1, d_out, cos, sin,
        dq0, dq1, dkv0, dkv1, sum0, sum1
    ):
        @pl.when(pl.program_id(0) == 0)
        def _():
            sum0[...] = jnp.zeros_like(sum0)
            sum1[...] = jnp.zeros_like(sum1)

        for q, dq, w in ((q0, dq0, w0), (q1, dq1, w1)):
            query = q[...]
            d_att = mm(d_out[...], w[...]).astype(BF16)
            parts = [
                scores(query, kv[:, :size], places[...], place[...])
                for kv, places in ((kv0, places0), (kv1, places1))
            ]
            scale = 1.0 / sum(jnp.sum(e, -1, keepdims=True) for _, e in parts)
            chances = [e * scale for _, e in parts]
            d_chances = [mm_nt(d_att, kv[:, size:]) for kv in (kv0, kv1)]
            inner = sum(
                jnp.sum(p * d, -1, keepdims=True) for p, d in zip(chances, d_chances)
            )
            d_query = 0.0
            for (t, _), p, d, kv, sums in zip(
                parts, chances, d_chances, (kv0, kv1), (sum0, sum1)
            ):
                d_raw = (p * (d - inner) * (1.0 - t * t) * scaling).astype(BF16)
                d_query = d_query + mm(d_raw, kv[:, :size])
                sums[:, :size] += mm_tn(d_raw, query)
                sums[:, size:] += mm_tn(p.astype(BF16), d_att)
            dq[...] = rotated(d_query, cos[...], sin[...], back=True).astype(BF16)

        @pl.when(pl.program_id(0) == pl.num_programs(0) - 1)
        def _():
            dkv0[...] = sum0[...]
            dkv1[...] = sum1[...].astype(BF16)

    by_rows, specs = attention_specs(rows, width, block)
    whole = pl.BlockSpec((rows, 2 * size), lambda i, c: (0, 0))
    return kernel_call(
        body,
        (2,),
        specs + [by_rows(width), by_rows(size // 2), by_rows(size // 2)],
        [by_rows(size), by_rows(size), whole, whole],
        [
            jax.ShapeDtypeStruct((rows, size), BF16),
            jax.ShapeDtypeStruct((rows, size), BF16),
            jax.ShapeDtypeStruct((rows, 2 * size), F32),
            jax.ShapeDtypeStruct((rows, 2 * size), BF16),
        ],
        [pltpu.VMEM((rows, 2 * size), F32)] * 2,
        40 * rows * rows * size + 4 * rows * width * size,
        4 * width * size + 2 * rows * width,
        prefetch=1,
    )(core, *queries, *kvs, row_places, *key_places, *attn, d_branch, cosine, sine)


def qkv_backward(inputs, dqs, dkv_mine, dkv_got, attn, cosine, sine, core):
    rows, width = inputs.shape
    block, size = rows // 2, HEAD_DIM

    def body(core_ref, x, q0, q1, mine, got, w0, w1, cos, sin, d_in, dp0, dp1, gain):
        both = mine[...] + got[...].astype(F32)
        d_key = rotated(both[:, :size], cos[...], sin[...], back=True)
        first = core_ref[0] == 0
        dp0[0, :, :size] = q0[...]
        dp1[0, :, :size] = q1[...]
        dp0[0, :, size:] = jnp.where(first, d_key, both[:, size:]).astype(BF16)
        dp1[0, :, size:] = jnp.where(first, both[:, size:], d_key).astype(BF16)
        total = mm_nt(dp0[0], w0[...]) + mm_nt(dp1[0], w1[...])
        d_in[...] = total.astype(BF16)
        source = x[...].astype(F32)
        term = jnp.sum(total * source * inverse_rms(source), 0, keepdims=True)

        @pl.when(pl.program_id(0) == 0)
        def _():
            gain[...] = jnp.zeros_like(gain)

        gain[...] += term

    def by_rows(columns):
        return pl.BlockSpec((block, columns), lambda i, c: (i, 0))

    weights = [pl.BlockSpec((width, 2 * size), lambda i, c: (0, 0))] * 2
    terms = pl.BlockSpec((1, block, 2 * size), lambda i, c: (0, i, 0))
    return kernel_call(
        body,
        (2,),
        [by_rows(width), by_rows(size), by_rows(size), by_rows(2 * size), by_rows(2 * size)]
        + weights
        + [by_rows(size // 2), by_rows(size // 2)],
        [by_rows(width), terms, terms, pl.BlockSpec((1, width), lambda i, c: (0, 0))],
        [
            jax.ShapeDtypeStruct((rows, width), BF16),
            jax.ShapeDtypeStruct((1, rows, 2 * size), BF16),
            jax.ShapeDtypeStruct((1, rows, 2 * size), BF16),
            jax.ShapeDtypeStruct((1, width), F32),
        ],
        [],
        8 * rows * width * size,
        8 * width * size + 4 * rows * width,
        prefetch=1,
    )(core, inputs, *dqs, dkv_mine, dkv_got, *attn, cosine, sine)


def both_columns(total, place, ctx_count):
    first_core = place % 2 == 0
    total = total.reshape(ctx_count // 2, 2, -1, total.shape[1])
    mine = jnp.where(first_core, total[:, 0], total[:, 1])
    theirs = swap(jnp.where(first_core, total[:, 1], total[:, 0]), "ctx", 1, ctx_count)
    both = (jnp.where(first_core, mine, theirs), jnp.where(first_core, theirs, mine))
    return jnp.stack(both, 1)


def rank_parts(both, place, ctx_count):
    return [
        lax.dynamic_index_in_dim(both, place // 2 ^ k, 0, keepdims=False)
        for k in range(ctx_count // 2)
    ]


def spread(parts, ctx_count):
    return [
        part if k == 0 else swap(part, "ctx", 2 * k, ctx_count) for k, part in enumerate(parts)
    ]


def put(into, piece, start):
    return lax.dynamic_update_slice_in_dim(into, piece.astype(F32), start, 1)


def local_kernels(
    layer_input, attn_weights, mlp_in_weights, mlp_out_weights, norm_gains, output_grad
):
    tokens, width = layer_input.shape[1:]
    half_block = tokens // 2
    ctx_count = lax.axis_size("ctx")
    fsdp_count = lax.axis_size("fsdp")
    ranks = ctx_count // 2
    place = lax.axis_index("ctx")
    fsdp_place = lax.axis_index("fsdp")
    rank, core = place // 2, place % 2
    query_cols, key_cols = HEADS * HEAD_DIM, KV_HEADS * HEAD_DIM
    qkv_cols = query_cols + 2 * key_cols
    hidden_width = mlp_out_weights.shape[1]
    f_own = hidden_width // ctx_count
    shard_rows = width // (ctx_count * fsdp_count)

    def partner(values):
        return swap(values, "ctx", 1, ctx_count)

    def columns(array, start, size):
        return lax.dynamic_slice_in_dim(array, start, size, 1)

    chip_groups = [
        [(2 * r + c) * fsdp_count + f for c in (0, 1) for f in range(fsdp_count)]
        for r in range(ranks)
    ]

    def chip_gather(piece):
        whole = lax.all_gather(
            piece, ("ctx", "fsdp"), axis=0, tiled=True, axis_index_groups=chip_groups
        )
        return whole.reshape(2, width, piece.shape[1])

    def over_sequences(product):
        product = product.reshape(width, product.shape[2])
        return lax.psum_scatter(product, "fsdp", scatter_dimension=0, tiled=True)

    def joined(pieces):
        return jnp.concatenate(pieces, 0)

    own_input = layer_input.reshape(tokens, width)
    source = own_input.astype(F32)
    upstream = output_grad.reshape(tokens, width).astype(F32)
    kv_start = query_cols + core * key_cols + rank * HEAD_DIM
    piece = [
        columns(attn_weights, place * HEAD_DIM, HEAD_DIM),
        columns(attn_weights, kv_start, HEAD_DIM),
        columns(attn_weights, qkv_cols + place * HEAD_DIM, HEAD_DIM),
        jnp.pad(norm_gains, ((0, 0), (0, 124))),
    ]
    piece = jnp.concatenate(piece, 1)
    if fsdp_count == 4:
        ways = (
            [swap(own_input, "ctx", 4, ctx_count), swap(own_input, "ctx", 2, ctx_count)],
            lambda got: swap(got[0], "ctx", 2, ctx_count),
        )
        attn_own, (slot_2, slot_1), slot_3 = square_gather(piece, fsdp_place, ways)
        inputs = joined([own_input, slot_1, slot_2, slot_3])
    else:
        attn_own = lax.all_gather(piece, "fsdp", axis=0, tiled=True)
        inputs = joined(line_gather(own_input, ranks))
    attn = (attn_own, partner(attn_own))
    gains = attn_own[:, 3 * HEAD_DIM : 3 * HEAD_DIM + 4].astype(F32)
    g_pre, g_post, g_mid, g_out = [gains[:, i] for i in range(4)]
    in_all = chip_gather(
        jnp.concatenate(
            [
                columns(mlp_in_weights, place * f_own, f_own),
                columns(mlp_in_weights, hidden_width + place * f_own, f_own),
            ],
            1,
        )
    )
    out_all = chip_gather(columns(mlp_out_weights, place * f_own, f_own))

    def places_of(which):
        owners = (2 * (rank ^ jnp.arange(ranks, dtype=jnp.int32)) + which)[:, None] * tokens
        gathered_rows = owners + jnp.arange(tokens, dtype=jnp.int32)[None, :]
        return positions_of(gathered_rows.reshape(-1), half_block, ctx_count)

    own_places, other_places = places_of(core), places_of(1 - core)
    cosine, sine = rotary_tables(own_places, HEAD_DIM)
    cosine, sine = cosine[:, : HEAD_DIM // 2], sine[:, : HEAD_DIM // 2]
    row_places, key_places = own_places[:, None], (own_places[None, :], other_places[None, :])
    core_word = core.reshape(1).astype(jnp.int32)

    normed_in, *queries, kv_own = qkv_kernel(inputs, attn, cosine, sine, core_word)
    attention = (core_word, queries, (kv_own, partner(kv_own)), row_places, key_places, attn)
    att_own, att_other, branch_parts = attention_forward(*attention)
    branch_parts = branch_parts.reshape(ranks, tokens, width)

    def own_rows(halves, beside=()):
        halves = [v.reshape(2, tokens, width) for v in halves]
        return line_scatter([halves[k % 2][k // 2] for k in range(4)], ranks, beside)

    def gathered_halves(values, work):
        slots = line_gather(values, ranks)
        first = joined([slots[0], slots[2]])
        done = work(first, 0)
        last, first, done = together(slots[3], first, done)
        second = joined([slots[1], last])
        return (first, second), (done, work(second, 1))

    branch_parts = branch_parts.reshape(ranks, tokens, width)
    branch = line_scatter(list(branch_parts), ranks)
    scale_branch = inverse_rms(branch)
    residual = source + branch * scale_branch * g_post
    scale_mid = inverse_rms(residual)
    mids, forward = gathered_halves(
        (residual * scale_mid * g_mid).astype(BF16), lambda v, _: gate_up_forward(v, in_all, core_word)
    )
    mixed_1 = down_forward(forward[1][:2], out_all, core_word)
    mixed_0 = down_forward(forward[0][:2], out_all, core_word, (mixed_1,))
    hidden_own = [f[0] for f in forward]
    hidden_got = [partner(f[1]) for f in forward]
    mid_got = [partner(v) for v in mids]
    mixed = own_rows((mixed_0, mixed_1))
    mixed, hidden_own, hidden_got, mid_got = together(mixed, hidden_own, hidden_got, mid_got)
    scale_mixed = inverse_rms(mixed)
    block_out = (residual + mixed * scale_mixed * g_out).astype(BF16)
    grad_out_gain = jnp.sum(upstream * mixed * scale_mixed, 0)
    d_mixeds, d_gate_ups = gathered_halves(
        norm_backward(mixed, scale_mixed, upstream * g_out).astype(BF16),
        lambda v, k: down_backward(v, *forward[k][2:], out_all, core_word),
    )

    def weight_grad(lefts, rights):
        return weight_grad_kernel(lefts, rights, ctx_count, fsdp_count)

    down_product = weight_grad(
        [*d_mixeds, *[partner(v) for v in d_mixeds]], hidden_own + hidden_got
    )
    d_gate_ups, down_product = together(d_gate_ups, down_product)
    down_total = over_sequences(down_product)
    d_mid_1 = gate_up_backward(d_gate_ups[1], in_all, core_word)
    d_mid_0 = gate_up_backward(d_gate_ups[0], in_all, core_word, (d_mid_1,))
    gate_up_product = weight_grad(
        [*mids, *mid_got], [v[0] for v in d_gate_ups] + [partner(v[1]) for v in d_gate_ups]
    )
    d_mid, (gate_up_product,) = own_rows((d_mid_0, d_mid_1), (gate_up_product,))
    gate_up_total = over_sequences(gate_up_product)
    grad_mid_gain = jnp.sum(d_mid * residual * scale_mid, 0)
    d_residual = upstream + norm_backward(residual, scale_mid, d_mid * g_mid)
    grad_post_gain = jnp.sum(d_residual * branch * scale_branch, 0)
    d_branches = joined(
        line_gather(
            norm_backward(branch, scale_branch, d_residual * g_post).astype(BF16), ranks
        )
    )

    down_parts = rank_parts(both_columns(down_total, place, ctx_count), place, ctx_count)
    d_branches, down_parts = together(d_branches, down_parts)
    down = spread(down_parts, ctx_count)
    *d_queries, dkv_own, dkv_other = attention_backward(d_branches, *attention, cosine, sine)
    dkv_got, down[1] = together(partner(dkv_other), down[1])
    d_in, dproj_own, dproj_other, grad_pre_gain = qkv_backward(
        inputs, d_queries, dkv_own, dkv_got, attn, cosine, sine, core_word
    )

    gain_terms = jnp.stack([grad_pre_gain[0], grad_post_gain, grad_mid_gain, grad_out_gain], 1)
    gain_terms = gain_terms.reshape(ctx_count, fsdp_count, shard_rows, 4)
    gain_terms = gain_terms.transpose(1, 0, 2, 3).reshape(fsdp_count, -1, 4)
    out_product = weight_grad(
        [d_branches, partner(d_branches)], [att_own[None], partner(att_other)[None]]
    )
    product = weight_grad([normed_in, partner(normed_in)], [dproj_own, partner(dproj_other)])
    product = jnp.concatenate([product, out_product, gain_terms.astype(BF16)], 2)
    gate_up_parts = rank_parts(both_columns(gate_up_total, place, ctx_count), place, ctx_count)
    gate_up_parts, product = together(gate_up_parts, product)
    gate_up_terms = spread(gate_up_parts, ctx_count)
    d_in = list(d_in.reshape(ranks, tokens, width))
    if fsdp_count == 4:
        parts = [
            lax.dynamic_index_in_dim(product, fsdp_place ^ k, 0, keepdims=False).astype(F32)
            for k in range(4)
        ]
        corners = corner_scatter(parts[3], 4)
        d_in, (corners,) = line_scatter(d_in, ranks, (corners,))
        attn_total = rows_scatter(parts, corners, 4).astype(BF16)
    else:
        d_in = line_scatter(d_in, ranks)
        attn_total = over_sequences(product)
    attn_parts = rank_parts(both_columns(attn_total, place, ctx_count), place, ctx_count)
    attn_terms = spread(attn_parts, ctx_count)
    d_source = d_residual + norm_backward(source, inverse_rms(source), d_in * g_pre)

    grad_mlp_out = jnp.zeros((shard_rows, hidden_width), F32)
    grad_mlp_in = jnp.zeros((shard_rows, 2 * hidden_width), F32)
    grad_attn = jnp.zeros((shard_rows, attn_weights.shape[1]), F32)
    grad_gains = jnp.zeros((shard_rows, 4), F32)
    for k in range(ranks):
        giver = rank ^ k
        for which in (0, 1):
            start = (2 * giver + which) * f_own
            grad_mlp_out = put(grad_mlp_out, down[k][which], start)
            term = gate_up_terms[k][which]
            grad_mlp_in = put(grad_mlp_in, term[:, :f_own], start)
            grad_mlp_in = put(grad_mlp_in, term[:, f_own:], hidden_width + start)
            term = attn_terms[k][which]
            start = (2 * giver + which) * HEAD_DIM
            grad_attn = put(grad_attn, term[:, :HEAD_DIM], start)
            grad_attn = put(grad_attn, term[:, 2 * HEAD_DIM : 3 * HEAD_DIM], qkv_cols + start)
            start = query_cols + which * key_cols + giver * HEAD_DIM
            grad_attn = put(grad_attn, term[:, HEAD_DIM : 2 * HEAD_DIM], start)
            grad_gains = grad_gains + term[:, 3 * HEAD_DIM :].astype(F32)
    return (
        block_out.reshape(layer_input.shape),
        d_source.reshape(layer_input.shape),
        grad_attn,
        grad_mlp_in,
        grad_mlp_out,
        grad_gains,
    )


def local(layer_input, attn_weights, mlp_in_weights, mlp_out_weights, norm_gains, output_grad):
    ctx_count, fsdp_count = lax.axis_size("ctx"), lax.axis_size("fsdp")
    width, hidden_width = layer_input.shape[2], mlp_out_weights.shape[1]
    fits = (
        ctx_count == HEADS == 2 * KV_HEADS == 8
        and hidden_width % (128 * ctx_count) == 0
        and width % 256 == 0
        and width % (8 * ctx_count * fsdp_count) == 0
        and (width // fsdp_count) % 32 == 0
    )
    path = local_kernels if fits else local_general
    return path(
        layer_input, attn_weights, mlp_in_weights, mlp_out_weights, norm_gains, output_grad
    )


def local_general(layer_input, attn_weights, mlp_in_weights, mlp_out_weights, norm_gains, output_grad):
    tokens, width = layer_input.shape[1:]
    half_block = tokens // 2
    ctx_count = lax.axis_size("ctx")
    fsdp_count = lax.axis_size("fsdp")
    ranks = ctx_count // 2
    place = lax.axis_index("ctx")
    rank, core = place // 2, place % 2
    first_core = core == 0
    query_cols, key_cols = HEADS * HEAD_DIM, KV_HEADS * HEAD_DIM
    qkv_cols = query_cols + 2 * key_cols
    heads = HEADS // ranks
    sharing = ranks // KV_HEADS
    hidden_width = mlp_out_weights.shape[1]
    q_own = query_cols // ctx_count
    f_own = hidden_width // ctx_count
    shard_rows = width // (ctx_count * fsdp_count)
    scaling = HEAD_DIM**-0.5

    def partner(values):
        return swap(values, "ctx", 1, ctx_count)

    def columns(array, start, size):
        return lax.dynamic_slice_in_dim(array, start, size, 1)


    kv_start = query_cols + core * key_cols + rank // sharing * HEAD_DIM
    attn_piece = (
        columns(attn_weights, place * q_own, q_own),
        columns(attn_weights, kv_start, HEAD_DIM),
        columns(attn_weights, qkv_cols + place * q_own, q_own),
    )
    attn_own = lax.all_gather(jnp.concatenate(attn_piece, 1), "fsdp", axis=0, tiled=True)
    in_piece = (
        columns(mlp_in_weights, place * f_own, f_own),
        columns(mlp_in_weights, hidden_width + place * f_own, f_own),
    )
    in_piece = jnp.concatenate(in_piece, 1)
    out_piece = columns(mlp_out_weights, place * f_own, f_own)
    in_own = lax.all_gather(in_piece, "fsdp", axis=0, tiled=True)
    out_own = lax.all_gather(out_piece, "fsdp", axis=0, tiled=True)
    gains = lax.all_gather(norm_gains, "fsdp", axis=0, tiled=True).astype(F32)
    g_pre, g_post, g_mid, g_out = [gains[:, i] for i in range(4)]
    attn_other = partner(attn_own)
    qkv_own, proj_own = attn_own[:, : q_own + HEAD_DIM], attn_own[:, q_own + HEAD_DIM :]
    qkv_other, proj_other = attn_other[:, : q_own + HEAD_DIM], attn_other[:, q_own + HEAD_DIM :]

    own_input = layer_input.reshape(tokens, width)
    source = own_input.astype(F32)
    upstream = output_grad.reshape(tokens, width).astype(F32)
    inputs = jnp.concatenate(line_gather(own_input, ranks), 0).astype(F32)
    scale_in = inverse_rms(inputs)
    plain_in = inputs * scale_in
    normed_in = (plain_in * g_pre).astype(BF16)

    def places_of(which):
        slots = rank ^ jnp.arange(ranks, dtype=jnp.int32)
        owners = (2 * slots + which)[:, None] * tokens
        rows = owners + jnp.arange(tokens, dtype=jnp.int32)[None, :]
        return positions_of(rows.reshape(-1), half_block, ctx_count)

    own_places, other_places = places_of(core), places_of(1 - core)
    cosine, sine_table = rotary_tables(own_places, HEAD_DIM)
    all_places = jnp.concatenate([own_places, other_places], 0)
    allowed = all_places[None, :] <= own_places[:, None]
    rows = ranks * tokens

    def ordered(mine, theirs):
        return jnp.where(first_core, mine, theirs), jnp.where(first_core, theirs, mine)

    proj_a, proj_b = dot(normed_in, qkv_own), dot(normed_in, qkv_other)
    query_raw = jnp.concatenate(ordered(proj_a[:, :q_own], proj_b[:, :q_own]), 1)
    key_raw, value_raw = ordered(proj_a[:, q_own:], proj_b[:, q_own:])
    query = rotate(
        query_raw.reshape(rows, heads, HEAD_DIM), cosine[:, None], sine_table[:, None]
    ).astype(BF16)
    key_own = rotate(key_raw, cosine, sine_table).astype(BF16)
    value_own = value_raw.astype(BF16)
    key_value = jnp.concatenate([key_own, value_own], 1)
    key_value = jnp.concatenate([key_value, partner(key_value)], 0)
    keys, values = key_value[:, :HEAD_DIM], key_value[:, HEAD_DIM:]

    def score_rows():
        raw_scores = jnp.einsum("tgd,ld->gtl", query, keys, preferred_element_type=F32)
        tanh_part = jnp.tanh(raw_scores * scaling / SOFT_CAP)
        return tanh_part, jnp.where(allowed, SOFT_CAP * tanh_part, MASKED_SCORE)

    tanh_part, capped = score_rows()
    row_max = jnp.max(capped, -1, keepdims=True)
    weights = jnp.exp(capped - row_max)
    row_total = jnp.sum(weights, -1, keepdims=True)
    log_total = row_max + jnp.log(row_total)
    chances = (weights / row_total).astype(BF16)
    attended = jnp.einsum("gtl,ld->tgd", chances, values, preferred_element_type=F32)
    attended = attended.reshape(rows, heads * HEAD_DIM).astype(BF16)
    att_own, att_other = ordered(attended[:, :q_own], attended[:, q_own:])
    branch_parts = (dot_t(att_own, proj_own) + dot_t(att_other, proj_other)).reshape(
        ranks, tokens, width
    )

    span = tokens // STREAMS
    cuts = [slice(s * span, (s + 1) * span) for s in range(STREAMS)]

    def own_rows(parts):
        return line_scatter(list(parts.reshape(ranks, -1, width)), ranks)

    def all_rows(values):
        return jnp.concatenate(line_gather(values, ranks), 0)

    branch = [own_rows(branch_parts[:, cut]) for cut in cuts]
    halves = ((in_own, out_own), (partner(in_own), partner(out_own)))
    scale_branch = [inverse_rms(v) for v in branch]
    residual = [source[cut] + v * w * g_post for cut, v, w in zip(cuts, branch, scale_branch)]
    scale_mid = [inverse_rms(v) for v in residual]
    mids = [all_rows((v * w * g_mid).astype(BF16)) for v, w in zip(residual, scale_mid)]
    hiddens, backs, mixed = [], [], []
    for values_in in mids:
        hidden_of, back_of, total = [], [], 0.0
        for w_in, w_out in halves:
            gate_up = dot(values_in, w_in)
            hidden, back = jax.vjp(geglu, gate_up[:, :f_own], gate_up[:, f_own:])
            hidden_of.append(hidden.astype(BF16))
            back_of.append(back)
            total = total + dot_t(hidden_of[-1], w_out)
        hiddens.append(hidden_of)
        backs.append(back_of)
        mixed.append(own_rows(total))
    scale_mixed = [inverse_rms(v) for v in mixed]
    block_out = [
        (r + v * w * g_out).astype(BF16) for r, v, w in zip(residual, mixed, scale_mixed)
    ]
    ups = [upstream[cut] for cut in cuts]
    grad_out_gain = sum(jnp.sum(u * v * w, 0) for u, v, w in zip(ups, mixed, scale_mixed))
    d_mixeds = [
        all_rows(norm_backward(v, w, u * g_out).astype(BF16))
        for u, v, w in zip(ups, mixed, scale_mixed)
    ]

    def both_cores(mine, others=None):
        return jnp.concatenate([mine, partner(mine if others is None else others)], 0)

    def joined(pieces):
        return jnp.concatenate(pieces, 0)

    def grouped(left):
        left = left.reshape(left.shape[0], ctx_count, fsdp_count, shard_rows)
        return left.transpose(0, 2, 1, 3).reshape(left.shape[0], fsdp_count, ctx_count * shard_rows)

    def weight_grad(left, right):
        product = jnp.einsum("tfr,tn->frn", grouped(left), right, preferred_element_type=F32)
        return product.reshape(width, right.shape[1]).astype(BF16)

    def over_sequences(product):
        total = lax.psum_scatter(product, "fsdp", scatter_dimension=0, tiled=True)
        return total.reshape(ranks, 2, shard_rows, product.shape[1])

    def spread(total):
        mine = jnp.where(first_core, total[:, 0], total[:, 1])
        theirs = partner(jnp.where(first_core, total[:, 1], total[:, 0]))
        both = jnp.stack(ordered(mine, theirs), 1)
        got = []
        for k in range(ranks):
            part = lax.dynamic_index_in_dim(both, rank ^ k, 0, keepdims=False)
            got.append(part if k == 0 else swap(part, "ctx", 2 * k, ctx_count))
        return got

    def put(into, piece, start, adds=False):
        piece = piece.astype(F32)
        if adds:
            piece = piece + lax.dynamic_slice_in_dim(into, start, piece.shape[1], 1)
        return lax.dynamic_update_slice_in_dim(into, piece, start, 1)

    mid_rows = both_cores(joined(mids))
    hidden_rows = both_cores(joined([h[0] for h in hiddens]), joined([h[1] for h in hiddens]))
    down_product = weight_grad(both_cores(joined(d_mixeds)), hidden_rows)
    d_mid, d_gate_ups = [], []
    for values_in, back_of in zip(d_mixeds, backs):
        total, d_gate_up_of = 0.0, []
        for (w_in, w_out), back in zip(halves, back_of):
            d_gate_up = jnp.concatenate(back(dot(values_in, w_out)), 1).astype(BF16)
            d_gate_up_of.append(d_gate_up)
            total = total + dot_t(d_gate_up, w_in)
        d_gate_ups.append(d_gate_up_of)
        d_mid.append(own_rows(total))
    down_total = over_sequences(down_product)
    dgu_rows = both_cores(joined([d[0] for d in d_gate_ups]), joined([d[1] for d in d_gate_ups]))
    gate_up_product = weight_grad(mid_rows, dgu_rows)
    gate_up_total = over_sequences(gate_up_product)

    grad_mid_gain = sum(jnp.sum(d * v * w, 0) for d, v, w in zip(d_mid, residual, scale_mid))
    d_residual = [
        u + norm_backward(v, w, d * g_mid) for u, v, w, d in zip(ups, residual, scale_mid, d_mid)
    ]
    grad_post_gain = sum(
        jnp.sum(d * v * w, 0) for d, v, w in zip(d_residual, branch, scale_branch)
    )
    d_branches = [
        line_gather(norm_backward(v, w, d * g_post).astype(BF16), ranks)
        for d, v, w in zip(d_residual, branch, scale_branch)
    ]
    d_branches = joined([d[k] for k in range(ranks) for d in d_branches])
    d_residual = joined(d_residual)

    down = spread(down_total)
    d_att_own, d_att_other = dot(d_branches, proj_own), dot(d_branches, proj_other)
    d_attended = jnp.concatenate(ordered(d_att_own, d_att_other), 1).astype(BF16)
    d_attended = d_attended.reshape(rows, heads, HEAD_DIM)
    tanh_again, capped_again = score_rows()
    chances_f = jnp.exp(capped_again - log_total)
    d_values = jnp.einsum(
        "gtl,tgd->ld", chances_f.astype(BF16), d_attended, preferred_element_type=F32
    )
    d_chances = jnp.einsum("tgd,ld->gtl", d_attended, values, preferred_element_type=F32)
    row_inner = jnp.sum(chances_f * d_chances, -1, keepdims=True)
    d_raw = (
        chances_f * (d_chances - row_inner) * (1.0 - tanh_again * tanh_again) * scaling
    ).astype(BF16)
    d_query = jnp.einsum("gtl,ld->tgd", d_raw, keys, preferred_element_type=F32)
    d_keys = jnp.einsum("gtl,tgd->ld", d_raw, query, preferred_element_type=F32)
    d_key_value = jnp.concatenate([d_keys, d_values], 1)
    d_key_value = d_key_value[:rows] + partner(d_key_value[rows:].astype(BF16)).astype(F32)
    d_query_raw = rotate_back(d_query, cosine[:, None], sine_table[:, None]).reshape(
        rows, heads * HEAD_DIM
    )
    d_key_raw = rotate_back(d_key_value[:, :HEAD_DIM], cosine, sine_table)
    dq_own, dq_other = ordered(d_query_raw[:, :q_own], d_query_raw[:, q_own:])
    dkv_own, dkv_other = ordered(d_key_raw, d_key_value[:, HEAD_DIM:])
    dproj_own = jnp.concatenate([dq_own, dkv_own], 1).astype(BF16)
    dproj_other = jnp.concatenate([dq_other, dkv_other], 1).astype(BF16)
    d_in = dot_t(dproj_own, qkv_own) + dot_t(dproj_other, qkv_other)
    grad_pre_gain = jnp.sum(d_in * plain_in, 0)
    d_in = own_rows(d_in)
    d_source = d_residual + norm_backward(source, scale_in[:tokens], d_in * g_pre)

    gate_up_terms = spread(gate_up_total)
    gain_terms = jnp.stack([grad_pre_gain, grad_post_gain, grad_mid_gain, grad_out_gain], 1)
    gain_terms = gain_terms.reshape(ctx_count, fsdp_count, shard_rows, 4)
    gain_terms = gain_terms.transpose(1, 0, 2, 3).reshape(fsdp_count, -1, 4)
    lefts = (grouped(both_cores(normed_in)), grouped(both_cores(d_branches)))
    rights = (both_cores(dproj_own, dproj_other), both_cores(att_own, att_other))

    def attn_part(index):
        at = [lax.dynamic_index_in_dim(v, index, 1, keepdims=False) for v in lefts]
        gain_rows = lax.dynamic_index_in_dim(gain_terms, index, 0, keepdims=False)
        pieces = [
            jnp.einsum("tr,tn->rn", v, right, preferred_element_type=F32)
            for v, right in zip(at, rights)
        ]
        return jnp.concatenate(pieces + [gain_rows], 1)

    attn_total = over_sequences(joined([attn_part(i).astype(BF16) for i in range(fsdp_count)]))
    attn_terms = spread(attn_total)

    grad_mlp_out = jnp.zeros((shard_rows, hidden_width), F32)
    grad_mlp_in = jnp.zeros((shard_rows, 2 * hidden_width), F32)
    grad_attn = jnp.zeros((shard_rows, attn_weights.shape[1]), F32)
    grad_gains = jnp.zeros((shard_rows, 4), F32)
    kv_end, out_end = q_own + HEAD_DIM, 2 * q_own + HEAD_DIM
    for k in range(ranks):
        giver = rank ^ k
        for which in (0, 1):
            start = (2 * giver + which) * f_own
            grad_mlp_out = put(grad_mlp_out, down[k][which], start)
            term = gate_up_terms[k][which]
            grad_mlp_in = put(grad_mlp_in, term[:, :f_own], start)
            grad_mlp_in = put(grad_mlp_in, term[:, f_own:], hidden_width + start)
            term = attn_terms[k][which]
            start = (2 * giver + which) * q_own
            grad_attn = put(grad_attn, term[:, :q_own], start)
            grad_attn = put(grad_attn, term[:, kv_end:out_end], qkv_cols + start)
            start = query_cols + which * key_cols + giver // sharing * HEAD_DIM
            grad_attn = put(grad_attn, term[:, q_own:kv_end], start, sharing > 1)
            grad_gains = grad_gains + term[:, out_end:].astype(F32)
    return (
        joined(block_out).reshape(layer_input.shape),
        d_source.reshape(layer_input.shape),
        grad_attn,
        grad_mlp_in,
        grad_mlp_out,
        grad_gains,
    )


def solution(mesh):
    in_specs = (
        P("fsdp", "ctx", None),
        P("fsdp", None),
        P("fsdp", None),
        P("fsdp", None),
        P("fsdp", None),
        P("fsdp", "ctx", None),
    )
    out_specs = (
        P("fsdp", "ctx", None),
        P("fsdp", "ctx", None),
        P(("ctx", "fsdp"), None),
        P(("ctx", "fsdp"), None),
        P(("ctx", "fsdp"), None),
        P(("ctx", "fsdp"), None),
    )
    return jax.shard_map(local, mesh=mesh, in_specs=in_specs, out_specs=out_specs, check_vma=False)
```

time: 920 us -> 702 us (0.76)
  Pallas kernels: 0 us -> 168 us
  matrix products: 161 us -> 0 us
  starting transfers between devices: 218 us -> 64 us
  blocking collectives: 48.9 us -> 0 us
  other arithmetic: 88.5 us -> 75.1 us
    pallas_call x0 -> x16, Pallas kernels: none -> 168 us  [the longest x4 39.2 us: weight_grad_kernel(): kernel_call(body, (halves, groups, steps), [pl.BlockSpec((n, part), lambd...]
    ppermute x113 -> x59, starting transfers between devices: 217 us -> 63.8 us  [swap(): return lax.ppermute(values, axis, [(i, i ^ distance) for i in range(count)])]
    dot_general x30 -> x0, matrix products: 125 us -> none  [the longest x12 48.9 us: dot(): return jnp.dot(a, b, preferred_element_type=F32)]
    unnamed x1 -> x0, blocking collectives: 41.9 us -> none
    all_gather x3 -> x2, waiting for transfers between devices: 40 us -> 0.02 us  [chip_gather(): lax.all_gather(piece, ('ctx', 'fsdp'), axis=0, tiled=True, axis_index_gro...]
    ppermute x113 -> x59, waiting for transfers between devices: 286 us -> 323 us  [swap(): return lax.ppermute(values, axis, [(i, i ^ distance) for i in range(count)])]
    unnamed x4 -> x0, matrix products: 36 us -> none
    unnamed x305 -> x82, local copies, waits for them, and re-layouts: 26.5 us -> 6.92 us
  transfers between devices with their start and end apart: 120 -> 63, of which waited for: 58 -> 28; matrix products, arithmetic and copies ran while one was open for 30% -> 16% of each run, Pallas kernels for 0% -> 21%
where the time goes in v2:
time: 702 us; the launch traced here: 698 us
  waiting for transfers between devices  323 us (46%)
  Pallas kernels  168 us (24%)
  other arithmetic  75.1 us (11%)
  starting transfers between devices  64 us (9%)
  local copies, waits for them, and re-layouts  53.6 us (8%)
  between operations  14.9 us (2%)
    ppermute x59, waiting for transfers between devices, swap(): return lax.ppermute(values, axis, [(i, i ^ distance) for i in range(count)])  323 us
    ppermute x59, starting transfers between devices, swap(): return lax.ppermute(values, axis, [(i, i ^ distance) for i in range(count)])  63.8 us
    pallas_call x4, Pallas kernels, weight_grad_kernel(): kernel_call(body, (halves, groups, steps), [pl.BlockSpec((n, part), lambd...  39.2 us
    pallas_call x2, Pallas kernels, gate_up_forward(): kernel_call(body, (2, steps), [pl.BlockSpec((rows, width), lambda h, i, c...  28.7 us
    pallas_call x2, Pallas kernels, gate_up_backward(): kernel_call(body, (width // tile,), [whole, whole, pl.BlockSpec((1, tile,...  25.4 us
    pallas_call x2, Pallas kernels, down_backward(): kernel_call(body, (2, steps), [pl.BlockSpec((rows, width), lambda h, i, c...  22.6 us
    dynamic_update_slice x48, other arithmetic, put(): return lax.dynamic_update_slice_in_dim(into, piece.astype(F32), start, 1)  18.2 us
    pallas_call x2, Pallas kernels, down_forward(): kernel_call(body, (width // tile,), [whole, whole, pl.BlockSpec((1, tile,...  15.8 us
  transfers between devices with their start and end apart: 63, of which 28 were waited for; matrix products, arithmetic and copies ran while one was open for 16% of the time, Pallas kernels for 21%

profile of v2, /device:TPU:13, one launch (start us, length us, event | category | flops | bytes accessed | tf_op | source)
XLA Modules:
  0.0 698.2 jit_solution(5147156000313156285)
XLA Ops:
  10.9 2.5 constant_dynamic-slice_fusion
  22.2 25.4 %collective-permute-done.2 = bf16[128,2304]{1,0:T(8,128)(2,1)S(1)} collective-permute-done((bf16[128,2304]{1,0:T(8,128)(2,1)S(1)}, bf16[128,2304]{1,0:T(8,128)(2,1)S(1)}, u32[]{:S(2)}, u32[]{:S(2)}) %collective-permute-start.2) | collective-permute-done | bytes 589856 | tf_op jit(solution)/shard_map/ppermute | solution.py:76
  47.6 11.5 %collective-permute-done = bf16[576,896]{1,0:T(8,128)(2,1)S(1)} collective-permute-done((bf16[576,896]{1,0:T(8,128)(2,1)S(1)}, bf16[576,896]{1,0:T(8,128)(2,1)S(1)}, u32[]{:S(2)}, u32[]{:S(2)}) %collective-permute-start) | collective-permute-done | bytes 1032224 | tf_op jit(solution)/shard_map/ppermute | solution.py:76
  59.2 2.4 collective-permute-done.1
  65.5 16.6 %collective-permute-done.4 = bf16[288,896]{1,0:T(8,128)(2,1)} collective-permute-done((bf16[288,896]{1,0:T(8,128)(2,1)}, bf16[288,896]{1,0:T(8,128)(2,1)}, u32[]{:S(2)}, u32[]{:S(2)}) %collective-permute-start.4) | collective-permute-done | bytes 516128 | tf_op jit(solution)/shard_map/ppermute | solution.py:76
  85.9 2.3 collective-permute-start.7
  90.5 2.7 pad_maximum_fusion.2.x
  93.2 6.4 collective-permute-done.7.w1
  99.6 7.7 %shard_map.109 = (bf16[512,2304]{1,0:T(8,128)(2,1)}, bf16[512,256]{1,0:T(8,128)(2,1)}, bf16[512,256]{1,0:T(8,128)(2,1)}, bf16[512,512]{1,0:T(8,128)(2,1)}) custom-call(s32[1]{0:T(128)} %bitcast.1.core_ref, bf16[512,2304]{1,0:T(8,128)(2,1)} %pad_maximum_fusion.2.x, bf16[2304,896]{1,0:T(8,128)(2,1)} %constant_dynamic-update-slice_fusion.gains.w0, ...), custom_call_target="tpu_custom_call" | custom-call | flops 2415919104 | bytes 9437184 | tf_op jit(solution)/shard_map/pallas_call | solution.py:407
  110.4 7.9 %shard_map.110 = (bf16[512,256]{1,0:T(8,128)(2,1)}, bf16[512,256]{1,0:T(8,128)(2,1)}, bf16[512,2304]{1,0:T(8,128)(2,1)}) custom-call(s32[1]{0:T(128)} %bitcast.1.core_ref, bf16[512,256]{1,0:T(8,128)(2,1)} %get-tuple-element.88.q0, bf16[512,256]{1,0:T(8,128)(2,1)} %get-tuple-element.89.q1, bf16[512,512]{1,0:T(8,128)(2,1)} %get-tuple-element.90.kv0, ...), custom_call_target="tpu_custom_call" | custom-call | flops 2281701376 | bytes 4718592 | tf_op jit(solution)/shard_map/pallas_call | solution.py:471
  121.2 13.2 %collective-permute-done.10 = bf16[128,2304]{1,0:T(8,128)(2,1)S(1)} collective-permute-done((bf16[128,2304]{1,0:T(8,128)(2,1)S(1)}, bf16[128,2304]{1,0:T(8,128)(2,1)S(1)}, u32[]{:S(2)}, u32[]{:S(2)}) %collective-permute-start.10) | collective-permute-done | bytes 589856 | tf_op jit(solution)/shard_map/ppermute | solution.py:76
  137.8 2.5 slice_reduce_fusion
  140.4 16.1 %collective-permute-done.9 = bf16[128,2304]{1,0:T(8,128)(2,1)S(1)} collective-permute-done((bf16[128,2304]{1,0:T(8,128)(2,1)S(1)}, bf16[128,2304]{1,0:T(8,128)(2,1)S(1)}, u32[]{:S(2)}, u32[]{:S(2)}) %collective-permute-start.9) | collective-permute-done | bytes 589856 | tf_op jit(solution)/shard_map/ppermute | solution.py:76
  156.4 4.1 collective-permute-done.11
  162.3 2.7 collective-permute-start.12
  165.0 24.3 %collective-permute-done.12 = bf16[128,2304]{1,0:T(8,128)(2,1)} collective-permute-done((bf16[128,2304]{1,0:T(8,128)(2,1)S(1)}, bf16[128,2304]{1,0:T(8,128)(2,1)}, u32[]{:S(2)}, u32[]{:S(2)}) %collective-permute-start.12) | collective-permute-done | bytes 589856 | tf_op jit(solution)/shard_map/ppermute | solution.py:76
  191.6 14.4 %shard_map.111 = (bf16[1,256,1152]{2,1,0:T(8,128)(2,1)}, bf16[1,256,1152]{2,1,0:T(8,128)(2,1)}, f32[2,256,1152]{2,1,0:T(8,128)}, f32[2,256,1152]{2,1,0:T(8,128)}) custom-call(s32[1]{0:T(128)} %bitcast.1.core_ref, bf16[256,2304]{1,0:T(8,128)(2,1)} %pad_maximum_fusion.4.x.refs_0_, bf16[2,2304,2304]{2,1,0:T(8,128)(2,1)} %bitcast.262, ...), custom_call_target="tpu_custom_call" | custom-call | flops 5435817984 | bytes 27131904 | tf_op jit(solution)/shard_map/pallas_call | solution.py:219
  208.1 14.3 %shard_map.112 = (bf16[1,256,1152]{2,1,0:T(8,128)(2,1)}, bf16[1,256,1152]{2,1,0:T(8,128)(2,1)}, f32[2,256,1152]{2,1,0:T(8,128)}, f32[2,256,1152]{2,1,0:T(8,128)}) custom-call(s32[1]{0:T(128)} %bitcast.1.core_ref, bf16[256,2304]{1,0:T(8,128)(2,1)} %copy-done.14, bf16[2,2304,2304]{2,1,0:T(8,128)(2,1)} %bitcast.264, bf16[2,2304,2304]{2,1,0:T(8,128)(2,1)} %bitcast.265), custom_call_target="tpu_custom_call" | custom-call | flops 5435817984 | bytes 27131904 | tf_op jit(solution)/shard_map/pallas_call | solution.py:219
  222.4 8.1 %shard_map.113.refs_0_ = bf16[256,2304]{1,0:T(8,128)(2,1)} custom-call(s32[1]{0:T(128)} %bitcast.1.core_ref, bf16[1,256,1152]{2,1,0:T(8,128)(2,1)} %get-tuple-element.116.h0.refs_5_, bf16[1,256,1152]{2,1,0:T(8,128)(2,1)} %get-tuple-element.100.h1, bf16[2,2304,1152]{2,1,0:T(8,128)(2,1)} %bitcast.270, bf16[2,2304,1152]{2,1,0:T(8,128)(2,1)} %bitcast.271), custom_call_target="tpu_custom_call" | custom-call | flops 2717908992 | bytes 11796480 | tf_op jit(solution)/shard_map/pallas_call | solution.py:247
  230.5 2.3 fusion.58
  234.6 7.7 %shard_map.114 = bf16[256,2304]{1,0:T(8,128)(2,1)} custom-call(s32[1]{0:T(128)} %bitcast.1.core_ref, bf16[1,256,1152]{2,1,0:T(8,128)(2,1)} %get-tuple-element.115.h0.refs_4_, bf16[1,256,1152]{2,1,0:T(8,128)(2,1)} %get-tuple-element.97.h1, bf16[2,2304,1152]{2,1,0:T(8,128)(2,1)} %bitcast.272, bf16[2,2304,1152]{2,1,0:T(8,128)(2,1)} %bitcast.273, ...), custom_call_target="tpu_custom_call" | custom-call | flops 2717908992 | bytes 11796480 | tf_op jit(solution)/shard_map/pallas_call | solution.py:247
  242.3 4.6 collective-permute-done.16
  248.2 4.2 collective-permute-start.17
  252.4 2.6 collective-permute-start.20
  255.6 14.8 %collective-permute-done.15 = bf16[128,2304]{1,0:T(8,128)(2,1)} collective-permute-done((bf16[128,2304]{1,0:T(8,128)(2,1)}, bf16[128,2304]{1,0:T(8,128)(2,1)}, u32[]{:S(2)}, u32[]{:S(2)}) %collective-permute-start.15) | collective-permute-done | bytes 589856 | tf_op jit(solution)/shard_map/ppermute | solution.py:76
  272.0 3.7 collective-permute-done.17
  280.4 2.9 collective-permute-start.22
  283.2 20.9 %collective-permute-done.22 = bf16[128,2304]{1,0:T(8,128)(2,1)} collective-permute-done((bf16[128,2304]{1,0:T(8,128)(2,1)}, bf16[128,2304]{1,0:T(8,128)(2,1)}, u32[]{:S(2)}, u32[]{:S(2)}) %collective-permute-start.22) | collective-permute-done | bytes 589856 | tf_op jit(solution)/shard_map/ppermute | solution.py:76
  305.3 2.4 pad_maximum_fusion.5.x.refs_0_
  307.7 11.3 %shard_map.115 = (bf16[2,256,1152]{2,1,0:T(8,128)(2,1)}, bf16[2,256,1152]{2,1,0:T(8,128)(2,1)}) custom-call(s32[1]{0:T(128)} %bitcast.1.core_ref, bf16[256,2304]{1,0:T(8,128)(2,1)} %pad_maximum_fusion.5.x.refs_0_, f32[2,256,1152]{2,1,0:T(8,128)} %get-tuple-element.103.gate, f32[2,256,1152]{2,1,0:T(8,128)} %get-tuple-element.104.up, ...), custom_call_target="tpu_custom_call" | custom-call | flops 2717908992 | bytes 17694720 | tf_op jit(solution)/shard_map/pallas_call | solution.py:289
  320.9 3.8 collective-permute-start.25
  326.7 11.2 %shard_map.116 = (bf16[2,256,1152]{2,1,0:T(8,128)(2,1)}, bf16[2,256,1152]{2,1,0:T(8,128)(2,1)}) custom-call(s32[1]{0:T(128)} %bitcast.1.core_ref, bf16[256,2304]{1,0:T(8,128)(2,1)} %constant_dynamic-update-slice_fusion.7.x.refs_1_, f32[2,256,1152]{2,1,0:T(8,128)} %get-tuple-element.110.gate, f32[2,256,1152]{2,1,0:T(8,128)} %get-tuple-element.111.up, ...), custom_call_target="tpu_custom_call" | custom-call | flops 2717908992 | bytes 17694720 | tf_op jit(solution)/shard_map/pallas_call | solution.py:289
  337.9 10.6 %shard_map.117 = bf16[4,576,1152]{2,1,0:T(8,128)(2,1)} custom-call(bf16[256,2304]{1,0:T(8,128)(2,1)} %pad_maximum_fusion.5.x.refs_0_, bf16[256,2304]{1,0:T(8,128)(2,1)} %constant_dynamic-update-slice_fusion.7.x.refs_1_, bf16[256,2304]{1,0:T(8,128)(2,1)} %collective-permute-done.25.refs_2_, bf16[256,2304]{1,0:T(8,128)(2,1)} %collective-permute-done.26.refs_3_, ...), custom_call_target="tpu_custom_call" | custom-call | flops 5435817984 | bytes 19464192 | tf_op jit(solution)/shard_map/pallas_call | solution.py:365
  349.2 12.2 %shard_map.118.refs_0_ = bf16[256,2304]{1,0:T(8,128)(2,1)} custom-call(s32[1]{0:T(128)} %bitcast.1.core_ref, bf16[2,256,1152]{2,1,0:T(8,128)(2,1)} %get-tuple-element.121.d0.refs_5_, bf16[2,256,1152]{2,1,0:T(8,128)(2,1)} %get-tuple-element.122.d1, bf16[2,2304,2304]{2,1,0:T(8,128)(2,1)} %bitcast.266, bf16[2,2304,2304]{2,1,0:T(8,128)(2,1)} %bitcast.267), custom_call_target="tpu_custom_call" | custom-call | flops 5435817984 | bytes 23592960 | tf_op jit(solution)/shard_map/pallas_call | solution.py:319
  361.5 2.3 fusion.57
  365.3 18.5 %shard_map.120 = bf16[4,576,2304]{2,1,0:T(8,128)(2,1)} custom-call(bf16[256,2304]{1,0:T(8,128)(2,1)} %pad_maximum_fusion.4.x.refs_0_, bf16[256,2304]{1,0:T(8,128)(2,1)} %copy-done.14, bf16[256,2304]{1,0:T(8,128)(2,1)} %copy-done.35, bf16[256,2304]{1,0:T(8,128)(2,1)} %copy-done.36, bf16[2,256,1152]{2,1,0:T(8,128)(2,1)} %get-tuple-element.119.d0.refs_4_, ...), custom_call_target="tpu_custom_call" | custom-call | flops 10871635968 | bytes 29491200 | tf_op jit(solution)/shard_map/pallas_call | solution.py:365
  383.8 7.2 %collective-permute-done.28 = bf16[128,2304]{1,0:T(8,128)(2,1)S(1)} collective-permute-done((bf16[128,2304]{1,0:T(8,128)(2,1)}, bf16[128,2304]{1,0:T(8,128)(2,1)S(1)}, u32[]{:S(2)}, u32[]{:S(2)}) %collective-permute-start.28) | collective-permute-done | bytes 589856 | tf_op jit(solution)/shard_map/ppermute | solution.py:76
  391.0 13.2 %shard_map.119 = bf16[256,2304]{1,0:T(8,128)(2,1)} custom-call(s32[1]{0:T(128)} %bitcast.1.core_ref, bf16[2,256,1152]{2,1,0:T(8,128)(2,1)} %get-tuple-element.119.d0.refs_4_, bf16[2,256,1152]{2,1,0:T(8,128)(2,1)} %get-tuple-element.120.d1, bf16[2,2304,2304]{2,1,0:T(8,128)(2,1)} %bitcast.268, bf16[2,2304,2304]{2,1,0:T(8,128)(2,1)} %bitcast.269, ...), custom_call_target="tpu_custom_call" | custom-call | flops 5435817984 | bytes 23592960 | tf_op jit(solution)/shard_map/pallas_call | solution.py:319
  406.7 24.7 %collective-permute-done.31 = bf16[128,2304]{1,0:T(8,128)(2,1)S(1)} collective-permute-done((bf16[128,2304]{1,0:T(8,128)(2,1)S(1)}, bf16[128,2304]{1,0:T(8,128)(2,1)S(1)}, u32[]{:S(2)}, u32[]{:S(2)}) %collective-permute-start.31) | collective-permute-done | bytes 589856 | tf_op jit(solution)/shard_map/ppermute | solution.py:76
  432.5 2.8 multiply_reduce_fusion.1
  435.8 3.1 collective-permute-start.33
  438.9 24.6 %collective-permute-done.33 = bf16[128,2304]{1,0:T(8,128)(2,1)S(1)} collective-permute-done((bf16[128,2304]{1,0:T(8,128)(2,1)S(1)}, bf16[128,2304]{1,0:T(8,128)(2,1)S(1)}, u32[]{:S(2)}, u32[]{:S(2)}) %collective-permute-start.33) | collective-permute-done | bytes 589856 | tf_op jit(solution)/shard_map/ppermute | solution.py:76
  463.4 3.1 collective-permute-start.34
  472.9 6.9 collective-permute-done.34
  479.8 2.6 pad_maximum_fusion.3.d_out.refs_0_
  485.1 12.6 %shard_map.121 = (bf16[512,256]{1,0:T(8,128)(2,1)}, bf16[512,256]{1,0:T(8,128)(2,1)}, f32[512,512]{1,0:T(8,128)}, bf16[512,512]{1,0:T(8,128)(2,1)}) custom-call(s32[1]{0:T(128)} %bitcast.1.core_ref, bf16[512,256]{1,0:T(8,128)(2,1)} %get-tuple-element.88.q0, bf16[512,256]{1,0:T(8,128)(2,1)} %get-tuple-element.89.q1, bf16[512,512]{1,0:T(8,128)(2,1)} %get-tuple-element.90.kv0, ...), custom_call_target="tpu_custom_call" | custom-call | flops 3892314112 | bytes 4718592 | tf_op jit(solution)/shard_map/pallas_call | solution.py:534
  502.0 5.3 collective-permute-done.37
  509.5 7.8 %shard_map.122 = (bf16[512,2304]{1,0:T(8,128)(2,1)}, bf16[1,512,512]{2,1,0:T(8,128)(2,1)}, bf16[1,512,512]{2,1,0:T(8,128)(2,1)}, f32[1,2304]{1,0:T(1,128)}) custom-call(s32[1]{0:T(128)} %bitcast.1.core_ref, bf16[512,2304]{1,0:T(8,128)(2,1)} %pad_maximum_fusion.2.x, bf16[512,256]{1,0:T(8,128)(2,1)} %get-tuple-element.129.q0, ...), custom_call_target="tpu_custom_call" | custom-call | flops 2415919104 | bytes 9437184 | tf_op jit(solution)/shard_map/pallas_call | solution.py:580
  519.8 2.4 fusion.55
  522.9 7.2 %collective-permute-done.57 = bf16[2,72,1152]{2,1,0:T(8,128)(2,1)} collective-permute-done((bf16[2,72,1152]{2,1,0:T(8,128)(2,1)S(1)}, bf16[2,72,1152]{2,1,0:T(8,128)(2,1)}, u32[]{:S(2)}, u32[]{:S(2)}) %collective-permute-start.57) | collective-permute-done | bytes 331808 | tf_op jit(solution)/shard_map/ppermute | solution.py:76
  534.0 2.9 select_bitcast_fusion
  542.5 5.9 shard_map.123
  548.4 4.3 shard_map.124
  552.6 2.3 pad_maximum_fusion
  555.5 2.5 fusion.8
  564.7 17.0 %collective-permute-done.39 = bf16[128,2304]{1,0:T(8,128)(2,1)} collective-permute-done((bf16[128,2304]{1,0:T(8,128)(2,1)}, bf16[128,2304]{1,0:T(8,128)(2,1)}, u32[]{:S(2)}, u32[]{:S(2)}) %collective-permute-start.39) | collective-permute-done | bytes 589856 | tf_op jit(solution)/shard_map/ppermute | solution.py:76
  583.9 4.3 collective-permute-start.47
  605.3 34.1 %collective-permute-done.56 = bf16[2,72,2304]{2,1,0:T(8,128)(2,1)} collective-permute-done((bf16[2,72,2304]{2,1,0:T(8,128)(2,1)}, bf16[2,72,2304]{2,1,0:T(8,128)(2,1)}, u32[]{:S(2)}, u32[]{:S(2)}) %collective-permute-start.56) | collective-permute-done | bytes 663584 | tf_op jit(solution)/shard_map/ppermute | solution.py:76
  643.5 6.5 collective-permute-done.47
  653.6 2.3 copy.99
  658.7 2.7 fusion.16
  661.8 3.1 collective-permute-start.51
  666.4 8.5 %collective-permute-done.51 = bf16[2,72,772]{2,1,0:T(8,128)(2,1)S(1)} collective-permute-done((bf16[2,72,772]{2,1,0:T(8,128)(2,1)S(1)}, bf16[2,72,772]{2,1,0:T(8,128)(2,1)S(1)}, u32[]{:S(2)}, u32[]{:S(2)}) %collective-permute-start.51) | collective-permute-done | bytes 222368 | tf_op jit(solution)/shard_map/ppermute | solution.py:76
  677.1 12.0 %collective-permute-done.53 = bf16[2,72,772]{2,1,0:T(8,128)(2,1)S(1)} collective-permute-done((bf16[2,72,772]{2,1,0:T(8,128)(2,1)S(1)}, bf16[2,72,772]{2,1,0:T(8,128)(2,1)S(1)}, u32[]{:S(2)}, u32[]{:S(2)}) %collective-permute-start.53) | collective-permute-done | bytes 222368 | tf_op jit(solution)/shard_map/ppermute | solution.py:76
  (309 shorter events, 130.4 us)
Async XLA Ops:
  7.2 184.4 %all-gather.3.cloned.1.call-start = ((), (), s32[]{:S(2)}) async-start(), calls=%async_computation.2 | async-start | bytes 23887872 | tf_op jit(solution)/shard_map/all_gather | solution.py:655
  10.9 211.5 %all-gather.5.cloned.1.call-start = ((), (), s32[]{:S(2)}) async-start(), calls=%async_computation.3 | async-start | bytes 11943936 | tf_op jit(solution)/shard_map/all_gather | solution.py:655
  13.4 453.1 %reduce-scatter.3.cloned.1.call-start = ((), (), s32[]{:S(2)}) async-start(), calls=%async_computation.4 | async-start | bytes 6635520 | tf_op jit(solution)/shard_map/reduce_scatter | solution.py:662
  18.3 40.8 %collective-permute-start = (bf16[576,896]{1,0:T(8,128)(2,1)S(1)}, bf16[576,896]{1,0:T(8,128)(2,1)S(1)}, u32[]{:S(2)}, u32[]{:S(2)}) collective-permute-start(bf16[576,896]{1,0:T(8,128)(2,1)S(1)} %get-tuple-element.214), channel_id=1, source_target_pairs={{0,1},{1,0},{2,3},{3,2},{4,5},{5,4},{6,7},{7,6},{8,9},{9,8},{10,11... | collective-permute-start | bytes 3096584 | tf_op jit(solution)/shard_map/ppermute | solution.py:76
  19.5 42.0 %collective-permute-start.1 = (bf16[576,896]{1,0:T(8,128)(2,1)S(1)}, bf16[576,896]{1,0:T(8,128)(2,1)S(1)}, u32[]{:S(2)}, u32[]{:S(2)}) collective-permute-start(bf16[576,896]{1,0:T(8,128)(2,1)S(1)} %get-tuple-element.214), channel_id=1, source_target_pairs={{0,2},{1,3},{2,0},{3,1},{4,6},{5,7},{6,4},{7,5},{8,10},{9,11},{10,... | collective-permute-start | bytes 3096584 | tf_op jit(solution)/shard_map/ppermute | solution.py:76
  19.7 27.9 %collective-permute-start.2 = (bf16[128,2304]{1,0:T(8,128)(2,1)S(1)}, bf16[128,2304]{1,0:T(8,128)(2,1)S(1)}, u32[]{:S(2)}, u32[]{:S(2)}) collective-permute-start(bf16[128,2304]{1,0:T(8,128)(2,1)S(1)} %bitcast.279), channel_id=1, source_target_pairs={{0,16},{4,20},{8,24},{12,28},{16,0},{20,4},{24,8},{28,12},{1,17},{... | collective-permute-start | bytes 1769480 | tf_op jit(solution)/shard_map/ppermute | solution.py:76
  22.0 25.6 %collective-permute-start.3 = (bf16[128,2304]{1,0:T(8,128)(2,1)S(1)}, bf16[128,2304]{1,0:T(8,128)(2,1)S(1)}, u32[]{:S(2)}, u32[]{:S(2)}) collective-permute-start(bf16[128,2304]{1,0:T(8,128)(2,1)S(1)} %bitcast.280), channel_id=1, source_target_pairs={{0,8},{4,12},{8,0},{12,4},{16,24},{20,28},{24,16},{28,20},{1,9},{5... | collective-permute-start | bytes 1769480 | tf_op jit(solution)/shard_map/ppermute | solution.py:76
  61.5 20.6 %collective-permute-start.6 = (bf16[128,2304]{1,0:T(8,128)(2,1)S(1)}, bf16[128,2304]{1,0:T(8,128)(2,1)}, u32[]{:S(2)}, u32[]{:S(2)}) collective-permute-start(bf16[128,2304]{1,0:T(8,128)(2,1)S(1)} %collective-permute-done.2), channel_id=1, source_target_pairs={{0,8},{4,12},{8,0},{12,4},{16,24},{20,28},{24,16},{28,20},{1,9},{5... | collective-permute-start | bytes 1769480 | tf_op jit(solution)/shard_map/ppermute | solution.py:76
  62.6 19.6 %collective-permute-start.4 = (bf16[288,896]{1,0:T(8,128)(2,1)}, bf16[288,896]{1,0:T(8,128)(2,1)}, u32[]{:S(2)}, u32[]{:S(2)}) collective-permute-start(bf16[288,896]{1,0:T(8,128)(2,1)} %slice.347), channel_id=1, source_target_pairs={{0,2},{1,3},{2,0},{3,1},{4,6},{5,7},{6,4},{7,5},{8,10},{9,11},{10,... | collective-permute-start | bytes 1548296 | tf_op jit(solution)/shard_map/ppermute | solution.py:76
  63.4 18.7 %collective-permute-start.5 = (bf16[288,896]{1,0:T(8,128)(2,1)}, bf16[288,896]{1,0:T(8,128)(2,1)}, u32[]{:S(2)}, u32[]{:S(2)}) collective-permute-start(bf16[288,896]{1,0:T(8,128)(2,1)} %slice.348), channel_id=1, source_target_pairs={{0,1},{1,0},{2,3},{3,2},{4,5},{5,4},{6,7},{7,6},{8,9},{9,8},{10,11... | collective-permute-start | bytes 1548296 | tf_op jit(solution)/shard_map/ppermute | solution.py:76
  85.9 13.7 %collective-permute-start.7 = (bf16[2304,896]{1,0:T(8,128)(2,1)}, bf16[2304,896]{1,0:T(8,128)(2,1)}, u32[]{:S(2)}, u32[]{:S(2)}) collective-permute-start(bf16[2304,896]{1,0:T(8,128)(2,1)} %constant_dynamic-update-slice_fusion.gains.w0), channel_id=1, source_target_pairs={{0,4},{4,0},{8,12},{12,8},{16,20},{20,16},{24,28},{28,24},{1,5},{5... | collective-permute-start | bytes 12386312 | tf_op jit(solution)/shard_map/ppermute | solution.py:76
  107.4 2.2 collective-permute-start.8
  119.7 14.7 %collective-permute-start.10 = (bf16[128,2304]{1,0:T(8,128)(2,1)S(1)}, bf16[128,2304]{1,0:T(8,128)(2,1)S(1)}, u32[]{:S(2)}, u32[]{:S(2)}) collective-permute-start(bf16[128,2304]{1,0:T(8,128)(2,1)S(1)} %get-tuple-element.195), channel_id=1, source_target_pairs={{0,8},{4,12},{8,0},{12,4},{16,24},{20,28},{24,16},{28,20},{1,9},{5... | collective-permute-start | bytes 1769480 | tf_op jit(solution)/shard_map/ppermute | solution.py:76
  120.4 36.0 %collective-permute-start.9 = (bf16[128,2304]{1,0:T(8,128)(2,1)S(1)}, bf16[128,2304]{1,0:T(8,128)(2,1)S(1)}, u32[]{:S(2)}, u32[]{:S(2)}) collective-permute-start(bf16[128,2304]{1,0:T(8,128)(2,1)S(1)} %get-tuple-element.194), channel_id=1, source_target_pairs={{0,8},{4,12},{8,0},{12,4},{16,24},{20,28},{24,16},{28,20},{1,9},{5... | collective-permute-start | bytes 1769480 | tf_op jit(solution)/shard_map/ppermute | solution.py:76
  134.5 26.0 %collective-permute-start.11 = (bf16[128,2304]{1,0:T(8,128)(2,1)S(1)}, bf16[128,2304]{1,0:T(8,128)(2,1)S(1)}, u32[]{:S(2)}, u32[]{:S(2)}) collective-permute-start(bf16[128,2304]{1,0:T(8,128)(2,1)S(1)} %add_convert_fusion.4), channel_id=1, source_target_pairs={{0,16},{4,20},{8,24},{12,28},{16,0},{20,4},{24,8},{28,12},{1,17},{... | collective-permute-start | bytes 1769480 | tf_op jit(solution)/shard_map/ppermute | solution.py:76
  162.3 27.0 %collective-permute-start.12 = (bf16[128,2304]{1,0:T(8,128)(2,1)S(1)}, bf16[128,2304]{1,0:T(8,128)(2,1)}, u32[]{:S(2)}, u32[]{:S(2)}) collective-permute-start(bf16[128,2304]{1,0:T(8,128)(2,1)S(1)} %multiply_convert_fusion.1), channel_id=1, source_target_pairs={{0,16},{4,20},{8,24},{12,28},{16,0},{20,4},{24,8},{28,12},{1,17},{... | collective-permute-start | bytes 1769480 | tf_op jit(solution)/shard_map/ppermute | solution.py:76
  165.0 26.5 %collective-permute-start.14 = (bf16[128,2304]{1,0:T(8,128)(2,1)S(1)}, bf16[128,2304]{1,0:T(8,128)(2,1)S(1)}, u32[]{:S(2)}, u32[]{:S(2)}) collective-permute-start(bf16[128,2304]{1,0:T(8,128)(2,1)S(1)} %multiply_convert_fusion.1), channel_id=1, source_target_pairs={{0,8},{4,12},{8,0},{12,4},{16,24},{20,28},{24,16},{28,20},{1,9},{5... | collective-permute-start | bytes 1769480 | tf_op jit(solution)/shard_map/ppermute | solution.py:76
  189.2 16.8 %collective-permute-start.13 = (bf16[128,2304]{1,0:T(8,128)(2,1)}, bf16[128,2304]{1,0:T(8,128)(2,1)}, u32[]{:S(2)}, u32[]{:S(2)}) collective-permute-start(bf16[128,2304]{1,0:T(8,128)(2,1)} %collective-permute-done.12), channel_id=1, source_target_pairs={{0,8},{4,12},{8,0},{12,4},{16,24},{20,28},{24,16},{28,20},{1,9},{5... | collective-permute-start | bytes 1769480 | tf_op jit(solution)/shard_map/ppermute | solution.py:76
  232.9 14.0 %collective-permute-start.16 = (bf16[128,2304]{1,0:T(8,128)(2,1)}, bf16[128,2304]{1,0:T(8,128)(2,1)}, u32[]{:S(2)}, u32[]{:S(2)}) collective-permute-start(bf16[128,2304]{1,0:T(8,128)(2,1)} %get-tuple-element.209), channel_id=1, source_target_pairs={{0,8},{4,12},{8,0},{12,4},{16,24},{20,28},{24,16},{28,20},{1,9},{5... | collective-permute-start | bytes 1769480 | tf_op jit(solution)/shard_map/ppermute | solution.py:76
  234.6 35.8 %collective-permute-start.15 = (bf16[128,2304]{1,0:T(8,128)(2,1)}, bf16[128,2304]{1,0:T(8,128)(2,1)}, u32[]{:S(2)}, u32[]{:S(2)}) collective-permute-start(bf16[128,2304]{1,0:T(8,128)(2,1)} %get-tuple-element.208), channel_id=1, source_target_pairs={{0,8},{4,12},{8,0},{12,4},{16,24},{20,28},{24,16},{28,20},{1,9},{5... | collective-permute-start | bytes 1769480 | tf_op jit(solution)/shard_map/ppermute | solution.py:76
  248.2 27.4 %collective-permute-start.17 = (bf16[128,2304]{1,0:T(8,128)(2,1)S(1)}, bf16[128,2304]{1,0:T(8,128)(2,1)S(1)}, u32[]{:S(2)}, u32[]{:S(2)}) collective-permute-start(bf16[128,2304]{1,0:T(8,128)(2,1)S(1)} %add_convert_fusion.3), channel_id=1, source_target_pairs={{0,16},{4,20},{8,24},{12,28},{16,0},{20,4},{24,8},{28,12},{1,17},{... | collective-permute-start | bytes 1769480 | tf_op jit(solution)/shard_map/ppermute | solution.py:76
  252.4 24.7 %collective-permute-start.20 = (bf16[256,2304]{1,0:T(8,128)(2,1)S(1)}, bf16[256,2304]{1,0:T(8,128)(2,1)S(1)}, u32[]{:S(2)}, u32[]{:S(2)}) collective-permute-start(bf16[256,2304]{1,0:T(8,128)(2,1)S(1)} %copy-done.12), channel_id=1, source_target_pairs={{0,4},{4,0},{8,12},{12,8},{16,20},{20,16},{24,28},{28,24},{1,5},{5... | collective-permute-start | bytes 3538952 | tf_op jit(solution)/shard_map/ppermute | solution.py:76
  255.1 22.1 %collective-permute-start.21 = (bf16[256,2304]{1,0:T(8,128)(2,1)}, bf16[256,2304]{1,0:T(8,128)(2,1)S(1)}, u32[]{:S(2)}, u32[]{:S(2)}) collective-permute-start(bf16[256,2304]{1,0:T(8,128)(2,1)} %copy-done.14), channel_id=1, source_target_pairs={{0,4},{4,0},{8,12},{12,8},{16,20},{20,16},{24,28},{28,24},{1,5},{5... | collective-permute-start | bytes 3538952 | tf_op jit(solution)/shard_map/ppermute | solution.py:76
  255.1 22.1 %collective-permute-start.18 = (bf16[1,256,1152]{2,1,0:T(8,128)(2,1)S(1)}, bf16[1,256,1152]{2,1,0:T(8,128)(2,1)S(1)}, u32[]{:S(2)}, u32[]{:S(2)}) collective-permute-start(bf16[1,256,1152]{2,1,0:T(8,128)(2,1)S(1)} %copy-done.19), channel_id=1, source_target_pairs={{0,4},{4,0},{8,12},{12,8},{16,20},{20,16},{24,28},{28,24},{1,5},{5... | collective-permute-start | bytes 1769480 | tf_op jit(solution)/shard_map/ppermute | solution.py:76
  270.4 6.8 collective-permute-start.19
  280.4 23.8 %collective-permute-start.22 = (bf16[128,2304]{1,0:T(8,128)(2,1)}, bf16[128,2304]{1,0:T(8,128)(2,1)}, u32[]{:S(2)}, u32[]{:S(2)}) collective-permute-start(bf16[128,2304]{1,0:T(8,128)(2,1)} %get-tuple-element.204), channel_id=1, source_target_pairs={{0,16},{4,20},{8,24},{12,28},{16,0},{20,4},{24,8},{28,12},{1,17},{... | collective-permute-start | bytes 1769480 | tf_op jit(solution)/shard_map/ppermute | solution.py:76
  283.2 35.8 %collective-permute-start.24 = (bf16[128,2304]{1,0:T(8,128)(2,1)}, bf16[128,2304]{1,0:T(8,128)(2,1)}, u32[]{:S(2)}, u32[]{:S(2)}) collective-permute-start(bf16[128,2304]{1,0:T(8,128)(2,1)} %get-tuple-element.204), channel_id=1, source_target_pairs={{0,8},{4,12},{8,0},{12,4},{16,24},{20,28},{24,16},{28,20},{1,9},{5... | collective-permute-start | bytes 1769480 | tf_op jit(solution)/shard_map/ppermute | solution.py:76
  304.1 16.8 %collective-permute-start.23 = (bf16[128,2304]{1,0:T(8,128)(2,1)}, bf16[128,2304]{1,0:T(8,128)(2,1)}, u32[]{:S(2)}, u32[]{:S(2)}) collective-permute-start(bf16[128,2304]{1,0:T(8,128)(2,1)} %collective-permute-done.22), channel_id=1, source_target_pairs={{0,8},{4,12},{8,0},{12,4},{16,24},{20,28},{24,16},{28,20},{1,9},{5... | collective-permute-start | bytes 1769480 | tf_op jit(solution)/shard_map/ppermute | solution.py:76
  320.9 17.0 %collective-permute-start.25 = (bf16[256,2304]{1,0:T(8,128)(2,1)S(1)}, bf16[256,2304]{1,0:T(8,128)(2,1)}, u32[]{:S(2)}, u32[]{:S(2)}) collective-permute-start(bf16[256,2304]{1,0:T(8,128)(2,1)S(1)} %copy-done.13), channel_id=1, source_target_pairs={{0,4},{4,0},{8,12},{12,8},{16,20},{20,16},{24,28},{28,24},{1,5},{5... | collective-permute-start | bytes 3538952 | tf_op jit(solution)/shard_map/ppermute | solution.py:76
  326.7 11.3 %collective-permute-start.26 = (bf16[256,2304]{1,0:T(8,128)(2,1)}, bf16[256,2304]{1,0:T(8,128)(2,1)}, u32[]{:S(2)}, u32[]{:S(2)}) collective-permute-start(bf16[256,2304]{1,0:T(8,128)(2,1)} %constant_dynamic-update-slice_fusion.7.x.refs_1_), channel_id=1, source_target_pairs={{0,4},{4,0},{8,12},{12,8},{16,20},{20,16},{24,28},{28,24},{1,5},{5... | collective-permute-start | bytes 3538952 | tf_op jit(solution)/shard_map/ppermute | solution.py:76
  348.6 185.5 %reduce-scatter.5.cloned.1.call-start = ((), (), s32[]{:S(2)}) async-start(), calls=%async_computation.5 | async-start | bytes 13271040 | tf_op jit(solution)/shard_map/reduce_scatter | solution.py:662
  348.6 16.6 %collective-permute-start.29 = (bf16[2,256,1152]{2,1,0:T(8,128)(2,1)}, bf16[2,256,1152]{2,1,0:T(8,128)(2,1)}, u32[]{:S(2)}, u32[]{:S(2)}) collective-permute-start(bf16[2,256,1152]{2,1,0:T(8,128)(2,1)} %get-tuple-element.120.d1), channel_id=1, source_target_pairs={{0,4},{4,0},{8,12},{12,8},{16,20},{20,16},{24,28},{28,24},{1,5},{5... | collective-permute-start | bytes 3538952 | tf_op jit(solution)/shard_map/ppermute | solution.py:76
  349.2 16.1 %collective-permute-start.30 = (bf16[2,256,1152]{2,1,0:T(8,128)(2,1)}, bf16[2,256,1152]{2,1,0:T(8,128)(2,1)}, u32[]{:S(2)}, u32[]{:S(2)}) collective-permute-start(bf16[2,256,1152]{2,1,0:T(8,128)(2,1)} %get-tuple-element.122.d1), channel_id=1, source_target_pairs={{0,4},{4,0},{8,12},{12,8},{16,20},{20,16},{24,28},{28,24},{1,5},{5... | collective-permute-start | bytes 3538952 | tf_op jit(solution)/shard_map/ppermute | solution.py:76
  363.8 19.9 %collective-permute-start.27 = (bf16[128,2304]{1,0:T(8,128)(2,1)}, bf16[128,2304]{1,0:T(8,128)(2,1)S(1)}, u32[]{:S(2)}, u32[]{:S(2)}) collective-permute-start(bf16[128,2304]{1,0:T(8,128)(2,1)} %get-tuple-element.207), channel_id=1, source_target_pairs={{0,8},{4,12},{8,0},{12,4},{16,24},{20,28},{24,16},{28,20},{1,9},{5... | collective-permute-start | bytes 1769480 | tf_op jit(solution)/shard_map/ppermute | solution.py:76
  363.9 27.1 %collective-permute-start.28 = (bf16[128,2304]{1,0:T(8,128)(2,1)}, bf16[128,2304]{1,0:T(8,128)(2,1)S(1)}, u32[]{:S(2)}, u32[]{:S(2)}) collective-permute-start(bf16[128,2304]{1,0:T(8,128)(2,1)} %get-tuple-element.206), channel_id=1, source_target_pairs={{0,8},{4,12},{8,0},{12,4},{16,24},{20,28},{24,16},{28,20},{1,9},{5... | collective-permute-start | bytes 1769480 | tf_op jit(solution)/shard_map/ppermute | solution.py:76
  383.7 47.6 %copy-start.15 = (bf16[128,2304]{1,0:T(8,128)(2,1)}, bf16[128,2304]{1,0:T(8,128)(2,1)S(1)}, u32[]{:S(2)}) copy-start(bf16[128,2304]{1,0:T(8,128)(2,1)S(1)} %collective-permute-done.27) | copy-start | bytes 1769476
  405.6 25.8 %collective-permute-start.31 = (bf16[128,2304]{1,0:T(8,128)(2,1)S(1)}, bf16[128,2304]{1,0:T(8,128)(2,1)S(1)}, u32[]{:S(2)}, u32[]{:S(2)}) collective-permute-start(bf16[128,2304]{1,0:T(8,128)(2,1)S(1)} %add_convert_fusion.1), channel_id=1, source_target_pairs={{0,16},{4,20},{8,24},{12,28},{16,0},{20,4},{24,8},{28,12},{1,17},{... | collective-permute-start | bytes 1769480 | tf_op jit(solution)/shard_map/ppermute | solution.py:76
  435.8 27.7 %collective-permute-start.33 = (bf16[128,2304]{1,0:T(8,128)(2,1)S(1)}, bf16[128,2304]{1,0:T(8,128)(2,1)S(1)}, u32[]{:S(2)}, u32[]{:S(2)}) collective-permute-start(bf16[128,2304]{1,0:T(8,128)(2,1)S(1)} %multiply_convert_fusion), channel_id=1, source_target_pairs={{0,16},{4,20},{8,24},{12,28},{16,0},{20,4},{24,8},{28,12},{1,17},{... | collective-permute-start | bytes 1769480 | tf_op jit(solution)/shard_map/ppermute | solution.py:76
  438.9 34.0 %collective-permute-start.32 = (bf16[128,2304]{1,0:T(8,128)(2,1)S(1)}, bf16[128,2304]{1,0:T(8,128)(2,1)S(1)}, u32[]{:S(2)}, u32[]{:S(2)}) collective-permute-start(bf16[128,2304]{1,0:T(8,128)(2,1)S(1)} %multiply_convert_fusion), channel_id=1, source_target_pairs={{0,8},{4,12},{8,0},{12,4},{16,24},{20,28},{24,16},{28,20},{1,9},{5... | collective-permute-start | bytes 1769480 | tf_op jit(solution)/shard_map/ppermute | solution.py:76
  463.4 16.4 %collective-permute-start.34 = (bf16[128,2304]{1,0:T(8,128)(2,1)S(1)}, bf16[128,2304]{1,0:T(8,128)(2,1)}, u32[]{:S(2)}, u32[]{:S(2)}) collective-permute-start(bf16[128,2304]{1,0:T(8,128)(2,1)S(1)} %collective-permute-done.33), channel_id=1, source_target_pairs={{0,8},{4,12},{8,0},{12,4},{16,24},{20,28},{24,16},{28,20},{1,9},{5... | collective-permute-start | bytes 1769480 | tf_op jit(solution)/shard_map/ppermute | solution.py:76
  468.7 13.7 %collective-permute-start.35 = (bf16[4,72,1152]{2,1,0:T(8,128)(2,1)}, bf16[4,72,1152]{2,1,0:T(8,128)(2,1)}, u32[]{:S(2)}, u32[]{:S(2)}) collective-permute-start(bf16[4,72,1152]{2,1,0:T(8,128)(2,1)} %select_bitcast_fusion.1), channel_id=1, source_target_pairs={{0,4},{4,0},{8,12},{12,8},{16,20},{20,16},{24,28},{28,24},{1,5},{5... | collective-permute-start | bytes 1990664 | tf_op jit(solution)/shard_map/ppermute | solution.py:76
  469.6 71.4 %collective-permute-start.41 = (bf16[512,2304]{1,0:T(8,128)(2,1)}, bf16[512,2304]{1,0:T(8,128)(2,1)}, u32[]{:S(2)}, u32[]{:S(2)}) collective-permute-start(bf16[512,2304]{1,0:T(8,128)(2,1)} %get-tuple-element.137.refs_0_), channel_id=1, source_target_pairs={{0,4},{4,0},{8,12},{12,8},{16,20},{20,16},{24,28},{28,24},{1,5},{5... | collective-permute-start | bytes 7077896 | tf_op jit(solution)/shard_map/ppermute | solution.py:76
  469.6 78.8 %collective-permute-start.44 = (bf16[512,256]{1,0:T(8,128)(2,1)}, bf16[512,256]{1,0:T(8,128)(2,1)}, u32[]{:S(2)}, u32[]{:S(2)}) collective-permute-start(bf16[512,256]{1,0:T(8,128)(2,1)} %get-tuple-element.141), channel_id=1, source_target_pairs={{0,4},{4,0},{8,12},{12,8},{16,20},{20,16},{24,28},{28,24},{1,5},{5... | collective-permute-start | bytes 786440 | tf_op jit(solution)/shard_map/ppermute | solution.py:76
  483.9 64.5 %collective-permute-start.43 = (bf16[512,2304]{1,0:T(8,128)(2,1)}, bf16[512,2304]{1,0:T(8,128)(2,1)}, u32[]{:S(2)}, u32[]{:S(2)}) collective-permute-start(bf16[512,2304]{1,0:T(8,128)(2,1)} %pad_maximum_fusion.3.d_out.refs_0_), channel_id=1, source_target_pairs={{0,4},{4,0},{8,12},{12,8},{16,20},{20,16},{24,28},{28,24},{1,5},{5... | collective-permute-start | bytes 7077896 | tf_op jit(solution)/shard_map/ppermute | solution.py:76
  497.7 11.0 %collective-permute-start.36 = (bf16[512,512]{1,0:T(8,128)(2,1)}, bf16[512,512]{1,0:T(8,128)(2,1)S(1)}, u32[]{:S(2)}, u32[]{:S(2)}) collective-permute-start(bf16[512,512]{1,0:T(8,128)(2,1)} %get-tuple-element.132), channel_id=1, source_target_pairs={{0,4},{4,0},{8,12},{12,8},{16,20},{20,16},{24,28},{28,24},{1,5},{5... | collective-permute-start | bytes 1572872 | tf_op jit(solution)/shard_map/ppermute | solution.py:76
  498.0 9.2 %collective-permute-start.37 = (bf16[2,72,1152]{2,1,0:T(8,128)(2,1)S(1)}, bf16[2,72,1152]{2,1,0:T(8,128)(2,1)S(1)}, u32[]{:S(2)}, u32[]{:S(2)}) collective-permute-start(bf16[2,72,1152]{2,1,0:T(8,128)(2,1)S(1)} %get-tuple-element.133), channel_id=1, source_target_pairs={{0,8},{4,12},{8,0},{12,4},{16,24},{20,28},{24,16},{28,20},{1,9},{5... | collective-permute-start | bytes 995336 | tf_op jit(solution)/shard_map/ppermute | solution.py:76
  507.3 22.9 %collective-permute-start.57 = (bf16[2,72,1152]{2,1,0:T(8,128)(2,1)S(1)}, bf16[2,72,1152]{2,1,0:T(8,128)(2,1)}, u32[]{:S(2)}, u32[]{:S(2)}) collective-permute-start(bf16[2,72,1152]{2,1,0:T(8,128)(2,1)S(1)} %get-tuple-element.154), channel_id=1, source_target_pairs={{0,16},{4,20},{8,24},{12,28},{16,0},{20,4},{24,8},{28,12},{1,17},{... | collective-permute-start | bytes 995336 | tf_op jit(solution)/shard_map/ppermute | solution.py:76
  508.7 29.2 %collective-permute-start.58 = (bf16[2,72,1152]{2,1,0:T(8,128)(2,1)S(1)}, bf16[2,72,1152]{2,1,0:T(8,128)(2,1)S(1)}, u32[]{:S(2)}, u32[]{:S(2)}) collective-permute-start(bf16[2,72,1152]{2,1,0:T(8,128)(2,1)S(1)} %get-tuple-element.155), channel_id=1, source_target_pairs={{0,24},{4,28},{8,16},{12,20},{16,8},{20,12},{24,0},{28,4},{1,25},{... | collective-permute-start | bytes 995336 | tf_op jit(solution)/shard_map/ppermute | solution.py:76
  530.1 12.2 %collective-permute-start.42 = (bf16[1,512,512]{2,1,0:T(8,128)(2,1)}, bf16[1,512,512]{2,1,0:T(8,128)(2,1)}, u32[]{:S(2)}, u32[]{:S(2)}) collective-permute-start(bf16[1,512,512]{2,1,0:T(8,128)(2,1)} %get-tuple-element.139), channel_id=1, source_target_pairs={{0,4},{4,0},{8,12},{12,8},{16,20},{20,16},{24,28},{28,24},{1,5},{5... | collective-permute-start | bytes 1572872 | tf_op jit(solution)/shard_map/ppermute | solution.py:76
  537.9 17.1 %collective-permute-start.40 = (bf16[4,72,2304]{2,1,0:T(8,128)(2,1)}, bf16[4,72,2304]{2,1,0:T(8,128)(2,1)}, u32[]{:S(2)}, u32[]{:S(2)}) collective-permute-start(bf16[4,72,2304]{2,1,0:T(8,128)(2,1)} %select_bitcast_fusion), channel_id=1, source_target_pairs={{0,4},{4,0},{8,12},{12,8},{16,20},{20,16},{24,28},{28,24},{1,5},{5... | collective-permute-start | bytes 3981320 | tf_op jit(solution)/shard_map/ppermute | solution.py:76
  541.0 22.6 %collective-permute-start.38 = (bf16[128,2304]{1,0:T(8,128)(2,1)}, bf16[128,2304]{1,0:T(8,128)(2,1)S(1)}, u32[]{:S(2)}, u32[]{:S(2)}) collective-permute-start(bf16[128,2304]{1,0:T(8,128)(2,1)} %get-tuple-element.193), channel_id=1, source_target_pairs={{0,8},{4,12},{8,0},{12,4},{16,24},{20,28},{24,16},{28,20},{1,9},{5... | collective-permute-start | bytes 1769480 | tf_op jit(solution)/shard_map/ppermute | solution.py:76
  542.3 39.4 %collective-permute-start.39 = (bf16[128,2304]{1,0:T(8,128)(2,1)}, bf16[128,2304]{1,0:T(8,128)(2,1)}, u32[]{:S(2)}, u32[]{:S(2)}) collective-permute-start(bf16[128,2304]{1,0:T(8,128)(2,1)} %get-tuple-element.192), channel_id=1, source_target_pairs={{0,8},{4,12},{8,0},{12,4},{16,24},{20,28},{24,16},{28,20},{1,9},{5... | collective-permute-start | bytes 1769480 | tf_op jit(solution)/shard_map/ppermute | solution.py:76
  560.4 21.3 %collective-permute-start.45 = (bf16[288,772]{1,0:T(8,128)(2,1)S(1)}, bf16[288,772]{1,0:T(8,128)(2,1)S(1)}, u32[]{:S(2)}, u32[]{:S(2)}) collective-permute-start(bf16[288,772]{1,0:T(8,128)(2,1)S(1)} %get-tuple-element.181), channel_id=1, source_target_pairs={{0,1},{1,0},{2,3},{3,2},{4,5},{5,4},{6,7},{7,6},{8,9},{9,8},{10,11... | collective-permute-start | bytes 1334024 | tf_op jit(solution)/shard_map/ppermute | solution.py:76
  561.6 20.1 %collective-permute-start.46 = (bf16[288,772]{1,0:T(8,128)(2,1)S(1)}, bf16[288,772]{1,0:T(8,128)(2,1)S(1)}, u32[]{:S(2)}, u32[]{:S(2)}) collective-permute-start(bf16[288,772]{1,0:T(8,128)(2,1)S(1)} %get-tuple-element.183), channel_id=1, source_target_pairs={{0,2},{1,3},{2,0},{3,1},{4,6},{5,7},{6,4},{7,5},{8,10},{9,11},{10,... | collective-permute-start | bytes 1334024 | tf_op jit(solution)/shard_map/ppermute | solution.py:76
  561.7 34.2 %collective-permute-start.54 = (bf16[2,72,2304]{2,1,0:T(8,128)(2,1)}, bf16[2,72,2304]{2,1,0:T(8,128)(2,1)}, u32[]{:S(2)}, u32[]{:S(2)}) collective-permute-start(bf16[2,72,2304]{2,1,0:T(8,128)(2,1)} %get-tuple-element.149), channel_id=1, source_target_pairs={{0,8},{4,12},{8,0},{12,4},{16,24},{20,28},{24,16},{28,20},{1,9},{5... | collective-permute-start | bytes 1990664 | tf_op jit(solution)/shard_map/ppermute | solution.py:76
  563.5 37.6 %collective-permute-start.55 = (bf16[2,72,2304]{2,1,0:T(8,128)(2,1)}, bf16[2,72,2304]{2,1,0:T(8,128)(2,1)}, u32[]{:S(2)}, u32[]{:S(2)}) collective-permute-start(bf16[2,72,2304]{2,1,0:T(8,128)(2,1)} %get-tuple-element.150), channel_id=1, source_target_pairs={{0,16},{4,20},{8,24},{12,28},{16,0},{20,4},{24,8},{28,12},{1,17},{... | collective-permute-start | bytes 1990664 | tf_op jit(solution)/shard_map/ppermute | solution.py:76
  581.6 57.7 %collective-permute-start.56 = (bf16[2,72,2304]{2,1,0:T(8,128)(2,1)}, bf16[2,72,2304]{2,1,0:T(8,128)(2,1)}, u32[]{:S(2)}, u32[]{:S(2)}) collective-permute-start(bf16[2,72,2304]{2,1,0:T(8,128)(2,1)} %get-tuple-element.151), channel_id=1, source_target_pairs={{0,24},{4,28},{8,16},{12,20},{16,8},{20,12},{24,0},{28,4},{1,25},{... | collective-permute-start | bytes 1990664 | tf_op jit(solution)/shard_map/ppermute | solution.py:76
  583.9 66.1 %collective-permute-start.47 = (bf16[128,2304]{1,0:T(8,128)(2,1)}, bf16[128,2304]{1,0:T(8,128)(2,1)}, u32[]{:S(2)}, u32[]{:S(2)}) collective-permute-start(bf16[128,2304]{1,0:T(8,128)(2,1)} %add_convert_fusion), channel_id=1, source_target_pairs={{0,16},{4,20},{8,24},{12,28},{16,0},{20,4},{24,8},{28,12},{1,17},{... | collective-permute-start | bytes 1769480 | tf_op jit(solution)/shard_map/ppermute | solution.py:76
  590.9 60.8 %collective-permute-start.49 = (bf16[576,772]{0,1:T(8,128)(2,1)}, bf16[576,772]{0,1:T(8,128)(2,1)}, u32[]{:S(2)}, u32[]{:S(2)}) collective-permute-start(bf16[576,772]{0,1:T(8,128)(2,1)} %copy.100), channel_id=1, source_target_pairs={{0,2},{1,3},{2,0},{3,1},{4,6},{5,7},{6,4},{7,5},{8,10},{9,11},{10,... | collective-permute-start | bytes 2668040 | tf_op jit(solution)/shard_map/ppermute | solution.py:76
  595.9 57.7 %collective-permute-start.48 = (bf16[576,772]{0,1:T(8,128)(2,1)}, bf16[576,772]{0,1:T(8,128)(2,1)}, u32[]{:S(2)}, u32[]{:S(2)}) collective-permute-start(bf16[576,772]{0,1:T(8,128)(2,1)} %copy.98), channel_id=1, source_target_pairs={{0,1},{1,0},{2,3},{3,2},{4,5},{5,4},{6,7},{7,6},{8,9},{9,8},{10,11... | collective-permute-start | bytes 2668040 | tf_op jit(solution)/shard_map/ppermute | solution.py:76
  657.9 3.5 collective-permute-start.50
  661.8 13.1 %collective-permute-start.51 = (bf16[2,72,772]{2,1,0:T(8,128)(2,1)S(1)}, bf16[2,72,772]{2,1,0:T(8,128)(2,1)S(1)}, u32[]{:S(2)}, u32[]{:S(2)}) collective-permute-start(bf16[2,72,772]{2,1,0:T(8,128)(2,1)S(1)} %get-tuple-element.212), channel_id=1, source_target_pairs={{0,8},{4,12},{8,0},{12,4},{16,24},{20,28},{24,16},{28,20},{1,9},{5... | collective-permute-start | bytes 667016 | tf_op jit(solution)/shard_map/ppermute | solution.py:76
  664.9 12.2 %collective-permute-start.52 = (bf16[2,72,772]{2,1,0:T(8,128)(2,1)S(1)}, bf16[2,72,772]{2,1,0:T(8,128)(2,1)S(1)}, u32[]{:S(2)}, u32[]{:S(2)}) collective-permute-start(bf16[2,72,772]{2,1,0:T(8,128)(2,1)S(1)} %get-tuple-element.213), channel_id=1, source_target_pairs={{0,16},{4,20},{8,24},{12,28},{16,0},{20,4},{24,8},{28,12},{1,17},{... | collective-permute-start | bytes 667016 | tf_op jit(solution)/shard_map/ppermute | solution.py:76
  665.0 24.1 %collective-permute-start.53 = (bf16[2,72,772]{2,1,0:T(8,128)(2,1)S(1)}, bf16[2,72,772]{2,1,0:T(8,128)(2,1)S(1)}, u32[]{:S(2)}, u32[]{:S(2)}) collective-permute-start(bf16[2,72,772]{2,1,0:T(8,128)(2,1)S(1)} %get-tuple-element.210), channel_id=1, source_target_pairs={{0,24},{4,28},{8,16},{12,20},{16,8},{20,12},{24,0},{28,4},{1,25},{... | collective-permute-start | bytes 667016 | tf_op jit(solution)/shard_map/ppermute | solution.py:76
  (38 other events, 648.8 us)
Sparse Core Ops, SparseCore 0:
  11.0 134.7 all-gather.2
  148.2 64.2 all-gather.4
  348.7 60.7 reduce-scatter.2
  412.5 104.6 reduce-scatter.4

commit v3 on v2

--- a/solution.py
+++ b/solution.py
@@ -85,21 +85,30 @@
     return [slots[k] for k in range(ranks)]
 
 
-def line_scatter(parts, ranks, beside=()):
+def line_scatter(parts, ranks):
     sums = {k: v.astype(F32) for k, v in enumerate(parts)}
     bit = 1
     while bit < ranks:
-        got = {
-            k: swap(sums.pop(k).astype(BF16), "ctx", 2 * bit, 2 * ranks)
-            for k in sorted(sums, reverse=True)
-            if k & bit
-        }
-        if beside and bit == 1:
-            got, beside = together(got, beside)
-        for k, v in got.items():
-            sums[k ^ bit] = sums[k ^ bit] + v.astype(F32)
+        for k in sorted(sums, reverse=True):
+            if k & bit:
+                got = swap(sums.pop(k).astype(BF16), "ctx", 2 * bit, 2 * ranks)
+                sums[k ^ bit] = sums[k ^ bit] + got.astype(F32)
         bit *= 2
-    return (sums[0], beside) if beside else sums[0]
+    return sums[0]
+
+
+def four_scatter(parts, ctx_count, with_first=(), with_far=()):
+    by_near = swap(parts[3].astype(BF16), "ctx", 2, ctx_count)
+    near, far, by_near, with_first = together(parts[1], parts[2], by_near, with_first)
+    far = (far.astype(F32) + by_near.astype(F32)).astype(BF16)
+    far = swap(far, "ctx", 4, ctx_count)
+    near = swap(near.astype(BF16), "ctx", 2, ctx_count)
+    near, far, with_far = together(near, far, with_far)
+    return (parts[0], near, far), with_first, with_far
+
+
+def sum_of(terms):
+    return sum(v.astype(F32) for v in terms)
 
 
 def square_gather(piece, place, beside):
@@ -335,7 +344,7 @@
     )(core, *dgu, w_in, w_in, *earlier)
 
 
-def weight_grad_kernel(lefts, rights, ctx_count, fsdp_count):
+def weight_grad_kernel(lefts, rights, ctx_count, fsdp_count, earlier=()):
     width = lefts[0].shape[1]
     groups, _, size = rights[0].shape
     counts = [v.shape[0] for v in lefts]
@@ -348,7 +357,7 @@
 
     def body(*refs):
         left_refs, right_refs = refs[: len(counts)], refs[len(counts) : 2 * len(counts)]
-        out, turned_left = refs[2 * len(counts) :]
+        out, turned_left = refs[-2:]
 
         @pl.when((pl.program_id(1) == 0) & (pl.program_id(2) == 0))
         def _():
@@ -366,13 +375,14 @@
         body,
         (halves, groups, steps),
         [pl.BlockSpec((n, part), lambda h, g, t: (0, h)) for n in counts]
-        + [pl.BlockSpec((1, n, tile), lambda h, g, t: (g, 0, t)) for n in counts],
+        + [pl.BlockSpec((1, n, tile), lambda h, g, t: (g, 0, t)) for n in counts]
+        + [pl.BlockSpec(memory_space=pl.ANY)] * len(earlier),
         pl.BlockSpec((fsdp_count, ctx_part * shard, tile), lambda h, g, t: (0, h, g * steps + t)),
         jax.ShapeDtypeStruct((fsdp_count, ctx_count * shard, groups * size), BF16),
         [pltpu.VMEM((part, sum(counts)), BF16)],
         2 * sum(counts) * width * groups * size,
         4 * sum(counts) * (width + groups * size) + 2 * width * groups * size,
-    )(*lefts, *rights)
+    )(*lefts, *rights, *earlier)
 
 
 def rotated(values, cosine, sine, back=False):
@@ -383,15 +393,14 @@
     return jnp.concatenate([low * cosine - high * sine, high * cosine + low * sine], 1)
 
 
-def qkv_kernel(inputs, attn, cosine, sine, core):
+def qkv_kernel(inputs, g_pre, attn, cosine, sine, core):
     rows, width = inputs.shape
     block = rows // 2
     size = HEAD_DIM
 
-    def body(core_ref, x, gains, w0, w1, cos, sin, normed_out, q0, q1, kv):
+    def body(core_ref, x, gain, w0, w1, cos, sin, normed_out, q0, q1, kv):
         source = x[...].astype(F32)
-        gain = gains[...].astype(F32).T[:1]
-        normed = (source * inverse_rms(source) * gain).astype(BF16)
+        normed = (source * inverse_rms(source) * gain[...]).astype(BF16)
         normed_out[...] = normed
         first = core_ref[0] == 0
         own, other = mm(normed, w0[...]), mm(normed, w1[...])
@@ -409,7 +418,7 @@
         (2,),
         [
             by_rows(width),
-            pl.BlockSpec((width, 128), lambda i, c: (0, 3 * size // 128)),
+            pl.BlockSpec((1, width), lambda i, c: (0, 0)),
             pl.BlockSpec((width, 2 * size), lambda i, c: (0, 0)),
             pl.BlockSpec((width, 2 * size), lambda i, c: (0, 0)),
             by_rows(size // 2),
@@ -426,7 +435,7 @@
         8 * rows * width * size,
         8 * width * size + 4 * rows * width,
         prefetch=1,
-    )(core, inputs, attn[0], *attn, cosine, sine)
+    )(core, inputs, g_pre, *attn, cosine, sine)
 
 
 def scores(query, key, key_place, query_place):
@@ -597,30 +606,39 @@
     )(core, inputs, *dqs, dkv_mine, dkv_got, *attn, cosine, sine)
 
 
-def both_columns(total, place, ctx_count):
-    first_core = place % 2 == 0
-    total = total.reshape(ctx_count // 2, 2, -1, total.shape[1])
-    mine = jnp.where(first_core, total[:, 0], total[:, 1])
-    theirs = swap(jnp.where(first_core, total[:, 1], total[:, 0]), "ctx", 1, ctx_count)
-    both = (jnp.where(first_core, mine, theirs), jnp.where(first_core, theirs, mine))
-    return jnp.stack(both, 1)
-
-
-def rank_parts(both, place, ctx_count):
-    return [
-        lax.dynamic_index_in_dim(both, place // 2 ^ k, 0, keepdims=False)
-        for k in range(ctx_count // 2)
-    ]
-
-
-def spread(parts, ctx_count):
-    return [
-        part if k == 0 else swap(part, "ctx", 2 * k, ctx_count) for k, part in enumerate(parts)
-    ]
-
-
-def put(into, piece, start):
-    return lax.dynamic_update_slice_in_dim(into, piece.astype(F32), start, 1)
+def to_owners(total, ctx_count):
+    total = total.reshape(ctx_count, -1, total.shape[1])
+    return lax.all_to_all(total, "ctx", split_axis=0, concat_axis=0, tiled=True)
+
+
+def side_by_side(terms):
+    return terms.astype(F32).transpose(1, 0, 2).reshape(terms.shape[1], -1)
+
+
+def attention_outputs(terms, columns):
+    count, rows, _ = terms.shape
+    size = HEAD_DIM
+
+    def body(t, grad, gains):
+        total = 0.0
+        for c in range(count):
+            part = t[c].astype(F32)
+            kv = count * size + (c % 2) * (count // 2) * size + c // 2 * size
+            grad[:, c * size : (c + 1) * size] = part[:, :size]
+            grad[:, kv : kv + size] = part[:, size : 2 * size]
+            out = columns - (count - c) * size
+            grad[:, out : out + size] = part[:, 2 * size : 3 * size]
+            total = total + part[:, 3 * size :]
+        gains[...] = total
+
+    return pl.pallas_call(
+        body,
+        out_shape=[
+            jax.ShapeDtypeStruct((rows, columns), F32),
+            jax.ShapeDtypeStruct((rows, terms.shape[2] - 3 * size), F32),
+        ],
+        compiler_params=pltpu.CompilerParams(vmem_limit_bytes=VMEM_BYTES),
+    )(terms)
 
 
 def local_kernels(
@@ -672,32 +690,40 @@
         columns(attn_weights, place * HEAD_DIM, HEAD_DIM),
         columns(attn_weights, kv_start, HEAD_DIM),
         columns(attn_weights, qkv_cols + place * HEAD_DIM, HEAD_DIM),
-        jnp.pad(norm_gains, ((0, 0), (0, 124))),
     ]
-    piece = jnp.concatenate(piece, 1)
+    piece, place_in = together(jnp.concatenate(piece, 1), place)
+    own_gains = norm_gains.T
     if fsdp_count == 4:
-        ways = (
-            [swap(own_input, "ctx", 4, ctx_count), swap(own_input, "ctx", 2, ctx_count)],
-            lambda got: swap(got[0], "ctx", 2, ctx_count),
+        ways = [swap(own_input, "ctx", 4, ctx_count), swap(own_input, "ctx", 2, ctx_count)]
+
+        def onward(got):
+            return swap(got[0], "ctx", 2, ctx_count), [swap(own_gains, "fsdp", k, 4) for k in (1, 2, 3)]
+
+        attn_own, (slot_2, slot_1), (slot_3, gains_got) = square_gather(
+            piece, fsdp_place, (ways, onward)
         )
-        attn_own, (slot_2, slot_1), slot_3 = square_gather(piece, fsdp_place, ways)
+        gains = jnp.zeros((4, width), BF16)
+        for k, block in enumerate([own_gains, *gains_got]):
+            start = (fsdp_place ^ k) * own_gains.shape[1]
+            gains = lax.dynamic_update_slice_in_dim(gains, block, start, 1)
+        gains = gains.astype(F32)
         inputs = joined([own_input, slot_1, slot_2, slot_3])
     else:
         attn_own = lax.all_gather(piece, "fsdp", axis=0, tiled=True)
         inputs = joined(line_gather(own_input, ranks))
+        gains = lax.all_gather(own_gains, "fsdp", axis=1, tiled=True).astype(F32)
     attn = (attn_own, partner(attn_own))
-    gains = attn_own[:, 3 * HEAD_DIM : 3 * HEAD_DIM + 4].astype(F32)
-    g_pre, g_post, g_mid, g_out = [gains[:, i] for i in range(4)]
+    g_pre, g_post, g_mid, g_out = [gains[i] for i in range(4)]
     in_all = chip_gather(
         jnp.concatenate(
             [
-                columns(mlp_in_weights, place * f_own, f_own),
-                columns(mlp_in_weights, hidden_width + place * f_own, f_own),
+                columns(mlp_in_weights, place_in * f_own, f_own),
+                columns(mlp_in_weights, hidden_width + place_in * f_own, f_own),
             ],
             1,
         )
     )
-    out_all = chip_gather(columns(mlp_out_weights, place * f_own, f_own))
+    out_all = chip_gather(columns(mlp_out_weights, place_in * f_own, f_own))
 
     def places_of(which):
         owners = (2 * (rank ^ jnp.arange(ranks, dtype=jnp.int32)) + which)[:, None] * tokens
@@ -710,14 +736,18 @@
     row_places, key_places = own_places[:, None], (own_places[None, :], other_places[None, :])
     core_word = core.reshape(1).astype(jnp.int32)
 
-    normed_in, *queries, kv_own = qkv_kernel(inputs, attn, cosine, sine, core_word)
+    normed_in, *queries, kv_own = qkv_kernel(
+        inputs, gains[:1], attn, cosine, sine, core_word
+    )
     attention = (core_word, queries, (kv_own, partner(kv_own)), row_places, key_places, attn)
     att_own, att_other, branch_parts = attention_forward(*attention)
     branch_parts = branch_parts.reshape(ranks, tokens, width)
 
-    def own_rows(halves, beside=()):
+    def own_rows(halves, with_first=(), with_far=()):
         halves = [v.reshape(2, tokens, width) for v in halves]
-        return line_scatter([halves[k % 2][k // 2] for k in range(4)], ranks, beside)
+        parts = [halves[k % 2][k // 2] for k in range(4)]
+        terms, with_first, with_far = four_scatter(parts, ctx_count, with_first, with_far)
+        return sum_of(terms), with_first, with_far
 
     def gathered_halves(values, work):
         slots = line_gather(values, ranks)
@@ -727,8 +757,7 @@
         second = joined([slots[1], last])
         return (first, second), (done, work(second, 1))
 
-    branch_parts = branch_parts.reshape(ranks, tokens, width)
-    branch = line_scatter(list(branch_parts), ranks)
+    branch = sum_of(four_scatter(branch_parts.reshape(ranks, tokens, width), ctx_count)[0])
     scale_branch = inverse_rms(branch)
     residual = source + branch * scale_branch * g_post
     scale_mid = inverse_rms(residual)
@@ -740,7 +769,7 @@
     hidden_own = [f[0] for f in forward]
     hidden_got = [partner(f[1]) for f in forward]
     mid_got = [partner(v) for v in mids]
-    mixed = own_rows((mixed_0, mixed_1))
+    mixed = own_rows((mixed_0, mixed_1))[0]
     mixed, hidden_own, hidden_got, mid_got = together(mixed, hidden_own, hidden_got, mid_got)
     scale_mixed = inverse_rms(mixed)
     block_out = (residual + mixed * scale_mixed * g_out).astype(BF16)
@@ -750,8 +779,8 @@
         lambda v, k: down_backward(v, *forward[k][2:], out_all, core_word),
     )
 
-    def weight_grad(lefts, rights):
-        return weight_grad_kernel(lefts, rights, ctx_count, fsdp_count)
+    def weight_grad(lefts, rights, *earlier):
+        return weight_grad_kernel(lefts, rights, ctx_count, fsdp_count, earlier)
 
     down_product = weight_grad(
         [*d_mixeds, *[partner(v) for v in d_mixeds]], hidden_own + hidden_got
@@ -761,9 +790,11 @@
     d_mid_1 = gate_up_backward(d_gate_ups[1], in_all, core_word)
     d_mid_0 = gate_up_backward(d_gate_ups[0], in_all, core_word, (d_mid_1,))
     gate_up_product = weight_grad(
-        [*mids, *mid_got], [v[0] for v in d_gate_ups] + [partner(v[1]) for v in d_gate_ups]
-    )
-    d_mid, (gate_up_product,) = own_rows((d_mid_0, d_mid_1), (gate_up_product,))
+        [*mids, *mid_got],
+        [v[0] for v in d_gate_ups] + [partner(v[1]) for v in d_gate_ups],
+        d_mid_0,
+    )
+    d_mid, _, (gate_up_product,) = own_rows((d_mid_0, d_mid_1), (), (gate_up_product,))
     gate_up_total = over_sequences(gate_up_product)
     grad_mid_gain = jnp.sum(d_mid * residual * scale_mid, 0)
     d_residual = upstream + norm_backward(residual, scale_mid, d_mid * g_mid)
@@ -774,13 +805,11 @@
         )
     )
 
-    down_parts = rank_parts(both_columns(down_total, place, ctx_count), place, ctx_count)
-    d_branches, down_parts = together(d_branches, down_parts)
-    down = spread(down_parts, ctx_count)
+    d_branches, down_total = together(d_branches, down_total)
+    down = to_owners(down_total, ctx_count)
     *d_queries, dkv_own, dkv_other = attention_backward(d_branches, *attention, cosine, sine)
-    dkv_got, down[1] = together(partner(dkv_other), down[1])
     d_in, dproj_own, dproj_other, grad_pre_gain = qkv_backward(
-        inputs, d_queries, dkv_own, dkv_got, attn, cosine, sine, core_word
+        inputs, d_queries, dkv_own, partner(dkv_other), attn, cosine, sine, core_word
     )
 
     gain_terms = jnp.stack([grad_pre_gain[0], grad_post_gain, grad_mid_gain, grad_out_gain], 1)
@@ -791,44 +820,31 @@
     )
     product = weight_grad([normed_in, partner(normed_in)], [dproj_own, partner(dproj_other)])
     product = jnp.concatenate([product, out_product, gain_terms.astype(BF16)], 2)
-    gate_up_parts = rank_parts(both_columns(gate_up_total, place, ctx_count), place, ctx_count)
-    gate_up_parts, product = together(gate_up_parts, product)
-    gate_up_terms = spread(gate_up_parts, ctx_count)
-    d_in = list(d_in.reshape(ranks, tokens, width))
+    d_in = d_in.reshape(ranks, tokens, width)
+    d_in, (down, product), (gate_up_total,) = four_scatter(
+        d_in, ctx_count, (down, product), (gate_up_total,)
+    )
+    gate_up_terms = to_owners(gate_up_total, ctx_count)
     if fsdp_count == 4:
         parts = [
             lax.dynamic_index_in_dim(product, fsdp_place ^ k, 0, keepdims=False).astype(F32)
             for k in range(4)
         ]
         corners = corner_scatter(parts[3], 4)
-        d_in, (corners,) = line_scatter(d_in, ranks, (corners,))
         attn_total = rows_scatter(parts, corners, 4).astype(BF16)
     else:
-        d_in = line_scatter(d_in, ranks)
         attn_total = over_sequences(product)
-    attn_parts = rank_parts(both_columns(attn_total, place, ctx_count), place, ctx_count)
-    attn_terms = spread(attn_parts, ctx_count)
+    gate_up_terms, attn_total = together(gate_up_terms, attn_total)
+    attn_terms = to_owners(attn_total, ctx_count)
+    d_in, attn_terms = together(d_in, attn_terms)
+    d_in = sum_of(d_in)
     d_source = d_residual + norm_backward(source, inverse_rms(source), d_in * g_pre)
 
-    grad_mlp_out = jnp.zeros((shard_rows, hidden_width), F32)
-    grad_mlp_in = jnp.zeros((shard_rows, 2 * hidden_width), F32)
-    grad_attn = jnp.zeros((shard_rows, attn_weights.shape[1]), F32)
-    grad_gains = jnp.zeros((shard_rows, 4), F32)
-    for k in range(ranks):
-        giver = rank ^ k
-        for which in (0, 1):
-            start = (2 * giver + which) * f_own
-            grad_mlp_out = put(grad_mlp_out, down[k][which], start)
-            term = gate_up_terms[k][which]
-            grad_mlp_in = put(grad_mlp_in, term[:, :f_own], start)
-            grad_mlp_in = put(grad_mlp_in, term[:, f_own:], hidden_width + start)
-            term = attn_terms[k][which]
-            start = (2 * giver + which) * HEAD_DIM
-            grad_attn = put(grad_attn, term[:, :HEAD_DIM], start)
-            grad_attn = put(grad_attn, term[:, 2 * HEAD_DIM : 3 * HEAD_DIM], qkv_cols + start)
-            start = query_cols + which * key_cols + giver * HEAD_DIM
-            grad_attn = put(grad_attn, term[:, HEAD_DIM : 2 * HEAD_DIM], start)
-            grad_gains = grad_gains + term[:, 3 * HEAD_DIM :].astype(F32)
+    grad_mlp_out = side_by_side(down)
+    grad_mlp_in = jnp.concatenate(
+        [side_by_side(gate_up_terms[:, :, :f_own]), side_by_side(gate_up_terms[:, :, f_own:])], 1
+    )
+    grad_attn, grad_gains = attention_outputs(attn_terms, attn_weights.shape[1])
     return (
         block_out.reshape(layer_input.shape),
         d_source.reshape(layer_input.shape),

time: 702 us -> 659 us (0.939)
  waiting for transfers between devices: 323 us -> 278 us
  other arithmetic: 75.1 us -> 50.5 us
  starting transfers between devices: 64 us -> 79.3 us
    ppermute x59 -> x50, waiting for transfers between devices: 323 us -> 257 us  [swap(): return lax.ppermute(values, axis, [(i, i ^ distance) for i in range(count)])]
    all_to_all x0 -> x3, starting transfers between devices: none -> 21.8 us  [to_owners(): return lax.all_to_all(total, 'ctx', split_axis=0, concat_axis=0, tiled=True)]
    all_to_all x0 -> x3, waiting for transfers between devices: none -> 20.6 us  [to_owners(): return lax.all_to_all(total, 'ctx', split_axis=0, concat_axis=0, tiled=True)]
    dynamic_update_slice x48 -> x0, other arithmetic: 18.2 us -> none  [put(): return lax.dynamic_update_slice_in_dim(into, piece.astype(F32), start, 1)]
    ppermute x59 -> x50, starting transfers between devices: 63.8 us -> 57.3 us  [swap(): return lax.ppermute(values, axis, [(i, i ^ distance) for i in range(count)])]
  transfers between devices with their start and end apart: 63 -> 57, of which waited for: 28 -> 26; matrix products, arithmetic and copies ran while one was open for 16% -> 14% of each run, Pallas kernels for 21% -> 23%
where the time goes in v3:
time: 659 us; the launch traced here: 652 us
  waiting for transfers between devices  278 us (42%)
  Pallas kernels  171 us (26%)
  starting transfers between devices  79.3 us (12%)
  local copies, waits for them, and re-layouts  59.6 us (9%)
  other arithmetic  50.5 us (8%)
  between operations  14.6 us (2%)
    ppermute x50, waiting for transfers between devices, swap(): return lax.ppermute(values, axis, [(i, i ^ distance) for i in range(count)])  257 us
    ppermute x50, starting transfers between devices, swap(): return lax.ppermute(values, axis, [(i, i ^ distance) for i in range(count)])  57.3 us
    pallas_call x4, Pallas kernels, weight_grad_kernel(): kernel_call(body, (halves, groups, steps), [pl.BlockSpec((n, part), lambd...  40.4 us
    pallas_call x2, Pallas kernels, gate_up_forward(): kernel_call(body, (2, steps), [pl.BlockSpec((rows, width), lambda h, i, c...  28.9 us
    pallas_call x2, Pallas kernels, gate_up_backward(): kernel_call(body, (width // tile,), [whole, whole, pl.BlockSpec((1, tile,...  25.3 us
    pallas_call x2, Pallas kernels, down_backward(): kernel_call(body, (2, steps), [pl.BlockSpec((rows, width), lambda h, i, c...  22.5 us
    all_to_all x3, starting transfers between devices, to_owners(): return lax.all_to_all(total, 'ctx', split_axis=0, concat_axis=0, tiled=True)  21.8 us
    all_to_all x3, waiting for transfers between devices, to_owners(): return lax.all_to_all(total, 'ctx', split_axis=0, concat_axis=0, tiled=True)  20.6 us
  transfers between devices with their start and end apart: 57, of which 26 were waited for; matrix products, arithmetic and copies ran while one was open for 14% of the time, Pallas kernels for 23%

profile of v3, /device:TPU:13, one launch (start us, length us, event | category | flops | bytes accessed | tf_op | source)
XLA Modules:
  0.0 652.3 jit_solution(11801633010770629965)
XLA Ops:
  12.6 2.5 constant_dynamic-slice_fusion
  16.7 2.3 collective-permute-start.2
  19.1 25.4 %collective-permute-done.2 = bf16[128,2304]{1,0:T(8,128)(2,1)} collective-permute-done((bf16[128,2304]{1,0:T(8,128)(2,1)S(1)}, bf16[128,2304]{1,0:T(8,128)(2,1)}, u32[]{:S(2)}, u32[]{:S(2)}) %collective-permute-start.2) | collective-permute-done | bytes 589856 | tf_op jit(solution)/shard_map/ppermute | solution.py:76
  54.5 15.0 %collective-permute-done.7 = bf16[4,576]{1,0:T(4,128)(2,1)S(1)} collective-permute-done((bf16[4,576]{1,0:T(4,128)(2,1)S(1)}, bf16[4,576]{1,0:T(4,128)(2,1)S(1)}, u32[]{:S(2)}, u32[]{:S(2)}) %collective-permute-start.7) | collective-permute-done | bytes 4640 | tf_op jit(solution)/shard_map/ppermute | solution.py:76
  75.2 6.8 %collective-permute-start.10 = (bf16[2304,768]{1,0:T(8,128)(2,1)S(1)}, bf16[2304,768]{1,0:T(8,128)(2,1)}, u32[]{:S(2)}, u32[]{:S(2)}) collective-permute-start(bf16[2304,768]{1,0:T(8,128)(2,1)S(1)} %constant_dynamic-update-slice_fusion.4.w0), channel_id=1, source_target_pairs={{0,4},{4,0},{8,12},{12,8},{16,20},{20,16},{24,28},{28,24},{1,5},{5... | collective-permute-start | bytes 10616840 | tf_op jit(solution)/shard_map/ppermute | solution.py:76
  92.3 3.2 pad_maximum_fusion.2.x
  95.5 7.4 %shard_map.109 = (bf16[512,2304]{1,0:T(8,128)(2,1)}, bf16[512,256]{1,0:T(8,128)(2,1)}, bf16[512,256]{1,0:T(8,128)(2,1)}, bf16[512,512]{1,0:T(8,128)(2,1)}) custom-call(s32[1]{0:T(128)} %bitcast.1.core_ref, bf16[512,2304]{1,0:T(8,128)(2,1)} %pad_maximum_fusion.2.x, f32[1,2304]{1,0:T(1,128)} %slice.173.gain, bf16[2304,768]{1,0:T(8,128)(2,1)} %copy-done, ...), custom_call_target="tpu_custom_call" | custom-call | flops 2415919104 | bytes 9437184 | tf_op jit(solution)/shard_map/pallas_call | solution.py:416
  105.7 7.9 %shard_map.110 = (bf16[512,256]{1,0:T(8,128)(2,1)}, bf16[512,256]{1,0:T(8,128)(2,1)}, bf16[512,2304]{1,0:T(8,128)(2,1)}) custom-call(s32[1]{0:T(128)} %bitcast.1.core_ref, bf16[512,256]{1,0:T(8,128)(2,1)} %get-tuple-element.112.q0, bf16[512,256]{1,0:T(8,128)(2,1)} %get-tuple-element.113.q1, bf16[512,512]{1,0:T(8,128)(2,1)} %get-tuple-element.114.kv0, ...), custom_call_target="tpu_custom_call" | custom-call | flops 2281701376 | bytes 4718592 | tf_op jit(solution)/shard_map/pallas_call | solution.py:480
  115.8 14.3 %collective-permute-done.12 = bf16[128,2304]{1,0:T(8,128)(2,1)S(1)} collective-permute-done((bf16[128,2304]{1,0:T(8,128)(2,1)S(1)}, bf16[128,2304]{1,0:T(8,128)(2,1)S(1)}, u32[]{:S(2)}, u32[]{:S(2)}) %collective-permute-start.12) | collective-permute-done | bytes 589856 | tf_op jit(solution)/shard_map/ppermute | solution.py:76
  130.7 2.5 collective-permute-start.14
  133.9 20.7 %collective-permute-done.13 = bf16[128,2304]{1,0:T(8,128)(2,1)S(1)} collective-permute-done((bf16[128,2304]{1,0:T(8,128)(2,1)S(1)}, bf16[128,2304]{1,0:T(8,128)(2,1)S(1)}, u32[]{:S(2)}, u32[]{:S(2)}) %collective-permute-start.13) | collective-permute-done | bytes 589856 | tf_op jit(solution)/shard_map/ppermute | solution.py:76
  154.5 3.4 collective-permute-done.14
  159.6 2.5 collective-permute-start.15
  162.1 24.1 %collective-permute-done.15 = bf16[128,2304]{1,0:T(8,128)(2,1)} collective-permute-done((bf16[128,2304]{1,0:T(8,128)(2,1)S(1)}, bf16[128,2304]{1,0:T(8,128)(2,1)}, u32[]{:S(2)}, u32[]{:S(2)}) %collective-permute-start.15) | collective-permute-done | bytes 589856 | tf_op jit(solution)/shard_map/ppermute | solution.py:76
  188.4 14.6 %shard_map.111 = (bf16[1,256,1152]{2,1,0:T(8,128)(2,1)}, bf16[1,256,1152]{2,1,0:T(8,128)(2,1)}, f32[2,256,1152]{2,1,0:T(8,128)}, f32[2,256,1152]{2,1,0:T(8,128)}) custom-call(s32[1]{0:T(128)} %bitcast.1.core_ref, bf16[256,2304]{1,0:T(8,128)(2,1)} %pad_maximum_fusion.4.x.refs_0_, bf16[2,2304,2304]{2,1,0:T(8,128)(2,1)} %bitcast.85, bf16[2,2304,2304]{2,1,0:T(8,128)(2,1)} %bitcast.86), custom_call_target="tpu_custom_call" | custom-call | flops 5435817984 | bytes 27131904 | tf_op jit(solution)/shard_map/pallas_call | solution.py:228
  205.2 14.3 %shard_map.112 = (bf16[1,256,1152]{2,1,0:T(8,128)(2,1)}, bf16[1,256,1152]{2,1,0:T(8,128)(2,1)}, f32[2,256,1152]{2,1,0:T(8,128)}, f32[2,256,1152]{2,1,0:T(8,128)}) custom-call(s32[1]{0:T(128)} %bitcast.1.core_ref, bf16[256,2304]{1,0:T(8,128)(2,1)} %copy-done.15, bf16[2,2304,2304]{2,1,0:T(8,128)(2,1)} %bitcast.87, bf16[2,2304,2304]{2,1,0:T(8,128)(2,1)} %bitcast.88), custom_call_target="tpu_custom_call" | custom-call | flops 5435817984 | bytes 27131904 | tf_op jit(solution)/shard_map/pallas_call | solution.py:228
  219.4 7.6 %shard_map.113.refs_0_ = bf16[256,2304]{1,0:T(8,128)(2,1)} custom-call(s32[1]{0:T(128)} %bitcast.1.core_ref, bf16[1,256,1152]{2,1,0:T(8,128)(2,1)} %get-tuple-element.151.h0.refs_5_, bf16[1,256,1152]{2,1,0:T(8,128)(2,1)} %get-tuple-element.130.h1, bf16[2,2304,1152]{2,1,0:T(8,128)(2,1)} %bitcast.93, bf16[2,2304,1152]{2,1,0:T(8,128)(2,1)} %bitcast.94), custom_call_target="tpu_custom_call" | custom-call | flops 2717908992 | bytes 11796480 | tf_op jit(solution)/shard_map/pallas_call | solution.py:256
  227.1 2.3 fusion.27
  230.9 8.0 %shard_map.114 = bf16[256,2304]{1,0:T(8,128)(2,1)} custom-call(s32[1]{0:T(128)} %bitcast.1.core_ref, bf16[1,256,1152]{2,1,0:T(8,128)(2,1)} %get-tuple-element.150.h0.refs_4_, bf16[1,256,1152]{2,1,0:T(8,128)(2,1)} %get-tuple-element.127.h1, bf16[2,2304,1152]{2,1,0:T(8,128)(2,1)} %bitcast.95, bf16[2,2304,1152]{2,1,0:T(8,128)(2,1)} %bitcast.96, ...), custom_call_target="tpu_custom_call" | custom-call | flops 2717908992 | bytes 11796480 | tf_op jit(solution)/shard_map/pallas_call | solution.py:256
  238.9 4.1 collective-permute-done.18
  246.5 3.2 collective-permute-start.20
  249.6 2.3 collective-permute-start.23
  252.5 16.4 %collective-permute-done.19 = bf16[128,2304]{1,0:T(8,128)(2,1)S(1)} collective-permute-done((bf16[128,2304]{1,0:T(8,128)(2,1)}, bf16[128,2304]{1,0:T(8,128)(2,1)S(1)}, u32[]{:S(2)}, u32[]{:S(2)}) %collective-permute-start.19) | collective-permute-done | bytes 589856 | tf_op jit(solution)/shard_map/ppermute | solution.py:76
  268.9 2.6 collective-permute-start.22
  277.0 3.1 collective-permute-start.25
  280.1 24.2 %collective-permute-done.25 = bf16[128,2304]{1,0:T(8,128)(2,1)} collective-permute-done((bf16[128,2304]{1,0:T(8,128)(2,1)}, bf16[128,2304]{1,0:T(8,128)(2,1)}, u32[]{:S(2)}, u32[]{:S(2)}) %collective-permute-start.25) | collective-permute-done | bytes 589856 | tf_op jit(solution)/shard_map/ppermute | solution.py:76
  304.3 2.9 collective-permute-start.26
  307.2 2.4 pad_maximum_fusion.5.x.refs_0_
  309.6 11.2 %shard_map.115 = (bf16[2,256,1152]{2,1,0:T(8,128)(2,1)}, bf16[2,256,1152]{2,1,0:T(8,128)(2,1)}) custom-call(s32[1]{0:T(128)} %bitcast.1.core_ref, bf16[256,2304]{1,0:T(8,128)(2,1)} %pad_maximum_fusion.5.x.refs_0_, f32[2,256,1152]{2,1,0:T(8,128)} %get-tuple-element.138.gate, f32[2,256,1152]{2,1,0:T(8,128)} %get-tuple-element.139.up, ...), custom_call_target="tpu_custom_call" | custom-call | flops 2717908992 | bytes 17694720 | tf_op jit(solution)/shard_map/pallas_call | solution.py:298
  326.1 11.3 %shard_map.116 = (bf16[2,256,1152]{2,1,0:T(8,128)(2,1)}, bf16[2,256,1152]{2,1,0:T(8,128)(2,1)}) custom-call(s32[1]{0:T(128)} %bitcast.1.core_ref, bf16[256,2304]{1,0:T(8,128)(2,1)} %constant_dynamic-update-slice_fusion.2.x.refs_1_, f32[2,256,1152]{2,1,0:T(8,128)} %get-tuple-element.145.gate, f32[2,256,1152]{2,1,0:T(8,128)} %get-tuple-element.146.up, ...), custom_call_target="tpu_custom_call" | custom-call | flops 2717908992 | bytes 17694720 | tf_op jit(solution)/shard_map/pallas_call | solution.py:298
  337.3 10.6 %shard_map.117 = bf16[4,576,1152]{2,1,0:T(8,128)(2,1)} custom-call(bf16[256,2304]{1,0:T(8,128)(2,1)} %pad_maximum_fusion.5.x.refs_0_, bf16[256,2304]{1,0:T(8,128)(2,1)} %constant_dynamic-update-slice_fusion.2.x.refs_1_, bf16[256,2304]{1,0:T(8,128)(2,1)} %collective-permute-done.28.refs_2_, bf16[256,2304]{1,0:T(8,128)(2,1)} %collective-permute-done.29.refs_3_, ...), custom_call_target="tpu_custom_call" | custom-call | flops 5435817984 | bytes 19464192 | tf_op jit(solution)/shard_map/pallas_call | solution.py:374
  348.0 12.7 %shard_map.118.refs_0_ = bf16[256,2304]{1,0:T(8,128)(2,1)} custom-call(s32[1]{0:T(128)} %bitcast.1.core_ref, bf16[2,256,1152]{2,1,0:T(8,128)(2,1)} %get-tuple-element.156.d0.refs_5_, bf16[2,256,1152]{2,1,0:T(8,128)(2,1)} %get-tuple-element.157.d1, bf16[2,2304,2304]{2,1,0:T(8,128)(2,1)} %bitcast.89, bf16[2,2304,2304]{2,1,0:T(8,128)(2,1)} %bitcast.90), custom_call_target="tpu_custom_call" | custom-call | flops 5435817984 | bytes 23592960 | tf_op jit(solution)/shard_map/pallas_call | solution.py:328
  360.7 2.4 fusion.26
  363.6 12.6 %shard_map.119.refs_8_ = bf16[256,2304]{1,0:T(8,128)(2,1)} custom-call(s32[1]{0:T(128)} %bitcast.1.core_ref, bf16[2,256,1152]{2,1,0:T(8,128)(2,1)} %get-tuple-element.154.d0.refs_4_, bf16[2,256,1152]{2,1,0:T(8,128)(2,1)} %get-tuple-element.155.d1, bf16[2,2304,2304]{2,1,0:T(8,128)(2,1)} %bitcast.91, bf16[2,2304,2304]{2,1,0:T(8,128)(2,1)} %bitcast.92, ...), custom_call_target="tpu_custom_call" | custom-call | flops 5435817984 | bytes 23592960 | tf_op jit(solution)/shard_map/pallas_call | solution.py:328
  382.0 19.3 %shard_map.120 = bf16[4,576,2304]{2,1,0:T(8,128)(2,1)} custom-call(bf16[256,2304]{1,0:T(8,128)(2,1)} %pad_maximum_fusion.4.x.refs_0_, bf16[256,2304]{1,0:T(8,128)(2,1)} %copy-done.15, bf16[256,2304]{1,0:T(8,128)(2,1)} %copy-done.42, bf16[256,2304]{1,0:T(8,128)(2,1)} %copy-done.43, bf16[2,256,1152]{2,1,0:T(8,128)(2,1)} %get-tuple-element.154.d0.refs_4_, ...), custom_call_target="tpu_custom_call" | custom-call | flops 10871635968 | bytes 29491200 | tf_op jit(solution)/shard_map/pallas_call | solution.py:374
  401.4 3.7 collective-permute-done.32
  406.4 2.5 multiply_reduce_fusion
  409.0 2.9 multiply_reduce_fusion.1
  413.4 4.3 collective-permute-start.36
  417.8 25.4 %collective-permute-done.36 = bf16[128,2304]{1,0:T(8,128)(2,1)S(1)} collective-permute-done((bf16[128,2304]{1,0:T(8,128)(2,1)S(1)}, bf16[128,2304]{1,0:T(8,128)(2,1)S(1)}, u32[]{:S(2)}, u32[]{:S(2)}) %collective-permute-start.36) | collective-permute-done | bytes 589856 | tf_op jit(solution)/shard_map/ppermute | solution.py:76
  446.1 12.5 %collective-permute-done.37 = bf16[128,2304]{1,0:T(8,128)(2,1)S(1)} collective-permute-done((bf16[128,2304]{1,0:T(8,128)(2,1)S(1)}, bf16[128,2304]{1,0:T(8,128)(2,1)S(1)}, u32[]{:S(2)}, u32[]{:S(2)}) %collective-permute-start.37) | collective-permute-done | bytes 589856 | tf_op jit(solution)/shard_map/ppermute | solution.py:76
  461.1 12.3 %shard_map.121 = (bf16[512,256]{1,0:T(8,128)(2,1)}, bf16[512,256]{1,0:T(8,128)(2,1)}, f32[512,512]{1,0:T(8,128)}, bf16[512,512]{1,0:T(8,128)(2,1)}) custom-call(s32[1]{0:T(128)} %bitcast.1.core_ref, bf16[512,256]{1,0:T(8,128)(2,1)} %get-tuple-element.112.q0, bf16[512,256]{1,0:T(8,128)(2,1)} %get-tuple-element.113.q1, ...), custom_call_target="tpu_custom_call" | custom-call | flops 3892314112 | bytes 4718592 | tf_op jit(solution)/shard_map/pallas_call | solution.py:543
  473.5 6.2 all-to-all-start
  481.2 8.1 %shard_map.122 = (bf16[512,2304]{1,0:T(8,128)(2,1)}, bf16[1,512,512]{2,1,0:T(8,128)(2,1)}, bf16[1,512,512]{2,1,0:T(8,128)(2,1)}, f32[1,2304]{1,0:T(1,128)}) custom-call(s32[1]{0:T(128)} %bitcast.1.core_ref, bf16[512,2304]{1,0:T(8,128)(2,1)} %pad_maximum_fusion.2.x, bf16[512,256]{1,0:T(8,128)(2,1)} %get-tuple-element.167.q0, ...), custom_call_target="tpu_custom_call" | custom-call | flops 2415919104 | bytes 9437184 | tf_op jit(solution)/shard_map/pallas_call | solution.py:589
  489.4 3.0 fusion.24
  494.3 5.9 shard_map.123
  500.2 4.6 shard_map.124
  504.8 3.6 pad_maximum_fusion
  508.4 6.8 %collective-permute-done.39 = bf16[128,2304]{1,0:T(8,128)(2,1)} collective-permute-done((bf16[128,2304]{1,0:T(8,128)(2,1)}, bf16[128,2304]{1,0:T(8,128)(2,1)}, u32[]{:S(2)}, u32[]{:S(2)}) %collective-permute-start.39) | collective-permute-done | bytes 589856 | tf_op jit(solution)/shard_map/ppermute | solution.py:76
  519.7 21.3 %collective-permute-done.44 = bf16[128,2304]{1,0:T(8,128)(2,1)S(1)} collective-permute-done((bf16[128,2304]{1,0:T(8,128)(2,1)}, bf16[128,2304]{1,0:T(8,128)(2,1)S(1)}, u32[]{:S(2)}, u32[]{:S(2)}) %collective-permute-start.44) | collective-permute-done | bytes 589856 | tf_op jit(solution)/shard_map/ppermute | solution.py:76
  541.0 2.9 collective-permute-done.45
  543.9 7.8 %all-to-all-start.1 = ((bf16[8,72,2304]{2,1,0:T(8,128)(2,1)}), bf16[8,72,2304]{2,1,0:T(8,128)(2,1)}, u32[]{:S(2)}, u32[]{:S(2)}) async-start(bf16[8,72,2304]{2,1,0:T(8,128)(2,1)} %bitcast.107), calls=%async_computation.3 | async-start | bytes 5308416 | tf_op jit(solution)/shard_map/all_to_all | solution.py:611
  551.7 2.5 dynamic-slice_bitcast_fusion.5
  554.7 12.4 %collective-permute-done.46 = bf16[288,772]{1,0:T(8,128)(2,1)S(1)} collective-permute-done((bf16[288,772]{1,0:T(8,128)(2,1)S(1)}, bf16[288,772]{1,0:T(8,128)(2,1)S(1)}, u32[]{:S(2)}, u32[]{:S(2)}) %collective-permute-start.46) | collective-permute-done | bytes 444704 | tf_op jit(solution)/shard_map/ppermute | solution.py:76
  582.3 13.0 %collective-permute-done.49 = bf16[576,772]{0,1:T(8,128)(2,1)} collective-permute-done((bf16[576,772]{0,1:T(8,128)(2,1)}, bf16[576,772]{0,1:T(8,128)(2,1)}, u32[]{:S(2)}, u32[]{:S(2)}) %collective-permute-start.49) | collective-permute-done | bytes 889376 | tf_op jit(solution)/shard_map/ppermute | solution.py:76
  595.3 2.3 copy.42
  597.6 3.0 collective-permute-done.47
  600.6 2.3 copy.40
  602.9 3.2 fusion.1
  606.1 3.0 all-to-all-done.1
  609.1 7.8 %all-to-all-start.2 = ((bf16[8,72,772]{2,1,0:T(8,128)(2,1)}), bf16[8,72,772]{2,1,0:T(8,128)(2,1)}, u32[]{:S(2)}, u32[]{:S(2)}) async-start(bf16[8,72,772]{2,1,0:T(8,128)(2,1)} %bitcast.106), calls=%async_computation.4 | async-start | bytes 2064384 | tf_op jit(solution)/shard_map/all_to_all | solution.py:611
  619.2 2.8 maximum_convert_fusion
  622.0 17.6 %all-to-all-done.2.t = bf16[8,72,772]{2,1,0:T(8,128)(2,1)} async-done(((bf16[8,72,772]{2,1,0:T(8,128)(2,1)}), bf16[8,72,772]{2,1,0:T(8,128)(2,1)}, u32[]{:S(2)}, u32[]{:S(2)}) %all-to-all-start.2) | async-done | bytes 889376 | tf_op jit(solution)/shard_map/all_to_all | solution.py:611
  641.6 2.5 shard_map.125
  (258 shorter events, 105.6 us)
Async XLA Ops:
  7.2 181.3 %all-gather.3.cloned.1.call-start = ((), (), s32[]{:S(2)}) async-start(), calls=%async_computation.5 | async-start | bytes 23887872 | tf_op jit(solution)/shard_map/all_gather | solution.py:673
  12.5 206.9 %all-gather.5.cloned.1.call-start = ((), (), s32[]{:S(2)}) async-start(), calls=%async_computation.6 | async-start | bytes 11943936 | tf_op jit(solution)/shard_map/all_gather | solution.py:673
  15.1 34.4 %copy-start.36 = (bf16[576,4]{0,1:T(4,128)(2,1)S(1)}, bf16[576,4]{0,1:T(4,128)(2,1)}, u32[]{:S(2)}) copy-start(bf16[576,4]{0,1:T(4,128)(2,1)} %param.10) | copy-start | bytes 13828
  15.1 445.1 %reduce-scatter.3.cloned.1.call-start = ((), (), s32[]{:S(2)}) async-start(), calls=%async_computation.7 | async-start | bytes 6635520 | tf_op jit(solution)/shard_map/reduce_scatter | solution.py:680
  15.1 29.8 %collective-permute-start = (bf16[576,768]{1,0:T(8,128)(2,1)S(1)}, bf16[576,768]{1,0:T(8,128)(2,1)S(1)}, u32[]{:S(2)}, u32[]{:S(2)}) collective-permute-start(bf16[576,768]{1,0:T(8,128)(2,1)S(1)} %pad_maximum_fusion.8), channel_id=1, source_target_pairs={{0,1},{1,0},{2,3},{3,2},{4,5},{5,4},{6,7},{7,6},{8,9},{9,8},{10,11... | collective-permute-start | bytes 2654216 | tf_op jit(solution)/shard_map/ppermute | solution.py:76
  16.4 30.8 %collective-permute-start.1 = (bf16[576,768]{1,0:T(8,128)(2,1)S(1)}, bf16[576,768]{1,0:T(8,128)(2,1)S(1)}, u32[]{:S(2)}, u32[]{:S(2)}) collective-permute-start(bf16[576,768]{1,0:T(8,128)(2,1)S(1)} %pad_maximum_fusion.8), channel_id=1, source_target_pairs={{0,2},{1,3},{2,0},{3,1},{4,6},{5,7},{6,4},{7,5},{8,10},{9,11},{10,... | collective-permute-start | bytes 2654216 | tf_op jit(solution)/shard_map/ppermute | solution.py:76
  16.7 27.9 %collective-permute-start.2 = (bf16[128,2304]{1,0:T(8,128)(2,1)S(1)}, bf16[128,2304]{1,0:T(8,128)(2,1)}, u32[]{:S(2)}, u32[]{:S(2)}) collective-permute-start(bf16[128,2304]{1,0:T(8,128)(2,1)S(1)} %bitcast.101), channel_id=1, source_target_pairs={{0,16},{4,20},{8,24},{12,28},{16,0},{20,4},{24,8},{28,12},{1,17},{... | collective-permute-start | bytes 1769480 | tf_op jit(solution)/shard_map/ppermute | solution.py:76
  19.0 25.6 %collective-permute-start.3 = (bf16[128,2304]{1,0:T(8,128)(2,1)S(1)}, bf16[128,2304]{1,0:T(8,128)(2,1)S(1)}, u32[]{:S(2)}, u32[]{:S(2)}) collective-permute-start(bf16[128,2304]{1,0:T(8,128)(2,1)S(1)} %bitcast.102), channel_id=1, source_target_pairs={{0,8},{4,12},{8,0},{12,4},{16,24},{20,28},{24,16},{28,20},{1,9},{5... | collective-permute-start | bytes 1769480 | tf_op jit(solution)/shard_map/ppermute | solution.py:76
  47.2 25.8 %collective-permute-start.6 = (bf16[128,2304]{1,0:T(8,128)(2,1)}, bf16[128,2304]{1,0:T(8,128)(2,1)}, u32[]{:S(2)}, u32[]{:S(2)}) collective-permute-start(bf16[128,2304]{1,0:T(8,128)(2,1)} %collective-permute-done.2), channel_id=1, source_target_pairs={{0,8},{4,12},{8,0},{12,4},{16,24},{20,28},{24,16},{28,20},{1,9},{5... | collective-permute-start | bytes 1769480 | tf_op jit(solution)/shard_map/ppermute | solution.py:76
  48.3 24.7 %collective-permute-start.4 = (bf16[288,768]{1,0:T(8,128)(2,1)}, bf16[288,768]{1,0:T(8,128)(2,1)}, u32[]{:S(2)}, u32[]{:S(2)}) collective-permute-start(bf16[288,768]{1,0:T(8,128)(2,1)} %slice.133), channel_id=1, source_target_pairs={{0,2},{1,3},{2,0},{3,1},{4,6},{5,7},{6,4},{7,5},{8,10},{9,11},{10,... | collective-permute-start | bytes 1327112 | tf_op jit(solution)/shard_map/ppermute | solution.py:76
  49.1 23.9 %collective-permute-start.5 = (bf16[288,768]{1,0:T(8,128)(2,1)}, bf16[288,768]{1,0:T(8,128)(2,1)}, u32[]{:S(2)}, u32[]{:S(2)}) collective-permute-start(bf16[288,768]{1,0:T(8,128)(2,1)} %slice.134), channel_id=1, source_target_pairs={{0,1},{1,0},{2,3},{3,2},{4,5},{5,4},{6,7},{7,6},{8,9},{9,8},{10,11... | collective-permute-start | bytes 1327112 | tf_op jit(solution)/shard_map/ppermute | solution.py:76
  49.5 20.0 %collective-permute-start.7 = (bf16[4,576]{1,0:T(4,128)(2,1)S(1)}, bf16[4,576]{1,0:T(4,128)(2,1)S(1)}, u32[]{:S(2)}, u32[]{:S(2)}) collective-permute-start(bf16[4,576]{1,0:T(4,128)(2,1)S(1)} %bitcast.115), channel_id=1, source_target_pairs={{0,1},{1,0},{2,3},{3,2},{4,5},{5,4},{6,7},{7,6},{8,9},{9,8},{10,11... | collective-permute-start | bytes 13832 | tf_op jit(solution)/shard_map/ppermute | solution.py:76
  50.6 20.1 %collective-permute-start.8 = (bf16[4,576]{1,0:T(4,128)(2,1)S(1)}, bf16[4,576]{1,0:T(4,128)(2,1)}, u32[]{:S(2)}, u32[]{:S(2)}) collective-permute-start(bf16[4,576]{1,0:T(4,128)(2,1)S(1)} %bitcast.116), channel_id=1, source_target_pairs={{0,2},{1,3},{2,0},{3,1},{4,6},{5,7},{6,4},{7,5},{8,10},{9,11},{10,... | collective-permute-start | bytes 13832 | tf_op jit(solution)/shard_map/ppermute | solution.py:76
  69.5 3.5 collective-permute-start.9
  75.2 20.3 %collective-permute-start.10 = (bf16[2304,768]{1,0:T(8,128)(2,1)S(1)}, bf16[2304,768]{1,0:T(8,128)(2,1)}, u32[]{:S(2)}, u32[]{:S(2)}) collective-permute-start(bf16[2304,768]{1,0:T(8,128)(2,1)S(1)} %constant_dynamic-update-slice_fusion.4.w0), channel_id=1, source_target_pairs={{0,4},{4,0},{8,12},{12,8},{16,20},{20,16},{24,28},{28,24},{1,5},{5... | collective-permute-start | bytes 10616840 | tf_op jit(solution)/shard_map/ppermute | solution.py:76
  102.8 2.1 collective-permute-start.11
  113.6 44.3 %copy-start.7 = (bf16[512,2304]{1,0:T(8,128)(2,1)S(1)}, bf16[512,2304]{1,0:T(8,128)(2,1)}, u32[]{:S(2)}) copy-start(bf16[512,2304]{1,0:T(8,128)(2,1)} %get-tuple-element.115) | copy-start | bytes 7077892
  115.3 14.8 %collective-permute-start.12 = (bf16[128,2304]{1,0:T(8,128)(2,1)S(1)}, bf16[128,2304]{1,0:T(8,128)(2,1)S(1)}, u32[]{:S(2)}, u32[]{:S(2)}) collective-permute-start(bf16[128,2304]{1,0:T(8,128)(2,1)S(1)} %get-tuple-element.250), channel_id=1, source_target_pairs={{0,8},{4,12},{8,0},{12,4},{16,24},{20,28},{24,16},{28,20},{1,9},{5... | collective-permute-start | bytes 1769480 | tf_op jit(solution)/shard_map/ppermute | solution.py:76
  130.1 24.4 %collective-permute-start.13 = (bf16[128,2304]{1,0:T(8,128)(2,1)S(1)}, bf16[128,2304]{1,0:T(8,128)(2,1)S(1)}, u32[]{:S(2)}, u32[]{:S(2)}) collective-permute-start(bf16[128,2304]{1,0:T(8,128)(2,1)S(1)} %get-tuple-element.116), channel_id=1, source_target_pairs={{0,8},{4,12},{8,0},{12,4},{16,24},{20,28},{24,16},{28,20},{1,9},{5... | collective-permute-start | bytes 1769480 | tf_op jit(solution)/shard_map/ppermute | solution.py:76
  130.7 27.6 %copy-start.2 = (bf16[1,128,2304]{2,1,0:T(8,128)(2,1)S(1)}, bf16[1,128,2304]{2,1,0:T(8,128)(2,1)}, u32[]{:S(2)}) copy-start(bf16[1,128,2304]{2,1,0:T(8,128)(2,1)} %param.6) | copy-start | bytes 1769476
  130.7 27.2 %collective-permute-start.14 = (bf16[128,2304]{1,0:T(8,128)(2,1)S(1)}, bf16[128,2304]{1,0:T(8,128)(2,1)S(1)}, u32[]{:S(2)}, u32[]{:S(2)}) collective-permute-start(bf16[128,2304]{1,0:T(8,128)(2,1)S(1)} %add_convert_fusion.4), channel_id=1, source_target_pairs={{0,16},{4,20},{8,24},{12,28},{16,0},{20,4},{24,8},{28,12},{1,17},{... | collective-permute-start | bytes 1769480 | tf_op jit(solution)/shard_map/ppermute | solution.py:76
  133.9 25.6 %copy-start.27 = (f32[2304]{0:T(1024)}, f32[2304]{0:T(1024)S(1)}, u32[]{:S(2)}) copy-start(f32[2304]{0:T(1024)S(1)} %get-tuple-element.228) | copy-start | bytes 27652
  159.4 26.7 %copy-start.38 = (f32[128]{0:T(128)}, f32[128]{0:T(128)S(1)}, u32[]{:S(2)}) copy-start(f32[128]{0:T(128)S(1)} %add_rsqrt_fusion.2) | copy-start | bytes 1540
  159.6 26.6 %collective-permute-start.15 = (bf16[128,2304]{1,0:T(8,128)(2,1)S(1)}, bf16[128,2304]{1,0:T(8,128)(2,1)}, u32[]{:S(2)}, u32[]{:S(2)}) collective-permute-start(bf16[128,2304]{1,0:T(8,128)(2,1)S(1)} %multiply_convert_fusion.1), channel_id=1, source_target_pairs={{0,16},{4,20},{8,24},{12,28},{16,0},{20,4},{24,8},{28,12},{1,17},{... | collective-permute-start | bytes 1769480 | tf_op jit(solution)/shard_map/ppermute | solution.py:76
  162.1 26.3 %collective-permute-start.17 = (bf16[128,2304]{1,0:T(8,128)(2,1)S(1)}, bf16[128,2304]{1,0:T(8,128)(2,1)S(1)}, u32[]{:S(2)}, u32[]{:S(2)}) collective-permute-start(bf16[128,2304]{1,0:T(8,128)(2,1)S(1)} %multiply_convert_fusion.1), channel_id=1, source_target_pairs={{0,8},{4,12},{8,0},{12,4},{16,24},{20,28},{24,16},{28,20},{1,9},{5... | collective-permute-start | bytes 1769480 | tf_op jit(solution)/shard_map/ppermute | solution.py:76
  186.2 16.9 %collective-permute-start.16 = (bf16[128,2304]{1,0:T(8,128)(2,1)}, bf16[128,2304]{1,0:T(8,128)(2,1)}, u32[]{:S(2)}, u32[]{:S(2)}) collective-permute-start(bf16[128,2304]{1,0:T(8,128)(2,1)} %collective-permute-done.15), channel_id=1, source_target_pairs={{0,8},{4,12},{8,0},{12,4},{16,24},{20,28},{24,16},{28,20},{1,9},{5... | collective-permute-start | bytes 1769480 | tf_op jit(solution)/shard_map/ppermute | solution.py:76
  229.4 13.7 %collective-permute-start.18 = (bf16[128,2304]{1,0:T(8,128)(2,1)}, bf16[128,2304]{1,0:T(8,128)(2,1)}, u32[]{:S(2)}, u32[]{:S(2)}) collective-permute-start(bf16[128,2304]{1,0:T(8,128)(2,1)} %get-tuple-element.257), channel_id=1, source_target_pairs={{0,8},{4,12},{8,0},{12,4},{16,24},{20,28},{24,16},{28,20},{1,9},{5... | collective-permute-start | bytes 1769480 | tf_op jit(solution)/shard_map/ppermute | solution.py:76
  230.9 21.0 %copy-start.16 = (bf16[256,2304]{1,0:T(8,128)(2,1)S(1)}, bf16[256,2304]{1,0:T(8,128)(2,1)}, u32[]{:S(2)}) copy-start(bf16[256,2304]{1,0:T(8,128)(2,1)} %copy-done.15) | copy-start | bytes 3538948
  238.9 34.0 %copy-start.12 = (bf16[256,2304]{1,0:T(8,128)(2,1)S(1)}, bf16[256,2304]{1,0:T(8,128)(2,1)}, u32[]{:S(2)}) copy-start(bf16[256,2304]{1,0:T(8,128)(2,1)} %shard_map.114) | copy-start | bytes 3538948
  243.1 25.8 %collective-permute-start.19 = (bf16[128,2304]{1,0:T(8,128)(2,1)}, bf16[128,2304]{1,0:T(8,128)(2,1)S(1)}, u32[]{:S(2)}, u32[]{:S(2)}) collective-permute-start(bf16[128,2304]{1,0:T(8,128)(2,1)} %get-tuple-element.131), channel_id=1, source_target_pairs={{0,8},{4,12},{8,0},{12,4},{16,24},{20,28},{24,16},{28,20},{1,9},{5... | collective-permute-start | bytes 1769480 | tf_op jit(solution)/shard_map/ppermute | solution.py:76
  246.5 26.5 %collective-permute-start.20 = (bf16[128,2304]{1,0:T(8,128)(2,1)S(1)}, bf16[128,2304]{1,0:T(8,128)(2,1)S(1)}, u32[]{:S(2)}, u32[]{:S(2)}) collective-permute-start(bf16[128,2304]{1,0:T(8,128)(2,1)S(1)} %add_convert_fusion.3), channel_id=1, source_target_pairs={{0,16},{4,20},{8,24},{12,28},{16,0},{20,4},{24,8},{28,12},{1,17},{... | collective-permute-start | bytes 1769480 | tf_op jit(solution)/shard_map/ppermute | solution.py:76
  249.6 23.7 %collective-permute-start.23 = (bf16[256,2304]{1,0:T(8,128)(2,1)S(1)}, bf16[256,2304]{1,0:T(8,128)(2,1)S(1)}, u32[]{:S(2)}, u32[]{:S(2)}) collective-permute-start(bf16[256,2304]{1,0:T(8,128)(2,1)S(1)} %copy-done.10), channel_id=1, source_target_pairs={{0,4},{4,0},{8,12},{12,8},{16,20},{20,16},{24,28},{28,24},{1,5},{5... | collective-permute-start | bytes 3538952 | tf_op jit(solution)/shard_map/ppermute | solution.py:76
  251.9 21.4 %collective-permute-start.24 = (bf16[256,2304]{1,0:T(8,128)(2,1)S(1)}, bf16[256,2304]{1,0:T(8,128)(2,1)S(1)}, u32[]{:S(2)}, u32[]{:S(2)}) collective-permute-start(bf16[256,2304]{1,0:T(8,128)(2,1)S(1)} %copy-done.16), channel_id=1, source_target_pairs={{0,4},{4,0},{8,12},{12,8},{16,20},{20,16},{24,28},{28,24},{1,5},{5... | collective-permute-start | bytes 3538952 | tf_op jit(solution)/shard_map/ppermute | solution.py:76
  252.0 21.2 %collective-permute-start.21 = (bf16[1,256,1152]{2,1,0:T(8,128)(2,1)}, bf16[1,256,1152]{2,1,0:T(8,128)(2,1)S(1)}, u32[]{:S(2)}, u32[]{:S(2)}) collective-permute-start(bf16[1,256,1152]{2,1,0:T(8,128)(2,1)} %get-tuple-element.127.h1), channel_id=1, source_target_pairs={{0,4},{4,0},{8,12},{12,8},{16,20},{20,16},{24,28},{28,24},{1,5},{5... | collective-permute-start | bytes 1769480 | tf_op jit(solution)/shard_map/ppermute | solution.py:76
  268.9 4.5 collective-permute-start.22
  277.0 27.3 %collective-permute-start.25 = (bf16[128,2304]{1,0:T(8,128)(2,1)}, bf16[128,2304]{1,0:T(8,128)(2,1)}, u32[]{:S(2)}, u32[]{:S(2)}) collective-permute-start(bf16[128,2304]{1,0:T(8,128)(2,1)} %get-tuple-element.253), channel_id=1, source_target_pairs={{0,16},{4,20},{8,24},{12,28},{16,0},{20,4},{24,8},{28,12},{1,17},{... | collective-permute-start | bytes 1769480 | tf_op jit(solution)/shard_map/ppermute | solution.py:76
  280.1 40.7 %collective-permute-start.27 = (bf16[128,2304]{1,0:T(8,128)(2,1)}, bf16[128,2304]{1,0:T(8,128)(2,1)}, u32[]{:S(2)}, u32[]{:S(2)}) collective-permute-start(bf16[128,2304]{1,0:T(8,128)(2,1)} %get-tuple-element.253), channel_id=1, source_target_pairs={{0,8},{4,12},{8,0},{12,4},{16,24},{20,28},{24,16},{28,20},{1,9},{5... | collective-permute-start | bytes 1769480 | tf_op jit(solution)/shard_map/ppermute | solution.py:76
  304.3 18.5 %collective-permute-start.26 = (bf16[128,2304]{1,0:T(8,128)(2,1)}, bf16[128,2304]{1,0:T(8,128)(2,1)}, u32[]{:S(2)}, u32[]{:S(2)}) collective-permute-start(bf16[128,2304]{1,0:T(8,128)(2,1)} %collective-permute-done.25), channel_id=1, source_target_pairs={{0,8},{4,12},{8,0},{12,4},{16,24},{20,28},{24,16},{28,20},{1,9},{5... | collective-permute-start | bytes 1769480 | tf_op jit(solution)/shard_map/ppermute | solution.py:76
  322.8 14.5 %collective-permute-start.28 = (bf16[256,2304]{1,0:T(8,128)(2,1)S(1)}, bf16[256,2304]{1,0:T(8,128)(2,1)}, u32[]{:S(2)}, u32[]{:S(2)}) collective-permute-start(bf16[256,2304]{1,0:T(8,128)(2,1)S(1)} %copy-done.11), channel_id=1, source_target_pairs={{0,4},{4,0},{8,12},{12,8},{16,20},{20,16},{24,28},{28,24},{1,5},{5... | collective-permute-start | bytes 3538952 | tf_op jit(solution)/shard_map/ppermute | solution.py:76
  326.1 11.3 %collective-permute-start.29 = (bf16[256,2304]{1,0:T(8,128)(2,1)}, bf16[256,2304]{1,0:T(8,128)(2,1)}, u32[]{:S(2)}, u32[]{:S(2)}) collective-permute-start(bf16[256,2304]{1,0:T(8,128)(2,1)} %constant_dynamic-update-slice_fusion.2.x.refs_1_), channel_id=1, source_target_pairs={{0,4},{4,0},{8,12},{12,8},{16,20},{20,16},{24,28},{28,24},{1,5},{5... | collective-permute-start | bytes 3538952 | tf_op jit(solution)/shard_map/ppermute | solution.py:76
  348.0 195.9 %reduce-scatter.5.cloned.1.call-start = ((), (), s32[]{:S(2)}) async-start(), calls=%async_computation.8 | async-start | bytes 13271040 | tf_op jit(solution)/shard_map/reduce_scatter | solution.py:680
  363.1 14.7 %collective-permute-start.30 = (bf16[128,2304]{1,0:T(8,128)(2,1)}, bf16[128,2304]{1,0:T(8,128)(2,1)S(1)}, u32[]{:S(2)}, u32[]{:S(2)}) collective-permute-start(bf16[128,2304]{1,0:T(8,128)(2,1)} %get-tuple-element.255), channel_id=1, source_target_pairs={{0,8},{4,12},{8,0},{12,4},{16,24},{20,28},{24,16},{28,20},{1,9},{5... | collective-permute-start | bytes 1769480 | tf_op jit(solution)/shard_map/ppermute | solution.py:76
  363.1 18.9 %collective-permute-start.34 = (bf16[2,256,1152]{2,1,0:T(8,128)(2,1)}, bf16[2,256,1152]{2,1,0:T(8,128)(2,1)}, u32[]{:S(2)}, u32[]{:S(2)}) collective-permute-start(bf16[2,256,1152]{2,1,0:T(8,128)(2,1)} %get-tuple-element.157.d1), channel_id=1, source_target_pairs={{0,4},{4,0},{8,12},{12,8},{16,20},{20,16},{24,28},{28,24},{1,5},{5... | collective-permute-start | bytes 3538952 | tf_op jit(solution)/shard_map/ppermute | solution.py:76
  363.6 18.4 %collective-permute-start.33 = (bf16[2,256,1152]{2,1,0:T(8,128)(2,1)}, bf16[2,256,1152]{2,1,0:T(8,128)(2,1)}, u32[]{:S(2)}, u32[]{:S(2)}) collective-permute-start(bf16[2,256,1152]{2,1,0:T(8,128)(2,1)} %get-tuple-element.155.d1), channel_id=1, source_target_pairs={{0,4},{4,0},{8,12},{12,8},{16,20},{20,16},{24,28},{28,24},{1,5},{5... | collective-permute-start | bytes 3538952 | tf_op jit(solution)/shard_map/ppermute | solution.py:76
  378.7 22.7 %collective-permute-start.31 = (bf16[128,2304]{1,0:T(8,128)(2,1)}, bf16[128,2304]{1,0:T(8,128)(2,1)S(1)}, u32[]{:S(2)}, u32[]{:S(2)}) collective-permute-start(bf16[128,2304]{1,0:T(8,128)(2,1)} %get-tuple-element.158), channel_id=1, source_target_pairs={{0,8},{4,12},{8,0},{12,4},{16,24},{20,28},{24,16},{28,20},{1,9},{5... | collective-permute-start | bytes 1769480 | tf_op jit(solution)/shard_map/ppermute | solution.py:76
  381.0 24.1 %collective-permute-start.32 = (bf16[128,2304]{1,0:T(8,128)(2,1)}, bf16[128,2304]{1,0:T(8,128)(2,1)}, u32[]{:S(2)}, u32[]{:S(2)}) collective-permute-start(bf16[128,2304]{1,0:T(8,128)(2,1)} %add_convert_fusion.1), channel_id=1, source_target_pairs={{0,16},{4,20},{8,24},{12,28},{16,0},{20,4},{24,8},{28,12},{1,17},{... | collective-permute-start | bytes 1769480 | tf_op jit(solution)/shard_map/ppermute | solution.py:76
  413.4 29.8 %collective-permute-start.36 = (bf16[128,2304]{1,0:T(8,128)(2,1)S(1)}, bf16[128,2304]{1,0:T(8,128)(2,1)S(1)}, u32[]{:S(2)}, u32[]{:S(2)}) collective-permute-start(bf16[128,2304]{1,0:T(8,128)(2,1)S(1)} %multiply_convert_fusion), channel_id=1, source_target_pairs={{0,16},{4,20},{8,24},{12,28},{16,0},{20,4},{24,8},{28,12},{1,17},{... | collective-permute-start | bytes 1769480 | tf_op jit(solution)/shard_map/ppermute | solution.py:76
  417.6 28.5 %collective-permute-start.35 = (bf16[128,2304]{1,0:T(8,128)(2,1)S(1)}, bf16[128,2304]{1,0:T(8,128)(2,1)S(1)}, u32[]{:S(2)}, u32[]{:S(2)}) collective-permute-start(bf16[128,2304]{1,0:T(8,128)(2,1)S(1)} %multiply_convert_fusion), channel_id=1, source_target_pairs={{0,8},{4,12},{8,0},{12,4},{16,24},{20,28},{24,16},{28,20},{1,9},{5... | collective-permute-start | bytes 1769480 | tf_op jit(solution)/shard_map/ppermute | solution.py:76
  443.2 15.4 %collective-permute-start.37 = (bf16[128,2304]{1,0:T(8,128)(2,1)S(1)}, bf16[128,2304]{1,0:T(8,128)(2,1)S(1)}, u32[]{:S(2)}, u32[]{:S(2)}) collective-permute-start(bf16[128,2304]{1,0:T(8,128)(2,1)S(1)} %collective-permute-done.36), channel_id=1, source_target_pairs={{0,8},{4,12},{8,0},{12,4},{16,24},{20,28},{24,16},{28,20},{1,9},{5... | collective-permute-start | bytes 1769480 | tf_op jit(solution)/shard_map/ppermute | solution.py:76
  445.3 49.0 %collective-permute-start.40 = (bf16[512,2304]{1,0:T(8,128)(2,1)}, bf16[512,2304]{1,0:T(8,128)(2,1)}, u32[]{:S(2)}, u32[]{:S(2)}) collective-permute-start(bf16[512,2304]{1,0:T(8,128)(2,1)} %get-tuple-element.173.refs_0_), channel_id=1, source_target_pairs={{0,4},{4,0},{8,12},{12,8},{16,20},{20,16},{24,28},{28,24},{1,5},{5... | collective-permute-start | bytes 7077896 | tf_op jit(solution)/shard_map/ppermute | solution.py:76
  460.2 40.0 %collective-permute-start.42 = (bf16[512,2304]{1,0:T(8,128)(2,1)}, bf16[512,2304]{1,0:T(8,128)(2,1)}, u32[]{:S(2)}, u32[]{:S(2)}) collective-permute-start(bf16[512,2304]{1,0:T(8,128)(2,1)} %pad_maximum_fusion.3.d_out.refs_0_), channel_id=1, source_target_pairs={{0,4},{4,0},{8,12},{12,8},{16,20},{20,16},{24,28},{28,24},{1,5},{5... | collective-permute-start | bytes 7077896 | tf_op jit(solution)/shard_map/ppermute | solution.py:76
  473.4 7.0 %collective-permute-start.38 = (bf16[512,512]{1,0:T(8,128)(2,1)}, bf16[512,512]{1,0:T(8,128)(2,1)S(1)}, u32[]{:S(2)}, u32[]{:S(2)}) collective-permute-start(bf16[512,512]{1,0:T(8,128)(2,1)} %get-tuple-element.170), channel_id=1, source_target_pairs={{0,4},{4,0},{8,12},{12,8},{16,20},{20,16},{24,28},{28,24},{1,5},{5... | collective-permute-start | bytes 1572872 | tf_op jit(solution)/shard_map/ppermute | solution.py:76
  473.5 41.7 %all-to-all-start = ((bf16[8,72,1152]{2,1,0:T(8,128)(2,1)}), bf16[8,72,1152]{2,1,0:T(8,128)(2,1)}, u32[]{:S(2)}, u32[]{:S(2)}) async-start(bf16[8,72,1152]{2,1,0:T(8,128)(2,1)} %bitcast.110), calls=%async_computation.1 | async-start | bytes 2654208 | tf_op jit(solution)/shard_map/all_to_all | solution.py:611
  479.7 20.4 %collective-permute-start.43 = (bf16[512,256]{1,0:T(8,128)(2,1)}, bf16[512,256]{1,0:T(8,128)(2,1)}, u32[]{:S(2)}, u32[]{:S(2)}) collective-permute-start(bf16[512,256]{1,0:T(8,128)(2,1)} %get-tuple-element.177), channel_id=1, source_target_pairs={{0,4},{4,0},{8,12},{12,8},{16,20},{20,16},{24,28},{28,24},{1,5},{5... | collective-permute-start | bytes 786440 | tf_op jit(solution)/shard_map/ppermute | solution.py:76
  489.3 5.0 collective-permute-start.41
  492.4 22.8 %collective-permute-start.39 = (bf16[128,2304]{1,0:T(8,128)(2,1)}, bf16[128,2304]{1,0:T(8,128)(2,1)}, u32[]{:S(2)}, u32[]{:S(2)}) collective-permute-start(bf16[128,2304]{1,0:T(8,128)(2,1)} %get-tuple-element.246), channel_id=1, source_target_pairs={{0,8},{4,12},{8,0},{12,4},{16,24},{20,28},{24,16},{28,20},{1,9},{5... | collective-permute-start | bytes 1769480 | tf_op jit(solution)/shard_map/ppermute | solution.py:76
  515.2 25.8 %collective-permute-start.44 = (bf16[128,2304]{1,0:T(8,128)(2,1)}, bf16[128,2304]{1,0:T(8,128)(2,1)S(1)}, u32[]{:S(2)}, u32[]{:S(2)}) collective-permute-start(bf16[128,2304]{1,0:T(8,128)(2,1)} %get-tuple-element.179), channel_id=1, source_target_pairs={{0,8},{4,12},{8,0},{12,4},{16,24},{20,28},{24,16},{28,20},{1,9},{5... | collective-permute-start | bytes 1769480 | tf_op jit(solution)/shard_map/ppermute | solution.py:76
  517.8 26.1 %collective-permute-start.45 = (bf16[128,2304]{1,0:T(8,128)(2,1)S(1)}, bf16[128,2304]{1,0:T(8,128)(2,1)S(1)}, u32[]{:S(2)}, u32[]{:S(2)}) collective-permute-start(bf16[128,2304]{1,0:T(8,128)(2,1)S(1)} %add_convert_fusion), channel_id=1, source_target_pairs={{0,16},{4,20},{8,24},{12,28},{16,0},{20,4},{24,8},{28,12},{1,17},{... | collective-permute-start | bytes 1769480 | tf_op jit(solution)/shard_map/ppermute | solution.py:76
  543.9 65.2 %all-to-all-start.1 = ((bf16[8,72,2304]{2,1,0:T(8,128)(2,1)}), bf16[8,72,2304]{2,1,0:T(8,128)(2,1)}, u32[]{:S(2)}, u32[]{:S(2)}) async-start(bf16[8,72,2304]{2,1,0:T(8,128)(2,1)} %bitcast.107), calls=%async_computation.3 | async-start | bytes 5308416 | tf_op jit(solution)/shard_map/all_to_all | solution.py:611
  554.1 13.0 %collective-permute-start.46 = (bf16[288,772]{1,0:T(8,128)(2,1)S(1)}, bf16[288,772]{1,0:T(8,128)(2,1)S(1)}, u32[]{:S(2)}, u32[]{:S(2)}) collective-permute-start(bf16[288,772]{1,0:T(8,128)(2,1)S(1)} %get-tuple-element.239), channel_id=1, source_target_pairs={{0,2},{1,3},{2,0},{3,1},{4,6},{5,7},{6,4},{7,5},{8,10},{9,11},{10,... | collective-permute-start | bytes 1334024 | tf_op jit(solution)/shard_map/ppermute | solution.py:76
  554.2 13.0 %collective-permute-start.48 = (bf16[288,772]{1,0:T(8,128)(2,1)S(1)}, bf16[288,772]{1,0:T(8,128)(2,1)S(1)}, u32[]{:S(2)}, u32[]{:S(2)}) collective-permute-start(bf16[288,772]{1,0:T(8,128)(2,1)S(1)} %get-tuple-element.241), channel_id=1, source_target_pairs={{0,1},{1,0},{2,3},{3,2},{4,5},{5,4},{6,7},{7,6},{8,9},{9,8},{10,11... | collective-permute-start | bytes 1334024 | tf_op jit(solution)/shard_map/ppermute | solution.py:76
  572.7 22.6 %collective-permute-start.49 = (bf16[576,772]{0,1:T(8,128)(2,1)}, bf16[576,772]{0,1:T(8,128)(2,1)}, u32[]{:S(2)}, u32[]{:S(2)}) collective-permute-start(bf16[576,772]{0,1:T(8,128)(2,1)} %copy.41), channel_id=1, source_target_pairs={{0,2},{1,3},{2,0},{3,1},{4,6},{5,7},{6,4},{7,5},{8,10},{9,11},{10,... | collective-permute-start | bytes 2668040 | tf_op jit(solution)/shard_map/ppermute | solution.py:76
  578.5 22.1 %collective-permute-start.47 = (bf16[576,772]{0,1:T(8,128)(2,1)}, bf16[576,772]{0,1:T(8,128)(2,1)}, u32[]{:S(2)}, u32[]{:S(2)}) collective-permute-start(bf16[576,772]{0,1:T(8,128)(2,1)} %copy.39), channel_id=1, source_target_pairs={{0,1},{1,0},{2,3},{3,2},{4,5},{5,4},{6,7},{7,6},{8,9},{9,8},{10,11... | collective-permute-start | bytes 2668040 | tf_op jit(solution)/shard_map/ppermute | solution.py:76
  609.1 30.5 %all-to-all-start.2 = ((bf16[8,72,772]{2,1,0:T(8,128)(2,1)}), bf16[8,72,772]{2,1,0:T(8,128)(2,1)}, u32[]{:S(2)}, u32[]{:S(2)}) async-start(bf16[8,72,772]{2,1,0:T(8,128)(2,1)} %bitcast.106), calls=%async_computation.4 | async-start | bytes 2064384 | tf_op jit(solution)/shard_map/all_to_all | solution.py:611
  (41 other events, 190.4 us)
Sparse Core Ops, SparseCore 0:
  12.6 130.3 all-gather.2
  145.4 64.2 all-gather.4
  348.1 59.8 reduce-scatter.2
  410.9 104.6 reduce-scatter.4

commit v4 on v3

--- a/solution.py
+++ b/solution.py
@@ -97,13 +97,19 @@
     return sums[0]
 
 
-def four_scatter(parts, ctx_count, with_first=(), with_far=()):
+def four_gather(values, ctx_count):
+    far, near = swap(values, "ctx", 4, ctx_count), swap(values, "ctx", 2, ctx_count)
+    far, near = together(far, near)
+    return [values, near, far, swap(far, "ctx", 2, ctx_count)]
+
+
+def four_scatter(parts, ctx_count, with_first=(), with_far=lambda first: ()):
     by_near = swap(parts[3].astype(BF16), "ctx", 2, ctx_count)
     near, far, by_near, with_first = together(parts[1], parts[2], by_near, with_first)
     far = (far.astype(F32) + by_near.astype(F32)).astype(BF16)
     far = swap(far, "ctx", 4, ctx_count)
     near = swap(near.astype(BF16), "ctx", 2, ctx_count)
-    near, far, with_far = together(near, far, with_far)
+    near, far, with_far = together(near, far, with_far(with_first))
     return (parts[0], near, far), with_first, with_far
 
 
@@ -196,6 +202,17 @@
     return gate * half, slope
 
 
+def stack_rows(pieces, into):
+    at = 0
+    for ref in pieces:
+        into[at : at + ref.shape[0]] = ref[...]
+        at += ref.shape[0]
+
+
+def whole_of(values):
+    return [pl.BlockSpec(v.shape, lambda *_, n=len(v.shape): (0,) * n) for v in values]
+
+
 def core_blocks(shape, steps):
     lead = (0,) * (len(shape) - 1)
     return [
@@ -205,12 +222,18 @@
 
 
 def gate_up_forward(values, w_in, core, most=384):
-    rows, width = values.shape
+    rows, width = sum(v.shape[0] for v in values), values[0].shape[1]
     size = w_in.shape[2] // 2
     tile = tile_of(size, most)
     steps = size // tile
 
-    def body(core_ref, x, g, u, hidden0, hidden1, gate_all, up_all):
+    def body(core_ref, *refs):
+        g, u, hidden0, hidden1, gate_all, up_all, x = refs[len(values) :]
+
+        @pl.when((pl.program_id(0) == 0) & (pl.program_id(1) == 0))
+        def _():
+            stack_rows(refs[: len(values)], x)
+
         gate, up = mm(x[...], g[0]), mm(x[...], u[0])
         gate_all[0] = gate
         up_all[0] = up
@@ -228,19 +251,19 @@
     return kernel_call(
         body,
         (2, steps),
-        [
-            pl.BlockSpec((rows, width), lambda h, i, c: (0, 0)),
+        whole_of(values)
+        + [
             pl.BlockSpec((1, width, tile), lambda h, i, c: (c[0] ^ h, 0, i)),
             pl.BlockSpec((1, width, tile), lambda h, i, c: (c[0] ^ h, 0, steps + i)),
         ],
         core_blocks((1, rows, tile), steps) + [saved, saved],
         [jax.ShapeDtypeStruct((1, rows, size), BF16)] * 2
         + [jax.ShapeDtypeStruct((2, rows, size), F32)] * 2,
-        [],
+        [pltpu.VMEM((rows, width), BF16)],
         8 * rows * width * size,
         8 * width * size + 20 * rows * size,
         prefetch=1,
-    )(core, values, w_in, w_in)
+    )(core, *values, w_in, w_in)
 
 
 def down_forward(hidden, w_out, core, earlier=(), most=768):
@@ -249,8 +272,9 @@
     tile = tile_of(width, most)
 
     def body(core_ref, h0, h1, o0, o1, *refs):
-        out = refs[-1]
-        out[...] = (mm_nt(h0[0], o0[0]) + mm_nt(h1[0], o1[0])).astype(BF16)
+        total = (mm_nt(h0[0], o0[0]) + mm_nt(h1[0], o1[0])).astype(BF16)
+        refs[-2][...] = total[: rows // 2]
+        refs[-1][...] = total[rows // 2 :]
 
     whole = pl.BlockSpec((1, rows, size), lambda i, c: (0, 0, 0))
     return kernel_call(
@@ -263,8 +287,8 @@
             pl.BlockSpec((1, tile, size), lambda i, c: (1 - c[0], i, 0)),
         ]
         + [pl.BlockSpec(memory_space=pl.ANY)] * len(earlier),
-        pl.BlockSpec((rows, tile), lambda i, c: (0, i)),
-        jax.ShapeDtypeStruct((rows, width), BF16),
+        [pl.BlockSpec((rows // 2, tile), lambda i, c: (0, i))] * 2,
+        [jax.ShapeDtypeStruct((rows // 2, width), BF16)] * 2,
         [],
         4 * rows * width * size,
         4 * width * size + 4 * rows * size,
@@ -273,12 +297,18 @@
 
 
 def down_backward(d_mixed, gate_all, up_all, w_out, core, most=384):
-    rows, width = d_mixed.shape
+    rows, width = sum(v.shape[0] for v in d_mixed), d_mixed[0].shape[1]
     size = w_out.shape[2]
     tile = tile_of(size, most)
     steps = size // tile
 
-    def body(core_ref, x, gate, up, o, dgu0, dgu1):
+    def body(core_ref, *refs):
+        gate, up, o, dgu0, dgu1, x = refs[len(d_mixed) :]
+
+        @pl.when((pl.program_id(0) == 0) & (pl.program_id(1) == 0))
+        def _():
+            stack_rows(refs[: len(d_mixed)], x)
+
         d_hidden = mm(x[...], o[0])
         value, slope = gelu_parts(gate[0])
         d_gate = (d_hidden * up[0] * slope).astype(BF16)
@@ -298,19 +328,15 @@
     return kernel_call(
         body,
         (2, steps),
-        [
-            pl.BlockSpec((rows, width), lambda h, i, c: (0, 0)),
-            saved,
-            saved,
-            pl.BlockSpec((1, width, tile), lambda h, i, c: (c[0] ^ h, 0, i)),
-        ],
+        whole_of(d_mixed)
+        + [saved, saved, pl.BlockSpec((1, width, tile), lambda h, i, c: (c[0] ^ h, 0, i))],
         core_blocks((2, rows, tile), steps),
         [jax.ShapeDtypeStruct((2, rows, size), BF16)] * 2,
-        [],
+        [pltpu.VMEM((rows, width), BF16)],
         4 * rows * width * size,
         4 * width * size + 24 * rows * size,
         prefetch=1,
-    )(core, d_mixed, gate_all, up_all, w_out)
+    )(core, *d_mixed, gate_all, up_all, w_out)
 
 
 def gate_up_backward(dgu, w_in, core, earlier=(), most=768):
@@ -319,10 +345,10 @@
     tile = tile_of(width, most)
 
     def body(core_ref, d0, d1, w0, w1, *refs):
-        out = refs[-1]
         total = mm_nt(d0[0], w0[0, :, :size]) + mm_nt(d0[1], w0[0, :, size:])
         total += mm_nt(d1[0], w1[0, :, :size]) + mm_nt(d1[1], w1[0, :, size:])
-        out[...] = total.astype(BF16)
+        refs[-2][...] = total[: rows // 2].astype(BF16)
+        refs[-1][...] = total[rows // 2 :].astype(BF16)
 
     whole = pl.BlockSpec((2, rows, size), lambda i, c: (0, 0, 0))
     return kernel_call(
@@ -335,8 +361,8 @@
             pl.BlockSpec((1, tile, 2 * size), lambda i, c: (1 - c[0], i, 0)),
         ]
         + [pl.BlockSpec(memory_space=pl.ANY)] * len(earlier),
-        pl.BlockSpec((rows, tile), lambda i, c: (0, i)),
-        jax.ShapeDtypeStruct((rows, width), BF16),
+        [pl.BlockSpec((rows // 2, tile), lambda i, c: (0, i))] * 2,
+        [jax.ShapeDtypeStruct((rows // 2, width), BF16)] * 2,
         [],
         8 * rows * width * size,
         8 * width * size + 8 * rows * size,
@@ -347,7 +373,8 @@
 def weight_grad_kernel(lefts, rights, ctx_count, fsdp_count, earlier=()):
     width = lefts[0].shape[1]
     groups, _, size = rights[0].shape
-    counts = [v.shape[0] for v in lefts]
+    left_counts = [v.shape[0] for v in lefts]
+    counts = [v.shape[1] for v in rights]
     starts = [sum(counts[:i]) for i in range(len(counts))]
     shard = width // (ctx_count * fsdp_count)
     halves = 2
@@ -356,13 +383,15 @@
     steps = size // tile
 
     def body(*refs):
-        left_refs, right_refs = refs[: len(counts)], refs[len(counts) : 2 * len(counts)]
+        left_refs, right_refs = refs[: len(lefts)], refs[len(lefts) :][: len(rights)]
         out, turned_left = refs[-2:]
 
         @pl.when((pl.program_id(1) == 0) & (pl.program_id(2) == 0))
         def _():
-            for ref, start, count in zip(left_refs, starts, counts):
-                turned_left[:, start : start + count] = ref[...].T
+            at = 0
+            for ref, count in zip(left_refs, left_counts):
+                turned_left[:, at : at + count] = ref[...].T
+                at += count
 
         product = 0.0
         for ref, start, count in zip(right_refs, starts, counts):
@@ -374,7 +403,7 @@
     return kernel_call(
         body,
         (halves, groups, steps),
-        [pl.BlockSpec((n, part), lambda h, g, t: (0, h)) for n in counts]
+        [pl.BlockSpec((n, part), lambda h, g, t: (0, h)) for n in left_counts]
         + [pl.BlockSpec((1, n, tile), lambda h, g, t: (g, 0, t)) for n in counts]
         + [pl.BlockSpec(memory_space=pl.ANY)] * len(earlier),
         pl.BlockSpec((fsdp_count, ctx_part * shard, tile), lambda h, g, t: (0, h, g * steps + t)),
@@ -394,11 +423,12 @@
 
 
 def qkv_kernel(inputs, g_pre, attn, cosine, sine, core):
-    rows, width = inputs.shape
+    rows, width = sum(v.shape[0] for v in inputs), inputs[0].shape[1]
     block = rows // 2
     size = HEAD_DIM
 
-    def body(core_ref, x, gain, w0, w1, cos, sin, normed_out, q0, q1, kv):
+    def body(core_ref, s0, s1, s2, s3, gain, w0, w1, cos, sin, normed_out, q0, q1, kv, x):
+        take_slots((s0, s1, s2, s3), x)
         source = x[...].astype(F32)
         normed = (source * inverse_rms(source) * gain[...]).astype(BF16)
         normed_out[...] = normed
@@ -416,8 +446,8 @@
     return kernel_call(
         body,
         (2,),
-        [
-            by_rows(width),
+        whole_of(inputs)
+        + [
             pl.BlockSpec((1, width), lambda i, c: (0, 0)),
             pl.BlockSpec((width, 2 * size), lambda i, c: (0, 0)),
             pl.BlockSpec((width, 2 * size), lambda i, c: (0, 0)),
@@ -431,11 +461,11 @@
             jax.ShapeDtypeStruct((rows, size), BF16),
             jax.ShapeDtypeStruct((rows, 2 * size), BF16),
         ],
-        [],
+        [pltpu.VMEM((block, width), BF16)],
         8 * rows * width * size,
         8 * width * size + 4 * rows * width,
         prefetch=1,
-    )(core, inputs, g_pre, *attn, cosine, sine)
+    )(core, *inputs, g_pre, *attn, cosine, sine)
 
 
 def scores(query, key, key_place, query_place):
@@ -455,11 +485,28 @@
     return by_rows, [by_rows(size), by_rows(size), kv, kv, by_rows(1), places, places] + weights
 
 
+def put_slots(total, slots):
+    rows = slots[0].shape[0]
+    for step in range(2):
+
+        @pl.when(pl.program_id(0) == step)
+        def _():
+            slots[2 * step][...] = total[:rows].astype(BF16)
+            slots[2 * step + 1][...] = total[rows:].astype(BF16)
+
+
+def take_slots(slots, into):
+    for step in range(2):
+        pl.when(pl.program_id(0) == step)(
+            lambda pair=slots[2 * step : 2 * step + 2]: stack_rows(pair, into)
+        )
+
+
 def attention_forward(core, queries, kvs, row_places, key_places, attn):
     rows, width, size = queries[0].shape[0], attn[0].shape[0], HEAD_DIM
     block = rows // 2
 
-    def body(core_ref, q0, q1, kv0, kv1, place, places0, places1, w0, w1, att0, att1, branch):
+    def body(core_ref, q0, q1, kv0, kv1, place, places0, places1, w0, w1, att0, att1, *branch):
         total = 0.0
         for q, att, w in ((q0, att0, w0), (q1, att1, w1)):
             parts = [
@@ -474,19 +521,16 @@
             attended = attended.astype(BF16)
             att[...] = attended
             total = total + mm_nt(attended, w[...])
-        branch[...] = total.astype(BF16)
+        put_slots(total, branch)
 
     by_rows, specs = attention_specs(rows, width, block)
+    slots = [jax.ShapeDtypeStruct((rows // 4, width), BF16)] * 4
     return kernel_call(
         body,
         (2,),
         specs,
-        [by_rows(size), by_rows(size), by_rows(width)],
-        [
-            jax.ShapeDtypeStruct((rows, size), BF16),
-            jax.ShapeDtypeStruct((rows, size), BF16),
-            jax.ShapeDtypeStruct((rows, width), BF16),
-        ],
+        [by_rows(size), by_rows(size)] + whole_of(slots),
+        [jax.ShapeDtypeStruct((rows, size), BF16)] * 2 + slots,
         [],
         16 * rows * rows * size + 4 * rows * width * size,
         4 * width * size + 2 * rows * width,
@@ -502,9 +546,11 @@
     scaling = size**-0.5
 
     def body(
-        core_ref, q0, q1, kv0, kv1, place, places0, places1, w0, w1, d_out, cos, sin,
-        dq0, dq1, dkv0, dkv1, sum0, sum1
+        core_ref, q0, q1, kv0, kv1, place, places0, places1, w0, w1, s0, s1, s2, s3, cos, sin,
+        dq0, dq1, dkv0, dkv1, sum0, sum1, d_out
     ):
+        take_slots((s0, s1, s2, s3), d_out)
+
         @pl.when(pl.program_id(0) == 0)
         def _():
             sum0[...] = jnp.zeros_like(sum0)
@@ -543,7 +589,7 @@
     return kernel_call(
         body,
         (2,),
-        specs + [by_rows(width), by_rows(size // 2), by_rows(size // 2)],
+        specs + whole_of(d_branch) + [by_rows(size // 2), by_rows(size // 2)],
         [by_rows(size), by_rows(size), whole, whole],
         [
             jax.ShapeDtypeStruct((rows, size), BF16),
@@ -551,18 +597,20 @@
             jax.ShapeDtypeStruct((rows, 2 * size), F32),
             jax.ShapeDtypeStruct((rows, 2 * size), BF16),
         ],
-        [pltpu.VMEM((rows, 2 * size), F32)] * 2,
+        [pltpu.VMEM((rows, 2 * size), F32)] * 2 + [pltpu.VMEM((block, width), BF16)],
         40 * rows * rows * size + 4 * rows * width * size,
         4 * width * size + 2 * rows * width,
         prefetch=1,
-    )(core, *queries, *kvs, row_places, *key_places, *attn, d_branch, cosine, sine)
+    )(core, *queries, *kvs, row_places, *key_places, *attn, *d_branch, cosine, sine)
 
 
 def qkv_backward(inputs, dqs, dkv_mine, dkv_got, attn, cosine, sine, core):
-    rows, width = inputs.shape
+    rows, width = sum(v.shape[0] for v in inputs), inputs[0].shape[1]
     block, size = rows // 2, HEAD_DIM
 
-    def body(core_ref, x, q0, q1, mine, got, w0, w1, cos, sin, d_in, dp0, dp1, gain):
+    def body(core_ref, s0, s1, s2, s3, q0, q1, mine, got, w0, w1, cos, sin, *refs):
+        d_in, (dp0, dp1, gain, x) = refs[:4], refs[4:]
+        take_slots((s0, s1, s2, s3), x)
         both = mine[...] + got[...].astype(F32)
         d_key = rotated(both[:, :size], cos[...], sin[...], back=True)
         first = core_ref[0] == 0
@@ -571,7 +619,7 @@
         dp0[0, :, size:] = jnp.where(first, d_key, both[:, size:]).astype(BF16)
         dp1[0, :, size:] = jnp.where(first, both[:, size:], d_key).astype(BF16)
         total = mm_nt(dp0[0], w0[...]) + mm_nt(dp1[0], w1[...])
-        d_in[...] = total.astype(BF16)
+        put_slots(total, d_in)
         source = x[...].astype(F32)
         term = jnp.sum(total * source * inverse_rms(source), 0, keepdims=True)
 
@@ -589,21 +637,22 @@
     return kernel_call(
         body,
         (2,),
-        [by_rows(width), by_rows(size), by_rows(size), by_rows(2 * size), by_rows(2 * size)]
+        whole_of(inputs)
+        + [by_rows(size), by_rows(size), by_rows(2 * size), by_rows(2 * size)]
         + weights
         + [by_rows(size // 2), by_rows(size // 2)],
-        [by_rows(width), terms, terms, pl.BlockSpec((1, width), lambda i, c: (0, 0))],
-        [
-            jax.ShapeDtypeStruct((rows, width), BF16),
+        whole_of(inputs) + [terms, terms, pl.BlockSpec((1, width), lambda i, c: (0, 0))],
+        [jax.ShapeDtypeStruct(v.shape, BF16) for v in inputs]
+        + [
             jax.ShapeDtypeStruct((1, rows, 2 * size), BF16),
             jax.ShapeDtypeStruct((1, rows, 2 * size), BF16),
             jax.ShapeDtypeStruct((1, width), F32),
         ],
-        [],
+        [pltpu.VMEM((block, width), BF16)],
         8 * rows * width * size,
         8 * width * size + 4 * rows * width,
         prefetch=1,
-    )(core, inputs, *dqs, dkv_mine, dkv_got, *attn, cosine, sine)
+    )(core, *inputs, *dqs, dkv_mine, dkv_got, *attn, cosine, sine)
 
 
 def to_owners(total, ctx_count):
@@ -679,9 +728,6 @@
         product = product.reshape(width, product.shape[2])
         return lax.psum_scatter(product, "fsdp", scatter_dimension=0, tiled=True)
 
-    def joined(pieces):
-        return jnp.concatenate(pieces, 0)
-
     own_input = layer_input.reshape(tokens, width)
     source = own_input.astype(F32)
     upstream = output_grad.reshape(tokens, width).astype(F32)
@@ -707,10 +753,10 @@
             start = (fsdp_place ^ k) * own_gains.shape[1]
             gains = lax.dynamic_update_slice_in_dim(gains, block, start, 1)
         gains = gains.astype(F32)
-        inputs = joined([own_input, slot_1, slot_2, slot_3])
+        inputs = [own_input, slot_1, slot_2, slot_3]
     else:
         attn_own = lax.all_gather(piece, "fsdp", axis=0, tiled=True)
-        inputs = joined(line_gather(own_input, ranks))
+        inputs = line_gather(own_input, ranks)
         gains = lax.all_gather(own_gains, "fsdp", axis=1, tiled=True).astype(F32)
     attn = (attn_own, partner(attn_own))
     g_pre, g_post, g_mid, g_out = [gains[i] for i in range(4)]
@@ -740,24 +786,20 @@
         inputs, gains[:1], attn, cosine, sine, core_word
     )
     attention = (core_word, queries, (kv_own, partner(kv_own)), row_places, key_places, attn)
-    att_own, att_other, branch_parts = attention_forward(*attention)
-    branch_parts = branch_parts.reshape(ranks, tokens, width)
-
-    def own_rows(halves, with_first=(), with_far=()):
-        halves = [v.reshape(2, tokens, width) for v in halves]
+    att_own, att_other, *branch_parts = attention_forward(*attention)
+
+    def own_rows(halves, beside=()):
         parts = [halves[k % 2][k // 2] for k in range(4)]
-        terms, with_first, with_far = four_scatter(parts, ctx_count, with_first, with_far)
-        return sum_of(terms), with_first, with_far
+        terms, _, beside = four_scatter(parts, ctx_count, (), lambda first: beside)
+        return sum_of(terms), beside
 
     def gathered_halves(values, work):
-        slots = line_gather(values, ranks)
-        first = joined([slots[0], slots[2]])
-        done = work(first, 0)
-        last, first, done = together(slots[3], first, done)
-        second = joined([slots[1], last])
-        return (first, second), (done, work(second, 1))
-
-    branch = sum_of(four_scatter(branch_parts.reshape(ranks, tokens, width), ctx_count)[0])
+        slots = four_gather(values, ctx_count)
+        done = work([slots[0], slots[2]], 0)
+        slots[3], done = together(slots[3], done)
+        return [slots[0], slots[2], slots[1], slots[3]], (done, work([slots[1], slots[3]], 1))
+
+    branch = sum_of(four_scatter(branch_parts, ctx_count)[0])
     scale_branch = inverse_rms(branch)
     residual = source + branch * scale_branch * g_post
     scale_mid = inverse_rms(residual)
@@ -765,7 +807,7 @@
         (residual * scale_mid * g_mid).astype(BF16), lambda v, _: gate_up_forward(v, in_all, core_word)
     )
     mixed_1 = down_forward(forward[1][:2], out_all, core_word)
-    mixed_0 = down_forward(forward[0][:2], out_all, core_word, (mixed_1,))
+    mixed_0 = down_forward(forward[0][:2], out_all, core_word, mixed_1)
     hidden_own = [f[0] for f in forward]
     hidden_got = [partner(f[1]) for f in forward]
     mid_got = [partner(v) for v in mids]
@@ -788,27 +830,25 @@
     d_gate_ups, down_product = together(d_gate_ups, down_product)
     down_total = over_sequences(down_product)
     d_mid_1 = gate_up_backward(d_gate_ups[1], in_all, core_word)
-    d_mid_0 = gate_up_backward(d_gate_ups[0], in_all, core_word, (d_mid_1,))
+    d_mid_0 = gate_up_backward(d_gate_ups[0], in_all, core_word, d_mid_1)
     gate_up_product = weight_grad(
         [*mids, *mid_got],
         [v[0] for v in d_gate_ups] + [partner(v[1]) for v in d_gate_ups],
-        d_mid_0,
-    )
-    d_mid, _, (gate_up_product,) = own_rows((d_mid_0, d_mid_1), (), (gate_up_product,))
+        *d_mid_0,
+    )
+    d_mid, (gate_up_product,) = own_rows((d_mid_0, d_mid_1), (gate_up_product,))
     gate_up_total = over_sequences(gate_up_product)
     grad_mid_gain = jnp.sum(d_mid * residual * scale_mid, 0)
     d_residual = upstream + norm_backward(residual, scale_mid, d_mid * g_mid)
     grad_post_gain = jnp.sum(d_residual * branch * scale_branch, 0)
-    d_branches = joined(
-        line_gather(
-            norm_backward(branch, scale_branch, d_residual * g_post).astype(BF16), ranks
-        )
+    d_branches = four_gather(
+        norm_backward(branch, scale_branch, d_residual * g_post).astype(BF16), ctx_count
     )
 
     d_branches, down_total = together(d_branches, down_total)
     down = to_owners(down_total, ctx_count)
     *d_queries, dkv_own, dkv_other = attention_backward(d_branches, *attention, cosine, sine)
-    d_in, dproj_own, dproj_other, grad_pre_gain = qkv_backward(
+    *d_in, dproj_own, dproj_other, grad_pre_gain = qkv_backward(
         inputs, d_queries, dkv_own, partner(dkv_other), attn, cosine, sine, core_word
     )
 
@@ -816,27 +856,28 @@
     gain_terms = gain_terms.reshape(ctx_count, fsdp_count, shard_rows, 4)
     gain_terms = gain_terms.transpose(1, 0, 2, 3).reshape(fsdp_count, -1, 4)
     out_product = weight_grad(
-        [d_branches, partner(d_branches)], [att_own[None], partner(att_other)[None]]
+        [*d_branches, *[partner(v) for v in d_branches]], [att_own[None], partner(att_other)[None]]
     )
     product = weight_grad([normed_in, partner(normed_in)], [dproj_own, partner(dproj_other)])
     product = jnp.concatenate([product, out_product, gain_terms.astype(BF16)], 2)
-    d_in = d_in.reshape(ranks, tokens, width)
-    d_in, (down, product), (gate_up_total,) = four_scatter(
-        d_in, ctx_count, (down, product), (gate_up_total,)
+
+    def part(product, k):
+        return lax.dynamic_index_in_dim(product, fsdp_place ^ k, 0, keepdims=False)
+
+    def corners_of(first):
+        return gate_up_total, corner_scatter(part(first[1], 3), 4) if fsdp_count == 4 else ()
+
+    d_in, (down, product), (gate_up_total, corners) = four_scatter(
+        d_in, ctx_count, (down, product), corners_of
     )
     gate_up_terms = to_owners(gate_up_total, ctx_count)
     if fsdp_count == 4:
-        parts = [
-            lax.dynamic_index_in_dim(product, fsdp_place ^ k, 0, keepdims=False).astype(F32)
-            for k in range(4)
-        ]
-        corners = corner_scatter(parts[3], 4)
+        parts = [part(product, k).astype(F32) for k in range(4)]
         attn_total = rows_scatter(parts, corners, 4).astype(BF16)
     else:
         attn_total = over_sequences(product)
     gate_up_terms, attn_total = together(gate_up_terms, attn_total)
     attn_terms = to_owners(attn_total, ctx_count)
-    d_in, attn_terms = together(d_in, attn_terms)
     d_in = sum_of(d_in)
     d_source = d_residual + norm_backward(source, inverse_rms(source), d_in * g_pre)
 

time: 659 us -> 645 us (0.979)
  local copies, waits for them, and re-layouts: 59.6 us -> 44.5 us
  starting transfers between devices: 79.3 us -> 89 us
  other arithmetic: 50.5 us -> 42.2 us
  waiting for transfers between devices: 278 us -> 271 us
    ppermute x50 -> x57, waiting for transfers between devices: 257 us -> 234 us  [swap(): return lax.ppermute(values, axis, [(i, i ^ distance) for i in range(count)])]
    all_to_all x3, waiting for transfers between devices: 20.6 us -> 36.9 us  [to_owners(): return lax.all_to_all(total, 'ctx', split_axis=0, concat_axis=0, tiled=True)]
    slice x8 -> x0, local copies, waits for them, and re-layouts: 9.42 us -> none  [the longest x6 4.75 us: own_rows(): parts = [halves[k % 2][k // 2] for k in range(4)]]
    ppermute x50 -> x57, starting transfers between devices: 57.3 us -> 66.8 us  [swap(): return lax.ppermute(values, axis, [(i, i ^ distance) for i in range(count)])]
    concatenate x4 -> x0, other arithmetic: 9.31 us -> none  [joined(): return jnp.concatenate(pieces, 0)]
    unnamed x96 -> x130, local copies, waits for them, and re-layouts: 13.2 us -> 12.9 us
  transfers between devices with their start and end apart: 57 -> 64, of which waited for: 26 -> 30; matrix products, arithmetic and copies ran while one was open for 14% -> 11% of each run, Pallas kernels for 23% -> 24%
where the time goes in v4:
time: 645 us; the launch traced here: 636 us
  waiting for transfers between devices  271 us (42%)
  Pallas kernels  174 us (27%)
  starting transfers between devices  89 us (14%)
  local copies, waits for them, and re-layouts  44.5 us (7%)
  other arithmetic  42.2 us (7%)
  between operations  14.8 us (2%)
    ppermute x57, waiting for transfers between devices, swap(): return lax.ppermute(values, axis, [(i, i ^ distance) for i in range(count)])  234 us
    ppermute x57, starting transfers between devices, swap(): return lax.ppermute(values, axis, [(i, i ^ distance) for i in range(count)])  66.8 us
    pallas_call x4, Pallas kernels, weight_grad_kernel(): kernel_call(body, (halves, groups, steps), [pl.BlockSpec((n, part), lambd...  40.4 us
    all_to_all x3, waiting for transfers between devices, to_owners(): return lax.all_to_all(total, 'ctx', split_axis=0, concat_axis=0, tiled=True)  36.9 us
    pallas_call x2, Pallas kernels, gate_up_forward(): kernel_call(body, (2, steps), whole_of(values) + [pl.BlockSpec((1, width,...  29.1 us
    pallas_call x2, Pallas kernels, gate_up_backward(): kernel_call(body, (width // tile,), [whole, whole, pl.BlockSpec((1, tile,...  25.8 us
    pallas_call x2, Pallas kernels, down_backward(): kernel_call(body, (2, steps), whole_of(d_mixed) + [saved, saved, pl.Block...  22.3 us
    all_to_all x3, starting transfers between devices, to_owners(): return lax.all_to_all(total, 'ctx', split_axis=0, concat_axis=0, tiled=True)  22 us
  transfers between devices with their start and end apart: 64, of which 30 were waited for; matrix products, arithmetic and copies ran while one was open for 11% of the time, Pallas kernels for 24%

profile of v4, /device:TPU:13, one launch (start us, length us, event | category | flops | bytes accessed | tf_op | source)
XLA Modules:
  0.0 636.0 jit_solution(10618394042802055784)
XLA Ops:
  8.5 2.3 constant_dynamic-slice_fusion.2
  12.6 2.5 constant_dynamic-slice_fusion
  16.7 2.3 collective-permute-start.2
  19.1 25.4 %collective-permute-done.2.s2 = bf16[128,2304]{1,0:T(8,128)(2,1)} collective-permute-done((bf16[128,2304]{1,0:T(8,128)(2,1)S(1)}, bf16[128,2304]{1,0:T(8,128)(2,1)}, u32[]{:S(2)}, u32[]{:S(2)}) %collective-permute-start.2) | collective-permute-done | bytes 589856 | tf_op jit(solution)/shard_map/ppermute | solution.py:76
  45.0 2.2 collective-permute-done.1
  54.5 15.0 %collective-permute-done.7 = bf16[4,576]{1,0:T(4,128)(2,1)S(1)} collective-permute-done((bf16[4,576]{1,0:T(4,128)(2,1)S(1)}, bf16[4,576]{1,0:T(4,128)(2,1)S(1)}, u32[]{:S(2)}, u32[]{:S(2)}) %collective-permute-start.7) | collective-permute-done | bytes 4640 | tf_op jit(solution)/shard_map/ppermute | solution.py:76
  70.7 2.3 collective-permute-done.9
  75.2 6.8 %collective-permute-start.10 = (bf16[2304,768]{1,0:T(8,128)(2,1)S(1)}, bf16[2304,768]{1,0:T(8,128)(2,1)}, u32[]{:S(2)}, u32[]{:S(2)}) collective-permute-start(bf16[2304,768]{1,0:T(8,128)(2,1)S(1)} %constant_dynamic-update-slice_fusion.w0), channel_id=1, source_target_pairs={{0,4},{4,0},{8,12},{12,8},{16,20},{20,16},{24,28},{28,24},{1,5},{5... | collective-permute-start | bytes 10616840 | tf_op jit(solution)/shard_map/ppermute | solution.py:76
  93.0 7.6 %shard_map.109 = (bf16[512,2304]{1,0:T(8,128)(2,1)}, bf16[512,256]{1,0:T(8,128)(2,1)}, bf16[512,256]{1,0:T(8,128)(2,1)}, bf16[512,512]{1,0:T(8,128)(2,1)}) custom-call(s32[1]{0:T(128)} %bitcast.1.core_ref, bf16[128,2304]{1,0:T(8,128)(2,1)} %bitcast.99, bf16[128,2304]{1,0:T(8,128)(2,1)} %copy-done.13, bf16[128,2304]{1,0:T(8,128)(2,1)} %collective-permute-done.2.s2, ...), custom_call_target="tpu_custom_call" | custom-call | flops 2415919104 | bytes 9437184 | tf_op jit(solution)/shard_map/pallas_call | solution.py:446
  103.7 8.7 %shard_map.110 = (bf16[512,256]{1,0:T(8,128)(2,1)}, bf16[512,256]{1,0:T(8,128)(2,1)}, bf16[128,2304]{1,0:T(8,128)(2,1)}, bf16[128,2304]{1,0:T(8,128)(2,1)}, bf16...) custom-call(s32[1]{0:T(128)} %bitcast.1.core_ref, bf16[512,256]{1,0:T(8,128)(2,1)} %get-tuple-element.133.q0, ...), custom_call_target="tpu_custom_call" | custom-call | flops 2281701376 | bytes 4718592 | tf_op jit(solution)/shard_map/pallas_call | solution.py:528
  112.8 14.7 %collective-permute-done.12 = bf16[128,2304]{1,0:T(8,128)(2,1)S(1)} collective-permute-done((bf16[128,2304]{1,0:T(8,128)(2,1)}, bf16[128,2304]{1,0:T(8,128)(2,1)S(1)}, u32[]{:S(2)}, u32[]{:S(2)}) %collective-permute-start.12) | collective-permute-done | bytes 589856 | tf_op jit(solution)/shard_map/ppermute | solution.py:76
  129.1 2.4 collective-permute-start.14
  132.1 19.3 %collective-permute-done.13 = bf16[128,2304]{1,0:T(8,128)(2,1)S(1)} collective-permute-done((bf16[128,2304]{1,0:T(8,128)(2,1)}, bf16[128,2304]{1,0:T(8,128)(2,1)S(1)}, u32[]{:S(2)}, u32[]{:S(2)}) %collective-permute-start.13) | collective-permute-done | bytes 589856 | tf_op jit(solution)/shard_map/ppermute | solution.py:76
  151.4 4.2 collective-permute-done.14
  157.9 3.2 collective-permute-start.15
  161.0 23.5 %collective-permute-done.15.refs_1_ = bf16[128,2304]{1,0:T(8,128)(2,1)S(1)} collective-permute-done((bf16[128,2304]{1,0:T(8,128)(2,1)S(1)}, bf16[128,2304]{1,0:T(8,128)(2,1)S(1)}, u32[]{:S(2)}, u32[]{:S(2)}) %collective-permute-start.15) | collective-permute-done | bytes 589856 | tf_op jit(solution)/shard_map/ppermute | solution.py:76
  185.6 14.7 %shard_map.111 = (bf16[1,256,1152]{2,1,0:T(8,128)(2,1)}, bf16[1,256,1152]{2,1,0:T(8,128)(2,1)}, f32[2,256,1152]{2,1,0:T(8,128)}, f32[2,256,1152]{2,1,0:T(8,128)}) custom-call(s32[1]{0:T(128)} %bitcast.1.core_ref, bf16[128,2304]{1,0:T(8,128)(2,1)} %copy-done.23, bf16[128,2304]{1,0:T(8,128)(2,1)} %copy-done.39, bf16[2,2304,2304]{2,1,0:T(8,128)(2,1)} %bitcast.85, ...), custom_call_target="tpu_custom_call" | custom-call | flops 5435817984 | bytes 27131904 | tf_op jit(solution)/shard_map/pallas_call | solution.py:251
  200.3 14.4 %shard_map.112 = (bf16[1,256,1152]{2,1,0:T(8,128)(2,1)}, bf16[1,256,1152]{2,1,0:T(8,128)(2,1)}, f32[2,256,1152]{2,1,0:T(8,128)}, f32[2,256,1152]{2,1,0:T(8,128)}) custom-call(s32[1]{0:T(128)} %bitcast.1.core_ref, bf16[128,2304]{1,0:T(8,128)(2,1)} %copy-done.40, bf16[128,2304]{1,0:T(8,128)(2,1)} %collective-permute-done.17.refs_1_.refs_3_, ...), custom_call_target="tpu_custom_call" | custom-call | flops 5435817984 | bytes 27131904 | tf_op jit(solution)/shard_map/pallas_call | solution.py:251
  214.7 7.6 %shard_map.113 = (bf16[128,2304]{1,0:T(8,128)(2,1)}, bf16[128,2304]{1,0:T(8,128)(2,1)}) custom-call(s32[1]{0:T(128)} %bitcast.1.core_ref, bf16[1,256,1152]{2,1,0:T(8,128)(2,1)} %get-tuple-element.181.h0.refs_9_, bf16[1,256,1152]{2,1,0:T(8,128)(2,1)} %get-tuple-element.156.h1, bf16[2,2304,1152]{2,1,0:T(8,128)(2,1)} %bitcast.93, bf16[2,2304,1152]{2,1,0:T(8,128)(2,1)} %bitcast.94), custom_call_target="tpu_custom_call" | custom-call | flops 2717908992 | bytes 11796480 | tf_op jit(solution)/shard_map/pallas_call | solution.py:280
  223.6 7.9 %shard_map.114 = (bf16[128,2304]{1,0:T(8,128)(2,1)}, bf16[128,2304]{1,0:T(8,128)(2,1)}) custom-call(s32[1]{0:T(128)} %bitcast.1.core_ref, bf16[1,256,1152]{2,1,0:T(8,128)(2,1)} %get-tuple-element.180.h0.refs_8_, bf16[1,256,1152]{2,1,0:T(8,128)(2,1)} %get-tuple-element.152.h1, bf16[2,2304,1152]{2,1,0:T(8,128)(2,1)} %bitcast.95, ...), custom_call_target="tpu_custom_call" | custom-call | flops 2717908992 | bytes 11796480 | tf_op jit(solution)/shard_map/pallas_call | solution.py:280
  231.6 4.0 collective-permute-done.18
  238.1 2.9 collective-permute-start.20
  240.9 3.5 collective-permute-start.23
  245.0 13.9 %collective-permute-done.19 = bf16[128,2304]{1,0:T(8,128)(2,1)S(1)} collective-permute-done((bf16[128,2304]{1,0:T(8,128)(2,1)S(1)}, bf16[128,2304]{1,0:T(8,128)(2,1)S(1)}, u32[]{:S(2)}, u32[]{:S(2)}) %collective-permute-start.19) | collective-permute-done | bytes 589856 | tf_op jit(solution)/shard_map/ppermute | solution.py:76
  258.9 3.6 collective-permute-start.21
  262.9 4.3 collective-permute-start.22
  272.9 3.1 collective-permute-start.27
  276.0 23.7 %collective-permute-done.27.refs_1_ = bf16[128,2304]{1,0:T(8,128)(2,1)S(1)} collective-permute-done((bf16[128,2304]{1,0:T(8,128)(2,1)S(1)}, bf16[128,2304]{1,0:T(8,128)(2,1)S(1)}, u32[]{:S(2)}, u32[]{:S(2)}) %collective-permute-start.27) | collective-permute-done | bytes 589856 | tf_op jit(solution)/shard_map/ppermute | solution.py:76
  300.6 2.1 collective-permute-start.29
  304.5 11.2 %shard_map.115 = (bf16[2,256,1152]{2,1,0:T(8,128)(2,1)}, bf16[2,256,1152]{2,1,0:T(8,128)(2,1)}) custom-call(s32[1]{0:T(128)} %bitcast.1.core_ref, bf16[128,2304]{1,0:T(8,128)(2,1)} %copy-done.17, bf16[128,2304]{1,0:T(8,128)(2,1)} %copy-done.36, f32[2,256,1152]{2,1,0:T(8,128)} %get-tuple-element.168.refs_2_, f32[2,256,1152]{2,1,0:T(8,128)} %get-tuple-element.169.refs_3_, ...), custom_call_target="tpu_custom_call" | custom-call | flops 2717908992 | bytes 17694720 | tf_op jit(solution)/shard_map/pallas_call | solution.py:328
  317.1 11.1 %shard_map.116 = (bf16[2,256,1152]{2,1,0:T(8,128)(2,1)}, bf16[2,256,1152]{2,1,0:T(8,128)(2,1)}) custom-call(s32[1]{0:T(128)} %bitcast.1.core_ref, bf16[128,2304]{1,0:T(8,128)(2,1)} %collective-permute-done.28.refs_0_.refs_2_, bf16[128,2304]{1,0:T(8,128)(2,1)} %collective-permute-done.29.refs_1_.refs_3_, f32[2,256,1152]{2,1,0:T(8,128)} %get-tuple-element.176.refs_2_, ...), custom_call_target="tpu_custom_call" | custom-call | flops 2717908992 | bytes 17694720 | tf_op jit(solution)/shard_map/pallas_call | solution.py:328
  328.2 10.7 %shard_map.117 = bf16[4,576,1152]{2,1,0:T(8,128)(2,1)} custom-call(bf16[128,2304]{1,0:T(8,128)(2,1)} %copy-done.17, bf16[128,2304]{1,0:T(8,128)(2,1)} %copy-done.36, bf16[128,2304]{1,0:T(8,128)(2,1)} %collective-permute-done.28.refs_0_.refs_2_, bf16[128,2304]{1,0:T(8,128)(2,1)} %collective-permute-done.29.refs_1_.refs_3_, ...), custom_call_target="tpu_custom_call" | custom-call | flops 5435817984 | bytes 19464192 | tf_op jit(solution)/shard_map/pallas_call | solution.py:403
  339.0 13.4 %shard_map.118 = (bf16[128,2304]{1,0:T(8,128)(2,1)}, bf16[128,2304]{1,0:T(8,128)(2,1)}) custom-call(s32[1]{0:T(128)} %bitcast.1.core_ref, bf16[2,256,1152]{2,1,0:T(8,128)(2,1)} %get-tuple-element.186.d0.refs_9_, bf16[2,256,1152]{2,1,0:T(8,128)(2,1)} %get-tuple-element.187.d1, bf16[2,2304,2304]{2,1,0:T(8,128)(2,1)} %bitcast.89, bf16[2,2304,2304]{2,1,0:T(8,128)(2,1)} %bitcast.90), custom_call_target="tpu_custom_call" | custom-call | flops 5435817984 | bytes 23592960 | tf_op jit(solution)/shard_map/pallas_call | solution.py:354
  353.5 12.4 %shard_map.119 = (bf16[128,2304]{1,0:T(8,128)(2,1)}, bf16[128,2304]{1,0:T(8,128)(2,1)}) custom-call(s32[1]{0:T(128)} %bitcast.1.core_ref, bf16[2,256,1152]{2,1,0:T(8,128)(2,1)} %get-tuple-element.184.d0.refs_8_, bf16[2,256,1152]{2,1,0:T(8,128)(2,1)} %get-tuple-element.185.d1, bf16[2,2304,2304]{2,1,0:T(8,128)(2,1)} %bitcast.91, ...), custom_call_target="tpu_custom_call" | custom-call | flops 5435817984 | bytes 23592960 | tf_op jit(solution)/shard_map/pallas_call | solution.py:354
  371.8 18.7 %shard_map.120 = bf16[4,576,2304]{2,1,0:T(8,128)(2,1)} custom-call(bf16[128,2304]{1,0:T(8,128)(2,1)} %copy-done.23, bf16[128,2304]{1,0:T(8,128)(2,1)} %copy-done.39, bf16[128,2304]{1,0:T(8,128)(2,1)} %copy-done.40, bf16[128,2304]{1,0:T(8,128)(2,1)} %collective-permute-done.17.refs_1_.refs_3_, bf16[128,2304]{1,0:T(8,128)(2,1)} %copy-done.58, ...), custom_call_target="tpu_custom_call" | custom-call | flops 10871635968 | bytes 29491200 | tf_op jit(solution)/shard_map/pallas_call | solution.py:403
  390.5 5.7 collective-permute-done.36
  398.2 2.3 multiply_reduce_fusion
  400.5 2.7 multiply_reduce_fusion.1
  403.7 3.1 collective-permute-start.39
  406.8 24.7 %collective-permute-done.39.s2.refs_2_ = bf16[128,2304]{1,0:T(8,128)(2,1)S(1)} collective-permute-done((bf16[128,2304]{1,0:T(8,128)(2,1)S(1)}, bf16[128,2304]{1,0:T(8,128)(2,1)S(1)}, u32[]{:S(2)}, u32[]{:S(2)}) %collective-permute-start.39) | collective-permute-done | bytes 589856 | tf_op jit(solution)/shard_map/ppermute | solution.py:76
  431.5 3.0 collective-permute-start.41
  435.5 12.2 %collective-permute-done.41.s3.refs_3_ = bf16[128,2304]{1,0:T(8,128)(2,1)} collective-permute-done((bf16[128,2304]{1,0:T(8,128)(2,1)S(1)}, bf16[128,2304]{1,0:T(8,128)(2,1)}, u32[]{:S(2)}, u32[]{:S(2)}) %collective-permute-start.41) | collective-permute-done | bytes 589856 | tf_op jit(solution)/shard_map/ppermute | solution.py:76
  447.7 7.0 %all-to-all-start = ((bf16[8,72,1152]{2,1,0:T(8,128)(2,1)}), bf16[8,72,1152]{2,1,0:T(8,128)(2,1)}, u32[]{:S(2)}, u32[]{:S(2)}) async-start(bf16[8,72,1152]{2,1,0:T(8,128)(2,1)} %bitcast.110), calls=%async_computation.1 | async-start | bytes 2654208 | tf_op jit(solution)/shard_map/all_to_all | solution.py:660
  454.7 12.6 %shard_map.121 = (bf16[512,256]{1,0:T(8,128)(2,1)}, bf16[512,256]{1,0:T(8,128)(2,1)}, f32[512,512]{1,0:T(8,128)}, bf16[512,512]{1,0:T(8,128)(2,1)}) custom-call(s32[1]{0:T(128)} %bitcast.1.core_ref, bf16[512,256]{1,0:T(8,128)(2,1)} %get-tuple-element.133.q0, bf16[512,256]{1,0:T(8,128)(2,1)} %get-tuple-element.134.q1, ...), custom_call_target="tpu_custom_call" | custom-call | flops 3892314112 | bytes 4718592 | tf_op jit(solution)/shard_map/pallas_call | solution.py:589
  468.4 2.2 collective-permute-done.50
  472.1 9.6 %shard_map.122 = (bf16[128,2304]{1,0:T(8,128)(2,1)}, bf16[128,2304]{1,0:T(8,128)(2,1)}, bf16[128,2304]{1,0:T(8,128)(2,1)}, bf16[128,2304]{1,0:T(8,128)(2,1)}, bf...) custom-call(s32[1]{0:T(128)} %bitcast.1.core_ref, bf16[128,2304]{1,0:T(8,128)(2,1)} %bitcast.100, ...), custom_call_target="tpu_custom_call" | custom-call | flops 2415919104 | bytes 9437184 | tf_op jit(solution)/shard_map/pallas_call | solution.py:637
  485.2 5.0 shard_map.124
  490.2 6.0 shard_map.123
  496.3 3.5 pad_maximum_fusion
  502.5 2.2 collective-permute-start.52
  504.6 2.5 dynamic-slice_bitcast_fusion.3
  508.6 10.7 %collective-permute-done.53 = bf16[288,772]{1,0:T(8,128)(2,1)S(1)} collective-permute-done((bf16[288,772]{1,0:T(8,128)(2,1)S(1)}, bf16[288,772]{1,0:T(8,128)(2,1)S(1)}, u32[]{:S(2)}, u32[]{:S(2)}) %collective-permute-start.53) | collective-permute-done | bytes 444704 | tf_op jit(solution)/shard_map/ppermute | solution.py:76
  519.5 6.3 collective-permute-done.51
  525.8 3.4 collective-permute-done.52
  529.2 7.9 %all-to-all-start.1 = ((bf16[8,72,2304]{2,1,0:T(8,128)(2,1)}), bf16[8,72,2304]{2,1,0:T(8,128)(2,1)}, u32[]{:S(2)}, u32[]{:S(2)}) async-start(bf16[8,72,2304]{2,1,0:T(8,128)(2,1)} %bitcast.107), calls=%async_computation.3 | async-start | bytes 5308416 | tf_op jit(solution)/shard_map/all_to_all | solution.py:660
  540.4 2.2 fusion.18
  550.5 2.7 fusion.13
  553.2 14.6 %collective-permute-done.56 = bf16[576,772]{0,1:T(8,128)(2,1)} collective-permute-done((bf16[576,772]{0,1:T(8,128)(2,1)}, bf16[576,772]{0,1:T(8,128)(2,1)}, u32[]{:S(2)}, u32[]{:S(2)}) %collective-permute-start.56) | collective-permute-done | bytes 889376 | tf_op jit(solution)/shard_map/ppermute | solution.py:76
  572.7 2.6 fusion.1
  575.2 19.3 %all-to-all-done.1 = bf16[8,72,2304]{2,1,0:T(8,128)(2,1)} async-done(((bf16[8,72,2304]{2,1,0:T(8,128)(2,1)}), bf16[8,72,2304]{2,1,0:T(8,128)(2,1)}, u32[]{:S(2)}, u32[]{:S(2)}) %all-to-all-start.1) | async-done | bytes 2654240 | tf_op jit(solution)/shard_map/all_to_all | solution.py:660
  594.5 7.1 %all-to-all-start.2 = ((bf16[8,72,772]{2,1,0:T(8,128)(2,1)}), bf16[8,72,772]{2,1,0:T(8,128)(2,1)S(1)}, u32[]{:S(2)}, u32[]{:S(2)}) async-start(bf16[8,72,772]{2,1,0:T(8,128)(2,1)} %bitcast.28), calls=%async_computation.4 | async-start | bytes 2064384 | tf_op jit(solution)/shard_map/all_to_all | solution.py:660
  603.9 2.8 maximum_convert_fusion
  606.7 17.6 %all-to-all-done.2.t = bf16[8,72,772]{2,1,0:T(8,128)(2,1)S(1)} async-done(((bf16[8,72,772]{2,1,0:T(8,128)(2,1)}), bf16[8,72,772]{2,1,0:T(8,128)(2,1)S(1)}, u32[]{:S(2)}, u32[]{:S(2)}) %all-to-all-start.2) | async-done | bytes 889376 | tf_op jit(solution)/shard_map/all_to_all | solution.py:660
  625.3 2.5 shard_map.125
  (292 shorter events, 91.6 us)
Async XLA Ops:
  7.2 178.3 %all-gather.3.cloned.1.call-start = ((), (), s32[]{:S(2)}) async-start(), calls=%async_computation.5 | async-start | bytes 23887872 | tf_op jit(solution)/shard_map/all_gather | solution.py:722
  12.5 202.2 %all-gather.5.cloned.1.call-start = ((), (), s32[]{:S(2)}) async-start(), calls=%async_computation.6 | async-start | bytes 11943936 | tf_op jit(solution)/shard_map/all_gather | solution.py:722
  15.1 432.6 %reduce-scatter.3.cloned.1.call-start = ((), (), s32[]{:S(2)}) async-start(), calls=%async_computation.7 | async-start | bytes 6635520 | tf_op jit(solution)/shard_map/reduce_scatter | solution.py:729
  15.1 29.8 %collective-permute-start = (bf16[576,768]{1,0:T(8,128)(2,1)S(1)}, bf16[576,768]{1,0:T(8,128)(2,1)S(1)}, u32[]{:S(2)}, u32[]{:S(2)}) collective-permute-start(bf16[576,768]{1,0:T(8,128)(2,1)S(1)} %pad_maximum_fusion.4), channel_id=1, source_target_pairs={{0,1},{1,0},{2,3},{3,2},{4,5},{5,4},{6,7},{7,6},{8,9},{9,8},{10,11... | collective-permute-start | bytes 2654216 | tf_op jit(solution)/shard_map/ppermute | solution.py:76
  16.4 30.8 %collective-permute-start.1 = (bf16[576,768]{1,0:T(8,128)(2,1)S(1)}, bf16[576,768]{1,0:T(8,128)(2,1)S(1)}, u32[]{:S(2)}, u32[]{:S(2)}) collective-permute-start(bf16[576,768]{1,0:T(8,128)(2,1)S(1)} %pad_maximum_fusion.4), channel_id=1, source_target_pairs={{0,2},{1,3},{2,0},{3,1},{4,6},{5,7},{6,4},{7,5},{8,10},{9,11},{10,... | collective-permute-start | bytes 2654216 | tf_op jit(solution)/shard_map/ppermute | solution.py:76
  16.7 27.9 %collective-permute-start.2 = (bf16[128,2304]{1,0:T(8,128)(2,1)S(1)}, bf16[128,2304]{1,0:T(8,128)(2,1)}, u32[]{:S(2)}, u32[]{:S(2)}) collective-permute-start(bf16[128,2304]{1,0:T(8,128)(2,1)S(1)} %bitcast.101), channel_id=1, source_target_pairs={{0,16},{4,20},{8,24},{12,28},{16,0},{20,4},{24,8},{28,12},{1,17},{... | collective-permute-start | bytes 1769480 | tf_op jit(solution)/shard_map/ppermute | solution.py:76
  19.0 25.6 %collective-permute-start.3 = (bf16[128,2304]{1,0:T(8,128)(2,1)S(1)}, bf16[128,2304]{1,0:T(8,128)(2,1)S(1)}, u32[]{:S(2)}, u32[]{:S(2)}) collective-permute-start(bf16[128,2304]{1,0:T(8,128)(2,1)S(1)} %bitcast.102), channel_id=1, source_target_pairs={{0,8},{4,12},{8,0},{12,4},{16,24},{20,28},{24,16},{28,20},{1,9},{5... | collective-permute-start | bytes 1769480 | tf_op jit(solution)/shard_map/ppermute | solution.py:76
  47.2 25.8 %collective-permute-start.6 = (bf16[128,2304]{1,0:T(8,128)(2,1)}, bf16[128,2304]{1,0:T(8,128)(2,1)}, u32[]{:S(2)}, u32[]{:S(2)}) collective-permute-start(bf16[128,2304]{1,0:T(8,128)(2,1)} %collective-permute-done.2.s2), channel_id=1, source_target_pairs={{0,8},{4,12},{8,0},{12,4},{16,24},{20,28},{24,16},{28,20},{1,9},{5... | collective-permute-start | bytes 1769480 | tf_op jit(solution)/shard_map/ppermute | solution.py:76
  48.3 24.7 %collective-permute-start.4 = (bf16[288,768]{1,0:T(8,128)(2,1)}, bf16[288,768]{1,0:T(8,128)(2,1)}, u32[]{:S(2)}, u32[]{:S(2)}) collective-permute-start(bf16[288,768]{1,0:T(8,128)(2,1)} %slice.69), channel_id=1, source_target_pairs={{0,2},{1,3},{2,0},{3,1},{4,6},{5,7},{6,4},{7,5},{8,10},{9,11},{10,... | collective-permute-start | bytes 1327112 | tf_op jit(solution)/shard_map/ppermute | solution.py:76
  49.1 23.9 %collective-permute-start.5 = (bf16[288,768]{1,0:T(8,128)(2,1)}, bf16[288,768]{1,0:T(8,128)(2,1)}, u32[]{:S(2)}, u32[]{:S(2)}) collective-permute-start(bf16[288,768]{1,0:T(8,128)(2,1)} %slice.70), channel_id=1, source_target_pairs={{0,1},{1,0},{2,3},{3,2},{4,5},{5,4},{6,7},{7,6},{8,9},{9,8},{10,11... | collective-permute-start | bytes 1327112 | tf_op jit(solution)/shard_map/ppermute | solution.py:76
  49.4 20.0 %collective-permute-start.7 = (bf16[4,576]{1,0:T(4,128)(2,1)S(1)}, bf16[4,576]{1,0:T(4,128)(2,1)S(1)}, u32[]{:S(2)}, u32[]{:S(2)}) collective-permute-start(bf16[4,576]{1,0:T(4,128)(2,1)S(1)} %bitcast.116), channel_id=1, source_target_pairs={{0,1},{1,0},{2,3},{3,2},{4,5},{5,4},{6,7},{7,6},{8,9},{9,8},{10,11... | collective-permute-start | bytes 13832 | tf_op jit(solution)/shard_map/ppermute | solution.py:76
  50.6 20.1 %collective-permute-start.8 = (bf16[4,576]{1,0:T(4,128)(2,1)S(1)}, bf16[4,576]{1,0:T(4,128)(2,1)}, u32[]{:S(2)}, u32[]{:S(2)}) collective-permute-start(bf16[4,576]{1,0:T(4,128)(2,1)S(1)} %bitcast.117), channel_id=1, source_target_pairs={{0,2},{1,3},{2,0},{3,1},{4,6},{5,7},{6,4},{7,5},{8,10},{9,11},{10,... | collective-permute-start | bytes 13832 | tf_op jit(solution)/shard_map/ppermute | solution.py:76
  69.5 3.5 collective-permute-start.9
  75.2 17.9 %collective-permute-start.10 = (bf16[2304,768]{1,0:T(8,128)(2,1)S(1)}, bf16[2304,768]{1,0:T(8,128)(2,1)}, u32[]{:S(2)}, u32[]{:S(2)}) collective-permute-start(bf16[2304,768]{1,0:T(8,128)(2,1)S(1)} %constant_dynamic-update-slice_fusion.w0), channel_id=1, source_target_pairs={{0,4},{4,0},{8,12},{12,8},{16,20},{20,16},{24,28},{28,24},{1,5},{5... | collective-permute-start | bytes 10616840 | tf_op jit(solution)/shard_map/ppermute | solution.py:76
  100.6 2.2 collective-permute-start.11
  112.4 15.2 %collective-permute-start.12 = (bf16[128,2304]{1,0:T(8,128)(2,1)}, bf16[128,2304]{1,0:T(8,128)(2,1)S(1)}, u32[]{:S(2)}, u32[]{:S(2)}) collective-permute-start(bf16[128,2304]{1,0:T(8,128)(2,1)} %get-tuple-element.139), channel_id=1, source_target_pairs={{0,8},{4,12},{8,0},{12,4},{16,24},{20,28},{24,16},{28,20},{1,9},{5... | collective-permute-start | bytes 1769480 | tf_op jit(solution)/shard_map/ppermute | solution.py:76
  127.6 23.9 %collective-permute-start.13 = (bf16[128,2304]{1,0:T(8,128)(2,1)}, bf16[128,2304]{1,0:T(8,128)(2,1)S(1)}, u32[]{:S(2)}, u32[]{:S(2)}) collective-permute-start(bf16[128,2304]{1,0:T(8,128)(2,1)} %get-tuple-element.140), channel_id=1, source_target_pairs={{0,8},{4,12},{8,0},{12,4},{16,24},{20,28},{24,16},{28,20},{1,9},{5... | collective-permute-start | bytes 1769480 | tf_op jit(solution)/shard_map/ppermute | solution.py:76
  129.1 26.6 %collective-permute-start.14 = (bf16[128,2304]{1,0:T(8,128)(2,1)S(1)}, bf16[128,2304]{1,0:T(8,128)(2,1)S(1)}, u32[]{:S(2)}, u32[]{:S(2)}) collective-permute-start(bf16[128,2304]{1,0:T(8,128)(2,1)S(1)} %add_convert_fusion.4), channel_id=1, source_target_pairs={{0,16},{4,20},{8,24},{12,28},{16,0},{20,4},{24,8},{28,12},{1,17},{... | collective-permute-start | bytes 1769480 | tf_op jit(solution)/shard_map/ppermute | solution.py:76
  157.9 26.7 %collective-permute-start.15 = (bf16[128,2304]{1,0:T(8,128)(2,1)S(1)}, bf16[128,2304]{1,0:T(8,128)(2,1)S(1)}, u32[]{:S(2)}, u32[]{:S(2)}) collective-permute-start(bf16[128,2304]{1,0:T(8,128)(2,1)S(1)} %multiply_convert_fusion.1.refs_0_), channel_id=1, source_target_pairs={{0,16},{4,20},{8,24},{12,28},{16,0},{20,4},{24,8},{28,12},{1,17},{... | collective-permute-start | bytes 1769480 | tf_op jit(solution)/shard_map/ppermute | solution.py:76
  161.0 23.5 %collective-permute-start.16 = (bf16[128,2304]{1,0:T(8,128)(2,1)S(1)}, bf16[128,2304]{1,0:T(8,128)(2,1)S(1)}, u32[]{:S(2)}, u32[]{:S(2)}) collective-permute-start(bf16[128,2304]{1,0:T(8,128)(2,1)S(1)} %multiply_convert_fusion.1.refs_0_), channel_id=1, source_target_pairs={{0,8},{4,12},{8,0},{12,4},{16,24},{20,28},{24,16},{28,20},{1,9},{5... | collective-permute-start | bytes 1769480 | tf_op jit(solution)/shard_map/ppermute | solution.py:76
  185.4 14.9 %collective-permute-start.17 = (bf16[128,2304]{1,0:T(8,128)(2,1)S(1)}, bf16[128,2304]{1,0:T(8,128)(2,1)}, u32[]{:S(2)}, u32[]{:S(2)}) collective-permute-start(bf16[128,2304]{1,0:T(8,128)(2,1)S(1)} %collective-permute-done.15.refs_1_), channel_id=1, source_target_pairs={{0,8},{4,12},{8,0},{12,4},{16,24},{20,28},{24,16},{28,20},{1,9},{5... | collective-permute-start | bytes 1769480 | tf_op jit(solution)/shard_map/ppermute | solution.py:76
  222.3 13.2 %collective-permute-start.18 = (bf16[128,2304]{1,0:T(8,128)(2,1)}, bf16[128,2304]{1,0:T(8,128)(2,1)S(1)}, u32[]{:S(2)}, u32[]{:S(2)}) collective-permute-start(bf16[128,2304]{1,0:T(8,128)(2,1)} %get-tuple-element.158.refs_1_), channel_id=1, source_target_pairs={{0,8},{4,12},{8,0},{12,4},{16,24},{20,28},{24,16},{28,20},{1,9},{5... | collective-permute-start | bytes 1769480 | tf_op jit(solution)/shard_map/ppermute | solution.py:76
  235.6 23.3 %collective-permute-start.19 = (bf16[128,2304]{1,0:T(8,128)(2,1)S(1)}, bf16[128,2304]{1,0:T(8,128)(2,1)S(1)}, u32[]{:S(2)}, u32[]{:S(2)}) collective-permute-start(bf16[128,2304]{1,0:T(8,128)(2,1)S(1)} %copy-done.37), channel_id=1, source_target_pairs={{0,8},{4,12},{8,0},{12,4},{16,24},{20,28},{24,16},{28,20},{1,9},{5... | collective-permute-start | bytes 1769480 | tf_op jit(solution)/shard_map/ppermute | solution.py:76
  238.1 24.8 %collective-permute-start.20 = (bf16[128,2304]{1,0:T(8,128)(2,1)S(1)}, bf16[128,2304]{1,0:T(8,128)(2,1)S(1)}, u32[]{:S(2)}, u32[]{:S(2)}) collective-permute-start(bf16[128,2304]{1,0:T(8,128)(2,1)S(1)} %add_convert_fusion.3), channel_id=1, source_target_pairs={{0,16},{4,20},{8,24},{12,28},{16,0},{20,4},{24,8},{28,12},{1,17},{... | collective-permute-start | bytes 1769480 | tf_op jit(solution)/shard_map/ppermute | solution.py:76
  240.9 26.2 %collective-permute-start.23 = (bf16[128,2304]{1,0:T(8,128)(2,1)S(1)}, bf16[128,2304]{1,0:T(8,128)(2,1)S(1)}, u32[]{:S(2)}, u32[]{:S(2)}) collective-permute-start(bf16[128,2304]{1,0:T(8,128)(2,1)S(1)} %copy-done.24), channel_id=1, source_target_pairs={{0,4},{4,0},{8,12},{12,8},{16,20},{20,16},{24,28},{28,24},{1,5},{5... | collective-permute-start | bytes 1769480 | tf_op jit(solution)/shard_map/ppermute | solution.py:76
  244.5 24.8 %collective-permute-start.24 = (bf16[128,2304]{1,0:T(8,128)(2,1)}, bf16[128,2304]{1,0:T(8,128)(2,1)S(1)}, u32[]{:S(2)}, u32[]{:S(2)}) collective-permute-start(bf16[128,2304]{1,0:T(8,128)(2,1)} %copy-done.39), channel_id=1, source_target_pairs={{0,4},{4,0},{8,12},{12,8},{16,20},{20,16},{24,28},{28,24},{1,5},{5... | collective-permute-start | bytes 1769480 | tf_op jit(solution)/shard_map/ppermute | solution.py:76
  244.5 24.8 %collective-permute-start.25 = (bf16[128,2304]{1,0:T(8,128)(2,1)}, bf16[128,2304]{1,0:T(8,128)(2,1)S(1)}, u32[]{:S(2)}, u32[]{:S(2)}) collective-permute-start(bf16[128,2304]{1,0:T(8,128)(2,1)} %copy-done.40), channel_id=1, source_target_pairs={{0,4},{4,0},{8,12},{12,8},{16,20},{20,16},{24,28},{28,24},{1,5},{5... | collective-permute-start | bytes 1769480 | tf_op jit(solution)/shard_map/ppermute | solution.py:76
  258.9 10.4 %collective-permute-start.21 = (bf16[1,256,1152]{2,1,0:T(8,128)(2,1)S(1)}, bf16[1,256,1152]{2,1,0:T(8,128)(2,1)S(1)}, u32[]{:S(2)}, u32[]{:S(2)}) collective-permute-start(bf16[1,256,1152]{2,1,0:T(8,128)(2,1)S(1)} %copy-done.34), channel_id=1, source_target_pairs={{0,4},{4,0},{8,12},{12,8},{16,20},{20,16},{24,28},{28,24},{1,5},{5... | collective-permute-start | bytes 1769480 | tf_op jit(solution)/shard_map/ppermute | solution.py:76
  262.9 6.4 %collective-permute-start.22 = (bf16[1,256,1152]{2,1,0:T(8,128)(2,1)S(1)}, bf16[1,256,1152]{2,1,0:T(8,128)(2,1)S(1)}, u32[]{:S(2)}, u32[]{:S(2)}) collective-permute-start(bf16[1,256,1152]{2,1,0:T(8,128)(2,1)S(1)} %copy-done.35), channel_id=1, source_target_pairs={{0,4},{4,0},{8,12},{12,8},{16,20},{20,16},{24,28},{28,24},{1,5},{5... | collective-permute-start | bytes 1769480 | tf_op jit(solution)/shard_map/ppermute | solution.py:76
  267.2 2.7 collective-permute-start.26
  272.9 26.8 %collective-permute-start.27 = (bf16[128,2304]{1,0:T(8,128)(2,1)S(1)}, bf16[128,2304]{1,0:T(8,128)(2,1)S(1)}, u32[]{:S(2)}, u32[]{:S(2)}) collective-permute-start(bf16[128,2304]{1,0:T(8,128)(2,1)S(1)} %get-tuple-element.288.refs_0_), channel_id=1, source_target_pairs={{0,16},{4,20},{8,24},{12,28},{16,0},{20,4},{24,8},{28,12},{1,17},{... | collective-permute-start | bytes 1769480 | tf_op jit(solution)/shard_map/ppermute | solution.py:76
  276.0 24.6 %collective-permute-start.28 = (bf16[128,2304]{1,0:T(8,128)(2,1)S(1)}, bf16[128,2304]{1,0:T(8,128)(2,1)}, u32[]{:S(2)}, u32[]{:S(2)}) collective-permute-start(bf16[128,2304]{1,0:T(8,128)(2,1)S(1)} %get-tuple-element.288.refs_0_), channel_id=1, source_target_pairs={{0,8},{4,12},{8,0},{12,4},{16,24},{20,28},{24,16},{28,20},{1,9},{5... | collective-permute-start | bytes 1769480 | tf_op jit(solution)/shard_map/ppermute | solution.py:76
  300.6 15.1 %collective-permute-start.29 = (bf16[128,2304]{1,0:T(8,128)(2,1)S(1)}, bf16[128,2304]{1,0:T(8,128)(2,1)}, u32[]{:S(2)}, u32[]{:S(2)}) collective-permute-start(bf16[128,2304]{1,0:T(8,128)(2,1)S(1)} %collective-permute-done.27.refs_1_), channel_id=1, source_target_pairs={{0,8},{4,12},{8,0},{12,4},{16,24},{20,28},{24,16},{28,20},{1,9},{5... | collective-permute-start | bytes 1769480 | tf_op jit(solution)/shard_map/ppermute | solution.py:76
  302.7 25.5 %collective-permute-start.30 = (bf16[128,2304]{1,0:T(8,128)(2,1)S(1)}, bf16[128,2304]{1,0:T(8,128)(2,1)}, u32[]{:S(2)}, u32[]{:S(2)}) collective-permute-start(bf16[128,2304]{1,0:T(8,128)(2,1)S(1)} %get-tuple-element.288.refs_0_), channel_id=1, source_target_pairs={{0,4},{4,0},{8,12},{12,8},{16,20},{20,16},{24,28},{28,24},{1,5},{5... | collective-permute-start | bytes 1769480 | tf_op jit(solution)/shard_map/ppermute | solution.py:76
  304.0 24.2 %collective-permute-start.31 = (bf16[128,2304]{1,0:T(8,128)(2,1)S(1)}, bf16[128,2304]{1,0:T(8,128)(2,1)}, u32[]{:S(2)}, u32[]{:S(2)}) collective-permute-start(bf16[128,2304]{1,0:T(8,128)(2,1)S(1)} %collective-permute-done.27.refs_1_), channel_id=1, source_target_pairs={{0,4},{4,0},{8,12},{12,8},{16,20},{20,16},{24,28},{28,24},{1,5},{5... | collective-permute-start | bytes 1769480 | tf_op jit(solution)/shard_map/ppermute | solution.py:76
  304.0 24.2 %collective-permute-start.32 = (bf16[128,2304]{1,0:T(8,128)(2,1)}, bf16[128,2304]{1,0:T(8,128)(2,1)}, u32[]{:S(2)}, u32[]{:S(2)}) collective-permute-start(bf16[128,2304]{1,0:T(8,128)(2,1)} %collective-permute-done.28.refs_0_.refs_2_), channel_id=1, source_target_pairs={{0,4},{4,0},{8,12},{12,8},{16,20},{20,16},{24,28},{28,24},{1,5},{5... | collective-permute-start | bytes 1769480 | tf_op jit(solution)/shard_map/ppermute | solution.py:76
  315.7 12.5 %collective-permute-start.33 = (bf16[128,2304]{1,0:T(8,128)(2,1)}, bf16[128,2304]{1,0:T(8,128)(2,1)}, u32[]{:S(2)}, u32[]{:S(2)}) collective-permute-start(bf16[128,2304]{1,0:T(8,128)(2,1)} %collective-permute-done.29.refs_1_.refs_3_), channel_id=1, source_target_pairs={{0,4},{4,0},{8,12},{12,8},{16,20},{20,16},{24,28},{28,24},{1,5},{5... | collective-permute-start | bytes 1769480 | tf_op jit(solution)/shard_map/ppermute | solution.py:76
  339.0 190.3 %reduce-scatter.5.cloned.1.call-start = ((), (), s32[]{:S(2)}) async-start(), calls=%async_computation.8 | async-start | bytes 13271040 | tf_op jit(solution)/shard_map/reduce_scatter | solution.py:729
  352.4 15.1 %collective-permute-start.34 = (bf16[128,2304]{1,0:T(8,128)(2,1)}, bf16[128,2304]{1,0:T(8,128)(2,1)S(1)}, u32[]{:S(2)}, u32[]{:S(2)}) collective-permute-start(bf16[128,2304]{1,0:T(8,128)(2,1)} %get-tuple-element.189.refs_1_), channel_id=1, source_target_pairs={{0,8},{4,12},{8,0},{12,4},{16,24},{20,28},{24,16},{28,20},{1,9},{5... | collective-permute-start | bytes 1769480 | tf_op jit(solution)/shard_map/ppermute | solution.py:76
  353.0 18.8 %collective-permute-start.38 = (bf16[2,256,1152]{2,1,0:T(8,128)(2,1)}, bf16[2,256,1152]{2,1,0:T(8,128)(2,1)}, u32[]{:S(2)}, u32[]{:S(2)}) collective-permute-start(bf16[2,256,1152]{2,1,0:T(8,128)(2,1)} %get-tuple-element.187.d1), channel_id=1, source_target_pairs={{0,4},{4,0},{8,12},{12,8},{16,20},{20,16},{24,28},{28,24},{1,5},{5... | collective-permute-start | bytes 3538952 | tf_op jit(solution)/shard_map/ppermute | solution.py:76
  353.5 18.4 %collective-permute-start.37 = (bf16[2,256,1152]{2,1,0:T(8,128)(2,1)}, bf16[2,256,1152]{2,1,0:T(8,128)(2,1)}, u32[]{:S(2)}, u32[]{:S(2)}) collective-permute-start(bf16[2,256,1152]{2,1,0:T(8,128)(2,1)} %get-tuple-element.185.d1), channel_id=1, source_target_pairs={{0,4},{4,0},{8,12},{12,8},{16,20},{20,16},{24,28},{28,24},{1,5},{5... | collective-permute-start | bytes 3538952 | tf_op jit(solution)/shard_map/ppermute | solution.py:76
  367.5 23.1 %collective-permute-start.35 = (bf16[128,2304]{1,0:T(8,128)(2,1)}, bf16[128,2304]{1,0:T(8,128)(2,1)S(1)}, u32[]{:S(2)}, u32[]{:S(2)}) collective-permute-start(bf16[128,2304]{1,0:T(8,128)(2,1)} %get-tuple-element.192.refs_0_), channel_id=1, source_target_pairs={{0,8},{4,12},{8,0},{12,4},{16,24},{20,28},{24,16},{28,20},{1,9},{5... | collective-permute-start | bytes 1769480 | tf_op jit(solution)/shard_map/ppermute | solution.py:76
  370.1 26.2 %collective-permute-start.36 = (bf16[128,2304]{1,0:T(8,128)(2,1)}, bf16[128,2304]{1,0:T(8,128)(2,1)S(1)}, u32[]{:S(2)}, u32[]{:S(2)}) collective-permute-start(bf16[128,2304]{1,0:T(8,128)(2,1)} %add_convert_fusion.1), channel_id=1, source_target_pairs={{0,16},{4,20},{8,24},{12,28},{16,0},{20,4},{24,8},{28,12},{1,17},{... | collective-permute-start | bytes 1769480 | tf_op jit(solution)/shard_map/ppermute | solution.py:76
  403.7 27.8 %collective-permute-start.39 = (bf16[128,2304]{1,0:T(8,128)(2,1)S(1)}, bf16[128,2304]{1,0:T(8,128)(2,1)S(1)}, u32[]{:S(2)}, u32[]{:S(2)}) collective-permute-start(bf16[128,2304]{1,0:T(8,128)(2,1)S(1)} %multiply_convert_fusion.s0.refs_0_), channel_id=1, source_target_pairs={{0,16},{4,20},{8,24},{12,28},{16,0},{20,4},{24,8},{28,12},{1,17},{... | collective-permute-start | bytes 1769480 | tf_op jit(solution)/shard_map/ppermute | solution.py:76
  406.8 24.7 %collective-permute-start.40 = (bf16[128,2304]{1,0:T(8,128)(2,1)S(1)}, bf16[128,2304]{1,0:T(8,128)(2,1)S(1)}, u32[]{:S(2)}, u32[]{:S(2)}) collective-permute-start(bf16[128,2304]{1,0:T(8,128)(2,1)S(1)} %multiply_convert_fusion.s0.refs_0_), channel_id=1, source_target_pairs={{0,8},{4,12},{8,0},{12,4},{16,24},{20,28},{24,16},{28,20},{1,9},{5... | collective-permute-start | bytes 1769480 | tf_op jit(solution)/shard_map/ppermute | solution.py:76
  431.5 16.2 %collective-permute-start.41 = (bf16[128,2304]{1,0:T(8,128)(2,1)S(1)}, bf16[128,2304]{1,0:T(8,128)(2,1)}, u32[]{:S(2)}, u32[]{:S(2)}) collective-permute-start(bf16[128,2304]{1,0:T(8,128)(2,1)S(1)} %collective-permute-done.39.s2.refs_2_), channel_id=1, source_target_pairs={{0,8},{4,12},{8,0},{12,4},{16,24},{20,28},{24,16},{28,20},{1,9},{5... | collective-permute-start | bytes 1769480 | tf_op jit(solution)/shard_map/ppermute | solution.py:76
  434.5 55.7 %collective-permute-start.44 = (bf16[512,2304]{1,0:T(8,128)(2,1)}, bf16[512,2304]{1,0:T(8,128)(2,1)}, u32[]{:S(2)}, u32[]{:S(2)}) collective-permute-start(bf16[512,2304]{1,0:T(8,128)(2,1)} %get-tuple-element.217.refs_0_), channel_id=1, source_target_pairs={{0,4},{4,0},{8,12},{12,8},{16,20},{20,16},{24,28},{28,24},{1,5},{5... | collective-permute-start | bytes 7077896 | tf_op jit(solution)/shard_map/ppermute | solution.py:76
  447.7 52.6 %all-to-all-start = ((bf16[8,72,1152]{2,1,0:T(8,128)(2,1)}), bf16[8,72,1152]{2,1,0:T(8,128)(2,1)}, u32[]{:S(2)}, u32[]{:S(2)}) async-start(bf16[8,72,1152]{2,1,0:T(8,128)(2,1)} %bitcast.110), calls=%async_computation.1 | async-start | bytes 2654208 | tf_op jit(solution)/shard_map/all_to_all | solution.py:660
  467.3 3.7 collective-permute-start.42
  467.7 14.0 %collective-permute-start.46 = (bf16[128,2304]{1,0:T(8,128)(2,1)S(1)}, bf16[128,2304]{1,0:T(8,128)(2,1)S(1)}, u32[]{:S(2)}, u32[]{:S(2)}) collective-permute-start(bf16[128,2304]{1,0:T(8,128)(2,1)S(1)} %copy-done.15), channel_id=1, source_target_pairs={{0,4},{4,0},{8,12},{12,8},{16,20},{20,16},{24,28},{28,24},{1,5},{5... | collective-permute-start | bytes 1769480 | tf_op jit(solution)/shard_map/ppermute | solution.py:76
  467.9 2.7 collective-permute-start.50
  468.2 16.9 %collective-permute-start.47 = (bf16[128,2304]{1,0:T(8,128)(2,1)S(1)}, bf16[128,2304]{1,0:T(8,128)(2,1)}, u32[]{:S(2)}, u32[]{:S(2)}) collective-permute-start(bf16[128,2304]{1,0:T(8,128)(2,1)S(1)} %copy-done.32), channel_id=1, source_target_pairs={{0,4},{4,0},{8,12},{12,8},{16,20},{20,16},{24,28},{28,24},{1,5},{5... | collective-permute-start | bytes 1769480 | tf_op jit(solution)/shard_map/ppermute | solution.py:76
  470.6 14.6 %collective-permute-start.48 = (bf16[128,2304]{1,0:T(8,128)(2,1)S(1)}, bf16[128,2304]{1,0:T(8,128)(2,1)}, u32[]{:S(2)}, u32[]{:S(2)}) collective-permute-start(bf16[128,2304]{1,0:T(8,128)(2,1)S(1)} %copy-done.30), channel_id=1, source_target_pairs={{0,4},{4,0},{8,12},{12,8},{16,20},{20,16},{24,28},{28,24},{1,5},{5... | collective-permute-start | bytes 1769480 | tf_op jit(solution)/shard_map/ppermute | solution.py:76
  471.3 13.9 %collective-permute-start.49 = (bf16[128,2304]{1,0:T(8,128)(2,1)}, bf16[128,2304]{1,0:T(8,128)(2,1)}, u32[]{:S(2)}, u32[]{:S(2)}) collective-permute-start(bf16[128,2304]{1,0:T(8,128)(2,1)} %collective-permute-done.41.s3.refs_3_), channel_id=1, source_target_pairs={{0,4},{4,0},{8,12},{12,8},{16,20},{20,16},{24,28},{28,24},{1,5},{5... | collective-permute-start | bytes 1769480 | tf_op jit(solution)/shard_map/ppermute | solution.py:76
  481.7 8.5 %collective-permute-start.45 = (bf16[1,512,512]{2,1,0:T(8,128)(2,1)}, bf16[1,512,512]{2,1,0:T(8,128)(2,1)}, u32[]{:S(2)}, u32[]{:S(2)}) collective-permute-start(bf16[1,512,512]{2,1,0:T(8,128)(2,1)} %get-tuple-element.219), channel_id=1, source_target_pairs={{0,4},{4,0},{8,12},{12,8},{16,20},{20,16},{24,28},{28,24},{1,5},{5... | collective-permute-start | bytes 1572872 | tf_op jit(solution)/shard_map/ppermute | solution.py:76
  485.1 15.2 %collective-permute-start.43 = (bf16[128,2304]{1,0:T(8,128)(2,1)}, bf16[128,2304]{1,0:T(8,128)(2,1)}, u32[]{:S(2)}, u32[]{:S(2)}) collective-permute-start(bf16[128,2304]{1,0:T(8,128)(2,1)} %get-tuple-element.215), channel_id=1, source_target_pairs={{0,8},{4,12},{8,0},{12,4},{16,24},{20,28},{24,16},{28,20},{1,9},{5... | collective-permute-start | bytes 1769480 | tf_op jit(solution)/shard_map/ppermute | solution.py:76
  500.3 25.5 %collective-permute-start.51 = (bf16[128,2304]{1,0:T(8,128)(2,1)}, bf16[128,2304]{1,0:T(8,128)(2,1)}, u32[]{:S(2)}, u32[]{:S(2)}) collective-permute-start(bf16[128,2304]{1,0:T(8,128)(2,1)} %get-tuple-element.223), channel_id=1, source_target_pairs={{0,8},{4,12},{8,0},{12,4},{16,24},{20,28},{24,16},{28,20},{1,9},{5... | collective-permute-start | bytes 1769480 | tf_op jit(solution)/shard_map/ppermute | solution.py:76
  502.5 26.7 %collective-permute-start.52 = (bf16[128,2304]{1,0:T(8,128)(2,1)S(1)}, bf16[128,2304]{1,0:T(8,128)(2,1)}, u32[]{:S(2)}, u32[]{:S(2)}) collective-permute-start(bf16[128,2304]{1,0:T(8,128)(2,1)S(1)} %add_convert_fusion), channel_id=1, source_target_pairs={{0,16},{4,20},{8,24},{12,28},{16,0},{20,4},{24,8},{28,12},{1,17},{... | collective-permute-start | bytes 1769480 | tf_op jit(solution)/shard_map/ppermute | solution.py:76
  507.1 12.2 %collective-permute-start.53 = (bf16[288,772]{1,0:T(8,128)(2,1)S(1)}, bf16[288,772]{1,0:T(8,128)(2,1)S(1)}, u32[]{:S(2)}, u32[]{:S(2)}) collective-permute-start(bf16[288,772]{1,0:T(8,128)(2,1)S(1)} %get-tuple-element.281), channel_id=1, source_target_pairs={{0,1},{1,0},{2,3},{3,2},{4,5},{5,4},{6,7},{7,6},{8,9},{9,8},{10,11... | collective-permute-start | bytes 1334024 | tf_op jit(solution)/shard_map/ppermute | solution.py:76
  507.6 11.9 %collective-permute-start.54 = (bf16[288,772]{1,0:T(8,128)(2,1)S(1)}, bf16[288,772]{1,0:T(8,128)(2,1)S(1)}, u32[]{:S(2)}, u32[]{:S(2)}) collective-permute-start(bf16[288,772]{1,0:T(8,128)(2,1)S(1)} %get-tuple-element.283), channel_id=1, source_target_pairs={{0,2},{1,3},{2,0},{3,1},{4,6},{5,7},{6,4},{7,5},{8,10},{9,11},{10,... | collective-permute-start | bytes 1334024 | tf_op jit(solution)/shard_map/ppermute | solution.py:76
  529.2 65.3 %all-to-all-start.1 = ((bf16[8,72,2304]{2,1,0:T(8,128)(2,1)}), bf16[8,72,2304]{2,1,0:T(8,128)(2,1)}, u32[]{:S(2)}, u32[]{:S(2)}) async-start(bf16[8,72,2304]{2,1,0:T(8,128)(2,1)} %bitcast.107), calls=%async_computation.3 | async-start | bytes 5308416 | tf_op jit(solution)/shard_map/all_to_all | solution.py:660
  544.3 23.5 %collective-permute-start.56 = (bf16[576,772]{0,1:T(8,128)(2,1)}, bf16[576,772]{0,1:T(8,128)(2,1)}, u32[]{:S(2)}, u32[]{:S(2)}) collective-permute-start(bf16[576,772]{0,1:T(8,128)(2,1)} %copy.41), channel_id=1, source_target_pairs={{0,2},{1,3},{2,0},{3,1},{4,6},{5,7},{6,4},{7,5},{8,10},{9,11},{10,... | collective-permute-start | bytes 2668040 | tf_op jit(solution)/shard_map/ppermute | solution.py:76
  547.5 23.2 %collective-permute-start.55 = (bf16[576,772]{0,1:T(8,128)(2,1)}, bf16[576,772]{0,1:T(8,128)(2,1)}, u32[]{:S(2)}, u32[]{:S(2)}) collective-permute-start(bf16[576,772]{0,1:T(8,128)(2,1)} %copy.39), channel_id=1, source_target_pairs={{0,1},{1,0},{2,3},{3,2},{4,5},{5,4},{6,7},{7,6},{8,9},{9,8},{10,11... | collective-permute-start | bytes 2668040 | tf_op jit(solution)/shard_map/ppermute | solution.py:76
  594.5 29.8 %all-to-all-start.2 = ((bf16[8,72,772]{2,1,0:T(8,128)(2,1)}), bf16[8,72,772]{2,1,0:T(8,128)(2,1)S(1)}, u32[]{:S(2)}, u32[]{:S(2)}) async-start(bf16[8,72,772]{2,1,0:T(8,128)(2,1)} %bitcast.28), calls=%async_computation.4 | async-start | bytes 2064384 | tf_op jit(solution)/shard_map/all_to_all | solution.py:660
  (64 other events, 581.7 us)
Sparse Core Ops, SparseCore 0:
  12.6 130.3 all-gather.2
  145.4 64.2 all-gather.4
  339.1 61.6 reduce-scatter.2
  403.7 104.6 reduce-scatter.4

commit v5 on v4

--- a/solution.py
+++ b/solution.py
@@ -296,7 +296,7 @@
     )(core, *hidden, w_out, w_out, *earlier)
 
 
-def down_backward(d_mixed, gate_all, up_all, w_out, core, most=384):
+def down_backward(d_mixed, gate_all, up_all, w_out, core, most=1152):
     rows, width = sum(v.shape[0] for v in d_mixed), d_mixed[0].shape[1]
     size = w_out.shape[2]
     tile = tile_of(size, most)

time: 645 us -> 643 us (level)
  transfers between devices with their start and end apart: 64 -> 64, of which waited for: 30 -> 31; matrix products, arithmetic and copies ran while one was open for 11% -> 11% of each run, Pallas kernels for 24% -> 24%
where the time goes in v5:
time: 643 us; the launch traced here: 635 us
  waiting for transfers between devices  272 us (42%)
  Pallas kernels  171 us (27%)
  starting transfers between devices  89.6 us (14%)
  local copies, waits for them, and re-layouts  44.6 us (7%)
  other arithmetic  42.2 us (7%)
  between operations  14.8 us (2%)
    ppermute x57, waiting for transfers between devices, swap(): return lax.ppermute(values, axis, [(i, i ^ distance) for i in range(count)])  235 us
    ppermute x57, starting transfers between devices, swap(): return lax.ppermute(values, axis, [(i, i ^ distance) for i in range(count)])  67.3 us
    pallas_call x4, Pallas kernels, weight_grad_kernel(): kernel_call(body, (halves, groups, steps), [pl.BlockSpec((n, part), lambd...  40.5 us
    all_to_all x3, waiting for transfers between devices, to_owners(): return lax.all_to_all(total, 'ctx', split_axis=0, concat_axis=0, tiled=True)  36.9 us
    pallas_call x2, Pallas kernels, gate_up_forward(): kernel_call(body, (2, steps), whole_of(values) + [pl.BlockSpec((1, width,...  29.1 us
    pallas_call x2, Pallas kernels, gate_up_backward(): kernel_call(body, (width // tile,), [whole, whole, pl.BlockSpec((1, tile,...  25.7 us
    all_to_all x3, starting transfers between devices, to_owners(): return lax.all_to_all(total, 'ctx', split_axis=0, concat_axis=0, tiled=True)  22.2 us
    pallas_call x2, Pallas kernels, down_backward(): kernel_call(body, (2, steps), whole_of(d_mixed) + [saved, saved, pl.Block...  19.1 us
  transfers between devices with their start and end apart: 64, of which 31 were waited for; matrix products, arithmetic and copies ran while one was open for 11% of the time, Pallas kernels for 24%

profile of v5, /device:TPU:13, one launch (start us, length us, event | category | flops | bytes accessed | tf_op | source)
XLA Modules:
  0.0 634.7 jit_solution(6387622419617722632)
XLA Ops:
  8.5 2.3 constant_dynamic-slice_fusion.2
  12.6 2.5 constant_dynamic-slice_fusion
  16.7 2.3 collective-permute-start.2
  19.1 25.4 %collective-permute-done.2.s2 = bf16[128,2304]{1,0:T(8,128)(2,1)} collective-permute-done((bf16[128,2304]{1,0:T(8,128)(2,1)S(1)}, bf16[128,2304]{1,0:T(8,128)(2,1)}, u32[]{:S(2)}, u32[]{:S(2)}) %collective-permute-start.2) | collective-permute-done | bytes 589856 | tf_op jit(solution)/shard_map/ppermute | solution.py:76
  45.0 2.2 collective-permute-done.1
  54.5 15.0 %collective-permute-done.7 = bf16[4,576]{1,0:T(4,128)(2,1)S(1)} collective-permute-done((bf16[4,576]{1,0:T(4,128)(2,1)S(1)}, bf16[4,576]{1,0:T(4,128)(2,1)S(1)}, u32[]{:S(2)}, u32[]{:S(2)}) %collective-permute-start.7) | collective-permute-done | bytes 4640 | tf_op jit(solution)/shard_map/ppermute | solution.py:76
  70.7 2.3 collective-permute-done.9
  75.2 6.8 %collective-permute-start.10 = (bf16[2304,768]{1,0:T(8,128)(2,1)S(1)}, bf16[2304,768]{1,0:T(8,128)(2,1)}, u32[]{:S(2)}, u32[]{:S(2)}) collective-permute-start(bf16[2304,768]{1,0:T(8,128)(2,1)S(1)} %constant_dynamic-update-slice_fusion.w0), channel_id=1, source_target_pairs={{0,4},{4,0},{8,12},{12,8},{16,20},{20,16},{24,28},{28,24},{1,5},{5... | collective-permute-start | bytes 10616840 | tf_op jit(solution)/shard_map/ppermute | solution.py:76
  93.0 7.6 %shard_map.109 = (bf16[512,2304]{1,0:T(8,128)(2,1)}, bf16[512,256]{1,0:T(8,128)(2,1)}, bf16[512,256]{1,0:T(8,128)(2,1)}, bf16[512,512]{1,0:T(8,128)(2,1)}) custom-call(s32[1]{0:T(128)} %bitcast.1.core_ref, bf16[128,2304]{1,0:T(8,128)(2,1)} %bitcast.99, bf16[128,2304]{1,0:T(8,128)(2,1)} %copy-done.13, bf16[128,2304]{1,0:T(8,128)(2,1)} %collective-permute-done.2.s2, ...), custom_call_target="tpu_custom_call" | custom-call | flops 2415919104 | bytes 9437184 | tf_op jit(solution)/shard_map/pallas_call | solution.py:446
  103.7 8.7 %shard_map.110 = (bf16[512,256]{1,0:T(8,128)(2,1)}, bf16[512,256]{1,0:T(8,128)(2,1)}, bf16[128,2304]{1,0:T(8,128)(2,1)}, bf16[128,2304]{1,0:T(8,128)(2,1)}, bf16...) custom-call(s32[1]{0:T(128)} %bitcast.1.core_ref, bf16[512,256]{1,0:T(8,128)(2,1)} %get-tuple-element.133.q0, ...), custom_call_target="tpu_custom_call" | custom-call | flops 2281701376 | bytes 4718592 | tf_op jit(solution)/shard_map/pallas_call | solution.py:528
  112.8 14.7 %collective-permute-done.12 = bf16[128,2304]{1,0:T(8,128)(2,1)S(1)} collective-permute-done((bf16[128,2304]{1,0:T(8,128)(2,1)}, bf16[128,2304]{1,0:T(8,128)(2,1)S(1)}, u32[]{:S(2)}, u32[]{:S(2)}) %collective-permute-start.12) | collective-permute-done | bytes 589856 | tf_op jit(solution)/shard_map/ppermute | solution.py:76
  129.0 2.4 collective-permute-start.14
  132.2 19.3 %collective-permute-done.13 = bf16[128,2304]{1,0:T(8,128)(2,1)S(1)} collective-permute-done((bf16[128,2304]{1,0:T(8,128)(2,1)}, bf16[128,2304]{1,0:T(8,128)(2,1)S(1)}, u32[]{:S(2)}, u32[]{:S(2)}) %collective-permute-start.13) | collective-permute-done | bytes 589856 | tf_op jit(solution)/shard_map/ppermute | solution.py:76
  151.4 4.3 collective-permute-done.14
  157.9 3.2 collective-permute-start.15
  161.1 23.5 %collective-permute-done.15.refs_1_ = bf16[128,2304]{1,0:T(8,128)(2,1)S(1)} collective-permute-done((bf16[128,2304]{1,0:T(8,128)(2,1)S(1)}, bf16[128,2304]{1,0:T(8,128)(2,1)S(1)}, u32[]{:S(2)}, u32[]{:S(2)}) %collective-permute-start.15) | collective-permute-done | bytes 589856 | tf_op jit(solution)/shard_map/ppermute | solution.py:76
  185.6 14.7 %shard_map.111 = (bf16[1,256,1152]{2,1,0:T(8,128)(2,1)}, bf16[1,256,1152]{2,1,0:T(8,128)(2,1)}, f32[2,256,1152]{2,1,0:T(8,128)}, f32[2,256,1152]{2,1,0:T(8,128)}) custom-call(s32[1]{0:T(128)} %bitcast.1.core_ref, bf16[128,2304]{1,0:T(8,128)(2,1)} %copy-done.23, bf16[128,2304]{1,0:T(8,128)(2,1)} %copy-done.39, bf16[2,2304,2304]{2,1,0:T(8,128)(2,1)} %bitcast.85, ...), custom_call_target="tpu_custom_call" | custom-call | flops 5435817984 | bytes 27131904 | tf_op jit(solution)/shard_map/pallas_call | solution.py:251
  200.3 14.5 %shard_map.112 = (bf16[1,256,1152]{2,1,0:T(8,128)(2,1)}, bf16[1,256,1152]{2,1,0:T(8,128)(2,1)}, f32[2,256,1152]{2,1,0:T(8,128)}, f32[2,256,1152]{2,1,0:T(8,128)}) custom-call(s32[1]{0:T(128)} %bitcast.1.core_ref, bf16[128,2304]{1,0:T(8,128)(2,1)} %copy-done.40, bf16[128,2304]{1,0:T(8,128)(2,1)} %collective-permute-done.17.refs_1_.refs_3_, ...), custom_call_target="tpu_custom_call" | custom-call | flops 5435817984 | bytes 27131904 | tf_op jit(solution)/shard_map/pallas_call | solution.py:251
  214.8 7.6 %shard_map.113 = (bf16[128,2304]{1,0:T(8,128)(2,1)}, bf16[128,2304]{1,0:T(8,128)(2,1)}) custom-call(s32[1]{0:T(128)} %bitcast.1.core_ref, bf16[1,256,1152]{2,1,0:T(8,128)(2,1)} %get-tuple-element.181.h0.refs_9_, bf16[1,256,1152]{2,1,0:T(8,128)(2,1)} %get-tuple-element.156.h1, bf16[2,2304,1152]{2,1,0:T(8,128)(2,1)} %bitcast.93, bf16[2,2304,1152]{2,1,0:T(8,128)(2,1)} %bitcast.94), custom_call_target="tpu_custom_call" | custom-call | flops 2717908992 | bytes 11796480 | tf_op jit(solution)/shard_map/pallas_call | solution.py:280
  223.6 8.2 %shard_map.114 = (bf16[128,2304]{1,0:T(8,128)(2,1)}, bf16[128,2304]{1,0:T(8,128)(2,1)}) custom-call(s32[1]{0:T(128)} %bitcast.1.core_ref, bf16[1,256,1152]{2,1,0:T(8,128)(2,1)} %get-tuple-element.180.h0.refs_8_, bf16[1,256,1152]{2,1,0:T(8,128)(2,1)} %get-tuple-element.152.h1, bf16[2,2304,1152]{2,1,0:T(8,128)(2,1)} %bitcast.95, ...), custom_call_target="tpu_custom_call" | custom-call | flops 2717908992 | bytes 11796480 | tf_op jit(solution)/shard_map/pallas_call | solution.py:280
  231.9 3.8 collective-permute-done.18
  238.1 2.9 collective-permute-start.20
  240.9 3.6 collective-permute-start.23
  245.0 13.9 %collective-permute-done.19 = bf16[128,2304]{1,0:T(8,128)(2,1)S(1)} collective-permute-done((bf16[128,2304]{1,0:T(8,128)(2,1)S(1)}, bf16[128,2304]{1,0:T(8,128)(2,1)S(1)}, u32[]{:S(2)}, u32[]{:S(2)}) %collective-permute-start.19) | collective-permute-done | bytes 589856 | tf_op jit(solution)/shard_map/ppermute | solution.py:76
  258.9 3.6 collective-permute-start.21
  262.7 4.5 collective-permute-start.22
  272.9 3.1 collective-permute-start.27
  276.0 23.6 %collective-permute-done.27.refs_1_ = bf16[128,2304]{1,0:T(8,128)(2,1)S(1)} collective-permute-done((bf16[128,2304]{1,0:T(8,128)(2,1)S(1)}, bf16[128,2304]{1,0:T(8,128)(2,1)S(1)}, u32[]{:S(2)}, u32[]{:S(2)}) %collective-permute-start.27) | collective-permute-done | bytes 589856 | tf_op jit(solution)/shard_map/ppermute | solution.py:76
  300.6 2.1 collective-permute-start.29
  304.5 9.5 %shard_map.115 = (bf16[2,256,1152]{2,1,0:T(8,128)(2,1)}, bf16[2,256,1152]{2,1,0:T(8,128)(2,1)}) custom-call(s32[1]{0:T(128)} %bitcast.1.core_ref, bf16[128,2304]{1,0:T(8,128)(2,1)} %copy-done.17, bf16[128,2304]{1,0:T(8,128)(2,1)} %copy-done.36, f32[2,256,1152]{2,1,0:T(8,128)} %get-tuple-element.168.refs_2_, f32[2,256,1152]{2,1,0:T(8,128)} %get-tuple-element.169.refs_3_, ...), custom_call_target="tpu_custom_call" | custom-call | flops 2717908992 | bytes 17694720 | tf_op jit(solution)/shard_map/pallas_call | solution.py:328
  317.0 9.5 %shard_map.116 = (bf16[2,256,1152]{2,1,0:T(8,128)(2,1)}, bf16[2,256,1152]{2,1,0:T(8,128)(2,1)}) custom-call(s32[1]{0:T(128)} %bitcast.1.core_ref, bf16[128,2304]{1,0:T(8,128)(2,1)} %collective-permute-done.28.refs_0_.refs_2_, bf16[128,2304]{1,0:T(8,128)(2,1)} %collective-permute-done.29.refs_1_.refs_3_, f32[2,256,1152]{2,1,0:T(8,128)} %get-tuple-element.176.refs_2_, ...), custom_call_target="tpu_custom_call" | custom-call | flops 2717908992 | bytes 17694720 | tf_op jit(solution)/shard_map/pallas_call | solution.py:328
  326.6 10.7 %shard_map.117 = bf16[4,576,1152]{2,1,0:T(8,128)(2,1)} custom-call(bf16[128,2304]{1,0:T(8,128)(2,1)} %copy-done.17, bf16[128,2304]{1,0:T(8,128)(2,1)} %copy-done.36, bf16[128,2304]{1,0:T(8,128)(2,1)} %collective-permute-done.28.refs_0_.refs_2_, bf16[128,2304]{1,0:T(8,128)(2,1)} %collective-permute-done.29.refs_1_.refs_3_, ...), custom_call_target="tpu_custom_call" | custom-call | flops 5435817984 | bytes 19464192 | tf_op jit(solution)/shard_map/pallas_call | solution.py:403
  337.4 13.2 %shard_map.118 = (bf16[128,2304]{1,0:T(8,128)(2,1)}, bf16[128,2304]{1,0:T(8,128)(2,1)}) custom-call(s32[1]{0:T(128)} %bitcast.1.core_ref, bf16[2,256,1152]{2,1,0:T(8,128)(2,1)} %get-tuple-element.186.d0.refs_9_, bf16[2,256,1152]{2,1,0:T(8,128)(2,1)} %get-tuple-element.187.d1, bf16[2,2304,2304]{2,1,0:T(8,128)(2,1)} %bitcast.89, bf16[2,2304,2304]{2,1,0:T(8,128)(2,1)} %bitcast.90), custom_call_target="tpu_custom_call" | custom-call | flops 5435817984 | bytes 23592960 | tf_op jit(solution)/shard_map/pallas_call | solution.py:354
  351.9 12.4 %shard_map.119 = (bf16[128,2304]{1,0:T(8,128)(2,1)}, bf16[128,2304]{1,0:T(8,128)(2,1)}) custom-call(s32[1]{0:T(128)} %bitcast.1.core_ref, bf16[2,256,1152]{2,1,0:T(8,128)(2,1)} %get-tuple-element.184.d0.refs_8_, bf16[2,256,1152]{2,1,0:T(8,128)(2,1)} %get-tuple-element.185.d1, bf16[2,2304,2304]{2,1,0:T(8,128)(2,1)} %bitcast.91, ...), custom_call_target="tpu_custom_call" | custom-call | flops 5435817984 | bytes 23592960 | tf_op jit(solution)/shard_map/pallas_call | solution.py:354
  370.3 18.7 %shard_map.120 = bf16[4,576,2304]{2,1,0:T(8,128)(2,1)} custom-call(bf16[128,2304]{1,0:T(8,128)(2,1)} %copy-done.23, bf16[128,2304]{1,0:T(8,128)(2,1)} %copy-done.39, bf16[128,2304]{1,0:T(8,128)(2,1)} %copy-done.40, bf16[128,2304]{1,0:T(8,128)(2,1)} %collective-permute-done.17.refs_1_.refs_3_, bf16[128,2304]{1,0:T(8,128)(2,1)} %copy-done.58, ...), custom_call_target="tpu_custom_call" | custom-call | flops 10871635968 | bytes 29491200 | tf_op jit(solution)/shard_map/pallas_call | solution.py:403
  389.0 5.8 collective-permute-done.36
  396.8 2.3 multiply_reduce_fusion
  399.2 2.7 multiply_reduce_fusion.1
  402.3 3.1 collective-permute-start.39
  405.4 24.6 %collective-permute-done.39.s2.refs_2_ = bf16[128,2304]{1,0:T(8,128)(2,1)S(1)} collective-permute-done((bf16[128,2304]{1,0:T(8,128)(2,1)S(1)}, bf16[128,2304]{1,0:T(8,128)(2,1)S(1)}, u32[]{:S(2)}, u32[]{:S(2)}) %collective-permute-start.39) | collective-permute-done | bytes 589856 | tf_op jit(solution)/shard_map/ppermute | solution.py:76
  430.1 3.1 collective-permute-start.41
  434.1 12.2 %collective-permute-done.41.s3.refs_3_ = bf16[128,2304]{1,0:T(8,128)(2,1)} collective-permute-done((bf16[128,2304]{1,0:T(8,128)(2,1)S(1)}, bf16[128,2304]{1,0:T(8,128)(2,1)}, u32[]{:S(2)}, u32[]{:S(2)}) %collective-permute-start.41) | collective-permute-done | bytes 589856 | tf_op jit(solution)/shard_map/ppermute | solution.py:76
  446.3 7.0 %all-to-all-start = ((bf16[8,72,1152]{2,1,0:T(8,128)(2,1)}), bf16[8,72,1152]{2,1,0:T(8,128)(2,1)}, u32[]{:S(2)}, u32[]{:S(2)}) async-start(bf16[8,72,1152]{2,1,0:T(8,128)(2,1)} %bitcast.110), calls=%async_computation.1 | async-start | bytes 2654208 | tf_op jit(solution)/shard_map/all_to_all | solution.py:660
  453.4 12.6 %shard_map.121 = (bf16[512,256]{1,0:T(8,128)(2,1)}, bf16[512,256]{1,0:T(8,128)(2,1)}, f32[512,512]{1,0:T(8,128)}, bf16[512,512]{1,0:T(8,128)(2,1)}) custom-call(s32[1]{0:T(128)} %bitcast.1.core_ref, bf16[512,256]{1,0:T(8,128)(2,1)} %get-tuple-element.133.q0, bf16[512,256]{1,0:T(8,128)(2,1)} %get-tuple-element.134.q1, ...), custom_call_target="tpu_custom_call" | custom-call | flops 3892314112 | bytes 4718592 | tf_op jit(solution)/shard_map/pallas_call | solution.py:589
  467.0 2.2 collective-permute-done.50
  470.7 9.6 %shard_map.122 = (bf16[128,2304]{1,0:T(8,128)(2,1)}, bf16[128,2304]{1,0:T(8,128)(2,1)}, bf16[128,2304]{1,0:T(8,128)(2,1)}, bf16[128,2304]{1,0:T(8,128)(2,1)}, bf...) custom-call(s32[1]{0:T(128)} %bitcast.1.core_ref, bf16[128,2304]{1,0:T(8,128)(2,1)} %bitcast.100, ...), custom_call_target="tpu_custom_call" | custom-call | flops 2415919104 | bytes 9437184 | tf_op jit(solution)/shard_map/pallas_call | solution.py:637
  483.9 5.1 shard_map.124
  489.0 5.9 shard_map.123
  494.9 3.5 pad_maximum_fusion
  501.0 2.2 collective-permute-start.52
  503.2 2.5 dynamic-slice_bitcast_fusion.3
  507.2 10.6 %collective-permute-done.53 = bf16[288,772]{1,0:T(8,128)(2,1)S(1)} collective-permute-done((bf16[288,772]{1,0:T(8,128)(2,1)S(1)}, bf16[288,772]{1,0:T(8,128)(2,1)S(1)}, u32[]{:S(2)}, u32[]{:S(2)}) %collective-permute-start.53) | collective-permute-done | bytes 444704 | tf_op jit(solution)/shard_map/ppermute | solution.py:76
  517.9 6.3 collective-permute-done.51
  524.2 3.5 collective-permute-done.52
  527.7 8.0 %all-to-all-start.1 = ((bf16[8,72,2304]{2,1,0:T(8,128)(2,1)}), bf16[8,72,2304]{2,1,0:T(8,128)(2,1)}, u32[]{:S(2)}, u32[]{:S(2)}) async-start(bf16[8,72,2304]{2,1,0:T(8,128)(2,1)} %bitcast.107), calls=%async_computation.3 | async-start | bytes 5308416 | tf_op jit(solution)/shard_map/all_to_all | solution.py:660
  539.0 2.2 fusion.18
  549.1 2.7 fusion.13
  551.9 14.5 %collective-permute-done.56 = bf16[576,772]{0,1:T(8,128)(2,1)} collective-permute-done((bf16[576,772]{0,1:T(8,128)(2,1)}, bf16[576,772]{0,1:T(8,128)(2,1)}, u32[]{:S(2)}, u32[]{:S(2)}) %collective-permute-start.56) | collective-permute-done | bytes 889376 | tf_op jit(solution)/shard_map/ppermute | solution.py:76
  571.3 2.6 fusion.1
  573.8 19.3 %all-to-all-done.1 = bf16[8,72,2304]{2,1,0:T(8,128)(2,1)} async-done(((bf16[8,72,2304]{2,1,0:T(8,128)(2,1)}), bf16[8,72,2304]{2,1,0:T(8,128)(2,1)}, u32[]{:S(2)}, u32[]{:S(2)}) %all-to-all-start.1) | async-done | bytes 2654240 | tf_op jit(solution)/shard_map/all_to_all | solution.py:660
  593.1 7.1 %all-to-all-start.2 = ((bf16[8,72,772]{2,1,0:T(8,128)(2,1)}), bf16[8,72,772]{2,1,0:T(8,128)(2,1)S(1)}, u32[]{:S(2)}, u32[]{:S(2)}) async-start(bf16[8,72,772]{2,1,0:T(8,128)(2,1)} %bitcast.28), calls=%async_computation.4 | async-start | bytes 2064384 | tf_op jit(solution)/shard_map/all_to_all | solution.py:660
  602.6 2.8 maximum_convert_fusion
  605.4 17.6 %all-to-all-done.2.t = bf16[8,72,772]{2,1,0:T(8,128)(2,1)S(1)} async-done(((bf16[8,72,772]{2,1,0:T(8,128)(2,1)}), bf16[8,72,772]{2,1,0:T(8,128)(2,1)S(1)}, u32[]{:S(2)}, u32[]{:S(2)}) %all-to-all-start.2) | async-done | bytes 889376 | tf_op jit(solution)/shard_map/all_to_all | solution.py:660
  623.9 2.5 shard_map.125
  (292 shorter events, 92.9 us)
Async XLA Ops:
  7.2 178.3 %all-gather.3.cloned.1.call-start = ((), (), s32[]{:S(2)}) async-start(), calls=%async_computation.5 | async-start | bytes 23887872 | tf_op jit(solution)/shard_map/all_gather | solution.py:722
  12.5 202.2 %all-gather.5.cloned.1.call-start = ((), (), s32[]{:S(2)}) async-start(), calls=%async_computation.6 | async-start | bytes 11943936 | tf_op jit(solution)/shard_map/all_gather | solution.py:722
  15.1 431.2 %reduce-scatter.3.cloned.1.call-start = ((), (), s32[]{:S(2)}) async-start(), calls=%async_computation.7 | async-start | bytes 6635520 | tf_op jit(solution)/shard_map/reduce_scatter | solution.py:729
  15.1 29.8 %collective-permute-start = (bf16[576,768]{1,0:T(8,128)(2,1)S(1)}, bf16[576,768]{1,0:T(8,128)(2,1)S(1)}, u32[]{:S(2)}, u32[]{:S(2)}) collective-permute-start(bf16[576,768]{1,0:T(8,128)(2,1)S(1)} %pad_maximum_fusion.4), channel_id=1, source_target_pairs={{0,1},{1,0},{2,3},{3,2},{4,5},{5,4},{6,7},{7,6},{8,9},{9,8},{10,11... | collective-permute-start | bytes 2654216 | tf_op jit(solution)/shard_map/ppermute | solution.py:76
  16.4 30.8 %collective-permute-start.1 = (bf16[576,768]{1,0:T(8,128)(2,1)S(1)}, bf16[576,768]{1,0:T(8,128)(2,1)S(1)}, u32[]{:S(2)}, u32[]{:S(2)}) collective-permute-start(bf16[576,768]{1,0:T(8,128)(2,1)S(1)} %pad_maximum_fusion.4), channel_id=1, source_target_pairs={{0,2},{1,3},{2,0},{3,1},{4,6},{5,7},{6,4},{7,5},{8,10},{9,11},{10,... | collective-permute-start | bytes 2654216 | tf_op jit(solution)/shard_map/ppermute | solution.py:76
  16.7 27.9 %collective-permute-start.2 = (bf16[128,2304]{1,0:T(8,128)(2,1)S(1)}, bf16[128,2304]{1,0:T(8,128)(2,1)}, u32[]{:S(2)}, u32[]{:S(2)}) collective-permute-start(bf16[128,2304]{1,0:T(8,128)(2,1)S(1)} %bitcast.101), channel_id=1, source_target_pairs={{0,16},{4,20},{8,24},{12,28},{16,0},{20,4},{24,8},{28,12},{1,17},{... | collective-permute-start | bytes 1769480 | tf_op jit(solution)/shard_map/ppermute | solution.py:76
  19.0 25.6 %collective-permute-start.3 = (bf16[128,2304]{1,0:T(8,128)(2,1)S(1)}, bf16[128,2304]{1,0:T(8,128)(2,1)S(1)}, u32[]{:S(2)}, u32[]{:S(2)}) collective-permute-start(bf16[128,2304]{1,0:T(8,128)(2,1)S(1)} %bitcast.102), channel_id=1, source_target_pairs={{0,8},{4,12},{8,0},{12,4},{16,24},{20,28},{24,16},{28,20},{1,9},{5... | collective-permute-start | bytes 1769480 | tf_op jit(solution)/shard_map/ppermute | solution.py:76
  47.2 25.8 %collective-permute-start.6 = (bf16[128,2304]{1,0:T(8,128)(2,1)}, bf16[128,2304]{1,0:T(8,128)(2,1)}, u32[]{:S(2)}, u32[]{:S(2)}) collective-permute-start(bf16[128,2304]{1,0:T(8,128)(2,1)} %collective-permute-done.2.s2), channel_id=1, source_target_pairs={{0,8},{4,12},{8,0},{12,4},{16,24},{20,28},{24,16},{28,20},{1,9},{5... | collective-permute-start | bytes 1769480 | tf_op jit(solution)/shard_map/ppermute | solution.py:76
  48.3 24.7 %collective-permute-start.4 = (bf16[288,768]{1,0:T(8,128)(2,1)}, bf16[288,768]{1,0:T(8,128)(2,1)}, u32[]{:S(2)}, u32[]{:S(2)}) collective-permute-start(bf16[288,768]{1,0:T(8,128)(2,1)} %slice.69), channel_id=1, source_target_pairs={{0,2},{1,3},{2,0},{3,1},{4,6},{5,7},{6,4},{7,5},{8,10},{9,11},{10,... | collective-permute-start | bytes 1327112 | tf_op jit(solution)/shard_map/ppermute | solution.py:76
  49.1 23.9 %collective-permute-start.5 = (bf16[288,768]{1,0:T(8,128)(2,1)}, bf16[288,768]{1,0:T(8,128)(2,1)}, u32[]{:S(2)}, u32[]{:S(2)}) collective-permute-start(bf16[288,768]{1,0:T(8,128)(2,1)} %slice.70), channel_id=1, source_target_pairs={{0,1},{1,0},{2,3},{3,2},{4,5},{5,4},{6,7},{7,6},{8,9},{9,8},{10,11... | collective-permute-start | bytes 1327112 | tf_op jit(solution)/shard_map/ppermute | solution.py:76
  49.4 20.0 %collective-permute-start.7 = (bf16[4,576]{1,0:T(4,128)(2,1)S(1)}, bf16[4,576]{1,0:T(4,128)(2,1)S(1)}, u32[]{:S(2)}, u32[]{:S(2)}) collective-permute-start(bf16[4,576]{1,0:T(4,128)(2,1)S(1)} %bitcast.116), channel_id=1, source_target_pairs={{0,1},{1,0},{2,3},{3,2},{4,5},{5,4},{6,7},{7,6},{8,9},{9,8},{10,11... | collective-permute-start | bytes 13832 | tf_op jit(solution)/shard_map/ppermute | solution.py:76
  50.6 20.1 %collective-permute-start.8 = (bf16[4,576]{1,0:T(4,128)(2,1)S(1)}, bf16[4,576]{1,0:T(4,128)(2,1)}, u32[]{:S(2)}, u32[]{:S(2)}) collective-permute-start(bf16[4,576]{1,0:T(4,128)(2,1)S(1)} %bitcast.117), channel_id=1, source_target_pairs={{0,2},{1,3},{2,0},{3,1},{4,6},{5,7},{6,4},{7,5},{8,10},{9,11},{10,... | collective-permute-start | bytes 13832 | tf_op jit(solution)/shard_map/ppermute | solution.py:76
  69.5 3.5 collective-permute-start.9
  75.2 17.9 %collective-permute-start.10 = (bf16[2304,768]{1,0:T(8,128)(2,1)S(1)}, bf16[2304,768]{1,0:T(8,128)(2,1)}, u32[]{:S(2)}, u32[]{:S(2)}) collective-permute-start(bf16[2304,768]{1,0:T(8,128)(2,1)S(1)} %constant_dynamic-update-slice_fusion.w0), channel_id=1, source_target_pairs={{0,4},{4,0},{8,12},{12,8},{16,20},{20,16},{24,28},{28,24},{1,5},{5... | collective-permute-start | bytes 10616840 | tf_op jit(solution)/shard_map/ppermute | solution.py:76
  100.6 2.2 collective-permute-start.11
  112.4 15.2 %collective-permute-start.12 = (bf16[128,2304]{1,0:T(8,128)(2,1)}, bf16[128,2304]{1,0:T(8,128)(2,1)S(1)}, u32[]{:S(2)}, u32[]{:S(2)}) collective-permute-start(bf16[128,2304]{1,0:T(8,128)(2,1)} %get-tuple-element.139), channel_id=1, source_target_pairs={{0,8},{4,12},{8,0},{12,4},{16,24},{20,28},{24,16},{28,20},{1,9},{5... | collective-permute-start | bytes 1769480 | tf_op jit(solution)/shard_map/ppermute | solution.py:76
  127.6 23.9 %collective-permute-start.13 = (bf16[128,2304]{1,0:T(8,128)(2,1)}, bf16[128,2304]{1,0:T(8,128)(2,1)S(1)}, u32[]{:S(2)}, u32[]{:S(2)}) collective-permute-start(bf16[128,2304]{1,0:T(8,128)(2,1)} %get-tuple-element.140), channel_id=1, source_target_pairs={{0,8},{4,12},{8,0},{12,4},{16,24},{20,28},{24,16},{28,20},{1,9},{5... | collective-permute-start | bytes 1769480 | tf_op jit(solution)/shard_map/ppermute | solution.py:76
  129.0 26.7 %collective-permute-start.14 = (bf16[128,2304]{1,0:T(8,128)(2,1)S(1)}, bf16[128,2304]{1,0:T(8,128)(2,1)S(1)}, u32[]{:S(2)}, u32[]{:S(2)}) collective-permute-start(bf16[128,2304]{1,0:T(8,128)(2,1)S(1)} %add_convert_fusion.4), channel_id=1, source_target_pairs={{0,16},{4,20},{8,24},{12,28},{16,0},{20,4},{24,8},{28,12},{1,17},{... | collective-permute-start | bytes 1769480 | tf_op jit(solution)/shard_map/ppermute | solution.py:76
  157.9 26.6 %collective-permute-start.15 = (bf16[128,2304]{1,0:T(8,128)(2,1)S(1)}, bf16[128,2304]{1,0:T(8,128)(2,1)S(1)}, u32[]{:S(2)}, u32[]{:S(2)}) collective-permute-start(bf16[128,2304]{1,0:T(8,128)(2,1)S(1)} %multiply_convert_fusion.1.refs_0_), channel_id=1, source_target_pairs={{0,16},{4,20},{8,24},{12,28},{16,0},{20,4},{24,8},{28,12},{1,17},{... | collective-permute-start | bytes 1769480 | tf_op jit(solution)/shard_map/ppermute | solution.py:76
  161.1 23.5 %collective-permute-start.16 = (bf16[128,2304]{1,0:T(8,128)(2,1)S(1)}, bf16[128,2304]{1,0:T(8,128)(2,1)S(1)}, u32[]{:S(2)}, u32[]{:S(2)}) collective-permute-start(bf16[128,2304]{1,0:T(8,128)(2,1)S(1)} %multiply_convert_fusion.1.refs_0_), channel_id=1, source_target_pairs={{0,8},{4,12},{8,0},{12,4},{16,24},{20,28},{24,16},{28,20},{1,9},{5... | collective-permute-start | bytes 1769480 | tf_op jit(solution)/shard_map/ppermute | solution.py:76
  185.4 14.9 %collective-permute-start.17 = (bf16[128,2304]{1,0:T(8,128)(2,1)S(1)}, bf16[128,2304]{1,0:T(8,128)(2,1)}, u32[]{:S(2)}, u32[]{:S(2)}) collective-permute-start(bf16[128,2304]{1,0:T(8,128)(2,1)S(1)} %collective-permute-done.15.refs_1_), channel_id=1, source_target_pairs={{0,8},{4,12},{8,0},{12,4},{16,24},{20,28},{24,16},{28,20},{1,9},{5... | collective-permute-start | bytes 1769480 | tf_op jit(solution)/shard_map/ppermute | solution.py:76
  222.4 13.2 %collective-permute-start.18 = (bf16[128,2304]{1,0:T(8,128)(2,1)}, bf16[128,2304]{1,0:T(8,128)(2,1)S(1)}, u32[]{:S(2)}, u32[]{:S(2)}) collective-permute-start(bf16[128,2304]{1,0:T(8,128)(2,1)} %get-tuple-element.158.refs_1_), channel_id=1, source_target_pairs={{0,8},{4,12},{8,0},{12,4},{16,24},{20,28},{24,16},{28,20},{1,9},{5... | collective-permute-start | bytes 1769480 | tf_op jit(solution)/shard_map/ppermute | solution.py:76
  235.6 23.3 %collective-permute-start.19 = (bf16[128,2304]{1,0:T(8,128)(2,1)S(1)}, bf16[128,2304]{1,0:T(8,128)(2,1)S(1)}, u32[]{:S(2)}, u32[]{:S(2)}) collective-permute-start(bf16[128,2304]{1,0:T(8,128)(2,1)S(1)} %copy-done.37), channel_id=1, source_target_pairs={{0,8},{4,12},{8,0},{12,4},{16,24},{20,28},{24,16},{28,20},{1,9},{5... | collective-permute-start | bytes 1769480 | tf_op jit(solution)/shard_map/ppermute | solution.py:76
  238.1 24.7 %collective-permute-start.20 = (bf16[128,2304]{1,0:T(8,128)(2,1)S(1)}, bf16[128,2304]{1,0:T(8,128)(2,1)S(1)}, u32[]{:S(2)}, u32[]{:S(2)}) collective-permute-start(bf16[128,2304]{1,0:T(8,128)(2,1)S(1)} %add_convert_fusion.3), channel_id=1, source_target_pairs={{0,16},{4,20},{8,24},{12,28},{16,0},{20,4},{24,8},{28,12},{1,17},{... | collective-permute-start | bytes 1769480 | tf_op jit(solution)/shard_map/ppermute | solution.py:76
  240.9 26.2 %collective-permute-start.23 = (bf16[128,2304]{1,0:T(8,128)(2,1)S(1)}, bf16[128,2304]{1,0:T(8,128)(2,1)S(1)}, u32[]{:S(2)}, u32[]{:S(2)}) collective-permute-start(bf16[128,2304]{1,0:T(8,128)(2,1)S(1)} %copy-done.24), channel_id=1, source_target_pairs={{0,4},{4,0},{8,12},{12,8},{16,20},{20,16},{24,28},{28,24},{1,5},{5... | collective-permute-start | bytes 1769480 | tf_op jit(solution)/shard_map/ppermute | solution.py:76
  244.5 24.8 %collective-permute-start.24 = (bf16[128,2304]{1,0:T(8,128)(2,1)}, bf16[128,2304]{1,0:T(8,128)(2,1)S(1)}, u32[]{:S(2)}, u32[]{:S(2)}) collective-permute-start(bf16[128,2304]{1,0:T(8,128)(2,1)} %copy-done.39), channel_id=1, source_target_pairs={{0,4},{4,0},{8,12},{12,8},{16,20},{20,16},{24,28},{28,24},{1,5},{5... | collective-permute-start | bytes 1769480 | tf_op jit(solution)/shard_map/ppermute | solution.py:76
  244.5 24.8 %collective-permute-start.25 = (bf16[128,2304]{1,0:T(8,128)(2,1)}, bf16[128,2304]{1,0:T(8,128)(2,1)S(1)}, u32[]{:S(2)}, u32[]{:S(2)}) collective-permute-start(bf16[128,2304]{1,0:T(8,128)(2,1)} %copy-done.40), channel_id=1, source_target_pairs={{0,4},{4,0},{8,12},{12,8},{16,20},{20,16},{24,28},{28,24},{1,5},{5... | collective-permute-start | bytes 1769480 | tf_op jit(solution)/shard_map/ppermute | solution.py:76
  258.9 10.4 %collective-permute-start.21 = (bf16[1,256,1152]{2,1,0:T(8,128)(2,1)S(1)}, bf16[1,256,1152]{2,1,0:T(8,128)(2,1)S(1)}, u32[]{:S(2)}, u32[]{:S(2)}) collective-permute-start(bf16[1,256,1152]{2,1,0:T(8,128)(2,1)S(1)} %copy-done.34), channel_id=1, source_target_pairs={{0,4},{4,0},{8,12},{12,8},{16,20},{20,16},{24,28},{28,24},{1,5},{5... | collective-permute-start | bytes 1769480 | tf_op jit(solution)/shard_map/ppermute | solution.py:76
  262.7 6.6 %collective-permute-start.22 = (bf16[1,256,1152]{2,1,0:T(8,128)(2,1)S(1)}, bf16[1,256,1152]{2,1,0:T(8,128)(2,1)S(1)}, u32[]{:S(2)}, u32[]{:S(2)}) collective-permute-start(bf16[1,256,1152]{2,1,0:T(8,128)(2,1)S(1)} %copy-done.35), channel_id=1, source_target_pairs={{0,4},{4,0},{8,12},{12,8},{16,20},{20,16},{24,28},{28,24},{1,5},{5... | collective-permute-start | bytes 1769480 | tf_op jit(solution)/shard_map/ppermute | solution.py:76
  267.2 2.7 collective-permute-start.26
  272.9 26.7 %collective-permute-start.27 = (bf16[128,2304]{1,0:T(8,128)(2,1)S(1)}, bf16[128,2304]{1,0:T(8,128)(2,1)S(1)}, u32[]{:S(2)}, u32[]{:S(2)}) collective-permute-start(bf16[128,2304]{1,0:T(8,128)(2,1)S(1)} %get-tuple-element.288.refs_0_), channel_id=1, source_target_pairs={{0,16},{4,20},{8,24},{12,28},{16,0},{20,4},{24,8},{28,12},{1,17},{... | collective-permute-start | bytes 1769480 | tf_op jit(solution)/shard_map/ppermute | solution.py:76
  276.0 24.6 %collective-permute-start.28 = (bf16[128,2304]{1,0:T(8,128)(2,1)S(1)}, bf16[128,2304]{1,0:T(8,128)(2,1)}, u32[]{:S(2)}, u32[]{:S(2)}) collective-permute-start(bf16[128,2304]{1,0:T(8,128)(2,1)S(1)} %get-tuple-element.288.refs_0_), channel_id=1, source_target_pairs={{0,8},{4,12},{8,0},{12,4},{16,24},{20,28},{24,16},{28,20},{1,9},{5... | collective-permute-start | bytes 1769480 | tf_op jit(solution)/shard_map/ppermute | solution.py:76
  300.6 14.8 %collective-permute-start.29 = (bf16[128,2304]{1,0:T(8,128)(2,1)S(1)}, bf16[128,2304]{1,0:T(8,128)(2,1)}, u32[]{:S(2)}, u32[]{:S(2)}) collective-permute-start(bf16[128,2304]{1,0:T(8,128)(2,1)S(1)} %collective-permute-done.27.refs_1_), channel_id=1, source_target_pairs={{0,8},{4,12},{8,0},{12,4},{16,24},{20,28},{24,16},{28,20},{1,9},{5... | collective-permute-start | bytes 1769480 | tf_op jit(solution)/shard_map/ppermute | solution.py:76
  302.6 23.9 %collective-permute-start.30 = (bf16[128,2304]{1,0:T(8,128)(2,1)S(1)}, bf16[128,2304]{1,0:T(8,128)(2,1)}, u32[]{:S(2)}, u32[]{:S(2)}) collective-permute-start(bf16[128,2304]{1,0:T(8,128)(2,1)S(1)} %get-tuple-element.288.refs_0_), channel_id=1, source_target_pairs={{0,4},{4,0},{8,12},{12,8},{16,20},{20,16},{24,28},{28,24},{1,5},{5... | collective-permute-start | bytes 1769480 | tf_op jit(solution)/shard_map/ppermute | solution.py:76
  303.9 22.6 %collective-permute-start.31 = (bf16[128,2304]{1,0:T(8,128)(2,1)S(1)}, bf16[128,2304]{1,0:T(8,128)(2,1)}, u32[]{:S(2)}, u32[]{:S(2)}) collective-permute-start(bf16[128,2304]{1,0:T(8,128)(2,1)S(1)} %collective-permute-done.27.refs_1_), channel_id=1, source_target_pairs={{0,4},{4,0},{8,12},{12,8},{16,20},{20,16},{24,28},{28,24},{1,5},{5... | collective-permute-start | bytes 1769480 | tf_op jit(solution)/shard_map/ppermute | solution.py:76
  303.9 22.6 %collective-permute-start.32 = (bf16[128,2304]{1,0:T(8,128)(2,1)}, bf16[128,2304]{1,0:T(8,128)(2,1)}, u32[]{:S(2)}, u32[]{:S(2)}) collective-permute-start(bf16[128,2304]{1,0:T(8,128)(2,1)} %collective-permute-done.28.refs_0_.refs_2_), channel_id=1, source_target_pairs={{0,4},{4,0},{8,12},{12,8},{16,20},{20,16},{24,28},{28,24},{1,5},{5... | collective-permute-start | bytes 1769480 | tf_op jit(solution)/shard_map/ppermute | solution.py:76
  315.4 11.2 %collective-permute-start.33 = (bf16[128,2304]{1,0:T(8,128)(2,1)}, bf16[128,2304]{1,0:T(8,128)(2,1)}, u32[]{:S(2)}, u32[]{:S(2)}) collective-permute-start(bf16[128,2304]{1,0:T(8,128)(2,1)} %collective-permute-done.29.refs_1_.refs_3_), channel_id=1, source_target_pairs={{0,4},{4,0},{8,12},{12,8},{16,20},{20,16},{24,28},{28,24},{1,5},{5... | collective-permute-start | bytes 1769480 | tf_op jit(solution)/shard_map/ppermute | solution.py:76
  337.4 190.4 %reduce-scatter.5.cloned.1.call-start = ((), (), s32[]{:S(2)}) async-start(), calls=%async_computation.8 | async-start | bytes 13271040 | tf_op jit(solution)/shard_map/reduce_scatter | solution.py:729
  350.7 15.2 %collective-permute-start.34 = (bf16[128,2304]{1,0:T(8,128)(2,1)}, bf16[128,2304]{1,0:T(8,128)(2,1)S(1)}, u32[]{:S(2)}, u32[]{:S(2)}) collective-permute-start(bf16[128,2304]{1,0:T(8,128)(2,1)} %get-tuple-element.189.refs_1_), channel_id=1, source_target_pairs={{0,8},{4,12},{8,0},{12,4},{16,24},{20,28},{24,16},{28,20},{1,9},{5... | collective-permute-start | bytes 1769480 | tf_op jit(solution)/shard_map/ppermute | solution.py:76
  351.4 19.0 %collective-permute-start.38 = (bf16[2,256,1152]{2,1,0:T(8,128)(2,1)}, bf16[2,256,1152]{2,1,0:T(8,128)(2,1)}, u32[]{:S(2)}, u32[]{:S(2)}) collective-permute-start(bf16[2,256,1152]{2,1,0:T(8,128)(2,1)} %get-tuple-element.187.d1), channel_id=1, source_target_pairs={{0,4},{4,0},{8,12},{12,8},{16,20},{20,16},{24,28},{28,24},{1,5},{5... | collective-permute-start | bytes 3538952 | tf_op jit(solution)/shard_map/ppermute | solution.py:76
  351.8 18.5 %collective-permute-start.37 = (bf16[2,256,1152]{2,1,0:T(8,128)(2,1)}, bf16[2,256,1152]{2,1,0:T(8,128)(2,1)}, u32[]{:S(2)}, u32[]{:S(2)}) collective-permute-start(bf16[2,256,1152]{2,1,0:T(8,128)(2,1)} %get-tuple-element.185.d1), channel_id=1, source_target_pairs={{0,4},{4,0},{8,12},{12,8},{16,20},{20,16},{24,28},{28,24},{1,5},{5... | collective-permute-start | bytes 3538952 | tf_op jit(solution)/shard_map/ppermute | solution.py:76
  365.9 23.1 %collective-permute-start.35 = (bf16[128,2304]{1,0:T(8,128)(2,1)}, bf16[128,2304]{1,0:T(8,128)(2,1)S(1)}, u32[]{:S(2)}, u32[]{:S(2)}) collective-permute-start(bf16[128,2304]{1,0:T(8,128)(2,1)} %get-tuple-element.192.refs_0_), channel_id=1, source_target_pairs={{0,8},{4,12},{8,0},{12,4},{16,24},{20,28},{24,16},{28,20},{1,9},{5... | collective-permute-start | bytes 1769480 | tf_op jit(solution)/shard_map/ppermute | solution.py:76
  368.4 26.4 %collective-permute-start.36 = (bf16[128,2304]{1,0:T(8,128)(2,1)}, bf16[128,2304]{1,0:T(8,128)(2,1)S(1)}, u32[]{:S(2)}, u32[]{:S(2)}) collective-permute-start(bf16[128,2304]{1,0:T(8,128)(2,1)} %add_convert_fusion.1), channel_id=1, source_target_pairs={{0,16},{4,20},{8,24},{12,28},{16,0},{20,4},{24,8},{28,12},{1,17},{... | collective-permute-start | bytes 1769480 | tf_op jit(solution)/shard_map/ppermute | solution.py:76
  402.3 27.7 %collective-permute-start.39 = (bf16[128,2304]{1,0:T(8,128)(2,1)S(1)}, bf16[128,2304]{1,0:T(8,128)(2,1)S(1)}, u32[]{:S(2)}, u32[]{:S(2)}) collective-permute-start(bf16[128,2304]{1,0:T(8,128)(2,1)S(1)} %multiply_convert_fusion.s0.refs_0_), channel_id=1, source_target_pairs={{0,16},{4,20},{8,24},{12,28},{16,0},{20,4},{24,8},{28,12},{1,17},{... | collective-permute-start | bytes 1769480 | tf_op jit(solution)/shard_map/ppermute | solution.py:76
  405.4 24.7 %collective-permute-start.40 = (bf16[128,2304]{1,0:T(8,128)(2,1)S(1)}, bf16[128,2304]{1,0:T(8,128)(2,1)S(1)}, u32[]{:S(2)}, u32[]{:S(2)}) collective-permute-start(bf16[128,2304]{1,0:T(8,128)(2,1)S(1)} %multiply_convert_fusion.s0.refs_0_), channel_id=1, source_target_pairs={{0,8},{4,12},{8,0},{12,4},{16,24},{20,28},{24,16},{28,20},{1,9},{5... | collective-permute-start | bytes 1769480 | tf_op jit(solution)/shard_map/ppermute | solution.py:76
  430.1 16.2 %collective-permute-start.41 = (bf16[128,2304]{1,0:T(8,128)(2,1)S(1)}, bf16[128,2304]{1,0:T(8,128)(2,1)}, u32[]{:S(2)}, u32[]{:S(2)}) collective-permute-start(bf16[128,2304]{1,0:T(8,128)(2,1)S(1)} %collective-permute-done.39.s2.refs_2_), channel_id=1, source_target_pairs={{0,8},{4,12},{8,0},{12,4},{16,24},{20,28},{24,16},{28,20},{1,9},{5... | collective-permute-start | bytes 1769480 | tf_op jit(solution)/shard_map/ppermute | solution.py:76
  433.1 55.9 %collective-permute-start.44 = (bf16[512,2304]{1,0:T(8,128)(2,1)}, bf16[512,2304]{1,0:T(8,128)(2,1)}, u32[]{:S(2)}, u32[]{:S(2)}) collective-permute-start(bf16[512,2304]{1,0:T(8,128)(2,1)} %get-tuple-element.217.refs_0_), channel_id=1, source_target_pairs={{0,4},{4,0},{8,12},{12,8},{16,20},{20,16},{24,28},{28,24},{1,5},{5... | collective-permute-start | bytes 7077896 | tf_op jit(solution)/shard_map/ppermute | solution.py:76
  446.3 52.6 %all-to-all-start = ((bf16[8,72,1152]{2,1,0:T(8,128)(2,1)}), bf16[8,72,1152]{2,1,0:T(8,128)(2,1)}, u32[]{:S(2)}, u32[]{:S(2)}) async-start(bf16[8,72,1152]{2,1,0:T(8,128)(2,1)} %bitcast.110), calls=%async_computation.1 | async-start | bytes 2654208 | tf_op jit(solution)/shard_map/all_to_all | solution.py:660
  465.9 3.7 collective-permute-start.42
  466.4 14.0 %collective-permute-start.46 = (bf16[128,2304]{1,0:T(8,128)(2,1)S(1)}, bf16[128,2304]{1,0:T(8,128)(2,1)S(1)}, u32[]{:S(2)}, u32[]{:S(2)}) collective-permute-start(bf16[128,2304]{1,0:T(8,128)(2,1)S(1)} %copy-done.15), channel_id=1, source_target_pairs={{0,4},{4,0},{8,12},{12,8},{16,20},{20,16},{24,28},{28,24},{1,5},{5... | collective-permute-start | bytes 1769480 | tf_op jit(solution)/shard_map/ppermute | solution.py:76
  466.5 2.7 collective-permute-start.50
  466.9 16.9 %collective-permute-start.47 = (bf16[128,2304]{1,0:T(8,128)(2,1)S(1)}, bf16[128,2304]{1,0:T(8,128)(2,1)}, u32[]{:S(2)}, u32[]{:S(2)}) collective-permute-start(bf16[128,2304]{1,0:T(8,128)(2,1)S(1)} %copy-done.32), channel_id=1, source_target_pairs={{0,4},{4,0},{8,12},{12,8},{16,20},{20,16},{24,28},{28,24},{1,5},{5... | collective-permute-start | bytes 1769480 | tf_op jit(solution)/shard_map/ppermute | solution.py:76
  469.2 14.6 %collective-permute-start.48 = (bf16[128,2304]{1,0:T(8,128)(2,1)S(1)}, bf16[128,2304]{1,0:T(8,128)(2,1)}, u32[]{:S(2)}, u32[]{:S(2)}) collective-permute-start(bf16[128,2304]{1,0:T(8,128)(2,1)S(1)} %copy-done.30), channel_id=1, source_target_pairs={{0,4},{4,0},{8,12},{12,8},{16,20},{20,16},{24,28},{28,24},{1,5},{5... | collective-permute-start | bytes 1769480 | tf_op jit(solution)/shard_map/ppermute | solution.py:76
  469.9 13.9 %collective-permute-start.49 = (bf16[128,2304]{1,0:T(8,128)(2,1)}, bf16[128,2304]{1,0:T(8,128)(2,1)}, u32[]{:S(2)}, u32[]{:S(2)}) collective-permute-start(bf16[128,2304]{1,0:T(8,128)(2,1)} %collective-permute-done.41.s3.refs_3_), channel_id=1, source_target_pairs={{0,4},{4,0},{8,12},{12,8},{16,20},{20,16},{24,28},{28,24},{1,5},{5... | collective-permute-start | bytes 1769480 | tf_op jit(solution)/shard_map/ppermute | solution.py:76
  480.4 8.6 %collective-permute-start.45 = (bf16[1,512,512]{2,1,0:T(8,128)(2,1)}, bf16[1,512,512]{2,1,0:T(8,128)(2,1)}, u32[]{:S(2)}, u32[]{:S(2)}) collective-permute-start(bf16[1,512,512]{2,1,0:T(8,128)(2,1)} %get-tuple-element.219), channel_id=1, source_target_pairs={{0,4},{4,0},{8,12},{12,8},{16,20},{20,16},{24,28},{28,24},{1,5},{5... | collective-permute-start | bytes 1572872 | tf_op jit(solution)/shard_map/ppermute | solution.py:76
  483.7 15.2 %collective-permute-start.43 = (bf16[128,2304]{1,0:T(8,128)(2,1)}, bf16[128,2304]{1,0:T(8,128)(2,1)}, u32[]{:S(2)}, u32[]{:S(2)}) collective-permute-start(bf16[128,2304]{1,0:T(8,128)(2,1)} %get-tuple-element.215), channel_id=1, source_target_pairs={{0,8},{4,12},{8,0},{12,4},{16,24},{20,28},{24,16},{28,20},{1,9},{5... | collective-permute-start | bytes 1769480 | tf_op jit(solution)/shard_map/ppermute | solution.py:76
  498.9 25.3 %collective-permute-start.51 = (bf16[128,2304]{1,0:T(8,128)(2,1)}, bf16[128,2304]{1,0:T(8,128)(2,1)}, u32[]{:S(2)}, u32[]{:S(2)}) collective-permute-start(bf16[128,2304]{1,0:T(8,128)(2,1)} %get-tuple-element.223), channel_id=1, source_target_pairs={{0,8},{4,12},{8,0},{12,4},{16,24},{20,28},{24,16},{28,20},{1,9},{5... | collective-permute-start | bytes 1769480 | tf_op jit(solution)/shard_map/ppermute | solution.py:76
  501.0 26.7 %collective-permute-start.52 = (bf16[128,2304]{1,0:T(8,128)(2,1)S(1)}, bf16[128,2304]{1,0:T(8,128)(2,1)}, u32[]{:S(2)}, u32[]{:S(2)}) collective-permute-start(bf16[128,2304]{1,0:T(8,128)(2,1)S(1)} %add_convert_fusion), channel_id=1, source_target_pairs={{0,16},{4,20},{8,24},{12,28},{16,0},{20,4},{24,8},{28,12},{1,17},{... | collective-permute-start | bytes 1769480 | tf_op jit(solution)/shard_map/ppermute | solution.py:76
  505.7 12.2 %collective-permute-start.53 = (bf16[288,772]{1,0:T(8,128)(2,1)S(1)}, bf16[288,772]{1,0:T(8,128)(2,1)S(1)}, u32[]{:S(2)}, u32[]{:S(2)}) collective-permute-start(bf16[288,772]{1,0:T(8,128)(2,1)S(1)} %get-tuple-element.281), channel_id=1, source_target_pairs={{0,1},{1,0},{2,3},{3,2},{4,5},{5,4},{6,7},{7,6},{8,9},{9,8},{10,11... | collective-permute-start | bytes 1334024 | tf_op jit(solution)/shard_map/ppermute | solution.py:76
  506.0 11.9 %collective-permute-start.54 = (bf16[288,772]{1,0:T(8,128)(2,1)S(1)}, bf16[288,772]{1,0:T(8,128)(2,1)S(1)}, u32[]{:S(2)}, u32[]{:S(2)}) collective-permute-start(bf16[288,772]{1,0:T(8,128)(2,1)S(1)} %get-tuple-element.283), channel_id=1, source_target_pairs={{0,2},{1,3},{2,0},{3,1},{4,6},{5,7},{6,4},{7,5},{8,10},{9,11},{10,... | collective-permute-start | bytes 1334024 | tf_op jit(solution)/shard_map/ppermute | solution.py:76
  527.7 65.4 %all-to-all-start.1 = ((bf16[8,72,2304]{2,1,0:T(8,128)(2,1)}), bf16[8,72,2304]{2,1,0:T(8,128)(2,1)}, u32[]{:S(2)}, u32[]{:S(2)}) async-start(bf16[8,72,2304]{2,1,0:T(8,128)(2,1)} %bitcast.107), calls=%async_computation.3 | async-start | bytes 5308416 | tf_op jit(solution)/shard_map/all_to_all | solution.py:660
  542.9 23.5 %collective-permute-start.56 = (bf16[576,772]{0,1:T(8,128)(2,1)}, bf16[576,772]{0,1:T(8,128)(2,1)}, u32[]{:S(2)}, u32[]{:S(2)}) collective-permute-start(bf16[576,772]{0,1:T(8,128)(2,1)} %copy.41), channel_id=1, source_target_pairs={{0,2},{1,3},{2,0},{3,1},{4,6},{5,7},{6,4},{7,5},{8,10},{9,11},{10,... | collective-permute-start | bytes 2668040 | tf_op jit(solution)/shard_map/ppermute | solution.py:76
  546.2 23.2 %collective-permute-start.55 = (bf16[576,772]{0,1:T(8,128)(2,1)}, bf16[576,772]{0,1:T(8,128)(2,1)}, u32[]{:S(2)}, u32[]{:S(2)}) collective-permute-start(bf16[576,772]{0,1:T(8,128)(2,1)} %copy.39), channel_id=1, source_target_pairs={{0,1},{1,0},{2,3},{3,2},{4,5},{5,4},{6,7},{7,6},{8,9},{9,8},{10,11... | collective-permute-start | bytes 2668040 | tf_op jit(solution)/shard_map/ppermute | solution.py:76
  593.1 29.8 %all-to-all-start.2 = ((bf16[8,72,772]{2,1,0:T(8,128)(2,1)}), bf16[8,72,772]{2,1,0:T(8,128)(2,1)S(1)}, u32[]{:S(2)}, u32[]{:S(2)}) async-start(bf16[8,72,772]{2,1,0:T(8,128)(2,1)} %bitcast.28), calls=%async_computation.4 | async-start | bytes 2064384 | tf_op jit(solution)/shard_map/all_to_all | solution.py:660
  (64 other events, 581.0 us)
Sparse Core Ops, SparseCore 0:
  12.6 130.3 all-gather.2
  145.4 64.2 all-gather.4
  337.5 61.7 reduce-scatter.2
  402.2 104.6 reduce-scatter.4

commit v6 on v5

--- a/solution.py
+++ b/solution.py
@@ -664,6 +664,34 @@
     return terms.astype(F32).transpose(1, 0, 2).reshape(terms.shape[1], -1)
 
 
+def whole_kernel(body, out_shape, *values):
+    return pl.pallas_call(
+        body,
+        out_shape=out_shape,
+        compiler_params=pltpu.CompilerParams(vmem_limit_bytes=VMEM_BYTES),
+        cost_estimate=pl.CostEstimate(
+            flops=0, bytes_accessed=sum(v.size * v.dtype.itemsize for v in values), transcendentals=0
+        ),
+    )(*values)
+
+
+def residual_backward(terms, residual, branch, upstream, g_mid, g_post):
+    def body(t0, t1, t2, res, br, up, gm, gp, d_res, d_br, gain_mid, gain_post):
+        d_mid = sum_of((t0[...], t1[...], t2[...]))
+        value, scale = res[...], inverse_rms(res[...])
+        gain_mid[...] = jnp.sum(d_mid * value * scale, 0, keepdims=True)
+        total = up[...].astype(F32) + norm_backward(value, scale, d_mid * gm[...])
+        d_res[...] = total
+        value, scale = br[...], inverse_rms(br[...])
+        gain_post[...] = jnp.sum(total * value * scale, 0, keepdims=True)
+        d_br[...] = norm_backward(value, scale, total * gp[...]).astype(BF16)
+
+    shape, width = residual.shape, residual.shape[1]
+    outs = [jax.ShapeDtypeStruct(shape, F32), jax.ShapeDtypeStruct(shape, BF16)]
+    outs += [jax.ShapeDtypeStruct((1, width), F32)] * 2
+    return whole_kernel(body, outs, *terms, residual, branch, upstream, g_mid, g_post)
+
+
 def attention_outputs(terms, columns):
     count, rows, _ = terms.shape
     size = HEAD_DIM
@@ -791,7 +819,7 @@
     def own_rows(halves, beside=()):
         parts = [halves[k % 2][k // 2] for k in range(4)]
         terms, _, beside = four_scatter(parts, ctx_count, (), lambda first: beside)
-        return sum_of(terms), beside
+        return terms, beside
 
     def gathered_halves(values, work):
         slots = four_gather(values, ctx_count)
@@ -811,7 +839,7 @@
     hidden_own = [f[0] for f in forward]
     hidden_got = [partner(f[1]) for f in forward]
     mid_got = [partner(v) for v in mids]
-    mixed = own_rows((mixed_0, mixed_1))[0]
+    mixed = sum_of(own_rows((mixed_0, mixed_1))[0])
     mixed, hidden_own, hidden_got, mid_got = together(mixed, hidden_own, hidden_got, mid_got)
     scale_mixed = inverse_rms(mixed)
     block_out = (residual + mixed * scale_mixed * g_out).astype(BF16)
@@ -838,12 +866,10 @@
     )
     d_mid, (gate_up_product,) = own_rows((d_mid_0, d_mid_1), (gate_up_product,))
     gate_up_total = over_sequences(gate_up_product)
-    grad_mid_gain = jnp.sum(d_mid * residual * scale_mid, 0)
-    d_residual = upstream + norm_backward(residual, scale_mid, d_mid * g_mid)
-    grad_post_gain = jnp.sum(d_residual * branch * scale_branch, 0)
-    d_branches = four_gather(
-        norm_backward(branch, scale_branch, d_residual * g_post).astype(BF16), ctx_count
-    )
+    d_residual, d_branch, grad_mid_gain, grad_post_gain = residual_backward(
+        d_mid, residual, branch, output_grad.reshape(tokens, width), gains[2:3], gains[1:2]
+    )
+    d_branches = four_gather(d_branch, ctx_count)
 
     d_branches, down_total = together(d_branches, down_total)
     down = to_owners(down_total, ctx_count)
@@ -852,7 +878,7 @@
         inputs, d_queries, dkv_own, partner(dkv_other), attn, cosine, sine, core_word
     )
 
-    gain_terms = jnp.stack([grad_pre_gain[0], grad_post_gain, grad_mid_gain, grad_out_gain], 1)
+    gain_terms = jnp.stack([grad_pre_gain[0], grad_post_gain[0], grad_mid_gain[0], grad_out_gain], 1)
     gain_terms = gain_terms.reshape(ctx_count, fsdp_count, shard_rows, 4)
     gain_terms = gain_terms.transpose(1, 0, 2, 3).reshape(fsdp_count, -1, 4)
     out_product = weight_grad(

time: 643 us -> 639 us (level)
  transfers between devices with their start and end apart: 64 -> 64, of which waited for: 31 -> 29; matrix products, arithmetic and copies ran while one was open for 11% -> 10% of each run, Pallas kernels for 24% -> 25%
where the time goes in v6:
time: 639 us; the launch traced here: 632 us
  waiting for transfers between devices  272 us (43%)
  Pallas kernels  177 us (28%)
  starting transfers between devices  86.5 us (14%)
  local copies, waits for them, and re-layouts  43.9 us (7%)
  other arithmetic  37.7 us (6%)
  between operations  14.8 us (2%)
    ppermute x57, waiting for transfers between devices, swap(): return lax.ppermute(values, axis, [(i, i ^ distance) for i in range(count)])  238 us
    ppermute x57, starting transfers between devices, swap(): return lax.ppermute(values, axis, [(i, i ^ distance) for i in range(count)])  64.7 us
    pallas_call x4, Pallas kernels, weight_grad_kernel(): kernel_call(body, (halves, groups, steps), [pl.BlockSpec((n, part), lambd...  40.5 us
    all_to_all x3, waiting for transfers between devices, to_owners(): return lax.all_to_all(total, 'ctx', split_axis=0, concat_axis=0, tiled=True)  34.1 us
    pallas_call x2, Pallas kernels, gate_up_forward(): kernel_call(body, (2, steps), whole_of(values) + [pl.BlockSpec((1, width,...  29 us
    pallas_call x2, Pallas kernels, gate_up_backward(): kernel_call(body, (width // tile,), [whole, whole, pl.BlockSpec((1, tile,...  26.8 us
    all_to_all x3, starting transfers between devices, to_owners(): return lax.all_to_all(total, 'ctx', split_axis=0, concat_axis=0, tiled=True)  21.7 us
    pallas_call x2, Pallas kernels, down_backward(): kernel_call(body, (2, steps), whole_of(d_mixed) + [saved, saved, pl.Block...  19.1 us
  transfers between devices with their start and end apart: 64, of which 29 were waited for; matrix products, arithmetic and copies ran while one was open for 10% of the time, Pallas kernels for 25%

profile of v6, /device:TPU:13, one launch (start us, length us, event | category | flops | bytes accessed | tf_op | source)
XLA Modules:
  0.0 631.6 jit_solution(11965159809747813892)
XLA Ops:
  8.5 2.3 constant_dynamic-slice_fusion.2
  12.6 2.5 constant_dynamic-slice_fusion
  16.6 2.3 collective-permute-start.2
  19.1 25.4 %collective-permute-done.2.s2 = bf16[128,2304]{1,0:T(8,128)(2,1)} collective-permute-done((bf16[128,2304]{1,0:T(8,128)(2,1)S(1)}, bf16[128,2304]{1,0:T(8,128)(2,1)}, u32[]{:S(2)}, u32[]{:S(2)}) %collective-permute-start.2) | collective-permute-done | bytes 589856 | tf_op jit(solution)/shard_map/ppermute | solution.py:76
  54.5 15.0 %collective-permute-done.7 = bf16[4,576]{1,0:T(4,128)(2,1)S(1)} collective-permute-done((bf16[4,576]{1,0:T(4,128)(2,1)S(1)}, bf16[4,576]{1,0:T(4,128)(2,1)S(1)}, u32[]{:S(2)}, u32[]{:S(2)}) %collective-permute-start.7) | collective-permute-done | bytes 4640 | tf_op jit(solution)/shard_map/ppermute | solution.py:76
  70.7 2.3 collective-permute-done.9
  75.1 6.8 %collective-permute-start.10 = (bf16[2304,768]{1,0:T(8,128)(2,1)S(1)}, bf16[2304,768]{1,0:T(8,128)(2,1)}, u32[]{:S(2)}, u32[]{:S(2)}) collective-permute-start(bf16[2304,768]{1,0:T(8,128)(2,1)S(1)} %constant_dynamic-update-slice_fusion.w0), channel_id=1, source_target_pairs={{0,4},{4,0},{8,12},{12,8},{16,20},{20,16},{24,28},{28,24},{1,5},{5... | collective-permute-start | bytes 10616840 | tf_op jit(solution)/shard_map/ppermute | solution.py:76
  93.0 7.6 %shard_map.109 = (bf16[512,2304]{1,0:T(8,128)(2,1)}, bf16[512,256]{1,0:T(8,128)(2,1)}, bf16[512,256]{1,0:T(8,128)(2,1)}, bf16[512,512]{1,0:T(8,128)(2,1)}) custom-call(s32[1]{0:T(128)} %bitcast.1.core_ref, bf16[128,2304]{1,0:T(8,128)(2,1)} %bitcast.96, bf16[128,2304]{1,0:T(8,128)(2,1)} %copy-done.11, bf16[128,2304]{1,0:T(8,128)(2,1)} %collective-permute-done.2.s2, ...), custom_call_target="tpu_custom_call" | custom-call | flops 2415919104 | bytes 9437184 | tf_op jit(solution)/shard_map/pallas_call | solution.py:446
  103.6 8.7 %shard_map.110 = (bf16[512,256]{1,0:T(8,128)(2,1)}, bf16[512,256]{1,0:T(8,128)(2,1)}, bf16[128,2304]{1,0:T(8,128)(2,1)}, bf16[128,2304]{1,0:T(8,128)(2,1)}, bf16...) custom-call(s32[1]{0:T(128)} %bitcast.1.core_ref, bf16[512,256]{1,0:T(8,128)(2,1)} %get-tuple-element.137.q0, ...), custom_call_target="tpu_custom_call" | custom-call | flops 2281701376 | bytes 4718592 | tf_op jit(solution)/shard_map/pallas_call | solution.py:528
  112.8 14.8 %collective-permute-done.12 = bf16[128,2304]{1,0:T(8,128)(2,1)S(1)} collective-permute-done((bf16[128,2304]{1,0:T(8,128)(2,1)}, bf16[128,2304]{1,0:T(8,128)(2,1)S(1)}, u32[]{:S(2)}, u32[]{:S(2)}) %collective-permute-start.12) | collective-permute-done | bytes 589856 | tf_op jit(solution)/shard_map/ppermute | solution.py:76
  129.0 2.4 collective-permute-start.14
  132.2 19.3 %collective-permute-done.13 = bf16[128,2304]{1,0:T(8,128)(2,1)S(1)} collective-permute-done((bf16[128,2304]{1,0:T(8,128)(2,1)}, bf16[128,2304]{1,0:T(8,128)(2,1)S(1)}, u32[]{:S(2)}, u32[]{:S(2)}) %collective-permute-start.13) | collective-permute-done | bytes 589856 | tf_op jit(solution)/shard_map/ppermute | solution.py:76
  151.5 4.2 collective-permute-done.14
  157.5 3.0 collective-permute-start.15
  160.5 23.5 %collective-permute-done.15.refs_1_ = bf16[128,2304]{1,0:T(8,128)(2,1)S(1)} collective-permute-done((bf16[128,2304]{1,0:T(8,128)(2,1)S(1)}, bf16[128,2304]{1,0:T(8,128)(2,1)S(1)}, u32[]{:S(2)}, u32[]{:S(2)}) %collective-permute-start.15) | collective-permute-done | bytes 589856 | tf_op jit(solution)/shard_map/ppermute | solution.py:76
  184.9 14.6 %shard_map.111 = (bf16[1,256,1152]{2,1,0:T(8,128)(2,1)}, bf16[1,256,1152]{2,1,0:T(8,128)(2,1)}, f32[2,256,1152]{2,1,0:T(8,128)}, f32[2,256,1152]{2,1,0:T(8,128)}) custom-call(s32[1]{0:T(128)} %bitcast.1.core_ref, bf16[128,2304]{1,0:T(8,128)(2,1)} %copy-done.14, bf16[128,2304]{1,0:T(8,128)(2,1)} %copy-done.37, bf16[2,2304,2304]{2,1,0:T(8,128)(2,1)} %bitcast.82, ...), custom_call_target="tpu_custom_call" | custom-call | flops 5435817984 | bytes 27131904 | tf_op jit(solution)/shard_map/pallas_call | solution.py:251
  200.3 14.4 %shard_map.112 = (bf16[1,256,1152]{2,1,0:T(8,128)(2,1)}, bf16[1,256,1152]{2,1,0:T(8,128)(2,1)}, f32[2,256,1152]{2,1,0:T(8,128)}, f32[2,256,1152]{2,1,0:T(8,128)}) custom-call(s32[1]{0:T(128)} %bitcast.1.core_ref, bf16[128,2304]{1,0:T(8,128)(2,1)} %copy-done.38, bf16[128,2304]{1,0:T(8,128)(2,1)} %copy-done.39, bf16[2,2304,2304]{2,1,0:T(8,128)(2,1)} %bitcast.84, ...), custom_call_target="tpu_custom_call" | custom-call | flops 5435817984 | bytes 27131904 | tf_op jit(solution)/shard_map/pallas_call | solution.py:251
  214.8 7.6 %shard_map.113 = (bf16[128,2304]{1,0:T(8,128)(2,1)}, bf16[128,2304]{1,0:T(8,128)(2,1)}) custom-call(s32[1]{0:T(128)} %bitcast.1.core_ref, bf16[1,256,1152]{2,1,0:T(8,128)(2,1)} %get-tuple-element.185.h0.refs_9_, bf16[1,256,1152]{2,1,0:T(8,128)(2,1)} %get-tuple-element.160.h1, bf16[2,2304,1152]{2,1,0:T(8,128)(2,1)} %bitcast.90, bf16[2,2304,1152]{2,1,0:T(8,128)(2,1)} %bitcast.91), custom_call_target="tpu_custom_call" | custom-call | flops 2717908992 | bytes 11796480 | tf_op jit(solution)/shard_map/pallas_call | solution.py:280
  223.2 8.2 %shard_map.114 = (bf16[128,2304]{1,0:T(8,128)(2,1)}, bf16[128,2304]{1,0:T(8,128)(2,1)}) custom-call(s32[1]{0:T(128)} %bitcast.1.core_ref, bf16[1,256,1152]{2,1,0:T(8,128)(2,1)} %get-tuple-element.184.h0.refs_8_, bf16[1,256,1152]{2,1,0:T(8,128)(2,1)} %get-tuple-element.156.h1, bf16[2,2304,1152]{2,1,0:T(8,128)(2,1)} %bitcast.92, ...), custom_call_target="tpu_custom_call" | custom-call | flops 2717908992 | bytes 11796480 | tf_op jit(solution)/shard_map/pallas_call | solution.py:280
  231.4 4.9 collective-permute-done.18
  237.7 3.0 collective-permute-start.20
  240.7 3.4 collective-permute-start.23
  244.6 13.2 %collective-permute-done.19 = bf16[128,2304]{1,0:T(8,128)(2,1)S(1)} collective-permute-done((bf16[128,2304]{1,0:T(8,128)(2,1)S(1)}, bf16[128,2304]{1,0:T(8,128)(2,1)S(1)}, u32[]{:S(2)}, u32[]{:S(2)}) %collective-permute-start.19) | collective-permute-done | bytes 589856 | tf_op jit(solution)/shard_map/ppermute | solution.py:76
  257.8 3.6 collective-permute-start.21
  262.7 4.3 collective-permute-start.22
  272.9 3.1 collective-permute-start.27
  276.0 24.4 %collective-permute-done.27.refs_1_ = bf16[128,2304]{1,0:T(8,128)(2,1)S(1)} collective-permute-done((bf16[128,2304]{1,0:T(8,128)(2,1)S(1)}, bf16[128,2304]{1,0:T(8,128)(2,1)S(1)}, u32[]{:S(2)}, u32[]{:S(2)}) %collective-permute-start.27) | collective-permute-done | bytes 589856 | tf_op jit(solution)/shard_map/ppermute | solution.py:76
  300.9 2.8 collective-permute-start.29
  305.1 9.5 %shard_map.115 = (bf16[2,256,1152]{2,1,0:T(8,128)(2,1)}, bf16[2,256,1152]{2,1,0:T(8,128)(2,1)}) custom-call(s32[1]{0:T(128)} %bitcast.1.core_ref, bf16[128,2304]{1,0:T(8,128)(2,1)} %copy-done.13, bf16[128,2304]{1,0:T(8,128)(2,1)} %copy-done.31, f32[2,256,1152]{2,1,0:T(8,128)} %get-tuple-element.172.refs_2_, f32[2,256,1152]{2,1,0:T(8,128)} %get-tuple-element.173.refs_3_, ...), custom_call_target="tpu_custom_call" | custom-call | flops 2717908992 | bytes 17694720 | tf_op jit(solution)/shard_map/pallas_call | solution.py:328
  318.0 9.5 %shard_map.116 = (bf16[2,256,1152]{2,1,0:T(8,128)(2,1)}, bf16[2,256,1152]{2,1,0:T(8,128)(2,1)}) custom-call(s32[1]{0:T(128)} %bitcast.1.core_ref, bf16[128,2304]{1,0:T(8,128)(2,1)} %copy-done.32, bf16[128,2304]{1,0:T(8,128)(2,1)} %copy-done.33, f32[2,256,1152]{2,1,0:T(8,128)} %get-tuple-element.180.refs_2_, f32[2,256,1152]{2,1,0:T(8,128)} %get-tuple-element.181.refs_3_, ...), custom_call_target="tpu_custom_call" | custom-call | flops 2717908992 | bytes 17694720 | tf_op jit(solution)/shard_map/pallas_call | solution.py:328
  328.6 10.7 %shard_map.117 = bf16[4,576,1152]{2,1,0:T(8,128)(2,1)} custom-call(bf16[128,2304]{1,0:T(8,128)(2,1)} %copy-done.13, bf16[128,2304]{1,0:T(8,128)(2,1)} %copy-done.31, bf16[128,2304]{1,0:T(8,128)(2,1)} %copy-done.32, bf16[128,2304]{1,0:T(8,128)(2,1)} %copy-done.33, bf16[128,2304]{1,0:T(8,128)(2,1)} %copy-done.58, bf16[128,2304]{1,0:T(8,128)(2,1)} %copy-done.59, ...), custom_call_target="tpu_custom_call" | custom-call | flops 5435817984 | bytes 19464192 | tf_op jit(solution)/shard_map/pallas_call | solution.py:403
  339.4 14.1 %shard_map.118 = (bf16[128,2304]{1,0:T(8,128)(2,1)}, bf16[128,2304]{1,0:T(8,128)(2,1)}) custom-call(s32[1]{0:T(128)} %bitcast.1.core_ref, bf16[2,256,1152]{2,1,0:T(8,128)(2,1)} %get-tuple-element.190.d0.refs_9_, bf16[2,256,1152]{2,1,0:T(8,128)(2,1)} %get-tuple-element.191.d1, bf16[2,2304,2304]{2,1,0:T(8,128)(2,1)} %bitcast.86, bf16[2,2304,2304]{2,1,0:T(8,128)(2,1)} %bitcast.87), custom_call_target="tpu_custom_call" | custom-call | flops 5435817984 | bytes 23592960 | tf_op jit(solution)/shard_map/pallas_call | solution.py:354
  356.1 12.6 %shard_map.119 = (bf16[128,2304]{1,0:T(8,128)(2,1)}, bf16[128,2304]{1,0:T(8,128)(2,1)}) custom-call(s32[1]{0:T(128)} %bitcast.1.core_ref, bf16[2,256,1152]{2,1,0:T(8,128)(2,1)} %get-tuple-element.188.d0.refs_8_, bf16[2,256,1152]{2,1,0:T(8,128)(2,1)} %get-tuple-element.189.d1, bf16[2,2304,2304]{2,1,0:T(8,128)(2,1)} %bitcast.88, ...), custom_call_target="tpu_custom_call" | custom-call | flops 5435817984 | bytes 23592960 | tf_op jit(solution)/shard_map/pallas_call | solution.py:354
  371.6 18.7 %shard_map.120 = bf16[4,576,2304]{2,1,0:T(8,128)(2,1)} custom-call(bf16[128,2304]{1,0:T(8,128)(2,1)} %copy-done.14, bf16[128,2304]{1,0:T(8,128)(2,1)} %copy-done.37, bf16[128,2304]{1,0:T(8,128)(2,1)} %copy-done.38, bf16[128,2304]{1,0:T(8,128)(2,1)} %copy-done.39, bf16[128,2304]{1,0:T(8,128)(2,1)} %copy-done.52, bf16[128,2304]{1,0:T(8,128)(2,1)} %copy-done.53, ...), custom_call_target="tpu_custom_call" | custom-call | flops 10871635968 | bytes 29491200 | tf_op jit(solution)/shard_map/pallas_call | solution.py:403
  391.3 4.8 collective-permute-done.36.t2
  397.0 4.9 shard_map.121
  401.8 3.1 collective-permute-start.39
  405.0 25.6 %collective-permute-done.39.s2.refs_2_ = bf16[128,2304]{1,0:T(8,128)(2,1)S(1)} collective-permute-done((bf16[128,2304]{1,0:T(8,128)(2,1)}, bf16[128,2304]{1,0:T(8,128)(2,1)S(1)}, u32[]{:S(2)}, u32[]{:S(2)}) %collective-permute-start.39) | collective-permute-done | bytes 589856 | tf_op jit(solution)/shard_map/ppermute | solution.py:76
  430.6 2.3 collective-permute-start.41
  433.9 12.0 %collective-permute-done.41.s3.refs_3_ = bf16[128,2304]{1,0:T(8,128)(2,1)} collective-permute-done((bf16[128,2304]{1,0:T(8,128)(2,1)S(1)}, bf16[128,2304]{1,0:T(8,128)(2,1)}, u32[]{:S(2)}, u32[]{:S(2)}) %collective-permute-start.41) | collective-permute-done | bytes 589856 | tf_op jit(solution)/shard_map/ppermute | solution.py:76
  445.9 6.5 %all-to-all-start = ((bf16[8,72,1152]{2,1,0:T(8,128)(2,1)}), bf16[8,72,1152]{2,1,0:T(8,128)(2,1)S(1)}, u32[]{:S(2)}, u32[]{:S(2)}) async-start(bf16[8,72,1152]{2,1,0:T(8,128)(2,1)} %bitcast.109), calls=%async_computation.1 | async-start | bytes 2654208 | tf_op jit(solution)/shard_map/all_to_all | solution.py:660
  452.5 12.3 %shard_map.122 = (bf16[512,256]{1,0:T(8,128)(2,1)}, bf16[512,256]{1,0:T(8,128)(2,1)}, f32[512,512]{1,0:T(8,128)}, bf16[512,512]{1,0:T(8,128)(2,1)}) custom-call(s32[1]{0:T(128)} %bitcast.1.core_ref, bf16[512,256]{1,0:T(8,128)(2,1)} %get-tuple-element.137.q0, bf16[512,256]{1,0:T(8,128)(2,1)} %get-tuple-element.138.q1, ...), custom_call_target="tpu_custom_call" | custom-call | flops 3892314112 | bytes 4718592 | tf_op jit(solution)/shard_map/pallas_call | solution.py:589
  468.4 9.7 %shard_map.123 = (bf16[128,2304]{1,0:T(8,128)(2,1)}, bf16[128,2304]{1,0:T(8,128)(2,1)}, bf16[128,2304]{1,0:T(8,128)(2,1)}, bf16[128,2304]{1,0:T(8,128)(2,1)}, bf...) custom-call(s32[1]{0:T(128)} %bitcast.1.core_ref, bf16[128,2304]{1,0:T(8,128)(2,1)} %bitcast.97, ...), custom_call_target="tpu_custom_call" | custom-call | flops 2415919104 | bytes 9437184 | tf_op jit(solution)/shard_map/pallas_call | solution.py:637
  480.3 4.9 shard_map.125
  486.0 6.2 shard_map.124
  492.2 3.4 pad_maximum_fusion
  500.7 2.5 dynamic-slice_bitcast_fusion.3
  504.2 13.5 %collective-permute-done.53 = bf16[288,772]{1,0:T(8,128)(2,1)S(1)} collective-permute-done((bf16[288,772]{1,0:T(8,128)(2,1)S(1)}, bf16[288,772]{1,0:T(8,128)(2,1)S(1)}, u32[]{:S(2)}, u32[]{:S(2)}) %collective-permute-start.53) | collective-permute-done | bytes 444704 | tf_op jit(solution)/shard_map/ppermute | solution.py:76
  517.6 3.9 collective-permute-done.51
  521.5 4.0 collective-permute-done.52
  525.6 7.5 %all-to-all-start.1 = ((bf16[8,72,2304]{2,1,0:T(8,128)(2,1)}), bf16[8,72,2304]{2,1,0:T(8,128)(2,1)S(1)}, u32[]{:S(2)}, u32[]{:S(2)}) async-start(bf16[8,72,2304]{2,1,0:T(8,128)(2,1)} %bitcast.106), calls=%async_computation.3 | async-start | bytes 5308416 | tf_op jit(solution)/shard_map/all_to_all | solution.py:660
  536.3 2.4 fusion.18
  539.8 2.3 copy.43
  544.2 2.4 copy.41
  549.4 2.8 fusion.10
  552.2 13.4 %collective-permute-done.56 = bf16[576,772]{0,1:T(8,128)(2,1)} collective-permute-done((bf16[576,772]{0,1:T(8,128)(2,1)}, bf16[576,772]{0,1:T(8,128)(2,1)}, u32[]{:S(2)}, u32[]{:S(2)}) %collective-permute-start.56) | collective-permute-done | bytes 889376 | tf_op jit(solution)/shard_map/ppermute | solution.py:76
  565.6 2.3 copy.44
  570.1 2.4 copy.42
  572.5 3.2 fusion.1
  575.6 14.8 %all-to-all-done.1 = bf16[8,72,2304]{2,1,0:T(8,128)(2,1)S(1)} async-done(((bf16[8,72,2304]{2,1,0:T(8,128)(2,1)}), bf16[8,72,2304]{2,1,0:T(8,128)(2,1)S(1)}, u32[]{:S(2)}, u32[]{:S(2)}) %all-to-all-start.1) | async-done | bytes 2654240 | tf_op jit(solution)/shard_map/all_to_all | solution.py:660
  590.5 7.7 %all-to-all-start.2 = ((bf16[8,72,772]{2,1,0:T(8,128)(2,1)}), bf16[8,72,772]{2,1,0:T(8,128)(2,1)}, u32[]{:S(2)}, u32[]{:S(2)}) async-start(bf16[8,72,772]{2,1,0:T(8,128)(2,1)} %bitcast.105), calls=%async_computation.4 | async-start | bytes 2064384 | tf_op jit(solution)/shard_map/all_to_all | solution.py:660
  598.7 2.8 maximum_convert_fusion
  601.5 19.3 %all-to-all-done.2.t = bf16[8,72,772]{2,1,0:T(8,128)(2,1)} async-done(((bf16[8,72,772]{2,1,0:T(8,128)(2,1)}), bf16[8,72,772]{2,1,0:T(8,128)(2,1)}, u32[]{:S(2)}, u32[]{:S(2)}) %all-to-all-start.2) | async-done | bytes 889376 | tf_op jit(solution)/shard_map/all_to_all | solution.py:660
  620.8 2.5 shard_map.126
  (284 shorter events, 88.5 us)
Async XLA Ops:
  7.2 177.0 %all-gather.3.cloned.1.call-start = ((), (), s32[]{:S(2)}) async-start(), calls=%async_computation.5 | async-start | bytes 23887872 | tf_op jit(solution)/shard_map/all_gather | solution.py:750
  12.5 202.2 %all-gather.5.cloned.1.call-start = ((), (), s32[]{:S(2)}) async-start(), calls=%async_computation.6 | async-start | bytes 11943936 | tf_op jit(solution)/shard_map/all_gather | solution.py:750
  15.1 430.8 %reduce-scatter.3.cloned.1.call-start = ((), (), s32[]{:S(2)}) async-start(), calls=%async_computation.7 | async-start | bytes 6635520 | tf_op jit(solution)/shard_map/reduce_scatter | solution.py:757
  15.1 29.8 %collective-permute-start = (bf16[576,768]{1,0:T(8,128)(2,1)S(1)}, bf16[576,768]{1,0:T(8,128)(2,1)S(1)}, u32[]{:S(2)}, u32[]{:S(2)}) collective-permute-start(bf16[576,768]{1,0:T(8,128)(2,1)S(1)} %pad_maximum_fusion.4), channel_id=1, source_target_pairs={{0,1},{1,0},{2,3},{3,2},{4,5},{5,4},{6,7},{7,6},{8,9},{9,8},{10,11... | collective-permute-start | bytes 2654216 | tf_op jit(solution)/shard_map/ppermute | solution.py:76
  16.4 30.8 %collective-permute-start.1 = (bf16[576,768]{1,0:T(8,128)(2,1)S(1)}, bf16[576,768]{1,0:T(8,128)(2,1)S(1)}, u32[]{:S(2)}, u32[]{:S(2)}) collective-permute-start(bf16[576,768]{1,0:T(8,128)(2,1)S(1)} %pad_maximum_fusion.4), channel_id=1, source_target_pairs={{0,2},{1,3},{2,0},{3,1},{4,6},{5,7},{6,4},{7,5},{8,10},{9,11},{10,... | collective-permute-start | bytes 2654216 | tf_op jit(solution)/shard_map/ppermute | solution.py:76
  16.6 27.9 %collective-permute-start.2 = (bf16[128,2304]{1,0:T(8,128)(2,1)S(1)}, bf16[128,2304]{1,0:T(8,128)(2,1)}, u32[]{:S(2)}, u32[]{:S(2)}) collective-permute-start(bf16[128,2304]{1,0:T(8,128)(2,1)S(1)} %bitcast.98), channel_id=1, source_target_pairs={{0,16},{4,20},{8,24},{12,28},{16,0},{20,4},{24,8},{28,12},{1,17},{... | collective-permute-start | bytes 1769480 | tf_op jit(solution)/shard_map/ppermute | solution.py:76
  19.0 25.6 %collective-permute-start.3 = (bf16[128,2304]{1,0:T(8,128)(2,1)S(1)}, bf16[128,2304]{1,0:T(8,128)(2,1)S(1)}, u32[]{:S(2)}, u32[]{:S(2)}) collective-permute-start(bf16[128,2304]{1,0:T(8,128)(2,1)S(1)} %bitcast.99), channel_id=1, source_target_pairs={{0,8},{4,12},{8,0},{12,4},{16,24},{20,28},{24,16},{28,20},{1,9},{5... | collective-permute-start | bytes 1769480 | tf_op jit(solution)/shard_map/ppermute | solution.py:76
  47.2 25.8 %collective-permute-start.6 = (bf16[128,2304]{1,0:T(8,128)(2,1)}, bf16[128,2304]{1,0:T(8,128)(2,1)}, u32[]{:S(2)}, u32[]{:S(2)}) collective-permute-start(bf16[128,2304]{1,0:T(8,128)(2,1)} %collective-permute-done.2.s2), channel_id=1, source_target_pairs={{0,8},{4,12},{8,0},{12,4},{16,24},{20,28},{24,16},{28,20},{1,9},{5... | collective-permute-start | bytes 1769480 | tf_op jit(solution)/shard_map/ppermute | solution.py:76
  48.3 24.7 %collective-permute-start.4 = (bf16[288,768]{1,0:T(8,128)(2,1)}, bf16[288,768]{1,0:T(8,128)(2,1)}, u32[]{:S(2)}, u32[]{:S(2)}) collective-permute-start(bf16[288,768]{1,0:T(8,128)(2,1)} %slice.71), channel_id=1, source_target_pairs={{0,2},{1,3},{2,0},{3,1},{4,6},{5,7},{6,4},{7,5},{8,10},{9,11},{10,... | collective-permute-start | bytes 1327112 | tf_op jit(solution)/shard_map/ppermute | solution.py:76
  49.1 23.9 %collective-permute-start.5 = (bf16[288,768]{1,0:T(8,128)(2,1)}, bf16[288,768]{1,0:T(8,128)(2,1)}, u32[]{:S(2)}, u32[]{:S(2)}) collective-permute-start(bf16[288,768]{1,0:T(8,128)(2,1)} %slice.72), channel_id=1, source_target_pairs={{0,1},{1,0},{2,3},{3,2},{4,5},{5,4},{6,7},{7,6},{8,9},{9,8},{10,11... | collective-permute-start | bytes 1327112 | tf_op jit(solution)/shard_map/ppermute | solution.py:76
  49.4 20.0 %collective-permute-start.7 = (bf16[4,576]{1,0:T(4,128)(2,1)S(1)}, bf16[4,576]{1,0:T(4,128)(2,1)S(1)}, u32[]{:S(2)}, u32[]{:S(2)}) collective-permute-start(bf16[4,576]{1,0:T(4,128)(2,1)S(1)} %bitcast.115), channel_id=1, source_target_pairs={{0,1},{1,0},{2,3},{3,2},{4,5},{5,4},{6,7},{7,6},{8,9},{9,8},{10,11... | collective-permute-start | bytes 13832 | tf_op jit(solution)/shard_map/ppermute | solution.py:76
  50.6 20.1 %collective-permute-start.8 = (bf16[4,576]{1,0:T(4,128)(2,1)S(1)}, bf16[4,576]{1,0:T(4,128)(2,1)}, u32[]{:S(2)}, u32[]{:S(2)}) collective-permute-start(bf16[4,576]{1,0:T(4,128)(2,1)S(1)} %bitcast.116), channel_id=1, source_target_pairs={{0,2},{1,3},{2,0},{3,1},{4,6},{5,7},{6,4},{7,5},{8,10},{9,11},{10,... | collective-permute-start | bytes 13832 | tf_op jit(solution)/shard_map/ppermute | solution.py:76
  69.5 3.5 collective-permute-start.9
  75.1 17.9 %collective-permute-start.10 = (bf16[2304,768]{1,0:T(8,128)(2,1)S(1)}, bf16[2304,768]{1,0:T(8,128)(2,1)}, u32[]{:S(2)}, u32[]{:S(2)}) collective-permute-start(bf16[2304,768]{1,0:T(8,128)(2,1)S(1)} %constant_dynamic-update-slice_fusion.w0), channel_id=1, source_target_pairs={{0,4},{4,0},{8,12},{12,8},{16,20},{20,16},{24,28},{28,24},{1,5},{5... | collective-permute-start | bytes 10616840 | tf_op jit(solution)/shard_map/ppermute | solution.py:76
  100.6 2.2 collective-permute-start.11
  112.4 15.2 %collective-permute-start.12 = (bf16[128,2304]{1,0:T(8,128)(2,1)}, bf16[128,2304]{1,0:T(8,128)(2,1)S(1)}, u32[]{:S(2)}, u32[]{:S(2)}) collective-permute-start(bf16[128,2304]{1,0:T(8,128)(2,1)} %get-tuple-element.143), channel_id=1, source_target_pairs={{0,8},{4,12},{8,0},{12,4},{16,24},{20,28},{24,16},{28,20},{1,9},{5... | collective-permute-start | bytes 1769480 | tf_op jit(solution)/shard_map/ppermute | solution.py:76
  127.6 24.0 %collective-permute-start.13 = (bf16[128,2304]{1,0:T(8,128)(2,1)}, bf16[128,2304]{1,0:T(8,128)(2,1)S(1)}, u32[]{:S(2)}, u32[]{:S(2)}) collective-permute-start(bf16[128,2304]{1,0:T(8,128)(2,1)} %get-tuple-element.144), channel_id=1, source_target_pairs={{0,8},{4,12},{8,0},{12,4},{16,24},{20,28},{24,16},{28,20},{1,9},{5... | collective-permute-start | bytes 1769480 | tf_op jit(solution)/shard_map/ppermute | solution.py:76
  129.0 26.7 %collective-permute-start.14 = (bf16[128,2304]{1,0:T(8,128)(2,1)S(1)}, bf16[128,2304]{1,0:T(8,128)(2,1)S(1)}, u32[]{:S(2)}, u32[]{:S(2)}) collective-permute-start(bf16[128,2304]{1,0:T(8,128)(2,1)S(1)} %add_convert_fusion.4), channel_id=1, source_target_pairs={{0,16},{4,20},{8,24},{12,28},{16,0},{20,4},{24,8},{28,12},{1,17},{... | collective-permute-start | bytes 1769480 | tf_op jit(solution)/shard_map/ppermute | solution.py:76
  157.5 26.6 %collective-permute-start.15 = (bf16[128,2304]{1,0:T(8,128)(2,1)S(1)}, bf16[128,2304]{1,0:T(8,128)(2,1)S(1)}, u32[]{:S(2)}, u32[]{:S(2)}) collective-permute-start(bf16[128,2304]{1,0:T(8,128)(2,1)S(1)} %multiply_convert_fusion.refs_0_), channel_id=1, source_target_pairs={{0,16},{4,20},{8,24},{12,28},{16,0},{20,4},{24,8},{28,12},{1,17},{... | collective-permute-start | bytes 1769480 | tf_op jit(solution)/shard_map/ppermute | solution.py:76
  160.5 23.5 %collective-permute-start.16 = (bf16[128,2304]{1,0:T(8,128)(2,1)S(1)}, bf16[128,2304]{1,0:T(8,128)(2,1)S(1)}, u32[]{:S(2)}, u32[]{:S(2)}) collective-permute-start(bf16[128,2304]{1,0:T(8,128)(2,1)S(1)} %multiply_convert_fusion.refs_0_), channel_id=1, source_target_pairs={{0,8},{4,12},{8,0},{12,4},{16,24},{20,28},{24,16},{28,20},{1,9},{5... | collective-permute-start | bytes 1769480 | tf_op jit(solution)/shard_map/ppermute | solution.py:76
  184.1 15.4 %collective-permute-start.17 = (bf16[128,2304]{1,0:T(8,128)(2,1)S(1)}, bf16[128,2304]{1,0:T(8,128)(2,1)S(1)}, u32[]{:S(2)}, u32[]{:S(2)}) collective-permute-start(bf16[128,2304]{1,0:T(8,128)(2,1)S(1)} %collective-permute-done.15.refs_1_), channel_id=1, source_target_pairs={{0,8},{4,12},{8,0},{12,4},{16,24},{20,28},{24,16},{28,20},{1,9},{5... | collective-permute-start | bytes 1769480 | tf_op jit(solution)/shard_map/ppermute | solution.py:76
  222.4 13.8 %collective-permute-start.18 = (bf16[128,2304]{1,0:T(8,128)(2,1)}, bf16[128,2304]{1,0:T(8,128)(2,1)S(1)}, u32[]{:S(2)}, u32[]{:S(2)}) collective-permute-start(bf16[128,2304]{1,0:T(8,128)(2,1)} %get-tuple-element.162.refs_1_), channel_id=1, source_target_pairs={{0,8},{4,12},{8,0},{12,4},{16,24},{20,28},{24,16},{28,20},{1,9},{5... | collective-permute-start | bytes 1769480 | tf_op jit(solution)/shard_map/ppermute | solution.py:76
  236.2 21.6 %collective-permute-start.19 = (bf16[128,2304]{1,0:T(8,128)(2,1)S(1)}, bf16[128,2304]{1,0:T(8,128)(2,1)S(1)}, u32[]{:S(2)}, u32[]{:S(2)}) collective-permute-start(bf16[128,2304]{1,0:T(8,128)(2,1)S(1)} %copy-done.34), channel_id=1, source_target_pairs={{0,8},{4,12},{8,0},{12,4},{16,24},{20,28},{24,16},{28,20},{1,9},{5... | collective-permute-start | bytes 1769480 | tf_op jit(solution)/shard_map/ppermute | solution.py:76
  237.7 25.0 %collective-permute-start.20 = (bf16[128,2304]{1,0:T(8,128)(2,1)S(1)}, bf16[128,2304]{1,0:T(8,128)(2,1)S(1)}, u32[]{:S(2)}, u32[]{:S(2)}) collective-permute-start(bf16[128,2304]{1,0:T(8,128)(2,1)S(1)} %add_convert_fusion.3), channel_id=1, source_target_pairs={{0,16},{4,20},{8,24},{12,28},{16,0},{20,4},{24,8},{28,12},{1,17},{... | collective-permute-start | bytes 1769480 | tf_op jit(solution)/shard_map/ppermute | solution.py:76
  240.7 26.2 %collective-permute-start.23 = (bf16[128,2304]{1,0:T(8,128)(2,1)S(1)}, bf16[128,2304]{1,0:T(8,128)(2,1)S(1)}, u32[]{:S(2)}, u32[]{:S(2)}) collective-permute-start(bf16[128,2304]{1,0:T(8,128)(2,1)S(1)} %copy-done.15), channel_id=1, source_target_pairs={{0,4},{4,0},{8,12},{12,8},{16,20},{20,16},{24,28},{28,24},{1,5},{5... | collective-permute-start | bytes 1769480 | tf_op jit(solution)/shard_map/ppermute | solution.py:76
  244.1 24.4 %collective-permute-start.24 = (bf16[128,2304]{1,0:T(8,128)(2,1)}, bf16[128,2304]{1,0:T(8,128)(2,1)S(1)}, u32[]{:S(2)}, u32[]{:S(2)}) collective-permute-start(bf16[128,2304]{1,0:T(8,128)(2,1)} %copy-done.37), channel_id=1, source_target_pairs={{0,4},{4,0},{8,12},{12,8},{16,20},{20,16},{24,28},{28,24},{1,5},{5... | collective-permute-start | bytes 1769480 | tf_op jit(solution)/shard_map/ppermute | solution.py:76
  244.1 24.4 %collective-permute-start.25 = (bf16[128,2304]{1,0:T(8,128)(2,1)}, bf16[128,2304]{1,0:T(8,128)(2,1)S(1)}, u32[]{:S(2)}, u32[]{:S(2)}) collective-permute-start(bf16[128,2304]{1,0:T(8,128)(2,1)} %copy-done.38), channel_id=1, source_target_pairs={{0,4},{4,0},{8,12},{12,8},{16,20},{20,16},{24,28},{28,24},{1,5},{5... | collective-permute-start | bytes 1769480 | tf_op jit(solution)/shard_map/ppermute | solution.py:76
  257.8 10.7 %collective-permute-start.21 = (bf16[1,256,1152]{2,1,0:T(8,128)(2,1)S(1)}, bf16[1,256,1152]{2,1,0:T(8,128)(2,1)S(1)}, u32[]{:S(2)}, u32[]{:S(2)}) collective-permute-start(bf16[1,256,1152]{2,1,0:T(8,128)(2,1)S(1)} %copy-done.29), channel_id=1, source_target_pairs={{0,4},{4,0},{8,12},{12,8},{16,20},{20,16},{24,28},{28,24},{1,5},{5... | collective-permute-start | bytes 1769480 | tf_op jit(solution)/shard_map/ppermute | solution.py:76
  262.7 5.9 collective-permute-start.22
  266.9 2.7 collective-permute-start.26
  272.9 27.5 %collective-permute-start.27 = (bf16[128,2304]{1,0:T(8,128)(2,1)S(1)}, bf16[128,2304]{1,0:T(8,128)(2,1)S(1)}, u32[]{:S(2)}, u32[]{:S(2)}) collective-permute-start(bf16[128,2304]{1,0:T(8,128)(2,1)S(1)} %get-tuple-element.293.refs_0_), channel_id=1, source_target_pairs={{0,16},{4,20},{8,24},{12,28},{16,0},{20,4},{24,8},{28,12},{1,17},{... | collective-permute-start | bytes 1769480 | tf_op jit(solution)/shard_map/ppermute | solution.py:76
  276.0 25.0 %collective-permute-start.28 = (bf16[128,2304]{1,0:T(8,128)(2,1)S(1)}, bf16[128,2304]{1,0:T(8,128)(2,1)S(1)}, u32[]{:S(2)}, u32[]{:S(2)}) collective-permute-start(bf16[128,2304]{1,0:T(8,128)(2,1)S(1)} %get-tuple-element.293.refs_0_), channel_id=1, source_target_pairs={{0,8},{4,12},{8,0},{12,4},{16,24},{20,28},{24,16},{28,20},{1,9},{5... | collective-permute-start | bytes 1769480 | tf_op jit(solution)/shard_map/ppermute | solution.py:76
  300.9 15.9 %collective-permute-start.29 = (bf16[128,2304]{1,0:T(8,128)(2,1)S(1)}, bf16[128,2304]{1,0:T(8,128)(2,1)S(1)}, u32[]{:S(2)}, u32[]{:S(2)}) collective-permute-start(bf16[128,2304]{1,0:T(8,128)(2,1)S(1)} %collective-permute-done.27.refs_1_), channel_id=1, source_target_pairs={{0,8},{4,12},{8,0},{12,4},{16,24},{20,28},{24,16},{28,20},{1,9},{5... | collective-permute-start | bytes 1769480 | tf_op jit(solution)/shard_map/ppermute | solution.py:76
  303.7 23.8 %collective-permute-start.30 = (bf16[128,2304]{1,0:T(8,128)(2,1)S(1)}, bf16[128,2304]{1,0:T(8,128)(2,1)S(1)}, u32[]{:S(2)}, u32[]{:S(2)}) collective-permute-start(bf16[128,2304]{1,0:T(8,128)(2,1)S(1)} %get-tuple-element.293.refs_0_), channel_id=1, source_target_pairs={{0,4},{4,0},{8,12},{12,8},{16,20},{20,16},{24,28},{28,24},{1,5},{5... | collective-permute-start | bytes 1769480 | tf_op jit(solution)/shard_map/ppermute | solution.py:76
  304.6 22.9 %collective-permute-start.31 = (bf16[128,2304]{1,0:T(8,128)(2,1)S(1)}, bf16[128,2304]{1,0:T(8,128)(2,1)S(1)}, u32[]{:S(2)}, u32[]{:S(2)}) collective-permute-start(bf16[128,2304]{1,0:T(8,128)(2,1)S(1)} %collective-permute-done.27.refs_1_), channel_id=1, source_target_pairs={{0,4},{4,0},{8,12},{12,8},{16,20},{20,16},{24,28},{28,24},{1,5},{5... | collective-permute-start | bytes 1769480 | tf_op jit(solution)/shard_map/ppermute | solution.py:76
  304.6 23.0 %collective-permute-start.32 = (bf16[128,2304]{1,0:T(8,128)(2,1)S(1)}, bf16[128,2304]{1,0:T(8,128)(2,1)}, u32[]{:S(2)}, u32[]{:S(2)}) collective-permute-start(bf16[128,2304]{1,0:T(8,128)(2,1)S(1)} %collective-permute-done.28.refs_0_.refs_2_), channel_id=1, source_target_pairs={{0,4},{4,0},{8,12},{12,8},{16,20},{20,16},{24,28},{28,24},{1,5},{5... | collective-permute-start | bytes 1769480 | tf_op jit(solution)/shard_map/ppermute | solution.py:76
  316.8 10.8 %collective-permute-start.33 = (bf16[128,2304]{1,0:T(8,128)(2,1)S(1)}, bf16[128,2304]{1,0:T(8,128)(2,1)}, u32[]{:S(2)}, u32[]{:S(2)}) collective-permute-start(bf16[128,2304]{1,0:T(8,128)(2,1)S(1)} %collective-permute-done.29.refs_1_.refs_3_), channel_id=1, source_target_pairs={{0,4},{4,0},{8,12},{12,8},{16,20},{20,16},{24,28},{28,24},{1,5},{5... | collective-permute-start | bytes 1769480 | tf_op jit(solution)/shard_map/ppermute | solution.py:76
  339.3 186.2 %reduce-scatter.5.cloned.1.call-start = ((), (), s32[]{:S(2)}) async-start(), calls=%async_computation.8 | async-start | bytes 13271040 | tf_op jit(solution)/shard_map/reduce_scatter | solution.py:757
  353.5 15.2 %collective-permute-start.34 = (bf16[128,2304]{1,0:T(8,128)(2,1)}, bf16[128,2304]{1,0:T(8,128)(2,1)S(1)}, u32[]{:S(2)}, u32[]{:S(2)}) collective-permute-start(bf16[128,2304]{1,0:T(8,128)(2,1)} %get-tuple-element.193.refs_1_), channel_id=1, source_target_pairs={{0,8},{4,12},{8,0},{12,4},{16,24},{20,28},{24,16},{28,20},{1,9},{5... | collective-permute-start | bytes 1769480 | tf_op jit(solution)/shard_map/ppermute | solution.py:76
  355.0 16.6 %collective-permute-start.38 = (bf16[2,256,1152]{2,1,0:T(8,128)(2,1)S(1)}, bf16[2,256,1152]{2,1,0:T(8,128)(2,1)}, u32[]{:S(2)}, u32[]{:S(2)}) collective-permute-start(bf16[2,256,1152]{2,1,0:T(8,128)(2,1)S(1)} %copy-done.22), channel_id=1, source_target_pairs={{0,4},{4,0},{8,12},{12,8},{16,20},{20,16},{24,28},{28,24},{1,5},{5... | collective-permute-start | bytes 3538952 | tf_op jit(solution)/shard_map/ppermute | solution.py:76
  356.0 15.6 %collective-permute-start.37 = (bf16[2,256,1152]{2,1,0:T(8,128)(2,1)S(1)}, bf16[2,256,1152]{2,1,0:T(8,128)(2,1)}, u32[]{:S(2)}, u32[]{:S(2)}) collective-permute-start(bf16[2,256,1152]{2,1,0:T(8,128)(2,1)S(1)} %copy-done.21), channel_id=1, source_target_pairs={{0,4},{4,0},{8,12},{12,8},{16,20},{20,16},{24,28},{28,24},{1,5},{5... | collective-permute-start | bytes 3538952 | tf_op jit(solution)/shard_map/ppermute | solution.py:76
  368.7 22.5 %collective-permute-start.35 = (bf16[128,2304]{1,0:T(8,128)(2,1)}, bf16[128,2304]{1,0:T(8,128)(2,1)}, u32[]{:S(2)}, u32[]{:S(2)}) collective-permute-start(bf16[128,2304]{1,0:T(8,128)(2,1)} %get-tuple-element.196.refs_0_), channel_id=1, source_target_pairs={{0,8},{4,12},{8,0},{12,4},{16,24},{20,28},{24,16},{28,20},{1,9},{5... | collective-permute-start | bytes 1769480 | tf_op jit(solution)/shard_map/ppermute | solution.py:76
  370.6 25.5 %collective-permute-start.36 = (bf16[128,2304]{1,0:T(8,128)(2,1)S(1)}, bf16[128,2304]{1,0:T(8,128)(2,1)S(1)}, u32[]{:S(2)}, u32[]{:S(2)}) collective-permute-start(bf16[128,2304]{1,0:T(8,128)(2,1)S(1)} %add_convert_fusion.1), channel_id=1, source_target_pairs={{0,16},{4,20},{8,24},{12,28},{16,0},{20,4},{24,8},{28,12},{1,17},{... | collective-permute-start | bytes 1769480 | tf_op jit(solution)/shard_map/ppermute | solution.py:76
  401.8 28.8 %collective-permute-start.39 = (bf16[128,2304]{1,0:T(8,128)(2,1)}, bf16[128,2304]{1,0:T(8,128)(2,1)S(1)}, u32[]{:S(2)}, u32[]{:S(2)}) collective-permute-start(bf16[128,2304]{1,0:T(8,128)(2,1)} %get-tuple-element.210.s0.refs_0_), channel_id=1, source_target_pairs={{0,16},{4,20},{8,24},{12,28},{16,0},{20,4},{24,8},{28,12},{1,17},{... | collective-permute-start | bytes 1769480 | tf_op jit(solution)/shard_map/ppermute | solution.py:76
  405.0 25.6 %collective-permute-start.40 = (bf16[128,2304]{1,0:T(8,128)(2,1)}, bf16[128,2304]{1,0:T(8,128)(2,1)S(1)}, u32[]{:S(2)}, u32[]{:S(2)}) collective-permute-start(bf16[128,2304]{1,0:T(8,128)(2,1)} %get-tuple-element.210.s0.refs_0_), channel_id=1, source_target_pairs={{0,8},{4,12},{8,0},{12,4},{16,24},{20,28},{24,16},{28,20},{1,9},{5... | collective-permute-start | bytes 1769480 | tf_op jit(solution)/shard_map/ppermute | solution.py:76
  430.6 15.3 %collective-permute-start.41 = (bf16[128,2304]{1,0:T(8,128)(2,1)S(1)}, bf16[128,2304]{1,0:T(8,128)(2,1)}, u32[]{:S(2)}, u32[]{:S(2)}) collective-permute-start(bf16[128,2304]{1,0:T(8,128)(2,1)S(1)} %collective-permute-done.39.s2.refs_2_), channel_id=1, source_target_pairs={{0,8},{4,12},{8,0},{12,4},{16,24},{20,28},{24,16},{28,20},{1,9},{5... | collective-permute-start | bytes 1769480 | tf_op jit(solution)/shard_map/ppermute | solution.py:76
  432.9 52.2 %collective-permute-start.44 = (bf16[512,2304]{1,0:T(8,128)(2,1)}, bf16[512,2304]{1,0:T(8,128)(2,1)}, u32[]{:S(2)}, u32[]{:S(2)}) collective-permute-start(bf16[512,2304]{1,0:T(8,128)(2,1)} %get-tuple-element.223.refs_0_), channel_id=1, source_target_pairs={{0,4},{4,0},{8,12},{12,8},{16,20},{20,16},{24,28},{28,24},{1,5},{5... | collective-permute-start | bytes 7077896 | tf_op jit(solution)/shard_map/ppermute | solution.py:76
  445.9 49.7 %all-to-all-start = ((bf16[8,72,1152]{2,1,0:T(8,128)(2,1)}), bf16[8,72,1152]{2,1,0:T(8,128)(2,1)S(1)}, u32[]{:S(2)}, u32[]{:S(2)}) async-start(bf16[8,72,1152]{2,1,0:T(8,128)(2,1)} %bitcast.109), calls=%async_computation.1 | async-start | bytes 2654208 | tf_op jit(solution)/shard_map/all_to_all | solution.py:660
  464.8 3.5 collective-permute-start.42
  465.4 12.8 %collective-permute-start.46 = (bf16[128,2304]{1,0:T(8,128)(2,1)S(1)}, bf16[128,2304]{1,0:T(8,128)(2,1)S(1)}, u32[]{:S(2)}, u32[]{:S(2)}) collective-permute-start(bf16[128,2304]{1,0:T(8,128)(2,1)S(1)} %copy-done.24), channel_id=1, source_target_pairs={{0,4},{4,0},{8,12},{12,8},{16,20},{20,16},{24,28},{28,24},{1,5},{5... | collective-permute-start | bytes 1769480 | tf_op jit(solution)/shard_map/ppermute | solution.py:76
  465.5 2.4 collective-permute-start.50
  466.0 14.2 %collective-permute-start.47 = (bf16[128,2304]{1,0:T(8,128)(2,1)}, bf16[128,2304]{1,0:T(8,128)(2,1)}, u32[]{:S(2)}, u32[]{:S(2)}) collective-permute-start(bf16[128,2304]{1,0:T(8,128)(2,1)} %copy-done.27), channel_id=1, source_target_pairs={{0,4},{4,0},{8,12},{12,8},{16,20},{20,16},{24,28},{28,24},{1,5},{5... | collective-permute-start | bytes 1769480 | tf_op jit(solution)/shard_map/ppermute | solution.py:76
  467.9 12.4 %collective-permute-start.48 = (bf16[128,2304]{1,0:T(8,128)(2,1)S(1)}, bf16[128,2304]{1,0:T(8,128)(2,1)}, u32[]{:S(2)}, u32[]{:S(2)}) collective-permute-start(bf16[128,2304]{1,0:T(8,128)(2,1)S(1)} %copy-done.26), channel_id=1, source_target_pairs={{0,4},{4,0},{8,12},{12,8},{16,20},{20,16},{24,28},{28,24},{1,5},{5... | collective-permute-start | bytes 1769480 | tf_op jit(solution)/shard_map/ppermute | solution.py:76
  468.3 12.0 %collective-permute-start.49 = (bf16[128,2304]{1,0:T(8,128)(2,1)}, bf16[128,2304]{1,0:T(8,128)(2,1)}, u32[]{:S(2)}, u32[]{:S(2)}) collective-permute-start(bf16[128,2304]{1,0:T(8,128)(2,1)} %collective-permute-done.41.s3.refs_3_), channel_id=1, source_target_pairs={{0,4},{4,0},{8,12},{12,8},{16,20},{20,16},{24,28},{28,24},{1,5},{5... | collective-permute-start | bytes 1769480 | tf_op jit(solution)/shard_map/ppermute | solution.py:76
  478.2 7.0 %collective-permute-start.45 = (bf16[1,512,512]{2,1,0:T(8,128)(2,1)}, bf16[1,512,512]{2,1,0:T(8,128)(2,1)S(1)}, u32[]{:S(2)}, u32[]{:S(2)}) collective-permute-start(bf16[1,512,512]{2,1,0:T(8,128)(2,1)} %get-tuple-element.225), channel_id=1, source_target_pairs={{0,4},{4,0},{8,12},{12,8},{16,20},{20,16},{24,28},{28,24},{1,5},{5... | collective-permute-start | bytes 1572872 | tf_op jit(solution)/shard_map/ppermute | solution.py:76
  480.2 15.4 %collective-permute-start.43 = (bf16[128,2304]{1,0:T(8,128)(2,1)}, bf16[128,2304]{1,0:T(8,128)(2,1)}, u32[]{:S(2)}, u32[]{:S(2)}) collective-permute-start(bf16[128,2304]{1,0:T(8,128)(2,1)} %get-tuple-element.221), channel_id=1, source_target_pairs={{0,8},{4,12},{8,0},{12,4},{16,24},{20,28},{24,16},{28,20},{1,9},{5... | collective-permute-start | bytes 1769480 | tf_op jit(solution)/shard_map/ppermute | solution.py:76
  495.6 26.0 %collective-permute-start.51 = (bf16[128,2304]{1,0:T(8,128)(2,1)}, bf16[128,2304]{1,0:T(8,128)(2,1)}, u32[]{:S(2)}, u32[]{:S(2)}) collective-permute-start(bf16[128,2304]{1,0:T(8,128)(2,1)} %get-tuple-element.231), channel_id=1, source_target_pairs={{0,8},{4,12},{8,0},{12,4},{16,24},{20,28},{24,16},{28,20},{1,9},{5... | collective-permute-start | bytes 1769480 | tf_op jit(solution)/shard_map/ppermute | solution.py:76
  498.7 26.8 %collective-permute-start.52 = (bf16[128,2304]{1,0:T(8,128)(2,1)S(1)}, bf16[128,2304]{1,0:T(8,128)(2,1)}, u32[]{:S(2)}, u32[]{:S(2)}) collective-permute-start(bf16[128,2304]{1,0:T(8,128)(2,1)S(1)} %add_convert_fusion), channel_id=1, source_target_pairs={{0,16},{4,20},{8,24},{12,28},{16,0},{20,4},{24,8},{28,12},{1,17},{... | collective-permute-start | bytes 1769480 | tf_op jit(solution)/shard_map/ppermute | solution.py:76
  503.2 14.5 %collective-permute-start.53 = (bf16[288,772]{1,0:T(8,128)(2,1)S(1)}, bf16[288,772]{1,0:T(8,128)(2,1)S(1)}, u32[]{:S(2)}, u32[]{:S(2)}) collective-permute-start(bf16[288,772]{1,0:T(8,128)(2,1)S(1)} %get-tuple-element.286), channel_id=1, source_target_pairs={{0,1},{1,0},{2,3},{3,2},{4,5},{5,4},{6,7},{7,6},{8,9},{9,8},{10,11... | collective-permute-start | bytes 1334024 | tf_op jit(solution)/shard_map/ppermute | solution.py:76
  503.2 14.5 %collective-permute-start.54 = (bf16[288,772]{1,0:T(8,128)(2,1)S(1)}, bf16[288,772]{1,0:T(8,128)(2,1)}, u32[]{:S(2)}, u32[]{:S(2)}) collective-permute-start(bf16[288,772]{1,0:T(8,128)(2,1)S(1)} %get-tuple-element.288), channel_id=1, source_target_pairs={{0,2},{1,3},{2,0},{3,1},{4,6},{5,7},{6,4},{7,5},{8,10},{9,11},{10,... | collective-permute-start | bytes 1334024 | tf_op jit(solution)/shard_map/ppermute | solution.py:76
  525.6 64.9 %all-to-all-start.1 = ((bf16[8,72,2304]{2,1,0:T(8,128)(2,1)}), bf16[8,72,2304]{2,1,0:T(8,128)(2,1)S(1)}, u32[]{:S(2)}, u32[]{:S(2)}) async-start(bf16[8,72,2304]{2,1,0:T(8,128)(2,1)} %bitcast.106), calls=%async_computation.3 | async-start | bytes 5308416 | tf_op jit(solution)/shard_map/all_to_all | solution.py:660
  542.1 23.5 %collective-permute-start.56 = (bf16[576,772]{0,1:T(8,128)(2,1)}, bf16[576,772]{0,1:T(8,128)(2,1)}, u32[]{:S(2)}, u32[]{:S(2)}) collective-permute-start(bf16[576,772]{0,1:T(8,128)(2,1)} %copy.43), channel_id=1, source_target_pairs={{0,2},{1,3},{2,0},{3,1},{4,6},{5,7},{6,4},{7,5},{8,10},{9,11},{10,... | collective-permute-start | bytes 2668040 | tf_op jit(solution)/shard_map/ppermute | solution.py:76
  546.6 23.5 %collective-permute-start.55 = (bf16[576,772]{0,1:T(8,128)(2,1)}, bf16[576,772]{0,1:T(8,128)(2,1)}, u32[]{:S(2)}, u32[]{:S(2)}) collective-permute-start(bf16[576,772]{0,1:T(8,128)(2,1)} %copy.41), channel_id=1, source_target_pairs={{0,1},{1,0},{2,3},{3,2},{4,5},{5,4},{6,7},{7,6},{8,9},{9,8},{10,11... | collective-permute-start | bytes 2668040 | tf_op jit(solution)/shard_map/ppermute | solution.py:76
  590.5 30.4 %all-to-all-start.2 = ((bf16[8,72,772]{2,1,0:T(8,128)(2,1)}), bf16[8,72,772]{2,1,0:T(8,128)(2,1)}, u32[]{:S(2)}, u32[]{:S(2)}) async-start(bf16[8,72,772]{2,1,0:T(8,128)(2,1)} %bitcast.105), calls=%async_computation.4 | async-start | bytes 2064384 | tf_op jit(solution)/shard_map/all_to_all | solution.py:660
  (61 other events, 656.6 us)
Sparse Core Ops, SparseCore 0:
  12.6 130.2 all-gather.2
  145.4 64.2 all-gather.4
  339.4 61.0 reduce-scatter.2
  403.5 105.0 reduce-scatter.4
